TPU v7x, 128 devices: a whole 4x4x4 slice. The times are simulated.
128 devices in a mesh: seq: 16 (over y, x), row: 4 (over z), col: 2 (over core).
Axes of the slice: x: 4, y: 4, z: 4, core: 2. Of those that a mesh axis runs over, the one named last changes fastest.
Arguments:
- student: bfloat16 [12288, 8192], P(('seq', 'row'), 'col'), may hold values from -130 to 130
- teacher: bfloat16 [12288, 8192], P('seq', ('row', 'col')), may hold values from -130 to 130
- starts: int32 [12288], P('seq'), may hold values from 0 to 12284, as said below
- weights: int32 [12288, 4], P('seq'), may hold values from 1 to 16
- counts: int32 [16, 4], P('seq'), may hold values from 2 to 192, as said below
Outputs:
- alignment: float32 [2, 16, 256, 8192], P('col', 'seq', None, 'row')
Inputs may be any that keep to these rules, and one draw needn't show every extreme that they name: counts[s, r] live student tokens are the first slots of block s * 4 + r of 192 slots; in every draw some block is full. For a student token of block b, starts lies between b * 192 - 16 and (b + 1) * 192 + 12.
All inputs are finite; a program needn't handle non-finite values.
Results may differ from a plain program's by a relative error of at most 0.0013.
Values may be sent and summed in bfloat16 or wider, within the bound.
No kernel may reach another device: no remote copies, remote signals or barrier semaphores. Data moves between devices by JAX's collectives and lax.ppermute only.
A program may use at most 128 MiB of HBM per device.

v0:
```python
import jax
import jax.numpy as jnp
from jax import lax
from jax.sharding import PartitionSpec as P

SUB = 192
BAND = 4
HALO = 16


epsilon = 1e-05


def with_halo(x, sides, width):
    for axis, dim in sides:
        size, length = (lax.axis_size(axis), x.shape[dim])
        up = [(i, (i + 1) % size) for i in range(size - 1)]
        down = [(j, i) for i, j in up]
        last = lax.slice_in_dim(x, length - width, length, axis=dim)
        leading = lax.slice_in_dim(x, 0, width, axis=dim)
        before = lax.ppermute(last, axis, up)
        after = lax.ppermute(leading, axis, down)
        x = jnp.concatenate([before, x, after], axis=dim)
    return x


def column_sums(values, keep_rows):
    return jnp.sum(values * keep_rows, axis=0)


def scaled_half(centered, column_var):
    return (centered * lax.rsqrt(column_var + epsilon)).astype(jnp.bfloat16)


def per_device(student, teacher, starts, weights, counts):
    shard_rows = starts.shape[0]
    row_slot = lax.axis_index("row")
    count_row = counts[0]
    own_count = jnp.sum(jnp.where(jnp.arange(count_row.shape[0]) == row_slot, count_row, 0))
    block_keep = (jnp.arange(SUB) < own_count).astype(jnp.float32)[:, None]
    shard_keep = (jnp.arange(shard_rows) % SUB < jnp.repeat(count_row, SUB)).astype(jnp.float32)[
        :, None
    ]
    shard_tokens = jnp.sum(count_row).astype(jnp.float32)
    padded = with_halo(teacher, (("seq", 0),), HALO)
    anchor = lax.axis_index("seq") * shard_rows - HALO
    local_starts = starts - anchor
    weighted = jnp.zeros((shard_rows, teacher.shape[1]), jnp.float32)
    for band_pos in range(BAND):
        rows_here = jnp.take(padded, local_starts + band_pos, axis=0)
        weighted = weighted + weights[:, band_pos : band_pos + 1].astype(
            jnp.float32
        ) * rows_here.astype(jnp.float32)
    pooled = weighted / jnp.sum(weights, axis=1, keepdims=True).astype(jnp.float32)
    total_tokens, pooled_sum = lax.psum((shard_tokens, column_sums(pooled, shard_keep)), "seq")
    pooled_dev = (pooled - pooled_sum / total_tokens) * shard_keep
    pooled_var = lax.psum(jnp.sum(pooled_dev * pooled_dev, axis=0), "seq") / total_tokens
    pooled_std = scaled_half(pooled_dev, pooled_var)
    student_values = student.astype(jnp.float32)
    student_sum = lax.psum(column_sums(student_values, block_keep), ("seq", "row"))
    student_dev = (student_values - student_sum / total_tokens) * block_keep
    student_var = (
        lax.psum(jnp.sum(student_dev * student_dev, axis=0), ("seq", "row")) / total_tokens
    )
    student_std = scaled_half(student_dev, student_var)
    norm_panel = lax.all_gather(student_std, "row", axis=0, tiled=True)
    pooled_panel = lax.all_gather(pooled_std, "col", axis=1, tiled=True)
    seq_count = lax.axis_size("seq")
    own_rows = norm_panel.shape[1] // seq_count
    product = lax.dot_general(
        norm_panel, pooled_panel, (((0,), (0,)), ((), ())), preferred_element_type=jnp.float32
    )
    rounded = product.astype(jnp.bfloat16).reshape(seq_count, own_rows, product.shape[1])
    arrived = lax.all_to_all(rounded, "seq", split_axis=0, concat_axis=0, tiled=True)
    summed = jnp.sum(arrived.astype(jnp.float32), axis=0)
    scaled = summed / jnp.sqrt(total_tokens)
    return scaled.reshape(1, 1, scaled.shape[0], scaled.shape[1])


def solution(mesh):
    placed = (
        P(("seq", "row"), "col"),
        P("seq", ("row", "col")),
        P("seq"),
        P("seq", None),
        P("seq", None),
    )
    return jax.shard_map(
        per_device,
        mesh=mesh,
        in_specs=placed,
        out_specs=P("col", "seq", None, "row"),
        check_vma=False,
    )
```

profile of v0, /device:TPU:0, one launch (start us, length us, event | category | flops | bytes accessed | tf_op | source)
XLA Modules:
  0.0 1164.3 jit_solution(725925008590990971)
XLA Ops:
  6.5 0.0 all-gather.5.cloned.1.call-start
  6.5 0.8 fusion.12
  7.3 1.3 collective-permute-start.1
  8.6 4.5 collective-permute-start
  13.2 0.7 broadcast_in_dim.24
  13.9 0.1 reshape.49
  14.0 0.9 convert_reduce_fusion.4
  14.9 0.7 compare_and_fusion.3
  15.6 1.3 reduce_sum.74
  16.9 0.7 reduce_sum.76
  18.3 0.0 collective-permute-done
  18.3 1.5 constant_dynamic-update-slice_fusion.1
  19.9 0.0 collective-permute-done.1
  19.9 3.6 gather_fusion.3
  23.4 3.6 gather_fusion.2
  27.0 3.6 gather_fusion.1
  30.6 3.5 gather_fusion
  34.1 4.7 multiply_reduce_fusion.1
  38.8 40.0 %all-reduce = (f32[]{:T(128)}, f32[1024]{0:T(1024)S(1)}) all-reduce(f32[]{:T(128)S(6)} %convert_element_type.66, f32[1024]{0:T(1024)S(1)} %get-tuple-element.12), channel_id=1, replica_groups=mesh['seq'=16,'row'=4,'col'=2] {'seq'}, use_global_device_ids=true, to_apply=%region_4.5 | all-reduce | flops 1025 | bytes 8200 | tf_op jit(solution)/shard_map/psum | solution.py:55
  78.9 0.7 broadcast_divide_fusion.1
  79.5 0.5 multiply_reduce_fusion
  80.0 35.5 %psum.39 = f32[1024]{0:T(1024)S(1)} all-reduce(f32[1024]{0:T(1024)S(1)} %multiply_reduce_fusion), channel_id=1, replica_groups=mesh['seq'=16,'row'=4,'col'=2] {'seq'}, use_global_device_ids=true, to_apply=%region_11.13 | all-reduce | flops 1024 | bytes 8192 | tf_op jit(solution)/shard_map/psum | solution.py:57
  115.5 0.7 add_rsqrt_fusion.1
  116.2 0.0 copy-start.1
  116.2 1.6 multiply_convert_fusion
  117.8 0.0 copy-start
  117.8 0.0 all-gather.5.cloned.1.call-update
  117.8 0.0 all-gather.3.cloned.1.call-start
  117.9 0.0 copy-done.1
  117.9 0.6 fusion.11
  118.5 0.6 compare_convert_fusion
  119.2 1.8 fusion
  121.0 346.9 %psum.35 = f32[4096]{0:T(1024)S(1)} all-reduce(f32[4096]{0:T(1024)S(1)} %fusion), channel_id=1, replica_groups=mesh['seq'=16,'row'=4,'col'=2] {'seq','row'}, use_global_device_ids=true, to_apply=%region_2.3 | all-reduce | flops 4096 | bytes 32768 | tf_op jit(solution)/shard_map/psum | solution.py:60
  467.9 0.7 broadcast_divide_fusion
  468.6 0.0 copy-done
  468.6 0.6 fusion.4
  469.2 341.7 %psum.37 = f32[4096]{0:T(1024)S(1)} all-reduce(f32[4096]{0:T(1024)S(1)} %fusion.4), channel_id=1, replica_groups=mesh['seq'=16,'row'=4,'col'=2] {'seq','row'}, use_global_device_ids=true, to_apply=%region_6.7 | all-reduce | flops 4096 | bytes 32768 | tf_op jit(solution)/shard_map/psum | solution.py:63
  810.9 0.7 add_rsqrt_fusion
  811.5 1.7 fusion.5
  813.2 0.0 all-gather.3.cloned.1.call-update
  813.2 0.0 all-gather.5.cloned.1.call-done
  813.3 59.4 %all-gather.3.cloned.1.call-done = bf16[768,4096]{1,0:T(8,128)(2,1)} async-done(((bf16[192,4096]{1,0:T(8,128)(2,1)}), bf16[768,4096]{1,0:T(8,128)(2,1)}) %all-gather.3.cloned.1.call-update) | async-done | bytes 6291472 | tf_op jit(solution)/shard_map/all_gather | solution.py:66
  872.7 19.6 %convolution_convert_fusion = bf16[4096,2048]{1,0:T(8,128)(2,1)} fusion(bf16[768,4096]{1,0:T(8,128)(2,1)} %all-gather.3.cloned.1.call-done, bf16[768,2048]{1,0:T(8,128)(2,1)} %all-gather.5.cloned.1.call-done), kind=kOutput, calls=%fused_computation.5 | convolution fusion | flops 12893290496 | bytes 26214400 | tf_op jit(solution)/shard_map/dot_general | solution.py:70
  892.2 6.9 all-to-all-start
  899.8 249.0 %all-to-all-done = bf16[16,256,2048]{2,1,0:T(8,128)(2,1)} async-done(((bf16[16,256,2048]{2,1,0:T(8,128)(2,1)}), bf16[16,256,2048]{2,1,0:T(8,128)(2,1)}, u32[]{:S(2)}, u32[]{:S(2)}) %all-to-all-start) | async-done | bytes 16777248 | tf_op jit(solution)/shard_map/all_to_all | solution.py:74
  1148.8 7.1 convert_reduce_fusion
  1156.0 1.5 divide_bitcast_fusion
  (6 shorter events, 0.0 us)
Async XLA Ops:
  6.5 806.7 %all-gather.5.cloned.1.call-start = ((), (), s32[]{:S(2)}) async-start(), calls=%async_computation.2 | async-start | bytes 4718592 | tf_op jit(solution)/shard_map/all_gather | solution.py:67
  7.3 12.5 %collective-permute-start.1 = (bf16[16,1024]{1,0:T(8,128)(2,1)S(1)}, bf16[16,1024]{1,0:T(8,128)(2,1)S(1)}, u32[]{:S(2)}, u32[]{:S(2)}) collective-permute-start(bf16[16,1024]{1,0:T(8,128)(2,1)S(1)} %get-tuple-element.22), channel_id=1, source_target_pairs={{8,0},{16,8},{24,16},{32,24},{40,32},{48,40},{56,48},{64,56},{72,6... | collective-permute-start | bytes 98312 | tf_op jit(solution)/shard_map/ppermute | solution.py:22
  8.6 9.7 collective-permute-start
  116.2 1.7 copy-start.1
  117.8 350.8 %copy-start = (bf16[192,4096]{1,0:T(8,128)(2,1)S(1)}, bf16[192,4096]{1,0:T(8,128)(2,1)}, u32[]{:S(2)}) copy-start(bf16[192,4096]{1,0:T(8,128)(2,1)} %param.7) | copy-start | bytes 4718596
  117.8 754.8 %all-gather.3.cloned.1.call-start = ((), (), s32[]{:S(2)}) async-start(), calls=%async_computation.1 | async-start | bytes 7864320 | tf_op jit(solution)/shard_map/all_gather | solution.py:66
  892.2 256.6 %all-to-all-start = ((bf16[16,256,2048]{2,1,0:T(8,128)(2,1)}), bf16[16,256,2048]{2,1,0:T(8,128)(2,1)}, u32[]{:S(2)}, u32[]{:S(2)}) async-start(bf16[16,256,2048]{2,1,0:T(8,128)(2,1)} %bitcast.7), calls=%async_computation | async-start | bytes 33554432 | tf_op jit(solution)/shard_map/all_to_all | solution.py:74
Sparse Core Ops, SparseCore 0:
  117.9 13.5 all-gather.4
  813.3 59.2 all-gather.2
where the time goes:
time: 1170 us; the launch traced here: 1160 us
  blocking collectives  764 us (65%)
  waiting for transfers between devices  308 us (26%)
  other arithmetic  27.1 us (2%)
  matrix products  19.6 us (2%)
  local copies, waits for them, and re-layouts  17.4 us (1%)
  between operations  15 us (1%)
  starting transfers between devices  12.7 us (1%)
    psum x1, blocking collectives, per_device(): lax.psum(column_sums(student_values, block_keep), ('seq', 'row'))  347 us
    psum x1, blocking collectives, per_device(): lax.psum(jnp.sum(student_dev * student_dev, axis=0), ('seq', 'row'))  342 us
    all_to_all x1, waiting for transfers between devices, per_device(): lax.all_to_all(rounded, 'seq', split_axis=0, concat_axis=0, tiled=True)  249 us
    all_gather x1, waiting for transfers between devices, per_device(): norm_panel = lax.all_gather(student_std, 'row', axis=0, tiled=True)  59.4 us
    psum x1, blocking collectives, per_device(): lax.psum((shard_tokens, column_sums(pooled, shard_keep)), 'seq')  40 us
    psum x1, blocking collectives, per_device(): lax.psum(jnp.sum(pooled_dev * pooled_dev, axis=0), 'seq') / total_tokens  35.5 us
  transfers between devices with their start and end apart: 5, of which 2 were waited for; matrix products, arithmetic and copies ran while one was open for 1% of the time, Pallas kernels for 0%

commit v1 on v0

v1 whole, which is shorter than its diff:
```python
import jax
import jax.numpy as jnp
from jax import lax
from jax.experimental import pallas as pl
from jax.experimental.pallas import tpu as pltpu
from jax.sharding import Mesh
from jax.sharding import PartitionSpec as P

SUB = 192
BAND = 4
HALO = 16
SIDE = 4
epsilon = 1e-05


def ring(value, axis, step):
    return lax.ppermute(value, axis, [(i, (i + step) % SIDE) for i in range(SIDE)])


def ring_all(value, axis):
    return [value, ring(value, axis, 1), ring(value, axis, -1), ring(value, axis, 2)]


def swap(value):
    return lax.ppermute(value, "col", [(0, 1), (1, 0)])


def pool_kernel(counts, before, teacher, after, meta, centered, stats, mix, share, pooled):
    window = SUB + 2 * HALO
    blocks = SIDE

    @pl.when(pl.program_id(0) == 0)
    def _():
        for r in range(blocks):
            rows = slice(r * SUB, (r + 1) * SUB)
            place = lax.broadcasted_iota(jnp.int32, (SUB, window), 1)
            local = meta[rows, 0:1] - (r * SUB - HALO)
            found = jnp.zeros((SUB, window), jnp.int32)
            whole = jnp.zeros((SUB, 1), jnp.int32)
            for k in range(BAND):
                weight = meta[rows, 1 + k : 2 + k]
                found = found + jnp.where(place == local + k, weight, 0)
                whole = whole + weight
            mix[rows, :] = found.astype(jnp.float32).astype(jnp.bfloat16)
            share[rows, :] = jnp.broadcast_to(whole.astype(jnp.float32), (SUB, 128))

    total = jnp.zeros((1, teacher.shape[1]), jnp.float32)
    alive = jnp.int32(0)
    length = teacher.shape[0]
    for r in range(blocks):
        rows = slice(r * SUB, (r + 1) * SUB)
        low, high = r * SUB - HALO, (r + 1) * SUB + HALO
        parts = [teacher[max(low, 0) : min(high, length), :]]
        if low < 0:
            parts = [before[...]] + parts
        if high > length:
            parts = parts + [after[...]]
        seen = jnp.concatenate(parts, axis=0) if len(parts) > 1 else parts[0]
        value = jnp.dot(mix[rows, :], seen, preferred_element_type=jnp.float32)
        value = value / share[rows, 0:1]
        pooled[rows, :] = value
        live = lax.broadcasted_iota(jnp.int32, value.shape, 0) < counts[r]
        total = total + jnp.sum(jnp.where(live, value, 0.0), axis=0, keepdims=True)
        alive = alive + counts[r]
    mean = total / alive.astype(jnp.float32)
    square = jnp.zeros_like(total)
    for r in range(blocks):
        rows = slice(r * SUB, (r + 1) * SUB)
        value = pooled[rows, :]
        live = lax.broadcasted_iota(jnp.int32, value.shape, 0) < counts[r]
        dev = jnp.where(live, value - mean, 0.0)
        centered[rows, :] = dev.astype(jnp.bfloat16)
        square = square + jnp.sum(dev * dev, axis=0, keepdims=True)
    stats[0:1, :] = total
    stats[1:2, :] = square
    stats[2:3, :] = jnp.broadcast_to(alive.astype(jnp.float32), total.shape)


def pool(counts, before, teacher, after, meta):
    rows, columns = teacher.shape
    tile = 256
    return pl.pallas_call(
        pool_kernel,
        grid=(columns // tile,),
        in_specs=[
            pl.BlockSpec(memory_space=pltpu.SMEM),
            pl.BlockSpec((HALO, tile), lambda j: (0, j)),
            pl.BlockSpec((rows, tile), lambda j: (0, j)),
            pl.BlockSpec((HALO, tile), lambda j: (0, j)),
            pl.BlockSpec(meta.shape, lambda j: (0, 0)),
        ],
        out_specs=[
            pl.BlockSpec((rows, tile), lambda j: (0, j)),
            pl.BlockSpec((3, tile), lambda j: (0, j)),
        ],
        out_shape=[
            jax.ShapeDtypeStruct((rows, columns), jnp.bfloat16),
            jax.ShapeDtypeStruct((3, columns), jnp.float32),
        ],
        scratch_shapes=[
            pltpu.VMEM((rows, SUB + 2 * HALO), jnp.bfloat16),
            pltpu.VMEM((rows, 128), jnp.float32),
            pltpu.VMEM((rows, tile), jnp.float32),
        ],
        compiler_params=pltpu.CompilerParams(vmem_limit_bytes=32 * 2**20),
        cost_estimate=pl.CostEstimate(
            flops=2 * rows * 224 * columns, bytes_accessed=6 * rows * columns, transcendentals=0
        ),
    )(counts, before, teacher, after, meta)


def product_kernel(place, a0, a1, a2, a3, b0, b1, b2, b3, mean, out, sums):
    z = place[0]
    order = (0, SIDE - 1, 1, 2)
    mine = []
    for step in order:
        first = pl.multiple_of(lax.rem(z + step, SIDE) * SUB, 16)
        mine.append(
            jnp.concatenate([b[pl.ds(first, SUB), :] for b in (b0, b1, b2, b3)], axis=0)
        )

    @pl.when(pl.program_id(0) == 0)
    def _():
        ones = jnp.ones((16, mine[0].shape[0]), jnp.bfloat16)
        sums[...] = sum(jnp.dot(ones, m, preferred_element_type=jnp.float32) for m in mine)

    acc = None
    for a, m in zip((a0, a1, a2, a3), mine):
        term = jnp.dot(a[...], m, preferred_element_type=jnp.float32)
        acc = term if acc is None else acc + term
    out[...] = acc - mean[...] * sums[0:1, :]


def product(place, left, right, mean):
    rows, depth = left[0].shape
    columns = right[0].shape[1]
    part = rows // SIDE

    def slice_of(i, place):
        step = jnp.where(i == 0, 2, jnp.where(i == 1, 1, jnp.where(i == 2, 3, 0)))
        return (lax.rem(place[1] + step, SIDE), 0)

    spec = pltpu.PrefetchScalarGridSpec(
        num_scalar_prefetch=1,
        grid=(SIDE,),
        in_specs=[pl.BlockSpec((part, depth), slice_of)] * SIDE
        + [pl.BlockSpec(right[0].shape, lambda i, place: (0, 0))] * SIDE
        + [pl.BlockSpec((part, 1), slice_of)],
        out_specs=pl.BlockSpec((part, columns), lambda i, place: (i, 0)),
        scratch_shapes=[pltpu.VMEM((16, columns), jnp.float32)],
    )
    return pl.pallas_call(
        product_kernel,
        grid_spec=spec,
        out_shape=jax.ShapeDtypeStruct((rows, columns), jnp.float32),
        compiler_params=pltpu.CompilerParams(vmem_limit_bytes=40 * 2**20),
        cost_estimate=pl.CostEstimate(
            flops=2 * rows * depth * SIDE * columns,
            bytes_accessed=2 * SIDE * depth * (rows + columns) + 4 * rows * columns,
            transcendentals=0,
        ),
    )(place, *left, *right, mean)


def per_device(student, teacher, starts, weights, counts):
    y, x, z, c = (lax.axis_index(n) for n in ("y", "x", "row", "col"))
    shard = y * SIDE + x
    rows = starts.shape[0]
    width = student.shape[1] // SIDE
    part = width // SIDE

    by_x = student.reshape(SUB, SIDE, SIDE, part).transpose(2, 0, 1, 3).reshape(SIDE, SUB, width)

    def for_x(step):
        return lax.dynamic_index_in_dim(by_x, lax.rem(x + step, SIDE), 0, keepdims=False)

    got = [
        for_x(0),
        ring(for_x(1), "x", 1),
        ring(for_x(SIDE - 1), "x", -1),
        ring(for_x(2), "x", 2),
    ]

    up = [(i, (i + 1) % 16) for i in range(16)]
    down = [(j, i) for i, j in up]
    before = lax.ppermute(teacher[rows - HALO :], ("y", "x"), up)
    after = lax.ppermute(teacher[:HALO], ("y", "x"), down)
    meta = jnp.concatenate([(starts - shard * rows)[:, None], weights], axis=1)
    standard, stats = pool(counts[0], before, teacher, after, meta)
    columns = standard.shape[1]

    half = columns // 2
    right1 = ring(standard, "x", 1)
    left1 = ring(standard, "x", -1)
    far = [ring(right1[:, :half], "x", 1), ring(left1[:, half:], "x", -1)]
    own_sides = [
        [p[:, :half] for p in (standard, right1, left1)] + [far[0]],
        [p[:, half:] for p in (standard, right1, left1)] + [far[1]],
    ]
    t_standard, t_right1, t_left1 = swap(standard), swap(right1), swap(left1)
    t_far = [swap(f) for f in far]
    mate_sides = [
        [p[:, :half] for p in (t_standard, t_right1, t_left1)] + [t_far[0]],
        [p[:, half:] for p in (t_standard, t_right1, t_left1)] + [t_far[1]],
    ]

    block = jnp.concatenate(got, axis=0)
    turned = block.T
    z_up = ring(turned, "row", 1)
    z_down = ring(turned, "row", -1)
    z_far = jnp.concatenate(
        [ring(z_up[: width // 2], "row", 1), ring(z_down[width // 2 :], "row", -1)], axis=0
    )
    left = [turned, z_up, z_down, z_far]

    counts_row = jnp.pad(counts.astype(jnp.float32), ((0, 0), (0, columns - SIDE)))
    near = jnp.stack(ring_all(jnp.concatenate([stats, counts_row]), "x"))
    group_counts = near[:, 3, :SIDE]
    shards = jnp.concatenate(ring_all(near[:, :3], "y"), axis=0)
    t_sum, t_square, t_count = shards[:, 0], shards[:, 1], shards[:, 2]
    tokens = jnp.sum(t_count[:, 0])
    t_local = t_sum / t_count
    t_mean = jnp.sum(t_sum, axis=0) / tokens
    t_off = t_local - t_mean
    t_var = (jnp.sum(t_square, axis=0) + jnp.sum(t_count * t_off * t_off, axis=0)) / tokens
    t_scale = lax.rsqrt(t_var + epsilon)
    t_rows = jnp.concatenate([t_scale[None], t_off * t_scale])
    t_mate = swap(t_rows)

    own_counts = lax.dynamic_index_in_dim(group_counts, z, 1, keepdims=True)
    values = block.astype(jnp.float32).reshape(SIDE, SUB, width)
    live = (jnp.arange(SUB).astype(jnp.float32) < own_counts)[:, :, None]
    s_sum = jnp.sum(jnp.where(live, values, 0.0), axis=1)
    s_dev = jnp.where(live, values - (s_sum / own_counts)[:, None], 0.0)
    s_parts = jnp.stack([s_sum, jnp.sum(s_dev * s_dev, axis=1)])
    s_z = jnp.stack(ring_all(s_parts, "row"))
    z_counts = jnp.stack(
        [
            lax.dynamic_index_in_dim(group_counts, lax.rem(z + k, SIDE), 1, keepdims=True)
            for k in (0, SIDE - 1, 1, 2)
        ]
    )
    shard_count = jnp.sum(group_counts, axis=1, keepdims=True)
    shard_sum = jnp.sum(s_z[:, 0], axis=0)
    shard_off = s_z[:, 0] / z_counts - shard_sum / shard_count
    shard_square = jnp.sum(s_z[:, 1] + z_counts * shard_off * shard_off, axis=0)
    s_group = (jnp.sum(shard_sum, axis=0) / jnp.sum(shard_count))[:, None]
    s_all = jnp.stack(ring_all(jnp.stack([shard_sum, shard_square]), "y"))
    s_all = lax.dynamic_slice_in_dim(s_all, y * part, part, axis=3)
    s_all = s_all.transpose(1, 0, 2, 3).reshape(2, SIDE * SIDE, part)
    s_count = t_count[:, :1]
    s_mean = jnp.sum(s_all[0], axis=0) / tokens
    s_off = s_all[0] / s_count - s_mean
    s_var = (jnp.sum(s_all[1], axis=0) + jnp.sum(s_count * s_off * s_off, axis=0)) / tokens
    inverse = 1.0 / jnp.sqrt(tokens)
    s_scale = lax.rsqrt(s_var + epsilon) * inverse
    s_rows = s_off * s_scale * s_count

    place = jnp.stack([z, y]).astype(jnp.int32)

    def finish(sides, direction, t_rows):
        partial = product(place, left, sides, s_group)
        far_p, next_p, back_p, own_p = (partial[i * part : (i + 1) * part] for i in range(SIDE))
        if direction < 0:
            next_p, back_p = back_p, next_p
        u = ring(far_p.astype(jnp.bfloat16), "y", direction)
        w = ring(back_p.astype(jnp.bfloat16), "y", -direction)
        v = ring((next_p + u.astype(jnp.float32)).astype(jnp.bfloat16), "y", direction)
        between = lax.dot_general(
            s_rows, t_rows[1:], (((0,), (0,)), ((), ())), precision=lax.Precision.HIGHEST
        )
        inside = own_p + v.astype(jnp.float32) + w.astype(jnp.float32)
        return inside * s_scale[:, None] * t_rows[0] + between

    own_out = [
        finish(own_sides[0], 1, t_rows[:, :half]),
        finish(own_sides[1], -1, t_rows[:, half:]),
    ]
    mate_out = [
        finish(mate_sides[0], 1, t_mate[:, :half]),
        finish(mate_sides[1], -1, t_mate[:, half:]),
    ]
    own_out = jnp.concatenate(own_out, axis=1)
    mate_out = jnp.concatenate(mate_out, axis=1)
    first = jnp.where(c == 0, own_out, mate_out)
    second = jnp.where(c == 0, mate_out, own_out)
    return jnp.concatenate([first, second], axis=1)[None, None]


def solution(mesh):
    fine = Mesh(mesh.devices.reshape(SIDE, SIDE, SIDE, 2), ("y", "x", "row", "col"))
    seq = ("y", "x")
    placed = (
        P(seq + ("row",), "col"),
        P(seq, ("row", "col")),
        P(seq),
        P(seq, None),
        P(seq, None),
    )
    return jax.shard_map(
        per_device,
        mesh=fine,
        in_specs=placed,
        out_specs=P("col", seq, None, "row"),
        check_vma=False,
    )
```

time: 1170 us -> 213 us (0.18)
  blocking collectives: 764 us -> 0 us
  waiting for transfers between devices: 308 us -> 79.8 us
  starting transfers between devices: 12.7 us -> 53 us
  Pallas kernels: 0 us -> 32.9 us
  matrix products: 19.6 us -> 2.89 us
  between operations: 15 us -> 1.34 us
    psum x4 -> x0, blocking collectives: 764 us -> none  [the longest x1 347 us: per_device(): lax.psum(column_sums(student_values, block_keep), ('seq', 'row'))]
    all_to_all x1 -> x0, waiting for transfers between devices: 249 us -> none  [per_device(): lax.all_to_all(rounded, 'seq', split_axis=0, concat_axis=0, tiled=True)]
    ppermute x2 -> x43, waiting for transfers between devices: 0.01 us -> 79.8 us  [the longest x35 70.5 us: ring(): lax.ppermute(value, axis, [(i, (i + step) % SIDE) for i in range(SIDE)])]
    all_gather x2 -> x0, waiting for transfers between devices: 59.4 us -> none  [the longest x1 59.4 us: per_device(): norm_panel = lax.all_gather(student_std, 'row', axis=0, tiled=True)]
    ppermute x2 -> x43, starting transfers between devices: 5.83 us -> 53 us  [the longest x35 46.9 us: ring(): lax.ppermute(value, axis, [(i, (i + step) % SIDE) for i in range(SIDE)])]
    pallas_call x0 -> x5, Pallas kernels: none -> 32.9 us  [the longest x4 27.6 us: product(): pl.pallas_call(product_kernel, grid_spec=spec, out_shape=jax.ShapeDtypeSt...]
    dot_general x1 -> x4, matrix products: 19.6 us -> 2.89 us  [finish(): lax.dot_general(s_rows, t_rows[1:], (((0,), (0,)), ((), ())), precision=l...]
    gather x4 -> x0, local copies, waits for them, and re-layouts: 14.2 us -> none  [per_device(): rows_here = jnp.take(padded, local_starts + band_pos, axis=0)]
  transfers between devices with their start and end apart: 5 -> 43, of which waited for: 2 -> 16; matrix products, arithmetic and copies ran while one was open for 1% -> 16% of each run, Pallas kernels for 0% -> 15%
where the time goes in v1:
time: 213 us
  waiting for transfers between devices  79.8 us (37%)
  starting transfers between devices  53 us (25%)
  Pallas kernels  32.9 us (15%)
  local copies, waits for them, and re-layouts  24 us (11%)
  other arithmetic  18.7 us (9%)
  matrix products  2.89 us (1%)
    ppermute x35, waiting for transfers between devices, ring(): lax.ppermute(value, axis, [(i, (i + step) % SIDE) for i in range(SIDE)])  70.5 us
    ppermute x35, starting transfers between devices, ring(): lax.ppermute(value, axis, [(i, (i + step) % SIDE) for i in range(SIDE)])  46.9 us
    pallas_call x4, Pallas kernels, product(): pl.pallas_call(product_kernel, grid_spec=spec, out_shape=jax.ShapeDtypeSt...  27.6 us
    ppermute x1, waiting for transfers between devices, per_device(): before = lax.ppermute(teacher[rows - HALO:], ('y', 'x'), up)  9.3 us
    slice x5, local copies, waits for them, and re-layouts, per_device(): p[:, :half]  5.89 us
    pallas_call x1, Pallas kernels, pool(): pl.pallas_call(pool_kernel, grid=(columns // tile,), in_specs=[pl.BlockSp...  5.32 us
    ppermute x1, starting transfers between devices, per_device(): after = lax.ppermute(teacher[:HALO], ('y', 'x'), down)  4.98 us
  transfers between devices with their start and end apart: 43, of which 16 were waited for; matrix products, arithmetic and copies ran while one was open for 16% of the time, Pallas kernels for 15%

profile of v1, /device:TPU:0, one launch (start us, length us, event | category | flops | bytes accessed | tf_op | source)
XLA Modules:
  0.0 212.7 jit_solution(9065841335713831607)
XLA Ops:
  0.0 2.9 %reshape.167 = bf16[192,4,4,256]{3,2,1,0:T(4,128)(2,1)S(1)} reshape(bf16[192,4096]{1,0:T(8,128)(2,1)} %param.5) | data formatting | bytes 3145728 | tf_op jit(solution)/shard_map/reshape | solution.py:172
  2.9 2.6 %copy.23 = bf16[4,192,4,256]{1,3,2,0:T(8,128)(2,1)} copy(bf16[4,192,4,256]{3,0,2,1:T(4,128)(2,1)S(1)} %bitcast.89) | data formatting | bytes 3145728 | tf_op jit(solution)/shard_map/transpose | solution.py:172
  5.5 2.8 %dynamic-slice_bitcast_fusion.3 = (bf16[192,1024]{0,1:T(8,128)(2,1)S(1)}, bf16[192,1024]{0,1:T(8,128)(2,1)S(1)}, bf16[192,1024]{0,1:T(8,128)(2,1)}, bf16[192,1024]{0,1:T(8,128)(2,1)}) fusion(bf16[4,192,1024]{1,2,0:T(8,128)(2,1)} %bitcast.88, s32[]{:T(128)S(6)} %select_n.52, s32[]{:T(128)S(6)} %select_n.55, s32[]{:T(128)S(6)} %select_n.54, s32[]{:T(128)S(6)} %select_n.53), kind=kLoop, calls=%fused_computation.39 | loop fusion | bytes 3145744 | tf_op jit(solution)/shard_map/jit(dynamic_index_in_dim)/squeeze | solution.py:175
  8.2 1.6 collective-permute-start
  9.8 1.7 collective-permute-start.1
  11.9 5.0 %collective-permute-start.8 = (bf16[16,1024]{1,0:T(8,128)(2,1)S(1)}, bf16[16,1024]{1,0:T(8,128)(2,1)S(1)}, u32[]{:S(2)}, u32[]{:S(2)}) collective-permute-start(bf16[16,1024]{1,0:T(8,128)(2,1)S(1)} %get-tuple-element.45), channel_id=1, source_target_pairs={{8,0},{16,8},{24,16},{32,24},{40,32},{48,40},{56,48},{64,56},{72,6... | collective-permute-start | bytes 98312 | tf_op jit(solution)/shard_map/ppermute | solution.py:187
  17.3 9.3 %collective-permute-done.7.before = bf16[16,1024]{1,0:T(8,128)(2,1)S(1)} collective-permute-done((bf16[16,1024]{1,0:T(8,128)(2,1)S(1)}, bf16[16,1024]{1,0:T(8,128)(2,1)S(1)}, u32[]{:S(2)}, u32[]{:S(2)}) %collective-permute-start.7) | collective-permute-done | bytes 32800 | tf_op jit(solution)/shard_map/ppermute | solution.py:186
  26.6 5.3 %shard_map.55 = (bf16[768,1024]{1,0:T(8,128)(2,1)}, f32[3,1024]{1,0:T(4,128)S(1)}) custom-call(s32[4]{0:T(128)S(1)} %bitcast.85, bf16[16,1024]{1,0:T(8,128)(2,1)S(1)} %collective-permute-done.7.before, bf16[768,1024]{1,0:T(8,128)(2,1)S(1)} %copy-done.3, bf16[16,1024]{1,0:T(8,128)(2,1)S(1)} %collective-permute-done.8.after, s32[768,5]{1,0:T(8,128)S(1)} %copy.24.meta), custom_call_target="tpu_custom_call" | custom-call | flops 352321536 | bytes 4718592 | tf_op jit(solution)/shard_map/pallas_call | solution.py:82
  32.0 3.2 %collective-permute-start.13 = (f32[4,1024]{1,0:T(4,128)S(1)}, f32[4,1024]{1,0:T(4,128)S(1)}, u32[]{:S(2)}, u32[]{:S(2)}) collective-permute-start(f32[4,1024]{1,0:T(4,128)S(1)} %select_maximum_fusion), channel_id=1, source_target_pairs={{0,24},{8,0},{16,8},{24,16},{1,25},{9,1},{17,9},{25,17},{2,26},{10... | collective-permute-start | bytes 49160 | tf_op jit(solution)/shard_map/ppermute | solution.py:17
  35.2 2.7 %fusion.56 = (bf16[768,512]{1,0:T(8,128)(2,1)}, bf16[768,512]{1,0:T(8,128)(2,1)}) fusion(bf16[768,1024]{1,0:T(8,128)(2,1)} %get-tuple-element.7), kind=kLoop, calls=%fused_computation.124 | loop fusion | bytes 3145728 | tf_op jit(solution)/shard_map/slice | solution.py:197
  37.9 2.5 %collective-permute-done.14 = f32[4,1024]{1,0:T(4,128)S(1)} collective-permute-done((f32[4,1024]{1,0:T(4,128)S(1)}, f32[4,1024]{1,0:T(4,128)S(1)}, u32[]{:S(2)}, u32[]{:S(2)}) %collective-permute-start.14) | collective-permute-done | bytes 16416 | tf_op jit(solution)/shard_map/ppermute | solution.py:17
  41.2 3.2 %collective-permute-start.25 = (f32[4,3,1024]{2,1,0:T(4,128)S(1)}, f32[4,3,1024]{2,1,0:T(4,128)S(1)}, u32[]{:S(2)}, u32[]{:S(2)}) collective-permute-start(f32[4,3,1024]{2,1,0:T(4,128)S(1)} %pad_maximum_fusion.9), channel_id=1, source_target_pairs={{0,96},{32,0},{64,32},{96,64},{1,97},{33,1},{65,33},{97,65},{2,98}... | collective-permute-start | bytes 147464 | tf_op jit(solution)/shard_map/ppermute | solution.py:17
  45.4 1.5 collective-permute-done.24
  46.9 1.4 collective-permute-start.2
  48.3 1.9 collective-permute-done.26
  52.4 10.8 %collective-permute-done.2 = bf16[192,1024]{0,1:T(8,128)(2,1)S(1)} collective-permute-done((bf16[192,1024]{0,1:T(8,128)(2,1)S(1)}, bf16[192,1024]{0,1:T(8,128)(2,1)S(1)}, u32[]{:S(2)}, u32[]{:S(2)}) %collective-permute-start.2) | collective-permute-done | bytes 393248 | tf_op jit(solution)/shard_map/ppermute | solution.py:17
  63.2 3.6 %fusion.45 = (bf16[1024,768]{1,0:T(8,128)(2,1)S(1)}, f32[768,1024]{0,1:T(8,128)}) fusion(bf16[192,1024]{0,1:T(8,128)(2,1)S(1)} %collective-permute-done.2, bf16[192,1024]{0,1:T(8,128)(2,1)} %collective-permute-done.1, bf16[192,1024]{0,1:T(8,128)(2,1)} %collective-permute-done, bf16[192,1024]{0,1:T(8,128)(2,1)S(1)} %get-tuple-element.29), kind=kLoop, calls=%fused_computation.94 | loop fusion | flops 7077888 | bytes 6291456 | tf_op jit(solution)/shard_map/transpose | solution.py:208
  66.8 3.6 %copy.25 = f32[768,1024]{1,0:T(8,128)} copy(f32[768,1024]{0,1:T(8,128)} %get-tuple-element.28) | data formatting | bytes 6291456 | tf_op jit(solution)/shard_map/convert_element_type | solution.py:231
  70.4 2.4 %select_reduce_fusion = f32[4,1024]{1,0:T(4,128)S(1)} fusion(f32[4,192,1024]{2,1,0:T(8,128)} %bitcast.86, pred[4,192]{1,0:T(4,128)(4,1)S(1)} %broadcast_compare_fusion), kind=kLoop, calls=%fused_computation.1 | loop fusion | flops 1568768 | bytes 3162880 | tf_op jit(solution)/shard_map/reduce_sum | solution.py:233
  73.9 2.0 collective-permute-start.15
  75.9 2.2 %collective-permute-start.16 = (f32[2,4,1024]{2,1,0:T(4,128)S(1)}, f32[2,4,1024]{2,1,0:T(4,128)S(1)}, u32[]{:S(2)}, u32[]{:S(2)}) collective-permute-start(f32[2,4,1024]{2,1,0:T(4,128)S(1)} %get-tuple-element.65), channel_id=1, source_target_pairs={{0,6},{2,0},{4,2},{6,4},{1,7},{3,1},{5,3},{7,5},{8,14},{10,8},{12,... | collective-permute-start | bytes 98312 | tf_op jit(solution)/shard_map/ppermute | solution.py:17
  78.1 1.8 collective-permute-start.17
  81.2 1.0 collective-permute-start.3
  82.2 2.2 %collective-permute-start.4 = (bf16[1024,768]{1,0:T(8,128)(2,1)S(1)}, bf16[1024,768]{1,0:T(8,128)(2,1)}, u32[]{:S(2)}, u32[]{:S(2)}) collective-permute-start(bf16[1024,768]{1,0:T(8,128)(2,1)S(1)} %get-tuple-element.27.a0), channel_id=1, source_target_pairs={{0,6},{2,0},{4,2},{6,4},{1,7},{3,1},{5,3},{7,5},{8,14},{10,8},{12,... | collective-permute-start | bytes 4718600 | tf_op jit(solution)/shard_map/ppermute | solution.py:17
  84.5 0.8 pad_maximum_fusion.3
  86.0 0.8 fusion.23
  86.9 3.2 %collective-permute-start.22 = (f32[2,4,1024]{2,1,0:T(4,128)S(1)}, f32[2,4,1024]{2,1,0:T(4,128)S(1)}, u32[]{:S(2)}, u32[]{:S(2)}) collective-permute-start(f32[2,4,1024]{2,1,0:T(4,128)S(1)} %get-tuple-element.62), channel_id=1, source_target_pairs={{0,96},{32,0},{64,32},{96,64},{1,97},{33,1},{65,33},{97,65},{2,98}... | collective-permute-start | bytes 98312 | tf_op jit(solution)/shard_map/ppermute | solution.py:17
  90.1 1.9 collective-permute-done.21
  92.0 0.8 collective-permute-start.23
  92.7 0.7 broadcast_divide_fusion.3
  93.4 1.0 copy.27.mean
  94.5 2.9 %collective-permute-done.23 = f32[2,4,1024]{2,1,0:T(4,128)S(1)} collective-permute-done((f32[2,4,1024]{2,1,0:T(4,128)S(1)}, f32[2,4,1024]{2,1,0:T(4,128)S(1)}, u32[]{:S(2)}, u32[]{:S(2)}) %collective-permute-start.23) | collective-permute-done | bytes 32800 | tf_op jit(solution)/shard_map/ppermute | solution.py:17
  98.1 0.8 fusion.43
  99.5 0.7 fusion.31
  100.2 19.1 %collective-permute-done.3.a1 = bf16[1024,768]{1,0:T(8,128)(2,1)S(1)} collective-permute-done((bf16[1024,768]{1,0:T(8,128)(2,1)S(1)}, bf16[1024,768]{1,0:T(8,128)(2,1)S(1)}, u32[]{:S(2)}, u32[]{:S(2)}) %collective-permute-start.3) | collective-permute-done | bytes 1572896 | tf_op jit(solution)/shard_map/ppermute | solution.py:17
  119.4 1.2 slice.232
  120.6 3.3 %collective-permute-start.6 = (bf16[512,768]{1,0:T(8,128)(2,1)S(1)}, bf16[512,768]{1,0:T(8,128)(2,1)S(1)}, u32[]{:S(2)}, u32[]{:S(2)}) collective-permute-start(bf16[512,768]{1,0:T(8,128)(2,1)S(1)} %slice.232), channel_id=1, source_target_pairs={{0,6},{2,0},{4,2},{6,4},{1,7},{3,1},{5,3},{7,5},{8,14},{10,8},{12,... | collective-permute-start | bytes 2359304 | tf_op jit(solution)/shard_map/ppermute | solution.py:17
  123.9 1.5 fusion.57
  125.4 0.7 fusion.33
  126.1 3.9 %collective-permute-done.10 = bf16[768,1024]{1,0:T(8,128)(2,1)} collective-permute-done((bf16[768,1024]{1,0:T(8,128)(2,1)}, bf16[768,1024]{1,0:T(8,128)(2,1)}, u32[]{:S(2)}, u32[]{:S(2)}) %collective-permute-start.10) | collective-permute-done | bytes 1572896 | tf_op jit(solution)/shard_map/ppermute | solution.py:17
  130.0 1.5 fusion.55
  131.5 1.6 collective-permute-start.27
  133.1 6.7 %collective-permute-done.5 = bf16[512,768]{1,0:T(8,128)(2,1)S(1)} collective-permute-done((bf16[512,768]{1,0:T(8,128)(2,1)S(1)}, bf16[512,768]{1,0:T(8,128)(2,1)S(1)}, u32[]{:S(2)}, u32[]{:S(2)}) %collective-permute-start.5) | collective-permute-done | bytes 786464 | tf_op jit(solution)/shard_map/ppermute | solution.py:17
  140.5 4.8 %collective-permute-done.11.b3 = bf16[768,512]{1,0:T(8,128)(2,1)S(1)} collective-permute-done((bf16[768,512]{1,0:T(8,128)(2,1)S(1)}, bf16[768,512]{1,0:T(8,128)(2,1)S(1)}, u32[]{:S(2)}, u32[]{:S(2)}) %collective-permute-start.11) | collective-permute-done | bytes 786464 | tf_op jit(solution)/shard_map/ppermute | solution.py:17
  145.3 6.9 %shard_map.56 = f32[1024,512]{1,0:T(8,128)S(1)} custom-call(s32[2]{0:T(128)S(1)} %pad_add_fusion.1.place, bf16[1024,768]{1,0:T(8,128)(2,1)S(1)} %get-tuple-element.27.a0, bf16[1024,768]{1,0:T(8,128)(2,1)S(1)} %collective-permute-done.3.a1, bf16[1024,768]{1,0:T(8,128)(2,1)} %collective-permute-done.4.a2, ...), custom_call_target="tpu_custom_call" | custom-call | flops 3221225472 | bytes 11534336 | tf_op jit(solution)/shard_map/pallas_call | solution.py:152
  152.5 0.8 copy-done.1
  153.3 6.9 %shard_map.57 = f32[1024,512]{1,0:T(8,128)S(1)} custom-call(s32[2]{0:T(128)S(1)} %pad_add_fusion.1.place, bf16[1024,768]{1,0:T(8,128)(2,1)S(1)} %get-tuple-element.27.a0, bf16[1024,768]{1,0:T(8,128)(2,1)S(1)} %collective-permute-done.3.a1, bf16[1024,768]{1,0:T(8,128)(2,1)} %collective-permute-done.4.a2, ...), custom_call_target="tpu_custom_call" | custom-call | flops 3221225472 | bytes 11534336 | tf_op jit(solution)/shard_map/pallas_call | solution.py:152
  160.4 2.4 %collective-permute-start.28 = (bf16[256,512]{1,0:T(8,128)(2,1)S(1)}, bf16[256,512]{1,0:T(8,128)(2,1)S(1)}, u32[]{:S(2)}, u32[]{:S(2)}) collective-permute-start(bf16[256,512]{1,0:T(8,128)(2,1)S(1)} %get-tuple-element.49), channel_id=1, source_target_pairs={{0,96},{32,0},{64,32},{96,64},{1,97},{33,1},{65,33},{97,65},{2,98}... | collective-permute-start | bytes 786440 | tf_op jit(solution)/shard_map/ppermute | solution.py:17
  162.8 1.5 fusion.60
  164.9 0.8 fusion.17
  165.7 1.2 collective-permute-done.28
  166.9 3.5 %collective-permute-start.20 = (bf16[256,512]{1,0:T(8,128)(2,1)S(1)}, bf16[256,512]{1,0:T(8,128)(2,1)S(1)}, u32[]{:S(2)}, u32[]{:S(2)}) collective-permute-start(bf16[256,512]{1,0:T(8,128)(2,1)S(1)} %get-tuple-element.48), channel_id=1, source_target_pairs={{0,96},{32,0},{64,32},{96,64},{1,97},{33,1},{65,33},{97,65},{2,98}... | collective-permute-start | bytes 786440 | tf_op jit(solution)/shard_map/ppermute | solution.py:17
  170.9 3.5 %collective-permute-start.29 = (bf16[256,512]{1,0:T(8,128)(2,1)S(1)}, bf16[256,512]{1,0:T(8,128)(2,1)S(1)}, u32[]{:S(2)}, u32[]{:S(2)}) collective-permute-start(bf16[256,512]{1,0:T(8,128)(2,1)S(1)} %fusion.12), channel_id=1, source_target_pairs={{0,96},{32,0},{64,32},{96,64},{1,97},{33,1},{65,33},{97,65},{2,98}... | collective-permute-start | bytes 786440 | tf_op jit(solution)/shard_map/ppermute | solution.py:17
  174.5 6.9 %shard_map.59 = f32[1024,512]{1,0:T(8,128)S(1)} custom-call(s32[2]{0:T(128)S(1)} %pad_add_fusion.1.place, bf16[1024,768]{1,0:T(8,128)(2,1)S(1)} %get-tuple-element.27.a0, bf16[1024,768]{1,0:T(8,128)(2,1)S(1)} %collective-permute-done.3.a1, bf16[1024,768]{1,0:T(8,128)(2,1)} %collective-permute-done.4.a2, ...), custom_call_target="tpu_custom_call" | custom-call | flops 3221225472 | bytes 11534336 | tf_op jit(solution)/shard_map/pallas_call | solution.py:152
  181.6 2.1 collective-permute-start.40
  183.6 6.9 %shard_map.58 = f32[1024,512]{1,0:T(8,128)S(1)} custom-call(s32[2]{0:T(128)S(1)} %pad_add_fusion.1.place, bf16[1024,768]{1,0:T(8,128)(2,1)S(1)} %get-tuple-element.27.a0, bf16[1024,768]{1,0:T(8,128)(2,1)S(1)} %collective-permute-done.3.a1, bf16[1024,768]{1,0:T(8,128)(2,1)} %collective-permute-done.4.a2, ...), custom_call_target="tpu_custom_call" | custom-call | flops 3221225472 | bytes 11534336 | tf_op jit(solution)/shard_map/pallas_call | solution.py:152
  190.9 0.7 fusion.21
  191.7 3.3 %collective-permute-start.37 = (bf16[256,512]{1,0:T(8,128)(2,1)S(1)}, bf16[256,512]{1,0:T(8,128)(2,1)S(1)}, u32[]{:S(2)}, u32[]{:S(2)}) collective-permute-start(bf16[256,512]{1,0:T(8,128)(2,1)S(1)} %get-tuple-element.52), channel_id=1, source_target_pairs={{0,96},{32,0},{64,32},{96,64},{1,97},{33,1},{65,33},{97,65},{2,98}... | collective-permute-start | bytes 786440 | tf_op jit(solution)/shard_map/ppermute | solution.py:17
  195.1 8.0 %collective-permute-done.35 = bf16[256,512]{1,0:T(8,128)(2,1)S(1)} collective-permute-done((bf16[256,512]{1,0:T(8,128)(2,1)S(1)}, bf16[256,512]{1,0:T(8,128)(2,1)S(1)}, u32[]{:S(2)}, u32[]{:S(2)}) %collective-permute-start.35) | collective-permute-done | bytes 262176 | tf_op jit(solution)/shard_map/ppermute | solution.py:17
  203.1 2.1 collective-permute-start.36
  205.2 0.7 fusion.16
  206.0 3.4 %collective-permute-done.41 = bf16[256,512]{1,0:T(8,128)(2,1)S(1)} collective-permute-done((bf16[256,512]{1,0:T(8,128)(2,1)S(1)}, bf16[256,512]{1,0:T(8,128)(2,1)S(1)}, u32[]{:S(2)}, u32[]{:S(2)}) %collective-permute-start.41) | collective-permute-done | bytes 262176 | tf_op jit(solution)/shard_map/ppermute | solution.py:17
  209.4 1.4 collective-permute-done.36
  211.2 1.5 maximum_bitcast_fusion
  (120 shorter events, 12.1 us)
Async XLA Ops:
  5.5 6.0 %copy-start.3 = (bf16[768,1024]{1,0:T(8,128)(2,1)S(1)}, bf16[768,1024]{1,0:T(8,128)(2,1)}, u32[]{:S(2)}) copy-start(bf16[768,1024]{1,0:T(8,128)(2,1)} %teacher.1) | copy-start | bytes 4718596
  5.5 11.4 %copy-start.7 = (s32[768]{0:T(1024)S(1)}, s32[768]{0:T(1024)}, u32[]{:S(2)}) copy-start(s32[768]{0:T(1024)} %param.7) | copy-start | bytes 9220
  5.5 11.4 %copy-start.6 = (s32[768,4]{0,1:T(4,128)S(1)}, s32[768,4]{0,1:T(4,128)}, u32[]{:S(2)}) copy-start(s32[768,4]{0,1:T(4,128)} %param.8) | copy-start | bytes 36868
  5.5 11.7 %copy-start.4 = (s32[1,4]{1,0:T(1,128)S(1)}, s32[1,4]{1,0:T(1,128)}, u32[]{:S(2)}) copy-start(s32[1,4]{1,0:T(1,128)} %param.9) | copy-start | bytes 52
  8.2 44.2 %collective-permute-start = (bf16[192,1024]{0,1:T(8,128)(2,1)}, bf16[192,1024]{0,1:T(8,128)(2,1)}, u32[]{:S(2)}, u32[]{:S(2)}) collective-permute-start(bf16[192,1024]{0,1:T(8,128)(2,1)} %get-tuple-element.32), channel_id=1, source_target_pairs={{0,8},{8,16},{16,24},{24,0},{1,9},{9,17},{17,25},{25,1},{2,10},{10... | collective-permute-start | bytes 1179656 | tf_op jit(solution)/shard_map/ppermute | solution.py:17
  9.8 42.6 %collective-permute-start.1 = (bf16[192,1024]{0,1:T(8,128)(2,1)}, bf16[192,1024]{0,1:T(8,128)(2,1)}, u32[]{:S(2)}, u32[]{:S(2)}) collective-permute-start(bf16[192,1024]{0,1:T(8,128)(2,1)} %get-tuple-element.31), channel_id=1, source_target_pairs={{0,24},{8,0},{16,8},{24,16},{1,25},{9,1},{17,9},{25,17},{2,26},{10... | collective-permute-start | bytes 1179656 | tf_op jit(solution)/shard_map/ppermute | solution.py:17
  11.5 15.1 %collective-permute-start.7 = (bf16[16,1024]{1,0:T(8,128)(2,1)S(1)}, bf16[16,1024]{1,0:T(8,128)(2,1)S(1)}, u32[]{:S(2)}, u32[]{:S(2)}) collective-permute-start(bf16[16,1024]{1,0:T(8,128)(2,1)S(1)} %get-tuple-element.46), channel_id=1, source_target_pairs={{0,8},{8,16},{16,24},{24,32},{32,40},{40,48},{48,56},{56,64},{64,7... | collective-permute-start | bytes 98312 | tf_op jit(solution)/shard_map/ppermute | solution.py:186
  11.9 14.6 %collective-permute-start.8 = (bf16[16,1024]{1,0:T(8,128)(2,1)S(1)}, bf16[16,1024]{1,0:T(8,128)(2,1)S(1)}, u32[]{:S(2)}, u32[]{:S(2)}) collective-permute-start(bf16[16,1024]{1,0:T(8,128)(2,1)S(1)} %get-tuple-element.45), channel_id=1, source_target_pairs={{8,0},{16,8},{24,16},{32,24},{40,32},{48,40},{56,48},{64,56},{72,6... | collective-permute-start | bytes 98312 | tf_op jit(solution)/shard_map/ppermute | solution.py:187
  31.9 6.0 %collective-permute-start.12 = (f32[4,1024]{1,0:T(4,128)S(1)}, f32[4,1024]{1,0:T(4,128)S(1)}, u32[]{:S(2)}, u32[]{:S(2)}) collective-permute-start(f32[4,1024]{1,0:T(4,128)S(1)} %select_maximum_fusion), channel_id=1, source_target_pairs={{0,8},{8,16},{16,24},{24,0},{1,9},{9,17},{17,25},{25,1},{2,10},{10... | collective-permute-start | bytes 49160 | tf_op jit(solution)/shard_map/ppermute | solution.py:17
  32.0 6.0 %collective-permute-start.13 = (f32[4,1024]{1,0:T(4,128)S(1)}, f32[4,1024]{1,0:T(4,128)S(1)}, u32[]{:S(2)}, u32[]{:S(2)}) collective-permute-start(f32[4,1024]{1,0:T(4,128)S(1)} %select_maximum_fusion), channel_id=1, source_target_pairs={{0,24},{8,0},{16,8},{24,16},{1,25},{9,1},{17,9},{25,17},{2,26},{10... | collective-permute-start | bytes 49160 | tf_op jit(solution)/shard_map/ppermute | solution.py:17
  35.2 5.2 %collective-permute-start.14 = (f32[4,1024]{1,0:T(4,128)S(1)}, f32[4,1024]{1,0:T(4,128)S(1)}, u32[]{:S(2)}, u32[]{:S(2)}) collective-permute-start(f32[4,1024]{1,0:T(4,128)S(1)} %select_maximum_fusion), channel_id=1, source_target_pairs={{0,16},{8,24},{16,0},{24,8},{1,17},{9,25},{17,1},{25,9},{2,18},{10... | collective-permute-start | bytes 49160 | tf_op jit(solution)/shard_map/ppermute | solution.py:17
  41.2 5.7 %collective-permute-start.24 = (f32[4,3,1024]{2,1,0:T(4,128)S(1)}, f32[4,3,1024]{2,1,0:T(4,128)S(1)}, u32[]{:S(2)}, u32[]{:S(2)}) collective-permute-start(f32[4,3,1024]{2,1,0:T(4,128)S(1)} %pad_maximum_fusion.9), channel_id=1, source_target_pairs={{0,32},{32,64},{64,96},{96,0},{1,33},{33,65},{65,97},{97,1},{2,34}... | collective-permute-start | bytes 147464 | tf_op jit(solution)/shard_map/ppermute | solution.py:17
  41.2 7.1 %collective-permute-start.25 = (f32[4,3,1024]{2,1,0:T(4,128)S(1)}, f32[4,3,1024]{2,1,0:T(4,128)S(1)}, u32[]{:S(2)}, u32[]{:S(2)}) collective-permute-start(f32[4,3,1024]{2,1,0:T(4,128)S(1)} %pad_maximum_fusion.9), channel_id=1, source_target_pairs={{0,96},{32,0},{64,32},{96,64},{1,97},{33,1},{65,33},{97,65},{2,98}... | collective-permute-start | bytes 147464 | tf_op jit(solution)/shard_map/ppermute | solution.py:17
  44.5 5.8 %collective-permute-start.26 = (f32[4,3,1024]{2,1,0:T(4,128)S(1)}, f32[4,3,1024]{2,1,0:T(4,128)S(1)}, u32[]{:S(2)}, u32[]{:S(2)}) collective-permute-start(f32[4,3,1024]{2,1,0:T(4,128)S(1)} %pad_maximum_fusion.9), channel_id=1, source_target_pairs={{0,64},{32,96},{64,0},{96,32},{1,65},{33,97},{65,1},{97,33},{2,66}... | collective-permute-start | bytes 147464 | tf_op jit(solution)/shard_map/ppermute | solution.py:17
  46.9 16.4 %collective-permute-start.2 = (bf16[192,1024]{0,1:T(8,128)(2,1)S(1)}, bf16[192,1024]{0,1:T(8,128)(2,1)S(1)}, u32[]{:S(2)}, u32[]{:S(2)}) collective-permute-start(bf16[192,1024]{0,1:T(8,128)(2,1)S(1)} %get-tuple-element.30), channel_id=1, source_target_pairs={{0,16},{8,24},{16,0},{24,8},{1,17},{9,25},{17,1},{25,9},{2,18},{10... | collective-permute-start | bytes 1179656 | tf_op jit(solution)/shard_map/ppermute | solution.py:17
  48.3 75.5 %collective-permute-start.9 = (bf16[768,1024]{1,0:T(8,128)(2,1)}, bf16[768,1024]{1,0:T(8,128)(2,1)}, u32[]{:S(2)}, u32[]{:S(2)}) collective-permute-start(bf16[768,1024]{1,0:T(8,128)(2,1)} %get-tuple-element.7), channel_id=1, source_target_pairs={{0,8},{8,16},{16,24},{24,0},{1,9},{9,17},{17,25},{25,1},{2,10},{10... | collective-permute-start | bytes 4718600 | tf_op jit(solution)/shard_map/ppermute | solution.py:17
  70.4 2.8 %copy-start.5 = (f32[768,1024]{1,0:T(8,128)S(1)}, f32[768,1024]{1,0:T(8,128)}, u32[]{:S(2)}) copy-start(f32[768,1024]{1,0:T(8,128)} %copy.25) | copy-start | bytes 9437188
  73.9 7.3 %collective-permute-start.15 = (f32[2,4,1024]{2,1,0:T(4,128)S(1)}, f32[2,4,1024]{2,1,0:T(4,128)S(1)}, u32[]{:S(2)}, u32[]{:S(2)}) collective-permute-start(f32[2,4,1024]{2,1,0:T(4,128)S(1)} %get-tuple-element.65), channel_id=1, source_target_pairs={{0,2},{2,4},{4,6},{6,0},{1,3},{3,5},{5,7},{7,1},{8,10},{10,12},{12... | collective-permute-start | bytes 98312 | tf_op jit(solution)/shard_map/ppermute | solution.py:17
  75.9 6.3 %collective-permute-start.16 = (f32[2,4,1024]{2,1,0:T(4,128)S(1)}, f32[2,4,1024]{2,1,0:T(4,128)S(1)}, u32[]{:S(2)}, u32[]{:S(2)}) collective-permute-start(f32[2,4,1024]{2,1,0:T(4,128)S(1)} %get-tuple-element.65), channel_id=1, source_target_pairs={{0,6},{2,0},{4,2},{6,4},{1,7},{3,1},{5,3},{7,5},{8,14},{10,8},{12,... | collective-permute-start | bytes 98312 | tf_op jit(solution)/shard_map/ppermute | solution.py:17
  78.1 6.4 %collective-permute-start.17 = (f32[2,4,1024]{2,1,0:T(4,128)S(1)}, f32[2,4,1024]{2,1,0:T(4,128)}, u32[]{:S(2)}, u32[]{:S(2)}) collective-permute-start(f32[2,4,1024]{2,1,0:T(4,128)S(1)} %get-tuple-element.65), channel_id=1, source_target_pairs={{0,4},{2,6},{4,0},{6,2},{1,5},{3,7},{5,1},{7,3},{8,12},{10,14},{12... | collective-permute-start | bytes 98312 | tf_op jit(solution)/shard_map/ppermute | solution.py:17
  81.2 5.7 %collective-permute-start.38 = (f32[17,1024]{1,0:T(8,128)S(1)}, f32[17,1024]{1,0:T(8,128)S(1)}, u32[]{:S(2)}, u32[]{:S(2)}) collective-permute-start(f32[17,1024]{1,0:T(8,128)S(1)} %pad_maximum_fusion.4), channel_id=1, source_target_pairs={{0,1},{1,0},{2,3},{3,2},{4,5},{5,4},{6,7},{7,6},{8,9},{9,8},{10,11... | collective-permute-start | bytes 208904 | tf_op jit(solution)/shard_map/ppermute | solution.py:25
  81.2 38.0 %collective-permute-start.3 = (bf16[1024,768]{1,0:T(8,128)(2,1)S(1)}, bf16[1024,768]{1,0:T(8,128)(2,1)S(1)}, u32[]{:S(2)}, u32[]{:S(2)}) collective-permute-start(bf16[1024,768]{1,0:T(8,128)(2,1)S(1)} %get-tuple-element.27.a0), channel_id=1, source_target_pairs={{0,2},{2,4},{4,6},{6,0},{1,3},{3,5},{5,7},{7,1},{8,10},{10,12},{12... | collective-permute-start | bytes 4718600 | tf_op jit(solution)/shard_map/ppermute | solution.py:17
  82.2 37.2 %collective-permute-start.4 = (bf16[1024,768]{1,0:T(8,128)(2,1)S(1)}, bf16[1024,768]{1,0:T(8,128)(2,1)}, u32[]{:S(2)}, u32[]{:S(2)}) collective-permute-start(bf16[1024,768]{1,0:T(8,128)(2,1)S(1)} %get-tuple-element.27.a0), channel_id=1, source_target_pairs={{0,6},{2,0},{4,2},{6,4},{1,7},{3,1},{5,3},{7,5},{8,14},{10,8},{12,... | collective-permute-start | bytes 4718600 | tf_op jit(solution)/shard_map/ppermute | solution.py:17
  86.8 5.2 %collective-permute-start.21 = (f32[2,4,1024]{2,1,0:T(4,128)S(1)}, f32[2,4,1024]{2,1,0:T(4,128)S(1)}, u32[]{:S(2)}, u32[]{:S(2)}) collective-permute-start(f32[2,4,1024]{2,1,0:T(4,128)S(1)} %get-tuple-element.62), channel_id=1, source_target_pairs={{0,32},{32,64},{64,96},{96,0},{1,33},{33,65},{65,97},{97,1},{2,34}... | collective-permute-start | bytes 98312 | tf_op jit(solution)/shard_map/ppermute | solution.py:17
  86.9 7.6 %collective-permute-start.22 = (f32[2,4,1024]{2,1,0:T(4,128)S(1)}, f32[2,4,1024]{2,1,0:T(4,128)S(1)}, u32[]{:S(2)}, u32[]{:S(2)}) collective-permute-start(f32[2,4,1024]{2,1,0:T(4,128)S(1)} %get-tuple-element.62), channel_id=1, source_target_pairs={{0,96},{32,0},{64,32},{96,64},{1,97},{33,1},{65,33},{97,65},{2,98}... | collective-permute-start | bytes 98312 | tf_op jit(solution)/shard_map/ppermute | solution.py:17
  92.0 5.4 %collective-permute-start.23 = (f32[2,4,1024]{2,1,0:T(4,128)S(1)}, f32[2,4,1024]{2,1,0:T(4,128)S(1)}, u32[]{:S(2)}, u32[]{:S(2)}) collective-permute-start(f32[2,4,1024]{2,1,0:T(4,128)S(1)} %get-tuple-element.62), channel_id=1, source_target_pairs={{0,64},{32,96},{64,0},{96,32},{1,65},{33,97},{65,1},{97,33},{2,66}... | collective-permute-start | bytes 98312 | tf_op jit(solution)/shard_map/ppermute | solution.py:17
  94.5 35.5 %collective-permute-start.10 = (bf16[768,1024]{1,0:T(8,128)(2,1)}, bf16[768,1024]{1,0:T(8,128)(2,1)}, u32[]{:S(2)}, u32[]{:S(2)}) collective-permute-start(bf16[768,1024]{1,0:T(8,128)(2,1)} %get-tuple-element.7), channel_id=1, source_target_pairs={{0,24},{8,0},{16,8},{24,16},{1,25},{9,1},{17,9},{25,17},{2,26},{10... | collective-permute-start | bytes 4718600 | tf_op jit(solution)/shard_map/ppermute | solution.py:17
  97.4 65.4 %collective-permute-start.31 = (bf16[768,1024]{1,0:T(8,128)(2,1)}, bf16[768,1024]{1,0:T(8,128)(2,1)}, u32[]{:S(2)}, u32[]{:S(2)}) collective-permute-start(bf16[768,1024]{1,0:T(8,128)(2,1)} %get-tuple-element.7), channel_id=1, source_target_pairs={{0,1},{1,0},{2,3},{3,2},{4,5},{5,4},{6,7},{7,6},{8,9},{9,8},{10,11... | collective-permute-start | bytes 4718600 | tf_op jit(solution)/shard_map/ppermute | solution.py:25
  119.3 20.5 %collective-permute-start.5 = (bf16[512,768]{1,0:T(8,128)(2,1)S(1)}, bf16[512,768]{1,0:T(8,128)(2,1)S(1)}, u32[]{:S(2)}, u32[]{:S(2)}) collective-permute-start(bf16[512,768]{1,0:T(8,128)(2,1)S(1)} %slice.231), channel_id=1, source_target_pairs={{0,2},{2,4},{4,6},{6,0},{1,3},{3,5},{5,7},{7,1},{8,10},{10,12},{12... | collective-permute-start | bytes 2359304 | tf_op jit(solution)/shard_map/ppermute | solution.py:17
  120.6 19.7 %collective-permute-start.6 = (bf16[512,768]{1,0:T(8,128)(2,1)S(1)}, bf16[512,768]{1,0:T(8,128)(2,1)S(1)}, u32[]{:S(2)}, u32[]{:S(2)}) collective-permute-start(bf16[512,768]{1,0:T(8,128)(2,1)S(1)} %slice.232), channel_id=1, source_target_pairs={{0,6},{2,0},{4,2},{6,4},{1,7},{3,1},{5,3},{7,5},{8,14},{10,8},{12,... | collective-permute-start | bytes 2359304 | tf_op jit(solution)/shard_map/ppermute | solution.py:17
  125.4 19.9 %collective-permute-start.11 = (bf16[768,512]{1,0:T(8,128)(2,1)S(1)}, bf16[768,512]{1,0:T(8,128)(2,1)S(1)}, u32[]{:S(2)}, u32[]{:S(2)}) collective-permute-start(bf16[768,512]{1,0:T(8,128)(2,1)S(1)} %get-tuple-element.38.b1), channel_id=1, source_target_pairs={{0,8},{8,16},{16,24},{24,0},{1,9},{9,17},{17,25},{25,1},{2,10},{10... | collective-permute-start | bytes 2359304 | tf_op jit(solution)/shard_map/ppermute | solution.py:17
  131.5 13.7 %copy-start = (f32[1024,1]{1,0:T(8,128)S(1)}, f32[1024,1]{1,0:T(8,128)}, u32[]{:S(2)}) copy-start(f32[1024,1]{1,0:T(8,128)} %copy.27.mean) | copy-start | bytes 12292
  131.5 13.7 %copy-start.2 = (bf16[768,512]{1,0:T(8,128)(2,1)S(1)}, bf16[768,512]{1,0:T(8,128)(2,1)}, u32[]{:S(2)}) copy-start(bf16[768,512]{1,0:T(8,128)(2,1)} %get-tuple-element.35.b0) | copy-start | bytes 2359300
  131.5 20.9 %collective-permute-start.27 = (bf16[768,512]{1,0:T(8,128)(2,1)S(1)}, bf16[768,512]{1,0:T(8,128)(2,1)S(1)}, u32[]{:S(2)}, u32[]{:S(2)}) collective-permute-start(bf16[768,512]{1,0:T(8,128)(2,1)S(1)} %get-tuple-element.34.b2), channel_id=1, source_target_pairs={{0,24},{8,0},{16,8},{24,16},{1,25},{9,1},{17,9},{25,17},{2,26},{10... | collective-permute-start | bytes 2359304 | tf_op jit(solution)/shard_map/ppermute | solution.py:17
  139.8 30.7 %collective-permute-start.33 = (bf16[768,1024]{1,0:T(8,128)(2,1)}, bf16[768,1024]{1,0:T(8,128)(2,1)S(1)}, u32[]{:S(2)}, u32[]{:S(2)}) collective-permute-start(bf16[768,1024]{1,0:T(8,128)(2,1)} %collective-permute-done.10), channel_id=1, source_target_pairs={{0,1},{1,0},{2,3},{3,2},{4,5},{5,4},{6,7},{7,6},{8,9},{9,8},{10,11... | collective-permute-start | bytes 4718600 | tf_op jit(solution)/shard_map/ppermute | solution.py:25
  140.3 30.4 %collective-permute-start.32 = (bf16[768,1024]{1,0:T(8,128)(2,1)}, bf16[768,1024]{1,0:T(8,128)(2,1)S(1)}, u32[]{:S(2)}, u32[]{:S(2)}) collective-permute-start(bf16[768,1024]{1,0:T(8,128)(2,1)} %collective-permute-done.9), channel_id=1, source_target_pairs={{0,1},{1,0},{2,3},{3,2},{4,5},{5,4},{6,7},{7,6},{8,9},{9,8},{10,11... | collective-permute-start | bytes 4718600 | tf_op jit(solution)/shard_map/ppermute | solution.py:25
  152.2 1.1 copy-start.1
  152.4 12.1 %collective-permute-start.18 = (bf16[256,512]{1,0:T(8,128)(2,1)S(1)}, bf16[256,512]{1,0:T(8,128)(2,1)S(1)}, u32[]{:S(2)}, u32[]{:S(2)}) collective-permute-start(bf16[256,512]{1,0:T(8,128)(2,1)S(1)} %get-tuple-element.47), channel_id=1, source_target_pairs={{0,32},{32,64},{64,96},{96,0},{1,33},{33,65},{65,97},{97,1},{2,34}... | collective-permute-start | bytes 786440 | tf_op jit(solution)/shard_map/ppermute | solution.py:17
  160.4 6.5 %collective-permute-start.28 = (bf16[256,512]{1,0:T(8,128)(2,1)S(1)}, bf16[256,512]{1,0:T(8,128)(2,1)S(1)}, u32[]{:S(2)}, u32[]{:S(2)}) collective-permute-start(bf16[256,512]{1,0:T(8,128)(2,1)S(1)} %get-tuple-element.49), channel_id=1, source_target_pairs={{0,96},{32,0},{64,32},{96,64},{1,97},{33,1},{65,33},{97,65},{2,98}... | collective-permute-start | bytes 786440 | tf_op jit(solution)/shard_map/ppermute | solution.py:17
  164.3 6.6 %collective-permute-start.39 = (bf16[768,512]{1,0:T(8,128)(2,1)S(1)}, bf16[768,512]{1,0:T(8,128)(2,1)S(1)}, u32[]{:S(2)}, u32[]{:S(2)}) collective-permute-start(bf16[768,512]{1,0:T(8,128)(2,1)S(1)} %collective-permute-done.27.b3), channel_id=1, source_target_pairs={{0,1},{1,0},{2,3},{3,2},{4,5},{5,4},{6,7},{7,6},{8,9},{9,8},{10,11... | collective-permute-start | bytes 2359304 | tf_op jit(solution)/shard_map/ppermute | solution.py:25
  164.4 17.1 %collective-permute-start.34 = (bf16[768,512]{1,0:T(8,128)(2,1)S(1)}, bf16[768,512]{1,0:T(8,128)(2,1)S(1)}, u32[]{:S(2)}, u32[]{:S(2)}) collective-permute-start(bf16[768,512]{1,0:T(8,128)(2,1)S(1)} %collective-permute-done.11.b3), channel_id=1, source_target_pairs={{0,1},{1,0},{2,3},{3,2},{4,5},{5,4},{6,7},{7,6},{8,9},{9,8},{10,11... | collective-permute-start | bytes 2359304 | tf_op jit(solution)/shard_map/ppermute | solution.py:25
  166.9 23.8 %collective-permute-start.20 = (bf16[256,512]{1,0:T(8,128)(2,1)S(1)}, bf16[256,512]{1,0:T(8,128)(2,1)S(1)}, u32[]{:S(2)}, u32[]{:S(2)}) collective-permute-start(bf16[256,512]{1,0:T(8,128)(2,1)S(1)} %get-tuple-element.48), channel_id=1, source_target_pairs={{0,96},{32,0},{64,32},{96,64},{1,97},{33,1},{65,33},{97,65},{2,98}... | collective-permute-start | bytes 786440 | tf_op jit(solution)/shard_map/ppermute | solution.py:17
  170.5 32.6 %collective-permute-start.30 = (bf16[256,512]{1,0:T(8,128)(2,1)S(1)}, bf16[256,512]{1,0:T(8,128)(2,1)S(1)}, u32[]{:S(2)}, u32[]{:S(2)}) collective-permute-start(bf16[256,512]{1,0:T(8,128)(2,1)S(1)} %get-tuple-element.50), channel_id=1, source_target_pairs={{0,32},{32,64},{64,96},{96,0},{1,33},{33,65},{65,97},{97,1},{2,34}... | collective-permute-start | bytes 786440 | tf_op jit(solution)/shard_map/ppermute | solution.py:17
  170.7 20.1 %collective-permute-start.19 = (bf16[256,512]{1,0:T(8,128)(2,1)}, bf16[256,512]{1,0:T(8,128)(2,1)S(1)}, u32[]{:S(2)}, u32[]{:S(2)}) collective-permute-start(bf16[256,512]{1,0:T(8,128)(2,1)} %fusion.17), channel_id=1, source_target_pairs={{0,32},{32,64},{64,96},{96,0},{1,33},{33,65},{65,97},{97,1},{2,34}... | collective-permute-start | bytes 786440 | tf_op jit(solution)/shard_map/ppermute | solution.py:17
  170.9 34.3 %collective-permute-start.29 = (bf16[256,512]{1,0:T(8,128)(2,1)S(1)}, bf16[256,512]{1,0:T(8,128)(2,1)S(1)}, u32[]{:S(2)}, u32[]{:S(2)}) collective-permute-start(bf16[256,512]{1,0:T(8,128)(2,1)S(1)} %fusion.12), channel_id=1, source_target_pairs={{0,96},{32,0},{64,32},{96,64},{1,97},{33,1},{65,33},{97,65},{2,98}... | collective-permute-start | bytes 786440 | tf_op jit(solution)/shard_map/ppermute | solution.py:17
  181.6 10.1 %collective-permute-start.40 = (bf16[256,512]{1,0:T(8,128)(2,1)S(1)}, bf16[256,512]{1,0:T(8,128)(2,1)S(1)}, u32[]{:S(2)}, u32[]{:S(2)}) collective-permute-start(bf16[256,512]{1,0:T(8,128)(2,1)S(1)} %get-tuple-element.53), channel_id=1, source_target_pairs={{0,96},{32,0},{64,32},{96,64},{1,97},{33,1},{65,33},{97,65},{2,98}... | collective-permute-start | bytes 786440 | tf_op jit(solution)/shard_map/ppermute | solution.py:17
  190.8 15.2 %collective-permute-start.42 = (bf16[256,512]{1,0:T(8,128)(2,1)S(1)}, bf16[256,512]{1,0:T(8,128)(2,1)S(1)}, u32[]{:S(2)}, u32[]{:S(2)}) collective-permute-start(bf16[256,512]{1,0:T(8,128)(2,1)S(1)} %get-tuple-element.54), channel_id=1, source_target_pairs={{0,32},{32,64},{64,96},{96,0},{1,33},{33,65},{65,97},{97,1},{2,34}... | collective-permute-start | bytes 786440 | tf_op jit(solution)/shard_map/ppermute | solution.py:17
  190.8 12.2 %collective-permute-start.35 = (bf16[256,512]{1,0:T(8,128)(2,1)S(1)}, bf16[256,512]{1,0:T(8,128)(2,1)S(1)}, u32[]{:S(2)}, u32[]{:S(2)}) collective-permute-start(bf16[256,512]{1,0:T(8,128)(2,1)S(1)} %get-tuple-element.51), channel_id=1, source_target_pairs={{0,32},{32,64},{64,96},{96,0},{1,33},{33,65},{65,97},{97,1},{2,34}... | collective-permute-start | bytes 786440 | tf_op jit(solution)/shard_map/ppermute | solution.py:17
  191.7 14.3 %collective-permute-start.37 = (bf16[256,512]{1,0:T(8,128)(2,1)S(1)}, bf16[256,512]{1,0:T(8,128)(2,1)S(1)}, u32[]{:S(2)}, u32[]{:S(2)}) collective-permute-start(bf16[256,512]{1,0:T(8,128)(2,1)S(1)} %get-tuple-element.52), channel_id=1, source_target_pairs={{0,96},{32,0},{64,32},{96,64},{1,97},{33,1},{65,33},{97,65},{2,98}... | collective-permute-start | bytes 786440 | tf_op jit(solution)/shard_map/ppermute | solution.py:17
  203.0 6.4 %collective-permute-start.41 = (bf16[256,512]{1,0:T(8,128)(2,1)S(1)}, bf16[256,512]{1,0:T(8,128)(2,1)S(1)}, u32[]{:S(2)}, u32[]{:S(2)}) collective-permute-start(bf16[256,512]{1,0:T(8,128)(2,1)S(1)} %fusion.2), channel_id=1, source_target_pairs={{0,96},{32,0},{64,32},{96,64},{1,97},{33,1},{65,33},{97,65},{2,98}... | collective-permute-start | bytes 786440 | tf_op jit(solution)/shard_map/ppermute | solution.py:17
  203.1 7.7 %collective-permute-start.36 = (bf16[256,512]{1,0:T(8,128)(2,1)S(1)}, bf16[256,512]{1,0:T(8,128)(2,1)S(1)}, u32[]{:S(2)}, u32[]{:S(2)}) collective-permute-start(bf16[256,512]{1,0:T(8,128)(2,1)S(1)} %fusion.7), channel_id=1, source_target_pairs={{0,32},{32,64},{64,96},{96,0},{1,33},{33,65},{65,97},{97,1},{2,34}... | collective-permute-start | bytes 786440 | tf_op jit(solution)/shard_map/ppermute | solution.py:17

commit v2 on v1

v2 whole, which is shorter than its diff:
```python
import jax
import jax.numpy as jnp
from jax import lax
from jax.experimental import pallas as pl
from jax.experimental.pallas import tpu as pltpu
from jax.sharding import Mesh
from jax.sharding import PartitionSpec as P

SUB = 192
BAND = 4
HALO = 16
SIDE = 4
COMING = (0, SIDE - 1, 1, 2)
epsilon = 1e-05
f32 = jnp.float32
bf16 = jnp.bfloat16


def ring(value, axis, step):
    return lax.ppermute(value, axis, [(i, (i + step) % SIDE) for i in range(SIDE)])


def ring_all(value, axis):
    return [value, ring(value, axis, 1), ring(value, axis, -1), ring(value, axis, 2)]


def swap(value):
    return lax.ppermute(value, "col", [(0, 1), (1, 0)])


def after(value, *others):
    return lax.optimization_barrier((value, others))[0]


def smem():
    return pl.BlockSpec(memory_space=pltpu.SMEM)


def vmem():
    return pl.BlockSpec(memory_space=pltpu.VMEM)


def pack_kernel(place, student, *outs):
    y, x = place[0], place[1]
    part = outs[0].shape[1] // 2
    for r, x_step in enumerate((0, 1, SIDE - 1, 2)):
        for k, y_steps in enumerate(((2, 0), (1, SIDE - 1))):
            for i, y_step in enumerate(y_steps):
                slot = lax.rem(y + y_step, SIDE) * SIDE + lax.rem(x + x_step, SIDE)
                first = pl.multiple_of(slot * part, 128)
                outs[2 * r + k][:, i * part : (i + 1) * part] = student[:, pl.ds(first, part)]


def pack(place, student):
    part = student.shape[1] // (SIDE * SIDE)
    shape = jax.ShapeDtypeStruct((SUB, 2 * part), bf16)
    return pl.pallas_call(
        pack_kernel,
        in_specs=[smem(), vmem()],
        out_specs=[vmem()] * 8,
        out_shape=[shape] * 8,
        compiler_params=pltpu.CompilerParams(vmem_limit_bytes=16 * 2**20),
        cost_estimate=pl.CostEstimate(
            flops=0, bytes_accessed=4 * SUB * student.shape[1], transcendentals=0
        ),
    )(place, student)


def turn_kernel(own_count, p0, p1, p2, p3, turned, near):
    rows = jnp.concatenate([p[...] for p in (p0, p1, p2, p3)], axis=0)
    flat = rows.T
    turned[...] = flat
    mine = flat[:, :SUB].astype(f32)
    live = lax.broadcasted_iota(jnp.int32, mine.shape, 1) < own_count[0]
    total = jnp.sum(jnp.where(live, mine, 0.0), axis=1, keepdims=True)
    near[...] = total / own_count[0].astype(f32)


def turn(own_count, pieces):
    width = pieces[0].shape[1]
    return pl.pallas_call(
        turn_kernel,
        in_specs=[smem()] + [vmem()] * SIDE,
        out_specs=[vmem()] * 2,
        out_shape=[
            jax.ShapeDtypeStruct((width, SIDE * SUB), bf16),
            jax.ShapeDtypeStruct((width, 1), f32),
        ],
        compiler_params=pltpu.CompilerParams(vmem_limit_bytes=16 * 2**20),
        cost_estimate=pl.CostEstimate(
            flops=0, bytes_accessed=4 * SUB * SIDE * width, transcendentals=0
        ),
    )(own_count, *pieces)


def moments_kernel(counts, *refs):
    out = refs[-1]
    for r in range(SIDE):
        for k in range(2):
            value = refs[2 * r + k][...].astype(f32)
            columns = slice(k * value.shape[1], (k + 1) * value.shape[1])
            live = lax.broadcasted_iota(jnp.int32, value.shape, 0) < counts[r]
            total = jnp.sum(jnp.where(live, value, 0.0), axis=0, keepdims=True)
            dev = jnp.where(live, value - total / counts[r].astype(f32), 0.0)
            out[r : r + 1, columns] = total
            out[SIDE + r : SIDE + r + 1, columns] = jnp.sum(dev * dev, axis=0, keepdims=True)


def moments(counts, pieces):
    width = pieces[0].shape[1]
    return pl.pallas_call(
        moments_kernel,
        in_specs=[smem()] + [vmem()] * len(pieces),
        out_specs=vmem(),
        out_shape=jax.ShapeDtypeStruct((2 * SIDE, 2 * width), f32),
        compiler_params=pltpu.CompilerParams(vmem_limit_bytes=16 * 2**20),
        cost_estimate=pl.CostEstimate(
            flops=8 * SUB * SIDE * width, bytes_accessed=4 * SUB * SIDE * width, transcendentals=0
        ),
    )(counts, *pieces)


def pool_kernel(counts, before, teacher, behind, meta, full, first, second, stats, mix, share, pooled):
    window = SUB + 2 * HALO
    length = teacher.shape[0]
    j = pl.program_id(0)

    @pl.when(j == 0)
    def _():
        for r in range(SIDE):
            rows = slice(r * SUB, (r + 1) * SUB)
            place = lax.broadcasted_iota(jnp.int32, (SUB, window), 1)
            local = meta[rows, 0:1] - (r * SUB - HALO)
            found = jnp.zeros((SUB, window), jnp.int32)
            whole = jnp.zeros((SUB, 1), jnp.int32)
            for k in range(BAND):
                weight = meta[rows, 1 + k : 2 + k]
                found = found + jnp.where(place == local + k, weight, 0)
                whole = whole + weight
            mix[rows, :] = found.astype(f32).astype(bf16)
            share[rows, :] = jnp.broadcast_to(whole.astype(f32), (SUB, 128))

    total = jnp.zeros((1, teacher.shape[1]), f32)
    alive = jnp.int32(0)
    for r in range(SIDE):
        rows = slice(r * SUB, (r + 1) * SUB)
        low, high = r * SUB - HALO, (r + 1) * SUB + HALO
        parts = [teacher[max(low, 0) : min(high, length), :]]
        if low < 0:
            parts = [before[...]] + parts
        if high > length:
            parts = parts + [behind[...]]
        seen = jnp.concatenate(parts, axis=0) if len(parts) > 1 else parts[0]
        value = jnp.dot(mix[rows, :], seen, preferred_element_type=f32)
        value = value / share[rows, 0:1]
        pooled[rows, :] = value
        live = lax.broadcasted_iota(jnp.int32, value.shape, 0) < counts[r]
        total = total + jnp.sum(jnp.where(live, value, 0.0), axis=0, keepdims=True)
        alive = alive + counts[r]
    mean = total / alive.astype(f32)
    square = jnp.zeros_like(total)
    for r in range(SIDE):
        rows = slice(r * SUB, (r + 1) * SUB)
        value = pooled[rows, :]
        live = lax.broadcasted_iota(jnp.int32, value.shape, 0) < counts[r]
        dev = jnp.where(live, value - mean, 0.0)
        small = dev.astype(bf16)
        full[rows, :] = small

        @pl.when(j < pl.num_programs(0) // 2)
        def _():
            first[rows, :] = small

        @pl.when(j >= pl.num_programs(0) // 2)
        def _():
            second[rows, :] = small

        square = square + jnp.sum(dev * dev, axis=0, keepdims=True)
    stats[0:1, :] = total
    stats[1:2, :] = square
    stats[2:3, :] = jnp.broadcast_to(alive.astype(f32), total.shape)


def pool(counts, before, teacher, behind, meta):
    rows, columns = teacher.shape
    tile = 256
    last = columns // tile // 2
    return pl.pallas_call(
        pool_kernel,
        grid=(columns // tile,),
        in_specs=[
            smem(),
            pl.BlockSpec((HALO, tile), lambda j: (0, j)),
            pl.BlockSpec((rows, tile), lambda j: (0, j)),
            pl.BlockSpec((HALO, tile), lambda j: (0, j)),
            pl.BlockSpec(meta.shape, lambda j: (0, 0)),
        ],
        out_specs=[
            pl.BlockSpec((rows, tile), lambda j: (0, j)),
            pl.BlockSpec((rows, tile), lambda j: (0, jnp.minimum(j, last - 1))),
            pl.BlockSpec((rows, tile), lambda j: (0, jnp.maximum(j - last, 0))),
            pl.BlockSpec((3, tile), lambda j: (0, j)),
        ],
        out_shape=[
            jax.ShapeDtypeStruct((rows, columns), bf16),
            jax.ShapeDtypeStruct((rows, columns // 2), bf16),
            jax.ShapeDtypeStruct((rows, columns // 2), bf16),
            jax.ShapeDtypeStruct((3, columns), f32),
        ],
        scratch_shapes=[
            pltpu.VMEM((rows, SUB + 2 * HALO), bf16),
            pltpu.VMEM((rows, 128), f32),
            pltpu.VMEM((rows, tile), f32),
        ],
        compiler_params=pltpu.CompilerParams(vmem_limit_bytes=32 * 2**20),
        cost_estimate=pl.CostEstimate(
            flops=2 * rows * 256 * columns, bytes_accessed=6 * rows * columns, transcendentals=0
        ),
    )(counts, before, teacher, behind, meta)


def sums_of(place, near, left, right):
    z = place[0]
    total = None
    for a, step in zip(left, COMING):
        first = pl.multiple_of(lax.rem(z + step, SIDE) * SUB, 16)
        rows = pl.ds(first, SUB)
        far = jnp.concatenate([right[3][rows, :], right[4][rows, :]], axis=1)
        b = jnp.concatenate([right[0][rows, :], right[1][rows, :], right[2][rows, :], far], axis=0)
        term = jnp.dot(a, b, preferred_element_type=f32)
        total = term if total is None else total + term
    part = total.shape[0] - 16
    return total[:part] - near * total[part : part + 1]


def left_of(refs, i):
    ones = jnp.ones((16, refs[0].shape[1]), bf16)
    far = jnp.where(i == 0, refs[3][...], refs[4][...])
    return [jnp.concatenate([a, ones], axis=0) for a in [r[...] for r in refs[:3]] + [far]]


def open_kernel(place, *refs):
    left, own, mate, near = refs[:5], refs[5:10], refs[10:15], refs[15]
    up, down, kept = refs[16:]
    i = pl.program_id(0)
    half = up.shape[1]
    a = left_of(left, i)
    results = [sums_of(place, near[...], a, side) for side in (own, mate)]

    @pl.when(i == 0)
    def _():
        up[...] = results[0].astype(bf16)
        down[...] = results[1].astype(bf16)

    @pl.when(i == 1)
    def _():
        kept[:, :half] = results[0]
        kept[:, half:] = results[1]


def close_kernel(place, *refs):
    left, own, mate, near = refs[:5], refs[5:10], refs[10:15], refs[15]
    from_back, from_next, up, down = refs[16:]
    i = pl.program_id(0)
    half = from_back.shape[1]
    a = left_of(left, i)
    results = [sums_of(place, near[...], a, side) for side in (own, mate)]

    @pl.when(i == 0)
    def _():
        up[:, :half] = (results[0] + from_back[...].astype(f32)).astype(bf16)
        up[:, half:] = results[1].astype(bf16)

    @pl.when(i == 1)
    def _():
        down[:, :half] = results[0].astype(bf16)
        down[:, half:] = (results[1] + from_next[...].astype(f32)).astype(bf16)


def product(place, k, left, own, mate, near, arrived=None):
    depth = left[0].shape[1]
    part = left[0].shape[0] // 2
    rows = own[1].shape[0]
    half = own[1].shape[1]
    one = lambda i, place: (0, 0)
    side = (
        [pl.BlockSpec((rows, half), lambda i, place: (0, k))]
        + [pl.BlockSpec((rows, half), one)] * 2
        + [pl.BlockSpec((rows, half // 2), one)] * 2
    )
    in_specs = (
        [pl.BlockSpec((part, depth), lambda i, place: (i, 0))] * 3
        + [pl.BlockSpec((part, depth), one)] * 2
        + side * 2
        + [pl.BlockSpec((part, 1), lambda i, place: (i, 0))]
    )
    S = jax.ShapeDtypeStruct
    if arrived is None:
        kernel, extra = open_kernel, ()
        shapes = [S((part, half), bf16), S((part, half), bf16), S((part, 2 * half), f32)]
    else:
        kernel, extra = close_kernel, arrived
        in_specs = in_specs + [pl.BlockSpec((part, half), one)] * 2
        shapes = [S((part, 2 * half), bf16), S((part, 2 * half), bf16)]
    return pl.pallas_call(
        kernel,
        grid_spec=pltpu.PrefetchScalarGridSpec(
            num_scalar_prefetch=1,
            grid=(2,),
            in_specs=in_specs,
            out_specs=[pl.BlockSpec(s.shape, one) for s in shapes],
        ),
        out_shape=shapes,
        compiler_params=pltpu.CompilerParams(vmem_limit_bytes=40 * 2**20),
        cost_estimate=pl.CostEstimate(
            flops=2 * 2 * part * depth * SIDE * 2 * half,
            bytes_accessed=2 * SIDE * depth * (2 * part + 2 * half) + 6 * part * half,
            transcendentals=0,
        ),
    )(place, *left, *own, *mate, near, *extra)


def final_kernel(place, kept, first, second, between, row_scale, column_scale, *rest):
    out = rest[-1]
    inside = kept[...] + first[...].astype(f32) + second[...].astype(f32)
    out[...] = inside * row_scale[...] * column_scale[...] + between[...]


def final(place, k, kept, first, second, between, row_scale, column_scale, whole=None):
    part, columns = kept.shape
    half = columns // 2
    block = pl.BlockSpec((part, half), lambda i, place: (0, i))
    in_specs = [block] * 4 + [
        pl.BlockSpec((part, 1), lambda i, place: (0, 0)),
        pl.BlockSpec((1, half), lambda i, place: (0, i)),
    ]
    more, aliases = (), {}
    if whole is not None:
        in_specs = in_specs + [pl.BlockSpec(memory_space=pl.ANY)]
        more, aliases = (whole,), {7: 0}
    return pl.pallas_call(
        final_kernel,
        grid_spec=pltpu.PrefetchScalarGridSpec(
            num_scalar_prefetch=1,
            grid=(2,),
            in_specs=in_specs,
            out_specs=pl.BlockSpec(
                (part, half), lambda i, place: (0, lax.rem(place[1] + i, 2) * 2 + k)
            ),
        ),
        out_shape=jax.ShapeDtypeStruct((part, 2 * columns), f32),
        input_output_aliases=aliases,
        compiler_params=pltpu.CompilerParams(vmem_limit_bytes=16 * 2**20),
        cost_estimate=pl.CostEstimate(
            flops=6 * part * columns, bytes_accessed=16 * part * columns, transcendentals=0
        ),
    )(place, kept, first, second, between, row_scale, column_scale, *more)


def per_device(student, teacher, starts, weights, counts):
    y, x, z, c = (lax.axis_index(n) for n in ("y", "x", "row", "col"))
    shard = y * SIDE + x
    rows = starts.shape[0]
    columns = teacher.shape[1]
    half = columns // 2
    width = student.shape[1] // SIDE
    part = width // SIDE

    up = [(i, (i + 1) % 16) for i in range(16)]
    down = [(j, i) for i, j in up]
    before = lax.ppermute(teacher[rows - HALO :], ("y", "x"), up)
    behind = lax.ppermute(teacher[:HALO], ("y", "x"), down)

    packed = pack(jnp.stack([y, x]).astype(jnp.int32), student)
    packed, before, behind = lax.optimization_barrier((packed, before, behind))
    steps = (0, 1, -1, 2)
    got0 = [packed[0]] + [ring(packed[2 * r], "x", steps[r]) for r in (1, 2, 3)]

    meta = jnp.concatenate([(starts - shard * rows)[:, None], weights], axis=1)
    standard, *halves, stats = pool(counts[0], before, teacher, behind, meta)
    later = after([packed[2 * r + 1] for r in range(SIDE)], stats)
    got1 = [later[0]] + [ring(later[r], "x", steps[r]) for r in (1, 2, 3)]

    counts_row = jnp.pad(counts.astype(f32), ((0, 0), (0, columns - SIDE)))
    near = jnp.stack(ring_all(jnp.concatenate([stats, counts_row]), "x"))
    group_counts = near[:, 3, :SIDE]
    halves = after(halves, near)

    own_count = lax.dynamic_slice_in_dim(counts[0], z, 1)
    lefts, means = [], []
    for got in (got0, got1):
        turned, mean = turn(own_count, got)
        z_up = ring(turned, "row", 1)
        z_down = ring(turned, "row", -1)
        far = [ring(z_up[:part], "row", 1), ring(z_down[part:], "row", -1)]
        lefts.append([turned, z_up, z_down] + far)
        means.append(mean)

    t_standard = swap(standard)
    owns, mates = [], []
    for k in range(2):
        right1 = ring(halves[k], "x", 1)
        left1 = ring(halves[k], "x", -1)
        quarter = half // 2
        far = [ring(right1[:, :quarter], "x", 1), ring(left1[:, quarter:], "x", -1)]
        own = [right1, left1] + far
        owns.append([standard] + own)
        mates.append([t_standard] + [swap(p) for p in own])

    own_counts = lax.dynamic_index_in_dim(group_counts, z, 1, keepdims=True)
    pieces = [p for pair in zip(got0, got1) for p in pair]
    s_z = jnp.stack(ring_all(moments(own_counts[:, 0].astype(jnp.int32), pieces), "row"))
    z_counts = jnp.stack(
        [
            lax.dynamic_index_in_dim(group_counts, lax.rem(z + k, SIDE), 1, keepdims=True)
            for k in COMING
        ]
    )
    shard_count = jnp.sum(group_counts, axis=1, keepdims=True)
    shard_sum = jnp.sum(s_z[:, :SIDE], axis=0)
    shard_off = s_z[:, :SIDE] / z_counts - shard_sum / shard_count
    shard_square = jnp.sum(s_z[:, SIDE:] + z_counts * shard_off * shard_off, axis=0)

    both = jnp.concatenate([near[:, 0], near[:, 1], near[:, 2], shard_sum, shard_square])
    every = ring_all(both, "y")
    t_sum, t_square, t_count = (
        jnp.concatenate([e[i * SIDE : (i + 1) * SIDE] for e in every]) for i in range(3)
    )
    s_sum, s_square = (
        jnp.concatenate(
            [
                e[i * SIDE : (i + 1) * SIDE, slot * part : (slot + 1) * part]
                for e, slot in zip(every, (1, 2, 3, 0))
            ]
        )
        for i in (3, 4)
    )
    s_count = t_count[:, :1]
    tokens = jnp.sum(s_count)
    t_local = t_sum / t_count
    t_mean = jnp.sum(t_sum, axis=0) / tokens
    t_off = t_local - t_mean
    t_var = (jnp.sum(t_square, axis=0) + jnp.sum(t_count * t_off * t_off, axis=0)) / tokens
    t_scale = lax.rsqrt(t_var + epsilon)
    t_rows = jnp.concatenate([t_off * t_scale, t_scale[None]])
    t_mate = swap(t_rows)
    s_mean = jnp.sum(s_sum, axis=0) / tokens
    s_off = s_sum / s_count - s_mean
    s_var = (jnp.sum(s_square, axis=0) + jnp.sum(s_count * s_off * s_off, axis=0)) / tokens
    s_scale = lax.rsqrt(s_var + epsilon) / jnp.sqrt(tokens)
    s_rows = s_off * s_scale * s_count

    place = jnp.stack([z, c]).astype(jnp.int32)
    opened = []
    for k in range(2):
        u_up, u_down, kept = product(place, k, lefts[0], owns[k], mates[k], means[0])
        opened.append((ring(u_up, "y", 1), ring(u_down, "y", -1), kept))
    out = None
    for k in range(2):
        u_up, u_down, kept = opened[k]
        v_up, v_down = product(place, k, lefts[1], owns[k], mates[k], means[1], (u_up, u_down))
        v_up, v_down = ring(v_up, "y", 1), ring(v_down, "y", -1)
        t_k = jnp.concatenate(
            [t[:, k * half : (k + 1) * half] for t in (t_rows, t_mate)], axis=1
        )
        between = lax.dot_general(
            s_rows, t_k[:-1], (((0,), (0,)), ((), ())), precision=lax.Precision.HIGHEST
        )
        out = final(
            place, k, kept, v_up, v_down, between, s_scale[:, None], t_k[-1:], out
        )
    return out[None, None]


def solution(mesh):
    fine = Mesh(mesh.devices.reshape(SIDE, SIDE, SIDE, 2), ("y", "x", "row", "col"))
    seq = ("y", "x")
    placed = (
        P(seq + ("row",), "col"),
        P(seq, ("row", "col")),
        P(seq),
        P(seq, None),
        P(seq, None),
    )
    return jax.shard_map(
        per_device,
        mesh=fine,
        in_specs=placed,
        out_specs=P("col", seq, None, "row"),
        check_vma=False,
    )
```

time: 213 us -> 210 us (0.986)
  waiting for transfers between devices: 79.8 us -> 52.3 us
  starting transfers between devices: 53 us -> 73 us
  Pallas kernels: 32.9 us -> 45.2 us
  local copies, waits for them, and re-layouts: 24 us -> 16.1 us
    ppermute x35 -> x39, starting transfers between devices: 46.9 us -> 65.5 us  [ring(): lax.ppermute(value, axis, [(i, (i + step) % SIDE) for i in range(SIDE)])]
    ppermute x35 -> x39, waiting for transfers between devices: 70.5 us -> 52.2 us  [ring(): lax.ppermute(value, axis, [(i, (i + step) % SIDE) for i in range(SIDE)])]
    pallas_call x5 -> x11, Pallas kernels: 32.9 us -> 45.2 us  [the longest x4 29.4 us: product(): pl.pallas_call(kernel, grid_spec=pltpu.PrefetchScalarGridSpec(num_scalar_...]
    ppermute x1, waiting for transfers between devices: 9.3 us -> 0.01 us  [per_device(): before = lax.ppermute(teacher[rows - HALO:], ('y', 'x'), up)]
    unnamed x18 -> x66, local copies, waits for them, and re-layouts: 1.34 us -> 5.36 us
    transpose x2 -> x0, other arithmetic: 3.61 us -> none  [the longest x1 3.6 us: per_device(): turned = block.T]
    convert_element_type x1 -> x0, local copies, waits for them, and re-layouts: 3.56 us -> none  [per_device(): values = block.astype(jnp.float32).reshape(SIDE, SUB, width)]
    concatenate x1 -> x5, other arithmetic: 0.01 us -> 2.93 us  [the longest x2 1.44 us: per_device(): t_rows = jnp.concatenate([t_off * t_scale, t_scale[None]])]
  transfers between devices with their start and end apart: 43 -> 51, of which waited for: 16 -> 16; matrix products, arithmetic and copies ran while one was open for 16% -> 14% of each run, Pallas kernels for 15% -> 17%
where the time goes in v2:
time: 210 us; the launch traced here: 208 us
  starting transfers between devices  73 us (35%)
  waiting for transfers between devices  52.3 us (25%)
  Pallas kernels  45.2 us (22%)
  other arithmetic  18.4 us (9%)
  local copies, waits for them, and re-layouts  16.1 us (8%)
  matrix products  2.21 us (1%)
    ppermute x39, starting transfers between devices, ring(): lax.ppermute(value, axis, [(i, (i + step) % SIDE) for i in range(SIDE)])  65.5 us
    ppermute x39, waiting for transfers between devices, ring(): lax.ppermute(value, axis, [(i, (i + step) % SIDE) for i in range(SIDE)])  52.2 us
    pallas_call x4, Pallas kernels, product(): pl.pallas_call(kernel, grid_spec=pltpu.PrefetchScalarGridSpec(num_scalar_...  29.4 us
    pallas_call x1, Pallas kernels, pool(): pl.pallas_call(pool_kernel, grid=(columns // tile,), in_specs=[smem(), pl...  5.43 us
    unnamed x66, local copies, waits for them, and re-layouts  5.36 us
    slice x4, local copies, waits for them, and re-layouts, per_device(): far = [ring(z_up[:part], 'row', 1), ring(z_down[part:], 'row', -1)]  4.85 us
    reduce_sum x4, other arithmetic, per_device(): jnp.sum(s_square, axis=0) + jnp.sum(s_count * s_off * s_off, axis=0)  4.43 us
  transfers between devices with their start and end apart: 51, of which 16 were waited for; matrix products, arithmetic and copies ran while one was open for 14% of the time, Pallas kernels for 17%

profile of v2, /device:TPU:0, one launch (start us, length us, event | category | flops | bytes accessed | tf_op | source)
XLA Modules:
  0.0 208.4 jit_solution(7628108316301169106)
XLA Ops:
  0.9 1.6 collective-permute-start
  2.5 3.8 %collective-permute-start.1 = (bf16[16,1024]{1,0:T(8,128)(2,1)S(1)}, bf16[16,1024]{1,0:T(8,128)(2,1)S(1)}, u32[]{:S(2)}, u32[]{:S(2)}) collective-permute-start(bf16[16,1024]{1,0:T(8,128)(2,1)S(1)} %get-tuple-element.109), channel_id=1, source_target_pairs={{8,0},{16,8},{24,16},{32,24},{40,32},{48,40},{56,48},{64,56},{72,6... | collective-permute-start | bytes 98312 | tf_op jit(solution)/shard_map/ppermute | solution.py:372
  8.6 1.4 copy-done.1
  10.0 1.5 shard_map.55
  11.6 5.4 %shard_map.57 = (bf16[768,1024]{1,0:T(8,128)(2,1)}, bf16[768,512]{1,0:T(8,128)(2,1)S(1)}, bf16[768,512]{1,0:T(8,128)(2,1)S(1)}, f32[3,1024]{1,0:T(4,128)S(1)}) custom-call(s32[4]{0:T(128)S(1)} %bitcast.29, bf16[16,1024]{1,0:T(8,128)(2,1)S(1)} %collective-permute-done.before, bf16[768,1024]{1,0:T(8,128)(2,1)S(1)} %copy-done, ...), custom_call_target="tpu_custom_call" | custom-call | flops 402653184 | bytes 4718592 | tf_op jit(solution)/shard_map/pallas_call | solution.py:188
  17.1 3.2 %collective-permute-start.10 = (f32[4,1024]{1,0:T(4,128)S(1)}, f32[4,1024]{1,0:T(4,128)S(1)}, u32[]{:S(2)}, u32[]{:S(2)}) collective-permute-start(f32[4,1024]{1,0:T(4,128)S(1)} %select_maximum_fusion), channel_id=1, source_target_pairs={{0,24},{8,0},{16,8},{24,16},{1,25},{9,1},{17,9},{25,17},{2,26},{10... | collective-permute-start | bytes 49160 | tf_op jit(solution)/shard_map/ppermute | solution.py:20
  21.2 2.4 %collective-permute-start.22 = (bf16[192,512]{1,0:T(8,128)(2,1)}, bf16[192,512]{1,0:T(8,128)(2,1)S(1)}, u32[]{:S(2)}, u32[]{:S(2)}) collective-permute-start(bf16[192,512]{1,0:T(8,128)(2,1)} %get-tuple-element.75), channel_id=1, source_target_pairs={{0,24},{8,0},{16,8},{24,16},{1,25},{9,1},{17,9},{25,17},{2,26},{10... | collective-permute-start | bytes 589832 | tf_op jit(solution)/shard_map/ppermute | solution.py:20
  23.7 2.3 %collective-permute-start.23 = (bf16[192,512]{1,0:T(8,128)(2,1)}, bf16[192,512]{1,0:T(8,128)(2,1)S(1)}, u32[]{:S(2)}, u32[]{:S(2)}) collective-permute-start(bf16[192,512]{1,0:T(8,128)(2,1)} %get-tuple-element.76), channel_id=1, source_target_pairs={{0,16},{8,24},{16,0},{24,8},{1,17},{9,25},{17,1},{25,9},{2,18},{10... | collective-permute-start | bytes 589832 | tf_op jit(solution)/shard_map/ppermute | solution.py:20
  26.1 3.3 %collective-permute-start.3 = (bf16[192,512]{1,0:T(8,128)(2,1)S(1)}, bf16[192,512]{1,0:T(8,128)(2,1)S(1)}, u32[]{:S(2)}, u32[]{:S(2)}) collective-permute-start(bf16[192,512]{1,0:T(8,128)(2,1)S(1)} %get-tuple-element.57), channel_id=1, source_target_pairs={{0,24},{8,0},{16,8},{24,16},{1,25},{9,1},{17,9},{25,17},{2,26},{10... | collective-permute-start | bytes 589832 | tf_op jit(solution)/shard_map/ppermute | solution.py:20
  29.5 1.3 collective-permute-done.21.p1.refs_3_
  30.8 3.7 %collective-permute-start.4 = (bf16[192,512]{1,0:T(8,128)(2,1)S(1)}, bf16[192,512]{1,0:T(8,128)(2,1)S(1)}, u32[]{:S(2)}, u32[]{:S(2)}) collective-permute-start(bf16[192,512]{1,0:T(8,128)(2,1)S(1)} %get-tuple-element.58), channel_id=1, source_target_pairs={{0,16},{8,24},{16,0},{24,8},{1,17},{9,25},{17,1},{25,9},{2,18},{10... | collective-permute-start | bytes 589832 | tf_op jit(solution)/shard_map/ppermute | solution.py:20
  35.2 2.2 %collective-permute-done.2.p1.refs_2_ = bf16[192,512]{1,0:T(8,128)(2,1)S(1)} collective-permute-done((bf16[192,512]{1,0:T(8,128)(2,1)}, bf16[192,512]{1,0:T(8,128)(2,1)S(1)}, u32[]{:S(2)}, u32[]{:S(2)}) %collective-permute-start.2) | collective-permute-done | bytes 196640 | tf_op jit(solution)/shard_map/ppermute | solution.py:20
  37.3 2.3 %collective-permute-done.3.p2.refs_4_ = bf16[192,512]{1,0:T(8,128)(2,1)S(1)} collective-permute-done((bf16[192,512]{1,0:T(8,128)(2,1)S(1)}, bf16[192,512]{1,0:T(8,128)(2,1)S(1)}, u32[]{:S(2)}, u32[]{:S(2)}) %collective-permute-start.3) | collective-permute-done | bytes 196640 | tf_op jit(solution)/shard_map/ppermute | solution.py:20
  39.6 1.1 collective-permute-done.4.p3.refs_6_
  40.7 1.6 shard_map.61
  42.3 1.9 collective-permute-start.32
  44.2 2.2 %collective-permute-start.33 = (f32[8,1024]{1,0:T(8,128)S(1)}, f32[8,1024]{1,0:T(8,128)S(1)}, u32[]{:S(2)}, u32[]{:S(2)}) collective-permute-start(f32[8,1024]{1,0:T(8,128)S(1)} %shard_map.61), channel_id=1, source_target_pairs={{0,6},{2,0},{4,2},{6,4},{1,7},{3,1},{5,3},{7,5},{8,14},{10,8},{12,... | collective-permute-start | bytes 98312 | tf_op jit(solution)/shard_map/ppermute | solution.py:20
  46.4 1.8 collective-permute-start.34
  48.5 3.4 %collective-permute-done.34 = f32[8,1024]{1,0:T(8,128)S(1)} collective-permute-done((f32[8,1024]{1,0:T(8,128)S(1)}, f32[8,1024]{1,0:T(8,128)S(1)}, u32[]{:S(2)}, u32[]{:S(2)}) %collective-permute-start.34) | collective-permute-done | bytes 32800 | tf_op jit(solution)/shard_map/ppermute | solution.py:20
  52.4 1.4 collective-permute-start.39
  53.8 1.8 collective-permute-start.40
  56.0 2.9 %collective-permute-start.13 = (bf16[768,512]{1,0:T(8,128)(2,1)}, bf16[768,512]{1,0:T(8,128)(2,1)S(1)}, u32[]{:S(2)}, u32[]{:S(2)}) collective-permute-start(bf16[768,512]{1,0:T(8,128)(2,1)} %copy-done.9), channel_id=1, source_target_pairs={{0,24},{8,0},{16,8},{24,16},{1,25},{9,1},{17,9},{25,17},{2,26},{10... | collective-permute-start | bytes 2359304 | tf_op jit(solution)/shard_map/ppermute | solution.py:20
  58.9 3.1 %collective-permute-start.36 = (f32[20,1024]{1,0:T(8,128)S(1)}, f32[20,1024]{1,0:T(8,128)S(1)}, u32[]{:S(2)}, u32[]{:S(2)}) collective-permute-start(f32[20,1024]{1,0:T(8,128)S(1)} %concatenate.31), channel_id=1, source_target_pairs={{0,96},{32,0},{64,32},{96,64},{1,97},{33,1},{65,33},{97,65},{2,98}... | collective-permute-start | bytes 245768 | tf_op jit(solution)/shard_map/ppermute | solution.py:20
  62.0 3.2 %collective-permute-done.36 = f32[20,1024]{1,0:T(8,128)S(1)} collective-permute-done((f32[20,1024]{1,0:T(8,128)S(1)}, f32[20,1024]{1,0:T(8,128)S(1)}, u32[]{:S(2)}, u32[]{:S(2)}) %collective-permute-start.36) | collective-permute-done | bytes 81952 | tf_op jit(solution)/shard_map/ppermute | solution.py:20
  65.2 1.9 collective-permute-start.37
  67.1 4.2 %collective-permute-done.37 = f32[20,1024]{1,0:T(8,128)S(1)} collective-permute-done((f32[20,1024]{1,0:T(8,128)S(1)}, f32[20,1024]{1,0:T(8,128)S(1)}, u32[]{:S(2)}, u32[]{:S(2)}) %collective-permute-start.37) | collective-permute-done | bytes 81952 | tf_op jit(solution)/shard_map/ppermute | solution.py:20
  76.4 1.7 shard_map.56
  79.5 1.7 shard_map.59
  81.9 3.2 %collective-permute-start.6 = (bf16[512,768]{1,0:T(8,128)(2,1)}, bf16[512,768]{1,0:T(8,128)(2,1)}, u32[]{:S(2)}, u32[]{:S(2)}) collective-permute-start(bf16[512,768]{1,0:T(8,128)(2,1)} %get-tuple-element.59.refs_0_), channel_id=1, source_target_pairs={{0,6},{2,0},{4,2},{6,4},{1,7},{3,1},{5,3},{7,5},{8,14},{10,8},{12,... | collective-permute-start | bytes 2359304 | tf_op jit(solution)/shard_map/ppermute | solution.py:20
  85.1 2.0 collective-permute-done.12.refs_6_
  87.2 2.0 collective-permute-start.25
  89.9 1.0 slice.204
  90.9 10.3 %collective-permute-done.5.refs_1_ = bf16[512,768]{1,0:T(8,128)(2,1)S(1)} collective-permute-done((bf16[512,768]{1,0:T(8,128)(2,1)}, bf16[512,768]{1,0:T(8,128)(2,1)S(1)}, u32[]{:S(2)}, u32[]{:S(2)}) %collective-permute-start.5) | collective-permute-done | bytes 786464 | tf_op jit(solution)/shard_map/ppermute | solution.py:20
  102.1 1.0 slice.205
  103.3 2.9 %collective-permute-start.42 = (bf16[768,256]{1,0:T(8,128)(2,1)S(1)}, bf16[768,256]{1,0:T(8,128)(2,1)S(1)}, u32[]{:S(2)}, u32[]{:S(2)}) collective-permute-start(bf16[768,256]{1,0:T(8,128)(2,1)S(1)} %slice.205), channel_id=1, source_target_pairs={{0,24},{8,0},{16,8},{24,16},{1,25},{9,1},{17,9},{25,17},{2,26},{10... | collective-permute-start | bytes 1179656 | tf_op jit(solution)/shard_map/ppermute | solution.py:20
  106.2 11.6 %collective-permute-done.24.refs_1_ = bf16[512,768]{1,0:T(8,128)(2,1)} collective-permute-done((bf16[512,768]{1,0:T(8,128)(2,1)}, bf16[512,768]{1,0:T(8,128)(2,1)}, u32[]{:S(2)}, u32[]{:S(2)}) %collective-permute-start.24) | collective-permute-done | bytes 786464 | tf_op jit(solution)/shard_map/ppermute | solution.py:20
  117.8 1.3 slice_reduce_fusion.10
  119.1 1.0 slice.169
  120.2 3.3 %collective-permute-start.15 = (bf16[768,256]{1,0:T(8,128)(2,1)S(1)}, bf16[768,256]{1,0:T(8,128)(2,1)}, u32[]{:S(2)}, u32[]{:S(2)}) collective-permute-start(bf16[768,256]{1,0:T(8,128)(2,1)S(1)} %slice.172), channel_id=1, source_target_pairs={{0,24},{8,0},{16,8},{24,16},{1,25},{9,1},{17,9},{25,17},{2,26},{10... | collective-permute-start | bytes 1179656 | tf_op jit(solution)/shard_map/ppermute | solution.py:20
  123.5 1.3 slice_reduce_fusion.9
  124.7 1.8 slice.170
  126.5 3.2 %collective-permute-start.8 = (bf16[256,768]{1,0:T(8,128)(2,1)}, bf16[256,768]{1,0:T(8,128)(2,1)}, u32[]{:S(2)}, u32[]{:S(2)}) collective-permute-start(bf16[256,768]{1,0:T(8,128)(2,1)} %slice.170), channel_id=1, source_target_pairs={{0,6},{2,0},{4,2},{6,4},{1,7},{3,1},{5,3},{7,5},{8,14},{10,8},{12,... | collective-permute-start | bytes 1179656 | tf_op jit(solution)/shard_map/ppermute | solution.py:20
  129.8 1.3 slice_reduce_fusion.8
  131.6 3.2 %collective-permute-done.7.refs_3_ = bf16[256,768]{1,0:T(8,128)(2,1)S(1)} collective-permute-done((bf16[256,768]{1,0:T(8,128)(2,1)S(1)}, bf16[256,768]{1,0:T(8,128)(2,1)S(1)}, u32[]{:S(2)}, u32[]{:S(2)}) %collective-permute-start.7) | collective-permute-done | bytes 393248 | tf_op jit(solution)/shard_map/ppermute | solution.py:20
  136.4 1.2 add_divide_fusion.1
  140.3 1.9 rsqrt_divide_fusion
  142.3 1.4 fusion.11
  146.7 1.0 slice.173
  147.7 1.0 slice.174
  148.8 3.2 %collective-permute-start.27 = (bf16[256,768]{1,0:T(8,128)(2,1)S(1)}, bf16[256,768]{1,0:T(8,128)(2,1)S(1)}, u32[]{:S(2)}, u32[]{:S(2)}) collective-permute-start(bf16[256,768]{1,0:T(8,128)(2,1)S(1)} %slice.174), channel_id=1, source_target_pairs={{0,6},{2,0},{4,2},{6,4},{1,7},{3,1},{5,3},{7,5},{8,14},{10,8},{12,... | collective-permute-start | bytes 1179656 | tf_op jit(solution)/shard_map/ppermute | solution.py:20
  152.1 7.3 %shard_map.62 = (bf16[256,512]{1,0:T(8,128)(2,1)S(1)}, bf16[256,512]{1,0:T(8,128)(2,1)S(1)}, f32[256,1024]{1,0:T(8,128)S(1)}) custom-call(s32[2]{0:T(128)S(1)} %pad_add_fusion.1.place, bf16[512,768]{1,0:T(8,128)(2,1)} %get-tuple-element.59.refs_0_, bf16[512,768]{1,0:T(8,128)(2,1)S(1)} %copy-done.7, bf16[512,768]{1,0:T(8,128)(2,1)} %collective-permute-done.6.refs_2_, ...), custom_call_target="tpu_custom_call" | custom-call | flops 3221225472 | bytes 10223616 | tf_op jit(solution)/shard_map/pallas_call | solution.py:305
  159.4 1.1 collective-permute-start.47
  160.4 3.0 %collective-permute-start.48 = (bf16[256,512]{1,0:T(8,128)(2,1)S(1)}, bf16[256,512]{1,0:T(8,128)(2,1)S(1)}, u32[]{:S(2)}, u32[]{:S(2)}) collective-permute-start(bf16[256,512]{1,0:T(8,128)(2,1)S(1)} %get-tuple-element.86), channel_id=1, source_target_pairs={{0,96},{32,0},{64,32},{96,64},{1,97},{33,1},{65,33},{97,65},{2,98}... | collective-permute-start | bytes 786440 | tf_op jit(solution)/shard_map/ppermute | solution.py:20
  163.4 7.3 %shard_map.58 = (bf16[256,512]{1,0:T(8,128)(2,1)S(1)}, bf16[256,512]{1,0:T(8,128)(2,1)S(1)}, f32[256,1024]{1,0:T(8,128)S(1)}) custom-call(s32[2]{0:T(128)S(1)} %pad_add_fusion.1.place, bf16[512,768]{1,0:T(8,128)(2,1)} %get-tuple-element.59.refs_0_, bf16[512,768]{1,0:T(8,128)(2,1)S(1)} %copy-done.7, bf16[512,768]{1,0:T(8,128)(2,1)} %collective-permute-done.6.refs_2_, ...), custom_call_target="tpu_custom_call" | custom-call | flops 3221225472 | bytes 10223616 | tf_op jit(solution)/shard_map/pallas_call | solution.py:305
  170.8 3.2 %collective-permute-start.29 = (bf16[256,512]{1,0:T(8,128)(2,1)S(1)}, bf16[256,512]{1,0:T(8,128)(2,1)S(1)}, u32[]{:S(2)}, u32[]{:S(2)}) collective-permute-start(bf16[256,512]{1,0:T(8,128)(2,1)S(1)} %get-tuple-element.80), channel_id=1, source_target_pairs={{0,96},{32,0},{64,32},{96,64},{1,97},{33,1},{65,33},{97,65},{2,98}... | collective-permute-start | bytes 786440 | tf_op jit(solution)/shard_map/ppermute | solution.py:20
  174.0 7.4 %shard_map.63 = (bf16[256,1024]{1,0:T(8,128)(2,1)S(1)}, bf16[256,1024]{1,0:T(8,128)(2,1)S(1)}) custom-call(s32[2]{0:T(128)S(1)} %pad_add_fusion.1.place, bf16[512,768]{1,0:T(8,128)(2,1)} %get-tuple-element.77.refs_0_, bf16[512,768]{1,0:T(8,128)(2,1)} %collective-permute-done.24.refs_1_, bf16[512,768]{1,0:T(8,128)(2,1)} %collective-permute-done.25.refs_2_, ...), custom_call_target="tpu_custom_call" | custom-call | flops 3221225472 | bytes 10223616 | tf_op jit(solution)/shard_map/pallas_call | solution.py:305
  181.6 3.3 %collective-permute-start.50 = (bf16[256,1024]{1,0:T(8,128)(2,1)S(1)}, bf16[256,1024]{1,0:T(8,128)(2,1)S(1)}, u32[]{:S(2)}, u32[]{:S(2)}) collective-permute-start(bf16[256,1024]{1,0:T(8,128)(2,1)S(1)} %get-tuple-element.88), channel_id=1, source_target_pairs={{0,96},{32,0},{64,32},{96,64},{1,97},{33,1},{65,33},{97,65},{2,98}... | collective-permute-start | bytes 1572872 | tf_op jit(solution)/shard_map/ppermute | solution.py:20
  184.9 7.4 %shard_map.60 = (bf16[256,1024]{1,0:T(8,128)(2,1)S(1)}, bf16[256,1024]{1,0:T(8,128)(2,1)S(1)}) custom-call(s32[2]{0:T(128)S(1)} %pad_add_fusion.1.place, bf16[512,768]{1,0:T(8,128)(2,1)} %get-tuple-element.77.refs_0_, bf16[512,768]{1,0:T(8,128)(2,1)} %collective-permute-done.24.refs_1_, bf16[512,768]{1,0:T(8,128)(2,1)} %collective-permute-done.25.refs_2_, ...), custom_call_target="tpu_custom_call" | custom-call | flops 3221225472 | bytes 10223616 | tf_op jit(solution)/shard_map/pallas_call | solution.py:305
  192.4 3.2 %collective-permute-start.31 = (bf16[256,1024]{1,0:T(8,128)(2,1)S(1)}, bf16[256,1024]{1,0:T(8,128)(2,1)S(1)}, u32[]{:S(2)}, u32[]{:S(2)}) collective-permute-start(bf16[256,1024]{1,0:T(8,128)(2,1)S(1)} %get-tuple-element.82), channel_id=1, source_target_pairs={{0,96},{32,0},{64,32},{96,64},{1,97},{33,1},{65,33},{97,65},{2,98}... | collective-permute-start | bytes 1572872 | tf_op jit(solution)/shard_map/ppermute | solution.py:20
  195.7 1.1 fusion.4.between
  196.8 1.1 fusion.7.between
  197.9 1.9 shard_map.64.rest_0_
  199.8 6.7 %collective-permute-done.30.first = bf16[256,1024]{1,0:T(8,128)(2,1)S(1)} collective-permute-done((bf16[256,1024]{1,0:T(8,128)(2,1)S(1)}, bf16[256,1024]{1,0:T(8,128)(2,1)S(1)}, u32[]{:S(2)}, u32[]{:S(2)}) %collective-permute-start.30) | collective-permute-done | bytes 524320 | tf_op jit(solution)/shard_map/ppermute | solution.py:20
  206.5 1.9 shard_map.65
  (174 shorter events, 22.6 us)
Async XLA Ops:
  0.9 10.6 %collective-permute-start = (bf16[16,1024]{1,0:T(8,128)(2,1)S(1)}, bf16[16,1024]{1,0:T(8,128)(2,1)S(1)}, u32[]{:S(2)}, u32[]{:S(2)}) collective-permute-start(bf16[16,1024]{1,0:T(8,128)(2,1)S(1)} %get-tuple-element.110), channel_id=1, source_target_pairs={{0,8},{8,16},{16,24},{24,32},{32,40},{40,48},{48,56},{56,64},{64,7... | collective-permute-start | bytes 98312 | tf_op jit(solution)/shard_map/ppermute | solution.py:371
  2.5 9.1 %collective-permute-start.1 = (bf16[16,1024]{1,0:T(8,128)(2,1)S(1)}, bf16[16,1024]{1,0:T(8,128)(2,1)S(1)}, u32[]{:S(2)}, u32[]{:S(2)}) collective-permute-start(bf16[16,1024]{1,0:T(8,128)(2,1)S(1)} %get-tuple-element.109), channel_id=1, source_target_pairs={{8,0},{16,8},{24,16},{32,24},{40,32},{48,40},{56,48},{64,56},{72,6... | collective-permute-start | bytes 98312 | tf_op jit(solution)/shard_map/ppermute | solution.py:372
  17.0 34.9 %copy-start.9 = (bf16[768,512]{1,0:T(8,128)(2,1)}, bf16[768,512]{1,0:T(8,128)(2,1)S(1)}, u32[]{:S(2)}) copy-start(bf16[768,512]{1,0:T(8,128)(2,1)S(1)} %get-tuple-element.66) | copy-start | bytes 2359300
  17.0 34.9 %copy-start.10 = (bf16[768,512]{1,0:T(8,128)(2,1)}, bf16[768,512]{1,0:T(8,128)(2,1)S(1)}, u32[]{:S(2)}) copy-start(bf16[768,512]{1,0:T(8,128)(2,1)S(1)} %get-tuple-element.83) | copy-start | bytes 2359300
  17.0 6.7 %collective-permute-start.9 = (f32[4,1024]{1,0:T(4,128)S(1)}, f32[4,1024]{1,0:T(4,128)S(1)}, u32[]{:S(2)}, u32[]{:S(2)}) collective-permute-start(f32[4,1024]{1,0:T(4,128)S(1)} %select_maximum_fusion), channel_id=1, source_target_pairs={{0,8},{8,16},{16,24},{24,0},{1,9},{9,17},{17,25},{25,1},{2,10},{10... | collective-permute-start | bytes 49160 | tf_op jit(solution)/shard_map/ppermute | solution.py:20
  17.1 8.9 %collective-permute-start.10 = (f32[4,1024]{1,0:T(4,128)S(1)}, f32[4,1024]{1,0:T(4,128)S(1)}, u32[]{:S(2)}, u32[]{:S(2)}) collective-permute-start(f32[4,1024]{1,0:T(4,128)S(1)} %select_maximum_fusion), channel_id=1, source_target_pairs={{0,24},{8,0},{16,8},{24,16},{1,25},{9,1},{17,9},{25,17},{2,26},{10... | collective-permute-start | bytes 49160 | tf_op jit(solution)/shard_map/ppermute | solution.py:20
  20.3 5.8 %collective-permute-start.11 = (f32[4,1024]{1,0:T(4,128)S(1)}, f32[4,1024]{1,0:T(4,128)S(1)}, u32[]{:S(2)}, u32[]{:S(2)}) collective-permute-start(f32[4,1024]{1,0:T(4,128)S(1)} %select_maximum_fusion), channel_id=1, source_target_pairs={{0,16},{8,24},{16,0},{24,8},{1,17},{9,25},{17,1},{25,9},{2,18},{10... | collective-permute-start | bytes 49160 | tf_op jit(solution)/shard_map/ppermute | solution.py:20
  20.3 10.5 %collective-permute-start.21 = (bf16[192,512]{1,0:T(8,128)(2,1)S(1)}, bf16[192,512]{1,0:T(8,128)(2,1)S(1)}, u32[]{:S(2)}, u32[]{:S(2)}) collective-permute-start(bf16[192,512]{1,0:T(8,128)(2,1)S(1)} %get-tuple-element.74), channel_id=1, source_target_pairs={{0,8},{8,16},{16,24},{24,0},{1,9},{9,17},{17,25},{25,1},{2,10},{10... | collective-permute-start | bytes 589832 | tf_op jit(solution)/shard_map/ppermute | solution.py:20
  21.2 13.9 %collective-permute-start.22 = (bf16[192,512]{1,0:T(8,128)(2,1)}, bf16[192,512]{1,0:T(8,128)(2,1)S(1)}, u32[]{:S(2)}, u32[]{:S(2)}) collective-permute-start(bf16[192,512]{1,0:T(8,128)(2,1)} %get-tuple-element.75), channel_id=1, source_target_pairs={{0,24},{8,0},{16,8},{24,16},{1,25},{9,1},{17,9},{25,17},{2,26},{10... | collective-permute-start | bytes 589832 | tf_op jit(solution)/shard_map/ppermute | solution.py:20
  23.7 11.5 %collective-permute-start.23 = (bf16[192,512]{1,0:T(8,128)(2,1)}, bf16[192,512]{1,0:T(8,128)(2,1)S(1)}, u32[]{:S(2)}, u32[]{:S(2)}) collective-permute-start(bf16[192,512]{1,0:T(8,128)(2,1)} %get-tuple-element.76), channel_id=1, source_target_pairs={{0,16},{8,24},{16,0},{24,8},{1,17},{9,25},{17,1},{25,9},{2,18},{10... | collective-permute-start | bytes 589832 | tf_op jit(solution)/shard_map/ppermute | solution.py:20
  26.0 11.3 %collective-permute-start.2 = (bf16[192,512]{1,0:T(8,128)(2,1)}, bf16[192,512]{1,0:T(8,128)(2,1)S(1)}, u32[]{:S(2)}, u32[]{:S(2)}) collective-permute-start(bf16[192,512]{1,0:T(8,128)(2,1)} %get-tuple-element.56), channel_id=1, source_target_pairs={{0,8},{8,16},{16,24},{24,0},{1,9},{9,17},{17,25},{25,1},{2,10},{10... | collective-permute-start | bytes 589832 | tf_op jit(solution)/shard_map/ppermute | solution.py:20
  26.1 13.5 %collective-permute-start.3 = (bf16[192,512]{1,0:T(8,128)(2,1)S(1)}, bf16[192,512]{1,0:T(8,128)(2,1)S(1)}, u32[]{:S(2)}, u32[]{:S(2)}) collective-permute-start(bf16[192,512]{1,0:T(8,128)(2,1)S(1)} %get-tuple-element.57), channel_id=1, source_target_pairs={{0,24},{8,0},{16,8},{24,16},{1,25},{9,1},{17,9},{25,17},{2,26},{10... | collective-permute-start | bytes 589832 | tf_op jit(solution)/shard_map/ppermute | solution.py:20
  30.8 9.8 %collective-permute-start.4 = (bf16[192,512]{1,0:T(8,128)(2,1)S(1)}, bf16[192,512]{1,0:T(8,128)(2,1)S(1)}, u32[]{:S(2)}, u32[]{:S(2)}) collective-permute-start(bf16[192,512]{1,0:T(8,128)(2,1)S(1)} %get-tuple-element.58), channel_id=1, source_target_pairs={{0,16},{8,24},{16,0},{24,8},{1,17},{9,25},{17,1},{25,9},{2,18},{10... | collective-permute-start | bytes 589832 | tf_op jit(solution)/shard_map/ppermute | solution.py:20
  35.1 18.7 %copy-start.22 = (f32[4,1024]{1,0:T(4,128)}, f32[4,1024]{1,0:T(4,128)S(1)}, u32[]{:S(2)}) copy-start(f32[4,1024]{1,0:T(4,128)S(1)} %get-tuple-element.124) | copy-start | bytes 49156
  35.1 18.7 %copy-start.23 = (f32[4,1024]{1,0:T(4,128)}, f32[4,1024]{1,0:T(4,128)S(1)}, u32[]{:S(2)}) copy-start(f32[4,1024]{1,0:T(4,128)S(1)} %get-tuple-element.126) | copy-start | bytes 49156
  42.3 6.0 %collective-permute-start.32 = (f32[8,1024]{1,0:T(8,128)S(1)}, f32[8,1024]{1,0:T(8,128)S(1)}, u32[]{:S(2)}, u32[]{:S(2)}) collective-permute-start(f32[8,1024]{1,0:T(8,128)S(1)} %shard_map.61), channel_id=1, source_target_pairs={{0,2},{2,4},{4,6},{6,0},{1,3},{3,5},{5,7},{7,1},{8,10},{10,12},{12... | collective-permute-start | bytes 98312 | tf_op jit(solution)/shard_map/ppermute | solution.py:20
  44.2 4.2 %collective-permute-start.33 = (f32[8,1024]{1,0:T(8,128)S(1)}, f32[8,1024]{1,0:T(8,128)S(1)}, u32[]{:S(2)}, u32[]{:S(2)}) collective-permute-start(f32[8,1024]{1,0:T(8,128)S(1)} %shard_map.61), channel_id=1, source_target_pairs={{0,6},{2,0},{4,2},{6,4},{1,7},{3,1},{5,3},{7,5},{8,14},{10,8},{12,... | collective-permute-start | bytes 98312 | tf_op jit(solution)/shard_map/ppermute | solution.py:20
  46.4 5.4 %collective-permute-start.34 = (f32[8,1024]{1,0:T(8,128)S(1)}, f32[8,1024]{1,0:T(8,128)S(1)}, u32[]{:S(2)}, u32[]{:S(2)}) collective-permute-start(f32[8,1024]{1,0:T(8,128)S(1)} %shard_map.61), channel_id=1, source_target_pairs={{0,4},{2,6},{4,0},{6,2},{1,5},{3,7},{5,1},{7,3},{8,12},{10,14},{12... | collective-permute-start | bytes 98312 | tf_op jit(solution)/shard_map/ppermute | solution.py:20
  52.2 6.7 %collective-permute-start.35 = (f32[20,1024]{1,0:T(8,128)S(1)}, f32[20,1024]{1,0:T(8,128)S(1)}, u32[]{:S(2)}, u32[]{:S(2)}) collective-permute-start(f32[20,1024]{1,0:T(8,128)S(1)} %concatenate.31), channel_id=1, source_target_pairs={{0,32},{32,64},{64,96},{96,0},{1,33},{33,65},{65,97},{97,1},{2,34}... | collective-permute-start | bytes 245768 | tf_op jit(solution)/shard_map/ppermute | solution.py:20
  52.4 29.5 %collective-permute-start.39 = (bf16[768,512]{1,0:T(8,128)(2,1)}, bf16[768,512]{1,0:T(8,128)(2,1)S(1)}, u32[]{:S(2)}, u32[]{:S(2)}) collective-permute-start(bf16[768,512]{1,0:T(8,128)(2,1)} %copy-done.10), channel_id=1, source_target_pairs={{0,8},{8,16},{16,24},{24,0},{1,9},{9,17},{17,25},{25,1},{2,10},{10... | collective-permute-start | bytes 2359304 | tf_op jit(solution)/shard_map/ppermute | solution.py:20
  53.8 31.3 %collective-permute-start.40 = (bf16[768,512]{1,0:T(8,128)(2,1)}, bf16[768,512]{1,0:T(8,128)(2,1)S(1)}, u32[]{:S(2)}, u32[]{:S(2)}) collective-permute-start(bf16[768,512]{1,0:T(8,128)(2,1)} %copy-done.10), channel_id=1, source_target_pairs={{0,24},{8,0},{16,8},{24,16},{1,25},{9,1},{17,9},{25,17},{2,26},{10... | collective-permute-start | bytes 2359304 | tf_op jit(solution)/shard_map/ppermute | solution.py:20
  55.6 31.5 %collective-permute-start.12 = (bf16[768,512]{1,0:T(8,128)(2,1)}, bf16[768,512]{1,0:T(8,128)(2,1)S(1)}, u32[]{:S(2)}, u32[]{:S(2)}) collective-permute-start(bf16[768,512]{1,0:T(8,128)(2,1)} %copy-done.9), channel_id=1, source_target_pairs={{0,8},{8,16},{16,24},{24,0},{1,9},{9,17},{17,25},{25,1},{2,10},{10... | collective-permute-start | bytes 2359304 | tf_op jit(solution)/shard_map/ppermute | solution.py:20
  56.0 33.2 %collective-permute-start.13 = (bf16[768,512]{1,0:T(8,128)(2,1)}, bf16[768,512]{1,0:T(8,128)(2,1)S(1)}, u32[]{:S(2)}, u32[]{:S(2)}) collective-permute-start(bf16[768,512]{1,0:T(8,128)(2,1)} %copy-done.9), channel_id=1, source_target_pairs={{0,24},{8,0},{16,8},{24,16},{1,25},{9,1},{17,9},{25,17},{2,26},{10... | collective-permute-start | bytes 2359304 | tf_op jit(solution)/shard_map/ppermute | solution.py:20
  58.9 6.3 %collective-permute-start.36 = (f32[20,1024]{1,0:T(8,128)S(1)}, f32[20,1024]{1,0:T(8,128)S(1)}, u32[]{:S(2)}, u32[]{:S(2)}) collective-permute-start(f32[20,1024]{1,0:T(8,128)S(1)} %concatenate.31), channel_id=1, source_target_pairs={{0,96},{32,0},{64,32},{96,64},{1,97},{33,1},{65,33},{97,65},{2,98}... | collective-permute-start | bytes 245768 | tf_op jit(solution)/shard_map/ppermute | solution.py:20
  65.2 6.1 %collective-permute-start.37 = (f32[20,1024]{1,0:T(8,128)S(1)}, f32[20,1024]{1,0:T(8,128)S(1)}, u32[]{:S(2)}, u32[]{:S(2)}) collective-permute-start(f32[20,1024]{1,0:T(8,128)S(1)} %concatenate.31), channel_id=1, source_target_pairs={{0,64},{32,96},{64,0},{96,32},{1,65},{33,97},{65,1},{97,33},{2,66}... | collective-permute-start | bytes 245768 | tf_op jit(solution)/shard_map/ppermute | solution.py:20
  75.7 3.1 %collective-permute-start.38 = (f32[17,1024]{1,0:T(8,128)S(1)}, f32[17,1024]{1,0:T(8,128)S(1)}, u32[]{:S(2)}, u32[]{:S(2)}) collective-permute-start(f32[17,1024]{1,0:T(8,128)S(1)} %pad_maximum_fusion), channel_id=1, source_target_pairs={{0,1},{1,0},{2,3},{3,2},{4,5},{5,4},{6,7},{7,6},{8,9},{9,8},{10,11... | collective-permute-start | bytes 208904 | tf_op jit(solution)/shard_map/ppermute | solution.py:28
  79.4 21.8 %collective-permute-start.5 = (bf16[512,768]{1,0:T(8,128)(2,1)}, bf16[512,768]{1,0:T(8,128)(2,1)S(1)}, u32[]{:S(2)}, u32[]{:S(2)}) collective-permute-start(bf16[512,768]{1,0:T(8,128)(2,1)} %get-tuple-element.59.refs_0_), channel_id=1, source_target_pairs={{0,2},{2,4},{4,6},{6,0},{1,3},{3,5},{5,7},{7,1},{8,10},{10,12},{12... | collective-permute-start | bytes 2359304 | tf_op jit(solution)/shard_map/ppermute | solution.py:20
  81.9 21.4 %collective-permute-start.6 = (bf16[512,768]{1,0:T(8,128)(2,1)}, bf16[512,768]{1,0:T(8,128)(2,1)}, u32[]{:S(2)}, u32[]{:S(2)}) collective-permute-start(bf16[512,768]{1,0:T(8,128)(2,1)} %get-tuple-element.59.refs_0_), channel_id=1, source_target_pairs={{0,6},{2,0},{4,2},{6,4},{1,7},{3,1},{5,3},{7,5},{8,14},{10,8},{12,... | collective-permute-start | bytes 2359304 | tf_op jit(solution)/shard_map/ppermute | solution.py:20
  85.1 32.6 %collective-permute-start.24 = (bf16[512,768]{1,0:T(8,128)(2,1)}, bf16[512,768]{1,0:T(8,128)(2,1)}, u32[]{:S(2)}, u32[]{:S(2)}) collective-permute-start(bf16[512,768]{1,0:T(8,128)(2,1)} %get-tuple-element.77.refs_0_), channel_id=1, source_target_pairs={{0,2},{2,4},{4,6},{6,0},{1,3},{3,5},{5,7},{7,1},{8,10},{10,12},{12... | collective-permute-start | bytes 2359304 | tf_op jit(solution)/shard_map/ppermute | solution.py:20
  87.2 33.0 %collective-permute-start.25 = (bf16[512,768]{1,0:T(8,128)(2,1)}, bf16[512,768]{1,0:T(8,128)(2,1)}, u32[]{:S(2)}, u32[]{:S(2)}) collective-permute-start(bf16[512,768]{1,0:T(8,128)(2,1)} %get-tuple-element.77.refs_0_), channel_id=1, source_target_pairs={{0,6},{2,0},{4,2},{6,4},{1,7},{3,1},{5,3},{7,5},{8,14},{10,8},{12,... | collective-permute-start | bytes 2359304 | tf_op jit(solution)/shard_map/ppermute | solution.py:20
  89.2 50.5 %collective-permute-start.16 = (bf16[768,1024]{1,0:T(8,128)(2,1)}, bf16[768,1024]{1,0:T(8,128)(2,1)}, u32[]{:S(2)}, u32[]{:S(2)}) collective-permute-start(bf16[768,1024]{1,0:T(8,128)(2,1)} %get-tuple-element.62.refs_5_), channel_id=1, source_target_pairs={{0,1},{1,0},{2,3},{3,2},{4,5},{5,4},{6,7},{7,6},{8,9},{9,8},{10,11... | collective-permute-start | bytes 4718600 | tf_op jit(solution)/shard_map/ppermute | solution.py:28
  101.2 22.2 %collective-permute-start.41 = (bf16[768,256]{1,0:T(8,128)(2,1)S(1)}, bf16[768,256]{1,0:T(8,128)(2,1)}, u32[]{:S(2)}, u32[]{:S(2)}) collective-permute-start(bf16[768,256]{1,0:T(8,128)(2,1)S(1)} %slice.204), channel_id=1, source_target_pairs={{0,8},{8,16},{16,24},{24,0},{1,9},{9,17},{17,25},{25,1},{2,10},{10... | collective-permute-start | bytes 1179656 | tf_op jit(solution)/shard_map/ppermute | solution.py:20
  103.1 28.3 %copy-start.3 = (bf16[768,512]{1,0:T(8,128)(2,1)S(1)}, bf16[768,512]{1,0:T(8,128)(2,1)}, u32[]{:S(2)}) copy-start(bf16[768,512]{1,0:T(8,128)(2,1)} %copy-done.2) | copy-start | bytes 2359300
  103.1 35.2 %copy-start.5 = (bf16[768,512]{1,0:T(8,128)(2,1)S(1)}, bf16[768,512]{1,0:T(8,128)(2,1)}, u32[]{:S(2)}) copy-start(bf16[768,512]{1,0:T(8,128)(2,1)} %copy-done.4) | copy-start | bytes 2359300
  103.3 23.2 %collective-permute-start.42 = (bf16[768,256]{1,0:T(8,128)(2,1)S(1)}, bf16[768,256]{1,0:T(8,128)(2,1)S(1)}, u32[]{:S(2)}, u32[]{:S(2)}) collective-permute-start(bf16[768,256]{1,0:T(8,128)(2,1)S(1)} %slice.205), channel_id=1, source_target_pairs={{0,24},{8,0},{16,8},{24,16},{1,25},{9,1},{17,9},{25,17},{2,26},{10... | collective-permute-start | bytes 1179656 | tf_op jit(solution)/shard_map/ppermute | solution.py:20
  117.8 12.0 %collective-permute-start.14 = (bf16[768,256]{1,0:T(8,128)(2,1)S(1)}, bf16[768,256]{1,0:T(8,128)(2,1)}, u32[]{:S(2)}, u32[]{:S(2)}) collective-permute-start(bf16[768,256]{1,0:T(8,128)(2,1)S(1)} %slice.171), channel_id=1, source_target_pairs={{0,8},{8,16},{16,24},{24,0},{1,9},{9,17},{17,25},{25,1},{2,10},{10... | collective-permute-start | bytes 1179656 | tf_op jit(solution)/shard_map/ppermute | solution.py:20
  120.2 11.3 %collective-permute-start.15 = (bf16[768,256]{1,0:T(8,128)(2,1)S(1)}, bf16[768,256]{1,0:T(8,128)(2,1)}, u32[]{:S(2)}, u32[]{:S(2)}) collective-permute-start(bf16[768,256]{1,0:T(8,128)(2,1)S(1)} %slice.172), channel_id=1, source_target_pairs={{0,24},{8,0},{16,8},{24,16},{1,25},{9,1},{17,9},{25,17},{2,26},{10... | collective-permute-start | bytes 1179656 | tf_op jit(solution)/shard_map/ppermute | solution.py:20
  123.5 11.4 %collective-permute-start.7 = (bf16[256,768]{1,0:T(8,128)(2,1)S(1)}, bf16[256,768]{1,0:T(8,128)(2,1)S(1)}, u32[]{:S(2)}, u32[]{:S(2)}) collective-permute-start(bf16[256,768]{1,0:T(8,128)(2,1)S(1)} %slice.169), channel_id=1, source_target_pairs={{0,2},{2,4},{4,6},{6,0},{1,3},{3,5},{5,7},{7,1},{8,10},{10,12},{12... | collective-permute-start | bytes 1179656 | tf_op jit(solution)/shard_map/ppermute | solution.py:20
  126.5 11.8 %collective-permute-start.8 = (bf16[256,768]{1,0:T(8,128)(2,1)}, bf16[256,768]{1,0:T(8,128)(2,1)}, u32[]{:S(2)}, u32[]{:S(2)}) collective-permute-start(bf16[256,768]{1,0:T(8,128)(2,1)} %slice.170), channel_id=1, source_target_pairs={{0,6},{2,0},{4,2},{6,4},{1,7},{3,1},{5,3},{7,5},{8,14},{10,8},{12,... | collective-permute-start | bytes 1179656 | tf_op jit(solution)/shard_map/ppermute | solution.py:20
  129.8 9.9 %collective-permute-start.45 = (bf16[768,256]{1,0:T(8,128)(2,1)}, bf16[768,256]{1,0:T(8,128)(2,1)}, u32[]{:S(2)}, u32[]{:S(2)}) collective-permute-start(bf16[768,256]{1,0:T(8,128)(2,1)} %collective-permute-done.41.refs_8_), channel_id=1, source_target_pairs={{0,1},{1,0},{2,3},{3,2},{4,5},{5,4},{6,7},{7,6},{8,9},{9,8},{10,11... | collective-permute-start | bytes 1179656 | tf_op jit(solution)/shard_map/ppermute | solution.py:28
  131.4 14.0 %collective-permute-start.43 = (bf16[768,512]{1,0:T(8,128)(2,1)S(1)}, bf16[768,512]{1,0:T(8,128)(2,1)}, u32[]{:S(2)}, u32[]{:S(2)}) collective-permute-start(bf16[768,512]{1,0:T(8,128)(2,1)S(1)} %copy-done.3), channel_id=1, source_target_pairs={{0,1},{1,0},{2,3},{3,2},{4,5},{5,4},{6,7},{7,6},{8,9},{9,8},{10,11... | collective-permute-start | bytes 2359304 | tf_op jit(solution)/shard_map/ppermute | solution.py:28
  135.6 6.5 %collective-permute-start.46 = (bf16[768,256]{1,0:T(8,128)(2,1)S(1)}, bf16[768,256]{1,0:T(8,128)(2,1)}, u32[]{:S(2)}, u32[]{:S(2)}) collective-permute-start(bf16[768,256]{1,0:T(8,128)(2,1)S(1)} %collective-permute-done.42.refs_9_), channel_id=1, source_target_pairs={{0,1},{1,0},{2,3},{3,2},{4,5},{5,4},{6,7},{7,6},{8,9},{9,8},{10,11... | collective-permute-start | bytes 1179656 | tf_op jit(solution)/shard_map/ppermute | solution.py:28
  138.3 10.5 %collective-permute-start.44 = (bf16[768,512]{1,0:T(8,128)(2,1)S(1)}, bf16[768,512]{1,0:T(8,128)(2,1)}, u32[]{:S(2)}, u32[]{:S(2)}) collective-permute-start(bf16[768,512]{1,0:T(8,128)(2,1)S(1)} %copy-done.5), channel_id=1, source_target_pairs={{0,1},{1,0},{2,3},{3,2},{4,5},{5,4},{6,7},{7,6},{8,9},{9,8},{10,11... | collective-permute-start | bytes 2359304 | tf_op jit(solution)/shard_map/ppermute | solution.py:28
  139.7 20.8 %collective-permute-start.17 = (bf16[768,512]{1,0:T(8,128)(2,1)S(1)}, bf16[768,512]{1,0:T(8,128)(2,1)}, u32[]{:S(2)}, u32[]{:S(2)}) collective-permute-start(bf16[768,512]{1,0:T(8,128)(2,1)S(1)} %collective-permute-done.12.refs_6_), channel_id=1, source_target_pairs={{0,1},{1,0},{2,3},{3,2},{4,5},{5,4},{6,7},{7,6},{8,9},{9,8},{10,11... | collective-permute-start | bytes 2359304 | tf_op jit(solution)/shard_map/ppermute | solution.py:28
  139.8 23.7 %collective-permute-start.18 = (bf16[768,512]{1,0:T(8,128)(2,1)S(1)}, bf16[768,512]{1,0:T(8,128)(2,1)}, u32[]{:S(2)}, u32[]{:S(2)}) collective-permute-start(bf16[768,512]{1,0:T(8,128)(2,1)S(1)} %collective-permute-done.13.refs_7_), channel_id=1, source_target_pairs={{0,1},{1,0},{2,3},{3,2},{4,5},{5,4},{6,7},{7,6},{8,9},{9,8},{10,11... | collective-permute-start | bytes 2359304 | tf_op jit(solution)/shard_map/ppermute | solution.py:28
  142.2 6.7 %collective-permute-start.19 = (bf16[768,256]{1,0:T(8,128)(2,1)}, bf16[768,256]{1,0:T(8,128)(2,1)}, u32[]{:S(2)}, u32[]{:S(2)}) collective-permute-start(bf16[768,256]{1,0:T(8,128)(2,1)} %collective-permute-done.14.refs_8_), channel_id=1, source_target_pairs={{0,1},{1,0},{2,3},{3,2},{4,5},{5,4},{6,7},{7,6},{8,9},{9,8},{10,11... | collective-permute-start | bytes 1179656 | tf_op jit(solution)/shard_map/ppermute | solution.py:28
  145.5 13.9 %collective-permute-start.20 = (bf16[768,256]{1,0:T(8,128)(2,1)}, bf16[768,256]{1,0:T(8,128)(2,1)S(1)}, u32[]{:S(2)}, u32[]{:S(2)}) collective-permute-start(bf16[768,256]{1,0:T(8,128)(2,1)} %collective-permute-done.15.refs_9_), channel_id=1, source_target_pairs={{0,1},{1,0},{2,3},{3,2},{4,5},{5,4},{6,7},{7,6},{8,9},{9,8},{10,11... | collective-permute-start | bytes 1179656 | tf_op jit(solution)/shard_map/ppermute | solution.py:28
  148.7 22.0 %collective-permute-start.26 = (bf16[256,768]{1,0:T(8,128)(2,1)S(1)}, bf16[256,768]{1,0:T(8,128)(2,1)S(1)}, u32[]{:S(2)}, u32[]{:S(2)}) collective-permute-start(bf16[256,768]{1,0:T(8,128)(2,1)S(1)} %slice.173), channel_id=1, source_target_pairs={{0,2},{2,4},{4,6},{6,0},{1,3},{3,5},{5,7},{7,1},{8,10},{10,12},{12... | collective-permute-start | bytes 1179656 | tf_op jit(solution)/shard_map/ppermute | solution.py:20
  148.8 25.2 %collective-permute-start.27 = (bf16[256,768]{1,0:T(8,128)(2,1)S(1)}, bf16[256,768]{1,0:T(8,128)(2,1)S(1)}, u32[]{:S(2)}, u32[]{:S(2)}) collective-permute-start(bf16[256,768]{1,0:T(8,128)(2,1)S(1)} %slice.174), channel_id=1, source_target_pairs={{0,6},{2,0},{4,2},{6,4},{1,7},{3,1},{5,3},{7,5},{8,14},{10,8},{12,... | collective-permute-start | bytes 1179656 | tf_op jit(solution)/shard_map/ppermute | solution.py:20
  159.4 14.6 %collective-permute-start.47 = (bf16[256,512]{1,0:T(8,128)(2,1)S(1)}, bf16[256,512]{1,0:T(8,128)(2,1)S(1)}, u32[]{:S(2)}, u32[]{:S(2)}) collective-permute-start(bf16[256,512]{1,0:T(8,128)(2,1)S(1)} %get-tuple-element.85), channel_id=1, source_target_pairs={{0,32},{32,64},{64,96},{96,0},{1,33},{33,65},{65,97},{97,1},{2,34}... | collective-permute-start | bytes 786440 | tf_op jit(solution)/shard_map/ppermute | solution.py:20
  160.4 13.6 %copy-start.16 = (f32[512,1]{1,0:T(8,128)S(1)}, f32[512,1]{1,0:T(8,128)}, u32[]{:S(2)}) copy-start(f32[512,1]{1,0:T(8,128)} %copy-done.15) | copy-start | bytes 6148
  160.4 13.6 %collective-permute-start.48 = (bf16[256,512]{1,0:T(8,128)(2,1)S(1)}, bf16[256,512]{1,0:T(8,128)(2,1)S(1)}, u32[]{:S(2)}, u32[]{:S(2)}) collective-permute-start(bf16[256,512]{1,0:T(8,128)(2,1)S(1)} %get-tuple-element.86), channel_id=1, source_target_pairs={{0,96},{32,0},{64,32},{96,64},{1,97},{33,1},{65,33},{97,65},{2,98}... | collective-permute-start | bytes 786440 | tf_op jit(solution)/shard_map/ppermute | solution.py:20
  170.7 14.2 %collective-permute-start.28 = (bf16[256,512]{1,0:T(8,128)(2,1)S(1)}, bf16[256,512]{1,0:T(8,128)(2,1)S(1)}, u32[]{:S(2)}, u32[]{:S(2)}) collective-permute-start(bf16[256,512]{1,0:T(8,128)(2,1)S(1)} %get-tuple-element.79), channel_id=1, source_target_pairs={{0,32},{32,64},{64,96},{96,0},{1,33},{33,65},{65,97},{97,1},{2,34}... | collective-permute-start | bytes 786440 | tf_op jit(solution)/shard_map/ppermute | solution.py:20
  170.8 14.1 %collective-permute-start.29 = (bf16[256,512]{1,0:T(8,128)(2,1)S(1)}, bf16[256,512]{1,0:T(8,128)(2,1)S(1)}, u32[]{:S(2)}, u32[]{:S(2)}) collective-permute-start(bf16[256,512]{1,0:T(8,128)(2,1)S(1)} %get-tuple-element.80), channel_id=1, source_target_pairs={{0,96},{32,0},{64,32},{96,64},{1,97},{33,1},{65,33},{97,65},{2,98}... | collective-permute-start | bytes 786440 | tf_op jit(solution)/shard_map/ppermute | solution.py:20
  181.5 16.4 %collective-permute-start.49 = (bf16[256,1024]{1,0:T(8,128)(2,1)S(1)}, bf16[256,1024]{1,0:T(8,128)(2,1)S(1)}, u32[]{:S(2)}, u32[]{:S(2)}) collective-permute-start(bf16[256,1024]{1,0:T(8,128)(2,1)S(1)} %get-tuple-element.87), channel_id=1, source_target_pairs={{0,32},{32,64},{64,96},{96,0},{1,33},{33,65},{65,97},{97,1},{2,34}... | collective-permute-start | bytes 1572872 | tf_op jit(solution)/shard_map/ppermute | solution.py:20
  181.6 14.1 %copy-start.20 = (f32[17,512]{1,0:T(8,128)S(1)}, f32[17,512]{1,0:T(8,128)}, u32[]{:S(2)}) copy-start(f32[17,512]{1,0:T(8,128)} %get-tuple-element.123) | copy-start | bytes 104452
  181.6 14.1 %copy-start.21 = (f32[17,512]{1,0:T(8,128)S(1)}, f32[17,512]{1,0:T(8,128)}, u32[]{:S(2)}) copy-start(f32[17,512]{1,0:T(8,128)} %get-tuple-element.122) | copy-start | bytes 104452
  181.6 14.1 %copy-start.25 = (f32[4,256]{1,0:T(4,128)S(1)}, f32[4,256]{1,0:T(4,128)}, u32[]{:S(2)}) copy-start(f32[4,256]{1,0:T(4,128)} %get-tuple-element.129) | copy-start | bytes 12292
  181.6 14.1 %copy-start.30 = (f32[256]{0:T(256)S(1)}, f32[256]{0:T(256)}, u32[]{:S(2)}) copy-start(f32[256]{0:T(256)} %rsqrt_divide_fusion) | copy-start | bytes 3076
  181.6 14.1 %copy-start.31 = (f32[256]{0:T(256)S(1)}, f32[256]{0:T(256)}, u32[]{:S(2)}) copy-start(f32[256]{0:T(256)} %add_divide_fusion.1) | copy-start | bytes 3076
  181.6 14.1 %copy-start.32 = (f32[16]{0:T(128)S(1)}, f32[16]{0:T(128)}, u32[]{:S(2)}) copy-start(f32[16]{0:T(128)} %get-tuple-element.101) | copy-start | bytes 196
  181.6 16.3 %collective-permute-start.50 = (bf16[256,1024]{1,0:T(8,128)(2,1)S(1)}, bf16[256,1024]{1,0:T(8,128)(2,1)S(1)}, u32[]{:S(2)}, u32[]{:S(2)}) collective-permute-start(bf16[256,1024]{1,0:T(8,128)(2,1)S(1)} %get-tuple-element.88), channel_id=1, source_target_pairs={{0,96},{32,0},{64,32},{96,64},{1,97},{33,1},{65,33},{97,65},{2,98}... | collective-permute-start | bytes 1572872 | tf_op jit(solution)/shard_map/ppermute | solution.py:20
  192.3 14.2 %collective-permute-start.30 = (bf16[256,1024]{1,0:T(8,128)(2,1)S(1)}, bf16[256,1024]{1,0:T(8,128)(2,1)S(1)}, u32[]{:S(2)}, u32[]{:S(2)}) collective-permute-start(bf16[256,1024]{1,0:T(8,128)(2,1)S(1)} %get-tuple-element.81), channel_id=1, source_target_pairs={{0,32},{32,64},{64,96},{96,0},{1,33},{33,65},{65,97},{97,1},{2,34}... | collective-permute-start | bytes 1572872 | tf_op jit(solution)/shard_map/ppermute | solution.py:20
  192.4 14.1 %collective-permute-start.31 = (bf16[256,1024]{1,0:T(8,128)(2,1)S(1)}, bf16[256,1024]{1,0:T(8,128)(2,1)S(1)}, u32[]{:S(2)}, u32[]{:S(2)}) collective-permute-start(bf16[256,1024]{1,0:T(8,128)(2,1)S(1)} %get-tuple-element.82), channel_id=1, source_target_pairs={{0,96},{32,0},{64,32},{96,64},{1,97},{33,1},{65,33},{97,65},{2,98}... | collective-permute-start | bytes 1572872 | tf_op jit(solution)/shard_map/ppermute | solution.py:20
  (20 other events, 83.8 us)

commit v3 on v2

--- a/solution.py
+++ b/solution.py
@@ -118,6 +118,83 @@
             flops=8 * SUB * SIDE * width, bytes_accessed=4 * SUB * SIDE * width, transcendentals=0
         ),
     )(counts, *pieces)
+
+
+def shards_kernel(counts, *refs):
+    blocks, teachers, out = refs[:SIDE], refs[SIDE : 2 * SIDE], refs[-1]
+    for r in range(SIDE):
+        for i in range(3):
+            out[i * SIDE + r : i * SIDE + r + 1, :] = teachers[r][i : i + 1, :]
+        size = [counts[q * SIDE + r].astype(f32) for q in range(SIDE)]
+        totals = [b[r : r + 1, :] for b in blocks]
+        total = totals[0] + totals[1] + totals[2] + totals[3]
+        mean = total / (size[0] + size[1] + size[2] + size[3])
+        square = jnp.zeros_like(total)
+        for q in range(SIDE):
+            off = totals[q] / size[q] - mean
+            square = square + blocks[q][SIDE + r : SIDE + r + 1, :] + size[q] * off * off
+        out[3 * SIDE + r : 3 * SIDE + r + 1, :] = total
+        out[4 * SIDE + r : 4 * SIDE + r + 1, :] = square
+
+
+def shards(counts, blocks, teachers):
+    columns = blocks[0].shape[1]
+    return pl.pallas_call(
+        shards_kernel,
+        in_specs=[smem()] + [vmem()] * (2 * SIDE),
+        out_specs=vmem(),
+        out_shape=jax.ShapeDtypeStruct((5 * SIDE, columns), f32),
+        compiler_params=pltpu.CompilerParams(vmem_limit_bytes=8 * 2**20),
+    )(counts, *blocks, *teachers)
+
+
+def settle_kernel(e0, e1, e2, e3, t_rows, s_left, work):
+    every = (e0, e1, e2, e3)
+    part = work.shape[1]
+
+    def pieces(first, columns):
+        return [e[first * SIDE : (first + 1) * SIDE, c] for e, c in zip(every, columns)]
+
+    def combine(totals, squares, counts):
+        tokens = sum(jnp.sum(n, axis=0, keepdims=True) for n in counts)
+        mean = sum(jnp.sum(t, axis=0, keepdims=True) for t in totals) / tokens
+        offs = [t / n - mean for t, n in zip(totals, counts)]
+        square = sum(
+            jnp.sum(q + n * o * o, axis=0, keepdims=True)
+            for q, n, o in zip(squares, counts, offs)
+        )
+        return offs, lax.rsqrt(square / tokens + epsilon), tokens
+
+    whole = [slice(None)] * SIDE
+    offs, scale, _ = combine(pieces(0, whole), pieces(1, whole), pieces(2, whole))
+    for j in range(SIDE):
+        t_rows[j * SIDE : (j + 1) * SIDE, :] = offs[j] * scale
+    t_rows[SIDE * SIDE : SIDE * SIDE + 1, :] = scale
+    slots = [slice(i * part, (i + 1) * part) for i in (1, 2, 3, 0)]
+    counts = pieces(2, [slice(0, part)] * SIDE)
+    offs, scale, tokens = combine(pieces(3, slots), pieces(4, slots), counts)
+    scale = scale / jnp.sqrt(tokens)
+    work[...] = jnp.zeros_like(work)
+    for j in range(SIDE):
+        work[j * SIDE : (j + 1) * SIDE, :] = offs[j] * scale * counts[j]
+    work[SIDE * SIDE : SIDE * SIDE + 1, :] = scale
+    s_left[...] = work[...].T
+
+
+def settle(every):
+    columns = every[0].shape[1]
+    part = columns // SIDE
+    return pl.pallas_call(
+        settle_kernel,
+        in_specs=[vmem()] * SIDE,
+        out_specs=[vmem()] * 2,
+        out_shape=[
+            jax.ShapeDtypeStruct((SIDE * SIDE + 1, columns), f32),
+            jax.ShapeDtypeStruct((part, 128), f32),
+        ],
+        scratch_shapes=[pltpu.VMEM((128, part), f32)],
+        compiler_params=pltpu.CompilerParams(vmem_limit_bytes=8 * 2**20),
+    )(*every)
 
 
 def pool_kernel(counts, before, teacher, behind, meta, full, first, second, stats, mix, share, pooled):
@@ -179,6 +256,11 @@
     stats[0:1, :] = total
     stats[1:2, :] = square
     stats[2:3, :] = jnp.broadcast_to(alive.astype(f32), total.shape)
+    lane = lax.broadcasted_iota(jnp.int32, total.shape, 1)
+    row = jnp.zeros(total.shape, jnp.int32)
+    for r in range(SIDE):
+        row = row + jnp.where(lane == r, counts[r], 0)
+    stats[3:4, :] = row.astype(f32)
 
 
 def pool(counts, before, teacher, behind, meta):
@@ -199,13 +281,13 @@
             pl.BlockSpec((rows, tile), lambda j: (0, j)),
             pl.BlockSpec((rows, tile), lambda j: (0, jnp.minimum(j, last - 1))),
             pl.BlockSpec((rows, tile), lambda j: (0, jnp.maximum(j - last, 0))),
-            pl.BlockSpec((3, tile), lambda j: (0, j)),
+            pl.BlockSpec((4, tile), lambda j: (0, j)),
         ],
         out_shape=[
             jax.ShapeDtypeStruct((rows, columns), bf16),
             jax.ShapeDtypeStruct((rows, columns // 2), bf16),
             jax.ShapeDtypeStruct((rows, columns // 2), bf16),
-            jax.ShapeDtypeStruct((3, columns), f32),
+            jax.ShapeDtypeStruct((4, columns), f32),
         ],
         scratch_shapes=[
             pltpu.VMEM((rows, SUB + 2 * HALO), bf16),
@@ -320,20 +402,30 @@
     )(place, *left, *own, *mate, near, *extra)
 
 
-def final_kernel(place, kept, first, second, between, row_scale, column_scale, *rest):
+def final_kernel(place, kept, first, second, s_left, t_own, t_mate, *rest):
     out = rest[-1]
+    t = jnp.where(pl.program_id(0) == 0, t_own[...], t_mate[...])
+    shards_all = SIDE * SIDE
+    between = jnp.dot(
+        s_left[:, :shards_all],
+        t[:shards_all],
+        preferred_element_type=f32,
+        precision=lax.Precision.HIGHEST,
+    )
     inside = kept[...] + first[...].astype(f32) + second[...].astype(f32)
-    out[...] = inside * row_scale[...] * column_scale[...] + between[...]
-
-
-def final(place, k, kept, first, second, between, row_scale, column_scale, whole=None):
+    row_scale = s_left[:, shards_all : shards_all + 1]
+    out[...] = inside * row_scale * t[shards_all : shards_all + 1] + between
+
+
+def final(place, k, kept, first, second, s_left, t_own, t_mate, whole=None):
     part, columns = kept.shape
     half = columns // 2
     block = pl.BlockSpec((part, half), lambda i, place: (0, i))
-    in_specs = [block] * 4 + [
-        pl.BlockSpec((part, 1), lambda i, place: (0, 0)),
-        pl.BlockSpec((1, half), lambda i, place: (0, i)),
-    ]
+    in_specs = (
+        [block] * 3
+        + [pl.BlockSpec(s_left.shape, lambda i, place: (0, 0))]
+        + [pl.BlockSpec((t_own.shape[0], half), lambda i, place: (0, k))] * 2
+    )
     more, aliases = (), {}
     if whole is not None:
         in_specs = in_specs + [pl.BlockSpec(memory_space=pl.ANY)]
@@ -352,9 +444,9 @@
         input_output_aliases=aliases,
         compiler_params=pltpu.CompilerParams(vmem_limit_bytes=16 * 2**20),
         cost_estimate=pl.CostEstimate(
-            flops=6 * part * columns, bytes_accessed=16 * part * columns, transcendentals=0
-        ),
-    )(place, kept, first, second, between, row_scale, column_scale, *more)
+            flops=6 * part * columns, bytes_accessed=12 * part * columns, transcendentals=0
+        ),
+    )(place, kept, first, second, s_left, t_own, t_mate, *more)
 
 
 def per_device(student, teacher, starts, weights, counts):
@@ -371,104 +463,81 @@
     before = lax.ppermute(teacher[rows - HALO :], ("y", "x"), up)
     behind = lax.ppermute(teacher[:HALO], ("y", "x"), down)
 
+    steps = (0, 1, -1, 2)
+
+    def send_x(chunk):
+        return [chunk[0]] + [ring(chunk[r], "x", steps[r]) for r in (1, 2, 3)]
+
     packed = pack(jnp.stack([y, x]).astype(jnp.int32), student)
     packed, before, behind = lax.optimization_barrier((packed, before, behind))
-    steps = (0, 1, -1, 2)
-    got0 = [packed[0]] + [ring(packed[2 * r], "x", steps[r]) for r in (1, 2, 3)]
-
+    got0 = send_x(packed[0::2])
     meta = jnp.concatenate([(starts - shard * rows)[:, None], weights], axis=1)
-    standard, *halves, stats = pool(counts[0], before, teacher, behind, meta)
-    later = after([packed[2 * r + 1] for r in range(SIDE)], stats)
-    got1 = [later[0]] + [ring(later[r], "x", steps[r]) for r in (1, 2, 3)]
-
-    counts_row = jnp.pad(counts.astype(f32), ((0, 0), (0, columns - SIDE)))
-    near = jnp.stack(ring_all(jnp.concatenate([stats, counts_row]), "x"))
-    group_counts = near[:, 3, :SIDE]
-    halves = after(halves, near)
-
+    standard, half0, half1, stats = pool(counts[0], before, teacher, behind, meta)
+    near = ring_all(stats, "x")
+    got0, standard, half0, half1, packed1 = lax.optimization_barrier(
+        (got0, standard, half0, half1, packed[1::2])
+    )
+
+    got1 = send_x(packed1)
     own_count = lax.dynamic_slice_in_dim(counts[0], z, 1)
-    lefts, means = [], []
-    for got in (got0, got1):
-        turned, mean = turn(own_count, got)
-        z_up = ring(turned, "row", 1)
-        z_down = ring(turned, "row", -1)
-        far = [ring(z_up[:part], "row", 1), ring(z_down[part:], "row", -1)]
-        lefts.append([turned, z_up, z_down] + far)
-        means.append(mean)
-
+    turned0, mean0 = turn(own_count, got0)
+    up0, down0 = ring(turned0, "row", 1), ring(turned0, "row", -1)
+    got1, half0, near, _ = lax.optimization_barrier((got1, half0, near, turned0))
+
+    quarter = half // 2
+    right0, left0 = ring(half0, "x", 1), ring(half0, "x", -1)
+    turned1, mean1 = turn(own_count, got1)
     t_standard = swap(standard)
-    owns, mates = [], []
-    for k in range(2):
-        right1 = ring(halves[k], "x", 1)
-        left1 = ring(halves[k], "x", -1)
-        quarter = half // 2
-        far = [ring(right1[:, :quarter], "x", 1), ring(left1[:, quarter:], "x", -1)]
-        own = [right1, left1] + far
-        owns.append([standard] + own)
-        mates.append([t_standard] + [swap(p) for p in own])
-
-    own_counts = lax.dynamic_index_in_dim(group_counts, z, 1, keepdims=True)
+    group = jnp.stack([n[3, :SIDE] for n in near])
+    z_counts = jnp.stack(
+        [lax.dynamic_index_in_dim(group, lax.rem(z + k, SIDE), 1, keepdims=False) for k in COMING]
+    )
+    z_counts = z_counts.reshape(SIDE * SIDE).astype(jnp.int32)
     pieces = [p for pair in zip(got0, got1) for p in pair]
-    s_z = jnp.stack(ring_all(moments(own_counts[:, 0].astype(jnp.int32), pieces), "row"))
-    z_counts = jnp.stack(
-        [
-            lax.dynamic_index_in_dim(group_counts, lax.rem(z + k, SIDE), 1, keepdims=True)
-            for k in COMING
-        ]
-    )
-    shard_count = jnp.sum(group_counts, axis=1, keepdims=True)
-    shard_sum = jnp.sum(s_z[:, :SIDE], axis=0)
-    shard_off = s_z[:, :SIDE] / z_counts - shard_sum / shard_count
-    shard_square = jnp.sum(s_z[:, SIDE:] + z_counts * shard_off * shard_off, axis=0)
-
-    both = jnp.concatenate([near[:, 0], near[:, 1], near[:, 2], shard_sum, shard_square])
-    every = ring_all(both, "y")
-    t_sum, t_square, t_count = (
-        jnp.concatenate([e[i * SIDE : (i + 1) * SIDE] for e in every]) for i in range(3)
-    )
-    s_sum, s_square = (
-        jnp.concatenate(
-            [
-                e[i * SIDE : (i + 1) * SIDE, slot * part : (slot + 1) * part]
-                for e, slot in zip(every, (1, 2, 3, 0))
-            ]
-        )
-        for i in (3, 4)
-    )
-    s_count = t_count[:, :1]
-    tokens = jnp.sum(s_count)
-    t_local = t_sum / t_count
-    t_mean = jnp.sum(t_sum, axis=0) / tokens
-    t_off = t_local - t_mean
-    t_var = (jnp.sum(t_square, axis=0) + jnp.sum(t_count * t_off * t_off, axis=0)) / tokens
-    t_scale = lax.rsqrt(t_var + epsilon)
-    t_rows = jnp.concatenate([t_off * t_scale, t_scale[None]])
+    moment = moments(z_counts, pieces)
+    up0, down0, turned1, moment = lax.optimization_barrier((up0, down0, turned1, moment))
+    far0 = [ring(up0[:part], "row", 1), ring(down0[part:], "row", -1)]
+    t_right0, t_left0 = swap(right0), swap(left0)
+    right0, left0, moment, _ = lax.optimization_barrier((right0, left0, moment, up0))
+    x_far0 = [ring(right0[:, :quarter], "x", 1), ring(left0[:, quarter:], "x", -1)]
+    far0, turned1, moment = lax.optimization_barrier((far0, turned1, moment))
+    every_z = ring_all(moment, "row")
+    turned1 = after(turned1, every_z)
+    up1, down1 = ring(turned1, "row", 1), ring(turned1, "row", -1)
+    t_x_far0 = [swap(f) for f in x_far0]
+    x_far0, half1 = lax.optimization_barrier((x_far0, half1))
+    right1, left1 = ring(half1, "x", 1), ring(half1, "x", -1)
+
+    every = ring_all(shards(z_counts, every_z, near), "y")
+    t_rows, s_left = settle(every)
     t_mate = swap(t_rows)
-    s_mean = jnp.sum(s_sum, axis=0) / tokens
-    s_off = s_sum / s_count - s_mean
-    s_var = (jnp.sum(s_square, axis=0) + jnp.sum(s_count * s_off * s_off, axis=0)) / tokens
-    s_scale = lax.rsqrt(s_var + epsilon) / jnp.sqrt(tokens)
-    s_rows = s_off * s_scale * s_count
 
     place = jnp.stack([z, c]).astype(jnp.int32)
-    opened = []
-    for k in range(2):
-        u_up, u_down, kept = product(place, k, lefts[0], owns[k], mates[k], means[0])
-        opened.append((ring(u_up, "y", 1), ring(u_down, "y", -1), kept))
-    out = None
-    for k in range(2):
-        u_up, u_down, kept = opened[k]
-        v_up, v_down = product(place, k, lefts[1], owns[k], mates[k], means[1], (u_up, u_down))
-        v_up, v_down = ring(v_up, "y", 1), ring(v_down, "y", -1)
-        t_k = jnp.concatenate(
-            [t[:, k * half : (k + 1) * half] for t in (t_rows, t_mate)], axis=1
-        )
-        between = lax.dot_general(
-            s_rows, t_k[:-1], (((0,), (0,)), ((), ())), precision=lax.Precision.HIGHEST
-        )
-        out = final(
-            place, k, kept, v_up, v_down, between, s_scale[:, None], t_k[-1:], out
-        )
+    z0 = [turned0, up0, down0] + far0
+    own0 = [standard, right0, left0] + x_far0
+    mate0 = [t_standard, t_right0, t_left0] + t_x_far0
+    open0 = product(place, 0, z0, own0, mate0, mean0)
+    open0, up1, down1, right1, left1 = lax.optimization_barrier(
+        (open0, up1, down1, right1, left1)
+    )
+    u0 = [ring(open0[0], "y", 1), ring(open0[1], "y", -1)]
+    far1 = [ring(up1[:part], "row", 1), ring(down1[part:], "row", -1)]
+    x_far1 = [ring(right1[:, :quarter], "x", 1), ring(left1[:, quarter:], "x", -1)]
+    t_right1, t_left1 = swap(right1), swap(left1)
+    u0, far1, t_rows, t_mate, s_left = lax.optimization_barrier((u0, far1, t_rows, t_mate, s_left))
+    z1 = [turned1, up1, down1] + far1
+    close0 = product(place, 0, z1, own0, mate0, mean1, u0)
+    close0, x_far1 = lax.optimization_barrier((close0, x_far1))
+    v0 = [ring(close0[0], "y", 1), ring(close0[1], "y", -1)]
+    t_x_far1 = [swap(f) for f in x_far1]
+    own1 = [standard, right1, left1] + x_far1
+    mate1 = [t_standard, t_right1, t_left1] + t_x_far1
+    open1 = product(place, 1, z0, own1, mate1, mean0)
+    u1 = [ring(open1[0], "y", 1), ring(open1[1], "y", -1)]
+    close1 = product(place, 1, z1, own1, mate1, mean1, u1)
+    v1 = [ring(close1[0], "y", 1), ring(close1[1], "y", -1)]
+    out = final(place, 0, open0[2], *v0, s_left, t_rows, t_mate)
+    out = final(place, 1, open1[2], *v1, s_left, t_rows, t_mate, out)
     return out[None, None]
 
 

time: 210 us -> 191 us (0.910)
  other arithmetic: 18.4 us -> 0.19 us
  starting transfers between devices: 73 us -> 68.4 us
  local copies, waits for them, and re-layouts: 16.1 us -> 19.9 us
  waiting for transfers between devices: 52.3 us -> 55.1 us
  matrix products: 2.21 us -> 0 us
    unnamed x66 -> x44, local copies, waits for them, and re-layouts: 5.36 us -> 12.8 us
    reduce_sum x13 -> x0, other arithmetic: 6.37 us -> none  [the longest x4 4.43 us: per_device(): jnp.sum(s_square, axis=0) + jnp.sum(s_count * s_off * s_off, axis=0)]
    ppermute x39, starting transfers between devices: 65.5 us -> 61.4 us  [ring(): lax.ppermute(value, axis, [(i, (i + step) % SIDE) for i in range(SIDE)])]
    div x4 -> x0, other arithmetic: 3.81 us -> none  [the longest x1 1.9 us: per_device(): s_scale = lax.rsqrt(s_var + epsilon) / jnp.sqrt(tokens)]
    concatenate x6 -> x0, other arithmetic: 2.94 us -> none  [the longest x2 1.44 us: per_device(): t_rows = jnp.concatenate([t_off * t_scale, t_scale[None]])]
    slice x9 -> x12, local copies, waits for them, and re-layouts: 7.89 us -> 5.21 us  [the longest x2 1.05 us: per_device(): far0 = [ring(up0[:part], 'row', 1), ring(down0[part:], 'row', -1)]]
    dot_general x2 -> x0, matrix products: 2.21 us -> none  [per_device(): lax.dot_general(s_rows, t_k[:-1], (((0,), (0,)), ((), ())), precision=lax...]
  transfers between devices with their start and end apart: 51 -> 51, of which waited for: 16 -> 21; matrix products, arithmetic and copies ran while one was open for 14% -> 3% of each run, Pallas kernels for 17% -> 18%
where the time goes in v3:
time: 191 us; the launch traced here: 190 us
  starting transfers between devices  68.4 us (36%)
  waiting for transfers between devices  55.1 us (29%)
  Pallas kernels  45.9 us (24%)
  local copies, waits for them, and re-layouts  19.9 us (10%)
    ppermute x39, starting transfers between devices, ring(): lax.ppermute(value, axis, [(i, (i + step) % SIDE) for i in range(SIDE)])  61.4 us
    ppermute x39, waiting for transfers between devices, ring(): lax.ppermute(value, axis, [(i, (i + step) % SIDE) for i in range(SIDE)])  53.3 us
    pallas_call x4, Pallas kernels, product(): pl.pallas_call(kernel, grid_spec=pltpu.PrefetchScalarGridSpec(num_scalar_...  27.4 us
    unnamed x44, local copies, waits for them, and re-layouts  12.8 us
    pallas_call x1, Pallas kernels, pool(): pl.pallas_call(pool_kernel, grid=(columns // tile,), in_specs=[smem(), pl...  5.75 us
    pallas_call x2, Pallas kernels, final(): pl.pallas_call(final_kernel, grid_spec=pltpu.PrefetchScalarGridSpec(num_s...  5.34 us
  transfers between devices with their start and end apart: 51, of which 21 were waited for; matrix products, arithmetic and copies ran while one was open for 3% of the time, Pallas kernels for 18%

profile of v3, /device:TPU:0, one launch (start us, length us, event | category | flops | bytes accessed | tf_op | source)
XLA Modules:
  0.0 189.8 jit_solution(14671228436006969290)
XLA Ops:
  0.9 1.6 collective-permute-start
  2.5 3.8 %collective-permute-start.1 = (bf16[16,1024]{1,0:T(8,128)(2,1)S(1)}, bf16[16,1024]{1,0:T(8,128)(2,1)S(1)}, u32[]{:S(2)}, u32[]{:S(2)}) collective-permute-start(bf16[16,1024]{1,0:T(8,128)(2,1)S(1)} %get-tuple-element.191), channel_id=1, source_target_pairs={{8,0},{16,8},{24,16},{32,24},{40,32},{48,40},{56,48},{64,56},{72,6... | collective-permute-start | bytes 98312 | tf_op jit(solution)/shard_map/ppermute | solution.py:464
  6.3 1.4 copy-done.1
  7.8 1.5 shard_map.55
  10.0 3.2 %collective-permute-start.3 = (bf16[192,512]{1,0:T(8,128)(2,1)}, bf16[192,512]{1,0:T(8,128)(2,1)S(1)}, u32[]{:S(2)}, u32[]{:S(2)}) collective-permute-start(bf16[192,512]{1,0:T(8,128)(2,1)} %get-tuple-element.106), channel_id=1, source_target_pairs={{0,24},{8,0},{16,8},{24,16},{1,25},{9,1},{17,9},{25,17},{2,26},{10... | collective-permute-start | bytes 589832 | tf_op jit(solution)/shard_map/ppermute | solution.py:20
  14.0 5.7 %shard_map.56 = (bf16[768,1024]{1,0:T(8,128)(2,1)}, bf16[768,512]{1,0:T(8,128)(2,1)}, bf16[768,512]{1,0:T(8,128)(2,1)}, f32[4,1024]{1,0:T(4,128)S(1)}) custom-call(s32[4]{0:T(128)S(1)} %bitcast.11, bf16[16,1024]{1,0:T(8,128)(2,1)S(1)} %collective-permute-done.before, bf16[768,1024]{1,0:T(8,128)(2,1)S(1)} %copy-done, ...), custom_call_target="tpu_custom_call" | custom-call | flops 402653184 | bytes 4718592 | tf_op jit(solution)/shard_map/pallas_call | solution.py:270
  19.8 2.2 %collective-permute-done.2.p1.refs_2_ = bf16[192,512]{1,0:T(8,128)(2,1)S(1)} collective-permute-done((bf16[192,512]{1,0:T(8,128)(2,1)}, bf16[192,512]{1,0:T(8,128)(2,1)S(1)}, u32[]{:S(2)}, u32[]{:S(2)}) %collective-permute-start.2) | collective-permute-done | bytes 196640 | tf_op jit(solution)/shard_map/ppermute | solution.py:20
  22.0 1.7 shard_map.57
  24.4 1.9 %collective-permute-start.5 = (bf16[512,768]{1,0:T(8,128)(2,1)}, bf16[512,768]{1,0:T(8,128)(2,1)S(1)}, u32[]{:S(2)}, u32[]{:S(2)}) collective-permute-start(bf16[512,768]{1,0:T(8,128)(2,1)} %get-tuple-element.121.refs_0_), channel_id=1, source_target_pairs={{0,2},{2,4},{4,6},{6,0},{1,3},{3,5},{5,7},{7,1},{8,10},{10,12},{12... | collective-permute-start | bytes 2359304 | tf_op jit(solution)/shard_map/ppermute | solution.py:20
  26.3 2.1 %collective-permute-start.6 = (bf16[512,768]{1,0:T(8,128)(2,1)}, bf16[512,768]{1,0:T(8,128)(2,1)}, u32[]{:S(2)}, u32[]{:S(2)}) collective-permute-start(bf16[512,768]{1,0:T(8,128)(2,1)} %get-tuple-element.121.refs_0_), channel_id=1, source_target_pairs={{0,6},{2,0},{4,2},{6,4},{1,7},{3,1},{5,3},{7,5},{8,14},{10,8},{12,... | collective-permute-start | bytes 2359304 | tf_op jit(solution)/shard_map/ppermute | solution.py:20
  29.3 2.4 %collective-permute-start.11 = (f32[4,1024]{1,0:T(4,128)S(1)}, f32[4,1024]{1,0:T(4,128)S(1)}, u32[]{:S(2)}, u32[]{:S(2)}) collective-permute-start(f32[4,1024]{1,0:T(4,128)S(1)} %get-tuple-element.133.refs_4_), channel_id=1, source_target_pairs={{0,24},{8,0},{16,8},{24,16},{1,25},{9,1},{17,9},{25,17},{2,26},{10... | collective-permute-start | bytes 49160 | tf_op jit(solution)/shard_map/ppermute | solution.py:20
  31.6 1.2 collective-permute-start.12
  34.3 2.5 %collective-permute-start.8 = (bf16[192,512]{1,0:T(8,128)(2,1)S(1)}, bf16[192,512]{1,0:T(8,128)(2,1)S(1)}, u32[]{:S(2)}, u32[]{:S(2)}) collective-permute-start(bf16[192,512]{1,0:T(8,128)(2,1)S(1)} %get-tuple-element.124), channel_id=1, source_target_pairs={{0,24},{8,0},{16,8},{24,16},{1,25},{9,1},{17,9},{25,17},{2,26},{10... | collective-permute-start | bytes 589832 | tf_op jit(solution)/shard_map/ppermute | solution.py:20
  37.0 1.1 collective-permute-start.9
  38.1 2.5 %collective-permute-done.7.p1.refs_3_ = bf16[192,512]{1,0:T(8,128)(2,1)S(1)} collective-permute-done((bf16[192,512]{1,0:T(8,128)(2,1)S(1)}, bf16[192,512]{1,0:T(8,128)(2,1)S(1)}, u32[]{:S(2)}, u32[]{:S(2)}) %collective-permute-start.7) | collective-permute-done | bytes 196640 | tf_op jit(solution)/shard_map/ppermute | solution.py:20
  40.6 4.7 %collective-permute-done.9.p3.refs_7_ = bf16[192,512]{1,0:T(8,128)(2,1)S(1)} collective-permute-done((bf16[192,512]{1,0:T(8,128)(2,1)S(1)}, bf16[192,512]{1,0:T(8,128)(2,1)S(1)}, u32[]{:S(2)}, u32[]{:S(2)}) %collective-permute-start.9) | collective-permute-done | bytes 196640 | tf_op jit(solution)/shard_map/ppermute | solution.py:20
  45.3 3.2 %collective-permute-start.16 = (bf16[768,512]{1,0:T(8,128)(2,1)}, bf16[768,512]{1,0:T(8,128)(2,1)}, u32[]{:S(2)}, u32[]{:S(2)}) collective-permute-start(bf16[768,512]{1,0:T(8,128)(2,1)} %get-tuple-element.140), channel_id=1, source_target_pairs={{0,24},{8,0},{16,8},{24,16},{1,25},{9,1},{17,9},{25,17},{2,26},{10... | collective-permute-start | bytes 2359304 | tf_op jit(solution)/shard_map/ppermute | solution.py:20
  48.9 1.7 shard_map.58
  50.6 1.6 shard_map.59.refs_0_
  52.7 1.0 slice.49
  53.8 2.9 %collective-permute-start.14 = (bf16[256,768]{1,0:T(8,128)(2,1)S(1)}, bf16[256,768]{1,0:T(8,128)(2,1)S(1)}, u32[]{:S(2)}, u32[]{:S(2)}) collective-permute-start(bf16[256,768]{1,0:T(8,128)(2,1)S(1)} %slice.49), channel_id=1, source_target_pairs={{0,6},{2,0},{4,2},{6,4},{1,7},{3,1},{5,3},{7,5},{8,14},{10,8},{12,... | collective-permute-start | bytes 1179656 | tf_op jit(solution)/shard_map/ppermute | solution.py:20
  56.7 4.4 %collective-permute-done.15.refs_6_ = bf16[768,512]{1,0:T(8,128)(2,1)} collective-permute-done((bf16[768,512]{1,0:T(8,128)(2,1)}, bf16[768,512]{1,0:T(8,128)(2,1)}, u32[]{:S(2)}, u32[]{:S(2)}) %collective-permute-start.15) | collective-permute-done | bytes 786464 | tf_op jit(solution)/shard_map/ppermute | solution.py:20
  61.1 1.0 slice.50
  62.2 1.0 slice.51
  63.3 3.3 %collective-permute-start.18 = (bf16[768,256]{1,0:T(8,128)(2,1)S(1)}, bf16[768,256]{1,0:T(8,128)(2,1)S(1)}, u32[]{:S(2)}, u32[]{:S(2)}) collective-permute-start(bf16[768,256]{1,0:T(8,128)(2,1)S(1)} %slice.51), channel_id=1, source_target_pairs={{0,24},{8,0},{16,8},{24,16},{1,25},{9,1},{17,9},{25,17},{2,26},{10... | collective-permute-start | bytes 1179656 | tf_op jit(solution)/shard_map/ppermute | solution.py:20
  67.2 4.0 %collective-permute-done.17.refs_8_ = bf16[768,256]{1,0:T(8,128)(2,1)S(1)} collective-permute-done((bf16[768,256]{1,0:T(8,128)(2,1)S(1)}, bf16[768,256]{1,0:T(8,128)(2,1)S(1)}, u32[]{:S(2)}, u32[]{:S(2)}) %collective-permute-start.17) | collective-permute-done | bytes 393248 | tf_op jit(solution)/shard_map/ppermute | solution.py:20
  73.3 2.3 %collective-permute-start.25 = (f32[8,1024]{1,0:T(8,128)S(1)}, f32[8,1024]{1,0:T(8,128)S(1)}, u32[]{:S(2)}, u32[]{:S(2)}) collective-permute-start(f32[8,1024]{1,0:T(8,128)S(1)} %shard_map.59.refs_0_), channel_id=1, source_target_pairs={{0,6},{2,0},{4,2},{6,4},{1,7},{3,1},{5,3},{7,5},{8,14},{10,8},{12,... | collective-permute-start | bytes 98312 | tf_op jit(solution)/shard_map/ppermute | solution.py:20
  75.6 1.6 collective-permute-done.25.refs_2_
  77.2 1.8 collective-permute-start.26
  79.0 3.6 %collective-permute-done.26.refs_3_ = f32[8,1024]{1,0:T(8,128)S(1)} collective-permute-done((f32[8,1024]{1,0:T(8,128)S(1)}, f32[8,1024]{1,0:T(8,128)S(1)}, u32[]{:S(2)}, u32[]{:S(2)}) %collective-permute-start.26) | collective-permute-done | bytes 32800 | tf_op jit(solution)/shard_map/ppermute | solution.py:20
  84.2 2.7 %collective-permute-start.28 = (bf16[512,768]{1,0:T(8,128)(2,1)}, bf16[512,768]{1,0:T(8,128)(2,1)S(1)}, u32[]{:S(2)}, u32[]{:S(2)}) collective-permute-start(bf16[512,768]{1,0:T(8,128)(2,1)} %get-tuple-element.157.refs_0_), channel_id=1, source_target_pairs={{0,6},{2,0},{4,2},{6,4},{1,7},{3,1},{5,3},{7,5},{8,14},{10,8},{12,... | collective-permute-start | bytes 2359304 | tf_op jit(solution)/shard_map/ppermute | solution.py:20
  89.3 2.5 %collective-permute-start.30 = (bf16[768,512]{1,0:T(8,128)(2,1)}, bf16[768,512]{1,0:T(8,128)(2,1)}, u32[]{:S(2)}, u32[]{:S(2)}) collective-permute-start(bf16[768,512]{1,0:T(8,128)(2,1)} %get-tuple-element.158), channel_id=1, source_target_pairs={{0,24},{8,0},{16,8},{24,16},{1,25},{9,1},{17,9},{25,17},{2,26},{10... | collective-permute-start | bytes 2359304 | tf_op jit(solution)/shard_map/ppermute | solution.py:20
  91.9 1.1 copy-done.4
  93.0 1.0 copy-done.6
  94.0 1.0 copy-done.8
  95.0 1.0 copy-done.10
  97.9 7.0 %shard_map.60 = (bf16[256,512]{1,0:T(8,128)(2,1)S(1)}, bf16[256,512]{1,0:T(8,128)(2,1)S(1)}, f32[256,1024]{1,0:T(8,128)S(1)}) custom-call(s32[2]{0:T(128)S(1)} %pad_add_fusion.1.place, bf16[512,768]{1,0:T(8,128)(2,1)} %get-tuple-element.121.refs_0_, bf16[512,768]{1,0:T(8,128)(2,1)S(1)} %collective-permute-done.5.refs_1_, ...), custom_call_target="tpu_custom_call" | custom-call | flops 3221225472 | bytes 10223616 | tf_op jit(solution)/shard_map/pallas_call | solution.py:387
  105.0 4.0 %collective-permute-done.29.refs_6_ = bf16[768,512]{1,0:T(8,128)(2,1)} collective-permute-done((bf16[768,512]{1,0:T(8,128)(2,1)}, bf16[768,512]{1,0:T(8,128)(2,1)}, u32[]{:S(2)}, u32[]{:S(2)}) %collective-permute-start.29) | collective-permute-done | bytes 786464 | tf_op jit(solution)/shard_map/ppermute | solution.py:20
  109.8 1.4 collective-permute-start.35
  111.2 3.3 %collective-permute-start.34 = (bf16[256,768]{1,0:T(8,128)(2,1)S(1)}, bf16[256,768]{1,0:T(8,128)(2,1)S(1)}, u32[]{:S(2)}, u32[]{:S(2)}) collective-permute-start(bf16[256,768]{1,0:T(8,128)(2,1)S(1)} %slice.53), channel_id=1, source_target_pairs={{0,6},{2,0},{4,2},{6,4},{1,7},{3,1},{5,3},{7,5},{8,14},{10,8},{12,... | collective-permute-start | bytes 1179656 | tf_op jit(solution)/shard_map/ppermute | solution.py:20
  114.5 1.6 collective-permute-start.31
  116.2 1.6 collective-permute-start.32
  118.4 6.0 %collective-permute-done.36.e2 = f32[20,1024]{1,0:T(8,128)S(1)} collective-permute-done((f32[20,1024]{1,0:T(8,128)S(1)}, f32[20,1024]{1,0:T(8,128)S(1)}, u32[]{:S(2)}, u32[]{:S(2)}) %collective-permute-start.36) | collective-permute-done | bytes 81952 | tf_op jit(solution)/shard_map/ppermute | solution.py:20
  124.5 2.0 %collective-permute-start.37 = (f32[20,1024]{1,0:T(8,128)S(1)}, f32[20,1024]{1,0:T(8,128)S(1)}, u32[]{:S(2)}, u32[]{:S(2)}) collective-permute-start(f32[20,1024]{1,0:T(8,128)S(1)} %shard_map.61.e0), channel_id=1, source_target_pairs={{0,64},{32,96},{64,0},{96,32},{1,65},{33,97},{65,1},{97,33},{2,66}... | collective-permute-start | bytes 245768 | tf_op jit(solution)/shard_map/ppermute | solution.py:20
  126.4 4.2 %collective-permute-done.37.e3 = f32[20,1024]{1,0:T(8,128)S(1)} collective-permute-done((f32[20,1024]{1,0:T(8,128)S(1)}, f32[20,1024]{1,0:T(8,128)S(1)}, u32[]{:S(2)}, u32[]{:S(2)}) %collective-permute-start.37) | collective-permute-done | bytes 81952 | tf_op jit(solution)/shard_map/ppermute | solution.py:20
  130.9 1.0 slice.54
  131.9 1.0 slice.55
  133.0 1.5 collective-permute-start.39
  134.5 1.8 collective-permute-start.40
  136.8 6.9 %shard_map.63 = (bf16[256,1024]{1,0:T(8,128)(2,1)S(1)}, bf16[256,1024]{1,0:T(8,128)(2,1)S(1)}) custom-call(s32[2]{0:T(128)S(1)} %pad_add_fusion.1.place, bf16[512,768]{1,0:T(8,128)(2,1)} %get-tuple-element.157.refs_0_, bf16[512,768]{1,0:T(8,128)(2,1)S(1)} %collective-permute-done.27.refs_1_, bf16[512,768]{1,0:T(8,128)(2,1)S(1)} %collective-permute-done.28.refs_2_, ...), custom_call_target="tpu_custom_call" | custom-call | flops 3221225472 | bytes 10223616 | tf_op jit(solution)/shard_map/pallas_call | solution.py:387
  143.7 2.2 %collective-permute-done.39.refs_8_ = bf16[768,256]{1,0:T(8,128)(2,1)S(1)} collective-permute-done((bf16[768,256]{1,0:T(8,128)(2,1)S(1)}, bf16[768,256]{1,0:T(8,128)(2,1)S(1)}, u32[]{:S(2)}, u32[]{:S(2)}) %collective-permute-start.39) | collective-permute-done | bytes 393248 | tf_op jit(solution)/shard_map/ppermute | solution.py:20
  146.4 1.2 collective-permute-done.43.refs_13_
  148.2 6.8 %shard_map.64 = (bf16[256,512]{1,0:T(8,128)(2,1)S(1)}, bf16[256,512]{1,0:T(8,128)(2,1)S(1)}, f32[256,1024]{1,0:T(8,128)S(1)}) custom-call(s32[2]{0:T(128)S(1)} %pad_add_fusion.1.place, bf16[512,768]{1,0:T(8,128)(2,1)} %get-tuple-element.121.refs_0_, bf16[512,768]{1,0:T(8,128)(2,1)S(1)} %collective-permute-done.5.refs_1_, ...), custom_call_target="tpu_custom_call" | custom-call | flops 3221225472 | bytes 10223616 | tf_op jit(solution)/shard_map/pallas_call | solution.py:387
  155.0 1.3 collective-permute-start.45
  156.3 2.0 %collective-permute-start.46 = (bf16[256,512]{1,0:T(8,128)(2,1)S(1)}, bf16[256,512]{1,0:T(8,128)(2,1)S(1)}, u32[]{:S(2)}, u32[]{:S(2)}) collective-permute-start(bf16[256,512]{1,0:T(8,128)(2,1)S(1)} %get-tuple-element.178), channel_id=1, source_target_pairs={{0,96},{32,0},{64,32},{96,64},{1,97},{33,1},{65,33},{97,65},{2,98}... | collective-permute-start | bytes 786440 | tf_op jit(solution)/shard_map/ppermute | solution.py:20
  158.3 3.2 %collective-permute-start.50 = (bf16[256,1024]{1,0:T(8,128)(2,1)S(1)}, bf16[256,1024]{1,0:T(8,128)(2,1)S(1)}, u32[]{:S(2)}, u32[]{:S(2)}) collective-permute-start(bf16[256,1024]{1,0:T(8,128)(2,1)S(1)} %get-tuple-element.186), channel_id=1, source_target_pairs={{0,96},{32,0},{64,32},{96,64},{1,97},{33,1},{65,33},{97,65},{2,98}... | collective-permute-start | bytes 1572872 | tf_op jit(solution)/shard_map/ppermute | solution.py:20
  161.5 3.9 %collective-permute-done.45.refs_16_ = bf16[256,512]{1,0:T(8,128)(2,1)S(1)} collective-permute-done((bf16[256,512]{1,0:T(8,128)(2,1)S(1)}, bf16[256,512]{1,0:T(8,128)(2,1)S(1)}, u32[]{:S(2)}, u32[]{:S(2)}) %collective-permute-start.45) | collective-permute-done | bytes 262176 | tf_op jit(solution)/shard_map/ppermute | solution.py:20
  165.5 6.7 %shard_map.65 = (bf16[256,1024]{1,0:T(8,128)(2,1)S(1)}, bf16[256,1024]{1,0:T(8,128)(2,1)S(1)}) custom-call(s32[2]{0:T(128)S(1)} %pad_add_fusion.1.place, bf16[512,768]{1,0:T(8,128)(2,1)} %get-tuple-element.157.refs_0_, bf16[512,768]{1,0:T(8,128)(2,1)S(1)} %collective-permute-done.27.refs_1_, bf16[512,768]{1,0:T(8,128)(2,1)S(1)} %collective-permute-done.28.refs_2_, ...), custom_call_target="tpu_custom_call" | custom-call | flops 3221225472 | bytes 10223616 | tf_op jit(solution)/shard_map/pallas_call | solution.py:387
  172.2 1.1 collective-permute-start.47
  173.3 2.2 %collective-permute-start.48 = (bf16[256,1024]{1,0:T(8,128)(2,1)S(1)}, bf16[256,1024]{1,0:T(8,128)(2,1)S(1)}, u32[]{:S(2)}, u32[]{:S(2)}) collective-permute-start(bf16[256,1024]{1,0:T(8,128)(2,1)S(1)} %get-tuple-element.180), channel_id=1, source_target_pairs={{0,96},{32,0},{64,32},{96,64},{1,97},{33,1},{65,33},{97,65},{2,98}... | collective-permute-start | bytes 1572872 | tf_op jit(solution)/shard_map/ppermute | solution.py:20
  175.5 1.1 collective-permute-done.49.first
  176.7 2.7 %shard_map.66.rest_0_ = f32[256,2048]{1,0:T(8,128)} custom-call(s32[2]{0:T(128)S(1)} %pad_add_fusion.1.place, f32[256,1024]{1,0:T(8,128)S(1)} %get-tuple-element.184.kept, bf16[256,1024]{1,0:T(8,128)(2,1)S(1)} %collective-permute-done.49.first, bf16[256,1024]{1,0:T(8,128)(2,1)S(1)} %collective-permute-done.50.second, ...), custom_call_target="tpu_custom_call" | custom-call | flops 1572864 | bytes 3145728 | tf_op jit(solution)/shard_map/pallas_call | solution.py:433
  179.4 7.7 %collective-permute-done.47.first = bf16[256,1024]{1,0:T(8,128)(2,1)S(1)} collective-permute-done((bf16[256,1024]{1,0:T(8,128)(2,1)S(1)}, bf16[256,1024]{1,0:T(8,128)(2,1)S(1)}, u32[]{:S(2)}, u32[]{:S(2)}) %collective-permute-start.47) | collective-permute-done | bytes 524320 | tf_op jit(solution)/shard_map/ppermute | solution.py:20
  187.1 2.7 %shard_map.67 = f32[256,2048]{1,0:T(8,128)} custom-call(s32[2]{0:T(128)S(1)} %pad_add_fusion.1.place, f32[256,1024]{1,0:T(8,128)S(1)} %get-tuple-element.176.kept, bf16[256,1024]{1,0:T(8,128)(2,1)S(1)} %collective-permute-done.47.first, bf16[256,1024]{1,0:T(8,128)(2,1)S(1)} %collective-permute-done.48.second, ...), custom_call_target="tpu_custom_call", output_to_operand_aliasing={{}: (7, {})} | custom-call | flops 1572864 | bytes 3145728 | tf_op jit(solution)/shard_map/pallas_call | solution.py:433
  (119 shorter events, 18.9 us)
Async XLA Ops:
  0.0 14.0 %copy-start = (bf16[768,1024]{1,0:T(8,128)(2,1)S(1)}, bf16[768,1024]{1,0:T(8,128)(2,1)}, u32[]{:S(2)}) copy-start(bf16[768,1024]{1,0:T(8,128)(2,1)} %teacher.1) | copy-start | bytes 4718596
  0.9 9.1 %collective-permute-start = (bf16[16,1024]{1,0:T(8,128)(2,1)S(1)}, bf16[16,1024]{1,0:T(8,128)(2,1)S(1)}, u32[]{:S(2)}, u32[]{:S(2)}) collective-permute-start(bf16[16,1024]{1,0:T(8,128)(2,1)S(1)} %get-tuple-element.192), channel_id=1, source_target_pairs={{0,8},{8,16},{16,24},{24,32},{32,40},{40,48},{48,56},{56,64},{64,7... | collective-permute-start | bytes 98312 | tf_op jit(solution)/shard_map/ppermute | solution.py:463
  2.5 7.5 %collective-permute-start.1 = (bf16[16,1024]{1,0:T(8,128)(2,1)S(1)}, bf16[16,1024]{1,0:T(8,128)(2,1)S(1)}, u32[]{:S(2)}, u32[]{:S(2)}) collective-permute-start(bf16[16,1024]{1,0:T(8,128)(2,1)S(1)} %get-tuple-element.191), channel_id=1, source_target_pairs={{8,0},{16,8},{24,16},{32,24},{40,32},{48,40},{56,48},{64,56},{72,6... | collective-permute-start | bytes 98312 | tf_op jit(solution)/shard_map/ppermute | solution.py:464
  6.3 1.4 copy-start.1
  7.7 5.5 %copy-start.21 = (s32[768]{0:T(1024)S(1)}, s32[768]{0:T(1024)}, u32[]{:S(2)}) copy-start(s32[768]{0:T(1024)} %param.7) | copy-start | bytes 9220
  7.7 5.5 %copy-start.20 = (s32[768,4]{0,1:T(4,128)S(1)}, s32[768,4]{0,1:T(4,128)}, u32[]{:S(2)}) copy-start(s32[768,4]{0,1:T(4,128)} %param.8) | copy-start | bytes 36868
  7.7 5.7 %copy-start.2 = (s32[1,4]{1,0:T(1,128)S(1)}, s32[1,4]{1,0:T(1,128)}, u32[]{:S(2)}) copy-start(s32[1,4]{1,0:T(1,128)} %param.9) | copy-start | bytes 52
  10.0 12.0 %collective-permute-start.2 = (bf16[192,512]{1,0:T(8,128)(2,1)}, bf16[192,512]{1,0:T(8,128)(2,1)S(1)}, u32[]{:S(2)}, u32[]{:S(2)}) collective-permute-start(bf16[192,512]{1,0:T(8,128)(2,1)} %get-tuple-element.105), channel_id=1, source_target_pairs={{0,8},{8,16},{16,24},{24,0},{1,9},{9,17},{17,25},{25,1},{2,10},{10... | collective-permute-start | bytes 589832 | tf_op jit(solution)/shard_map/ppermute | solution.py:20
  10.0 12.0 %collective-permute-start.3 = (bf16[192,512]{1,0:T(8,128)(2,1)}, bf16[192,512]{1,0:T(8,128)(2,1)S(1)}, u32[]{:S(2)}, u32[]{:S(2)}) collective-permute-start(bf16[192,512]{1,0:T(8,128)(2,1)} %get-tuple-element.106), channel_id=1, source_target_pairs={{0,24},{8,0},{16,8},{24,16},{1,25},{9,1},{17,9},{25,17},{2,26},{10... | collective-permute-start | bytes 589832 | tf_op jit(solution)/shard_map/ppermute | solution.py:20
  13.2 8.8 %collective-permute-start.4 = (bf16[192,512]{1,0:T(8,128)(2,1)}, bf16[192,512]{1,0:T(8,128)(2,1)S(1)}, u32[]{:S(2)}, u32[]{:S(2)}) collective-permute-start(bf16[192,512]{1,0:T(8,128)(2,1)} %get-tuple-element.107), channel_id=1, source_target_pairs={{0,16},{8,24},{16,0},{24,8},{1,17},{9,25},{17,1},{25,9},{2,18},{10... | collective-permute-start | bytes 589832 | tf_op jit(solution)/shard_map/ppermute | solution.py:20
  13.5 20.1 %copy-start.19 = (bf16[192,512]{1,0:T(8,128)(2,1)S(1)}, bf16[192,512]{1,0:T(8,128)(2,1)}, u32[]{:S(2)}) copy-start(bf16[192,512]{1,0:T(8,128)(2,1)} %copy-done.18) | copy-start | bytes 589828
  24.4 27.9 %collective-permute-start.5 = (bf16[512,768]{1,0:T(8,128)(2,1)}, bf16[512,768]{1,0:T(8,128)(2,1)S(1)}, u32[]{:S(2)}, u32[]{:S(2)}) collective-permute-start(bf16[512,768]{1,0:T(8,128)(2,1)} %get-tuple-element.121.refs_0_), channel_id=1, source_target_pairs={{0,2},{2,4},{4,6},{6,0},{1,3},{3,5},{5,7},{7,1},{8,10},{10,12},{12... | collective-permute-start | bytes 2359304 | tf_op jit(solution)/shard_map/ppermute | solution.py:20
  26.3 26.0 %collective-permute-start.6 = (bf16[512,768]{1,0:T(8,128)(2,1)}, bf16[512,768]{1,0:T(8,128)(2,1)}, u32[]{:S(2)}, u32[]{:S(2)}) collective-permute-start(bf16[512,768]{1,0:T(8,128)(2,1)} %get-tuple-element.121.refs_0_), channel_id=1, source_target_pairs={{0,6},{2,0},{4,2},{6,4},{1,7},{3,1},{5,3},{7,5},{8,14},{10,8},{12,... | collective-permute-start | bytes 2359304 | tf_op jit(solution)/shard_map/ppermute | solution.py:20
  28.4 5.1 %collective-permute-start.10 = (f32[4,1024]{1,0:T(4,128)S(1)}, f32[4,1024]{1,0:T(4,128)S(1)}, u32[]{:S(2)}, u32[]{:S(2)}) collective-permute-start(f32[4,1024]{1,0:T(4,128)S(1)} %get-tuple-element.133.refs_4_), channel_id=1, source_target_pairs={{0,8},{8,16},{16,24},{24,0},{1,9},{9,17},{17,25},{25,1},{2,10},{10... | collective-permute-start | bytes 49160 | tf_op jit(solution)/shard_map/ppermute | solution.py:20
  29.3 5.0 %collective-permute-start.11 = (f32[4,1024]{1,0:T(4,128)S(1)}, f32[4,1024]{1,0:T(4,128)S(1)}, u32[]{:S(2)}, u32[]{:S(2)}) collective-permute-start(f32[4,1024]{1,0:T(4,128)S(1)} %get-tuple-element.133.refs_4_), channel_id=1, source_target_pairs={{0,24},{8,0},{16,8},{24,16},{1,25},{9,1},{17,9},{25,17},{2,26},{10... | collective-permute-start | bytes 49160 | tf_op jit(solution)/shard_map/ppermute | solution.py:20
  31.6 5.3 %collective-permute-start.12 = (f32[4,1024]{1,0:T(4,128)S(1)}, f32[4,1024]{1,0:T(4,128)S(1)}, u32[]{:S(2)}, u32[]{:S(2)}) collective-permute-start(f32[4,1024]{1,0:T(4,128)S(1)} %get-tuple-element.133.refs_4_), channel_id=1, source_target_pairs={{0,16},{8,24},{16,0},{24,8},{1,17},{9,25},{17,1},{25,9},{2,18},{10... | collective-permute-start | bytes 49160 | tf_op jit(solution)/shard_map/ppermute | solution.py:20
  33.5 7.0 %collective-permute-start.7 = (bf16[192,512]{1,0:T(8,128)(2,1)S(1)}, bf16[192,512]{1,0:T(8,128)(2,1)S(1)}, u32[]{:S(2)}, u32[]{:S(2)}) collective-permute-start(bf16[192,512]{1,0:T(8,128)(2,1)S(1)} %copy-done.19), channel_id=1, source_target_pairs={{0,8},{8,16},{16,24},{24,0},{1,9},{9,17},{17,25},{25,1},{2,10},{10... | collective-permute-start | bytes 589832 | tf_op jit(solution)/shard_map/ppermute | solution.py:20
  34.3 6.3 %collective-permute-start.8 = (bf16[192,512]{1,0:T(8,128)(2,1)S(1)}, bf16[192,512]{1,0:T(8,128)(2,1)S(1)}, u32[]{:S(2)}, u32[]{:S(2)}) collective-permute-start(bf16[192,512]{1,0:T(8,128)(2,1)S(1)} %get-tuple-element.124), channel_id=1, source_target_pairs={{0,24},{8,0},{16,8},{24,16},{1,25},{9,1},{17,9},{25,17},{2,26},{10... | collective-permute-start | bytes 589832 | tf_op jit(solution)/shard_map/ppermute | solution.py:20
  37.0 8.3 %collective-permute-start.9 = (bf16[192,512]{1,0:T(8,128)(2,1)S(1)}, bf16[192,512]{1,0:T(8,128)(2,1)S(1)}, u32[]{:S(2)}, u32[]{:S(2)}) collective-permute-start(bf16[192,512]{1,0:T(8,128)(2,1)S(1)} %get-tuple-element.125), channel_id=1, source_target_pairs={{0,16},{8,24},{16,0},{24,8},{1,17},{9,25},{17,1},{25,9},{2,18},{10... | collective-permute-start | bytes 589832 | tf_op jit(solution)/shard_map/ppermute | solution.py:20
  45.3 15.9 %collective-permute-start.15 = (bf16[768,512]{1,0:T(8,128)(2,1)}, bf16[768,512]{1,0:T(8,128)(2,1)}, u32[]{:S(2)}, u32[]{:S(2)}) collective-permute-start(bf16[768,512]{1,0:T(8,128)(2,1)} %get-tuple-element.140), channel_id=1, source_target_pairs={{0,8},{8,16},{16,24},{24,0},{1,9},{9,17},{17,25},{25,1},{2,10},{10... | collective-permute-start | bytes 2359304 | tf_op jit(solution)/shard_map/ppermute | solution.py:20
  45.3 15.9 %collective-permute-start.16 = (bf16[768,512]{1,0:T(8,128)(2,1)}, bf16[768,512]{1,0:T(8,128)(2,1)}, u32[]{:S(2)}, u32[]{:S(2)}) collective-permute-start(bf16[768,512]{1,0:T(8,128)(2,1)} %get-tuple-element.140), channel_id=1, source_target_pairs={{0,24},{8,0},{16,8},{24,16},{1,25},{9,1},{17,9},{25,17},{2,26},{10... | collective-permute-start | bytes 2359304 | tf_op jit(solution)/shard_map/ppermute | solution.py:20
  48.5 34.1 %collective-permute-start.19 = (bf16[768,1024]{1,0:T(8,128)(2,1)}, bf16[768,1024]{1,0:T(8,128)(2,1)}, u32[]{:S(2)}, u32[]{:S(2)}) collective-permute-start(bf16[768,1024]{1,0:T(8,128)(2,1)} %get-tuple-element.145.refs_5_), channel_id=1, source_target_pairs={{0,1},{1,0},{2,3},{3,2},{4,5},{5,4},{6,7},{7,6},{8,9},{9,8},{10,11... | collective-permute-start | bytes 4718600 | tf_op jit(solution)/shard_map/ppermute | solution.py:28
  50.6 3.2 %copy-start.16 = (f32[512,1]{1,0:T(8,128)}, f32[512,1]{1,0:T(8,128)S(1)}, u32[]{:S(2)}) copy-start(f32[512,1]{1,0:T(8,128)S(1)} %get-tuple-element.169.refs_15_) | copy-start | bytes 6148
  52.3 14.3 %collective-permute-start.13 = (bf16[256,768]{1,0:T(8,128)(2,1)S(1)}, bf16[256,768]{1,0:T(8,128)(2,1)S(1)}, u32[]{:S(2)}, u32[]{:S(2)}) collective-permute-start(bf16[256,768]{1,0:T(8,128)(2,1)S(1)} %slice.48), channel_id=1, source_target_pairs={{0,2},{2,4},{4,6},{6,0},{1,3},{3,5},{5,7},{7,1},{8,10},{10,12},{12... | collective-permute-start | bytes 1179656 | tf_op jit(solution)/shard_map/ppermute | solution.py:20
  53.8 12.8 %collective-permute-start.14 = (bf16[256,768]{1,0:T(8,128)(2,1)S(1)}, bf16[256,768]{1,0:T(8,128)(2,1)S(1)}, u32[]{:S(2)}, u32[]{:S(2)}) collective-permute-start(bf16[256,768]{1,0:T(8,128)(2,1)S(1)} %slice.49), channel_id=1, source_target_pairs={{0,6},{2,0},{4,2},{6,4},{1,7},{3,1},{5,3},{7,5},{8,14},{10,8},{12,... | collective-permute-start | bytes 1179656 | tf_op jit(solution)/shard_map/ppermute | solution.py:20
  62.2 9.1 %collective-permute-start.17 = (bf16[768,256]{1,0:T(8,128)(2,1)S(1)}, bf16[768,256]{1,0:T(8,128)(2,1)S(1)}, u32[]{:S(2)}, u32[]{:S(2)}) collective-permute-start(bf16[768,256]{1,0:T(8,128)(2,1)S(1)} %slice.50), channel_id=1, source_target_pairs={{0,8},{8,16},{16,24},{24,0},{1,9},{9,17},{17,25},{25,1},{2,10},{10... | collective-permute-start | bytes 1179656 | tf_op jit(solution)/shard_map/ppermute | solution.py:20
  63.3 8.7 %collective-permute-start.18 = (bf16[768,256]{1,0:T(8,128)(2,1)S(1)}, bf16[768,256]{1,0:T(8,128)(2,1)S(1)}, u32[]{:S(2)}, u32[]{:S(2)}) collective-permute-start(bf16[768,256]{1,0:T(8,128)(2,1)S(1)} %slice.51), channel_id=1, source_target_pairs={{0,24},{8,0},{16,8},{24,16},{1,25},{9,1},{17,9},{25,17},{2,26},{10... | collective-permute-start | bytes 1179656 | tf_op jit(solution)/shard_map/ppermute | solution.py:20
  66.6 21.9 %collective-permute-start.20 = (bf16[768,512]{1,0:T(8,128)(2,1)}, bf16[768,512]{1,0:T(8,128)(2,1)S(1)}, u32[]{:S(2)}, u32[]{:S(2)}) collective-permute-start(bf16[768,512]{1,0:T(8,128)(2,1)} %collective-permute-done.15.refs_6_), channel_id=1, source_target_pairs={{0,1},{1,0},{2,3},{3,2},{4,5},{5,4},{6,7},{7,6},{8,9},{9,8},{10,11... | collective-permute-start | bytes 2359304 | tf_op jit(solution)/shard_map/ppermute | solution.py:28
  66.6 6.7 %collective-permute-start.24 = (f32[8,1024]{1,0:T(8,128)S(1)}, f32[8,1024]{1,0:T(8,128)S(1)}, u32[]{:S(2)}, u32[]{:S(2)}) collective-permute-start(f32[8,1024]{1,0:T(8,128)S(1)} %shard_map.59.refs_0_), channel_id=1, source_target_pairs={{0,2},{2,4},{4,6},{6,0},{1,3},{3,5},{5,7},{7,1},{8,10},{10,12},{12... | collective-permute-start | bytes 98312 | tf_op jit(solution)/shard_map/ppermute | solution.py:20
  71.2 12.3 %collective-permute-start.22 = (bf16[768,256]{1,0:T(8,128)(2,1)S(1)}, bf16[768,256]{1,0:T(8,128)(2,1)S(1)}, u32[]{:S(2)}, u32[]{:S(2)}) collective-permute-start(bf16[768,256]{1,0:T(8,128)(2,1)S(1)} %collective-permute-done.17.refs_8_), channel_id=1, source_target_pairs={{0,1},{1,0},{2,3},{3,2},{4,5},{5,4},{6,7},{7,6},{8,9},{9,8},{10,11... | collective-permute-start | bytes 1179656 | tf_op jit(solution)/shard_map/ppermute | solution.py:28
  72.0 14.9 %collective-permute-start.23 = (bf16[768,256]{1,0:T(8,128)(2,1)S(1)}, bf16[768,256]{1,0:T(8,128)(2,1)S(1)}, u32[]{:S(2)}, u32[]{:S(2)}) collective-permute-start(bf16[768,256]{1,0:T(8,128)(2,1)S(1)} %collective-permute-done.18.refs_9_), channel_id=1, source_target_pairs={{0,1},{1,0},{2,3},{3,2},{4,5},{5,4},{6,7},{7,6},{8,9},{9,8},{10,11... | collective-permute-start | bytes 1179656 | tf_op jit(solution)/shard_map/ppermute | solution.py:28
  73.3 3.9 %collective-permute-start.25 = (f32[8,1024]{1,0:T(8,128)S(1)}, f32[8,1024]{1,0:T(8,128)S(1)}, u32[]{:S(2)}, u32[]{:S(2)}) collective-permute-start(f32[8,1024]{1,0:T(8,128)S(1)} %shard_map.59.refs_0_), channel_id=1, source_target_pairs={{0,6},{2,0},{4,2},{6,4},{1,7},{3,1},{5,3},{7,5},{8,14},{10,8},{12,... | collective-permute-start | bytes 98312 | tf_op jit(solution)/shard_map/ppermute | solution.py:20
  77.2 5.4 %collective-permute-start.26 = (f32[8,1024]{1,0:T(8,128)S(1)}, f32[8,1024]{1,0:T(8,128)S(1)}, u32[]{:S(2)}, u32[]{:S(2)}) collective-permute-start(f32[8,1024]{1,0:T(8,128)S(1)} %shard_map.59.refs_0_), channel_id=1, source_target_pairs={{0,4},{2,6},{4,0},{6,2},{1,5},{3,7},{5,1},{7,3},{8,12},{10,14},{12... | collective-permute-start | bytes 98312 | tf_op jit(solution)/shard_map/ppermute | solution.py:20
  82.6 9.2 %collective-permute-start.21 = (bf16[768,512]{1,0:T(8,128)(2,1)}, bf16[768,512]{1,0:T(8,128)(2,1)}, u32[]{:S(2)}, u32[]{:S(2)}) collective-permute-start(bf16[768,512]{1,0:T(8,128)(2,1)} %collective-permute-done.16.refs_7_), channel_id=1, source_target_pairs={{0,1},{1,0},{2,3},{3,2},{4,5},{5,4},{6,7},{7,6},{8,9},{9,8},{10,11... | collective-permute-start | bytes 2359304 | tf_op jit(solution)/shard_map/ppermute | solution.py:28
  82.6 22.3 %collective-permute-start.27 = (bf16[512,768]{1,0:T(8,128)(2,1)}, bf16[512,768]{1,0:T(8,128)(2,1)S(1)}, u32[]{:S(2)}, u32[]{:S(2)}) collective-permute-start(bf16[512,768]{1,0:T(8,128)(2,1)} %get-tuple-element.157.refs_0_), channel_id=1, source_target_pairs={{0,2},{2,4},{4,6},{6,0},{1,3},{3,5},{5,7},{7,1},{8,10},{10,12},{12... | collective-permute-start | bytes 2359304 | tf_op jit(solution)/shard_map/ppermute | solution.py:20
  84.2 20.7 %collective-permute-start.28 = (bf16[512,768]{1,0:T(8,128)(2,1)}, bf16[512,768]{1,0:T(8,128)(2,1)S(1)}, u32[]{:S(2)}, u32[]{:S(2)}) collective-permute-start(bf16[512,768]{1,0:T(8,128)(2,1)} %get-tuple-element.157.refs_0_), channel_id=1, source_target_pairs={{0,6},{2,0},{4,2},{6,4},{1,7},{3,1},{5,3},{7,5},{8,14},{10,8},{12,... | collective-permute-start | bytes 2359304 | tf_op jit(solution)/shard_map/ppermute | solution.py:20
  87.7 21.3 %collective-permute-start.29 = (bf16[768,512]{1,0:T(8,128)(2,1)}, bf16[768,512]{1,0:T(8,128)(2,1)}, u32[]{:S(2)}, u32[]{:S(2)}) collective-permute-start(bf16[768,512]{1,0:T(8,128)(2,1)} %get-tuple-element.158), channel_id=1, source_target_pairs={{0,8},{8,16},{16,24},{24,0},{1,9},{9,17},{17,25},{25,1},{2,10},{10... | collective-permute-start | bytes 2359304 | tf_op jit(solution)/shard_map/ppermute | solution.py:20
  89.3 19.8 %collective-permute-start.30 = (bf16[768,512]{1,0:T(8,128)(2,1)}, bf16[768,512]{1,0:T(8,128)(2,1)}, u32[]{:S(2)}, u32[]{:S(2)}) collective-permute-start(bf16[768,512]{1,0:T(8,128)(2,1)} %get-tuple-element.158), channel_id=1, source_target_pairs={{0,24},{8,0},{16,8},{24,16},{1,25},{9,1},{17,9},{25,17},{2,26},{10... | collective-permute-start | bytes 2359304 | tf_op jit(solution)/shard_map/ppermute | solution.py:20
  91.9 1.1 copy-start.4
  93.0 1.0 copy-start.6
  94.0 1.0 copy-start.8
  96.0 1.0 copy-start.12
  109.1 27.7 %copy-start.17 = (f32[512,1]{1,0:T(8,128)S(1)}, f32[512,1]{1,0:T(8,128)}, u32[]{:S(2)}) copy-start(f32[512,1]{1,0:T(8,128)} %copy-done.16) | copy-start | bytes 6148
  109.1 27.3 %collective-permute-start.33 = (bf16[256,768]{1,0:T(8,128)(2,1)S(1)}, bf16[256,768]{1,0:T(8,128)(2,1)S(1)}, u32[]{:S(2)}, u32[]{:S(2)}) collective-permute-start(bf16[256,768]{1,0:T(8,128)(2,1)S(1)} %slice.52), channel_id=1, source_target_pairs={{0,2},{2,4},{4,6},{6,0},{1,3},{3,5},{5,7},{7,1},{8,10},{10,12},{12... | collective-permute-start | bytes 1179656 | tf_op jit(solution)/shard_map/ppermute | solution.py:20
  109.8 8.0 %collective-permute-start.35 = (f32[20,1024]{1,0:T(8,128)S(1)}, f32[20,1024]{1,0:T(8,128)S(1)}, u32[]{:S(2)}, u32[]{:S(2)}) collective-permute-start(f32[20,1024]{1,0:T(8,128)S(1)} %shard_map.61.e0), channel_id=1, source_target_pairs={{0,32},{32,64},{64,96},{96,0},{1,33},{33,65},{65,97},{97,1},{2,34}... | collective-permute-start | bytes 245768 | tf_op jit(solution)/shard_map/ppermute | solution.py:20
  111.2 25.5 %collective-permute-start.34 = (bf16[256,768]{1,0:T(8,128)(2,1)S(1)}, bf16[256,768]{1,0:T(8,128)(2,1)S(1)}, u32[]{:S(2)}, u32[]{:S(2)}) collective-permute-start(bf16[256,768]{1,0:T(8,128)(2,1)S(1)} %slice.53), channel_id=1, source_target_pairs={{0,6},{2,0},{4,2},{6,4},{1,7},{3,1},{5,3},{7,5},{8,14},{10,8},{12,... | collective-permute-start | bytes 1179656 | tf_op jit(solution)/shard_map/ppermute | solution.py:20
  114.5 19.9 %collective-permute-start.31 = (bf16[256,512]{1,0:T(8,128)(2,1)S(1)}, bf16[256,512]{1,0:T(8,128)(2,1)S(1)}, u32[]{:S(2)}, u32[]{:S(2)}) collective-permute-start(bf16[256,512]{1,0:T(8,128)(2,1)S(1)} %get-tuple-element.163), channel_id=1, source_target_pairs={{0,32},{32,64},{64,96},{96,0},{1,33},{33,65},{65,97},{97,1},{2,34}... | collective-permute-start | bytes 786440 | tf_op jit(solution)/shard_map/ppermute | solution.py:20
  116.2 20.1 %collective-permute-start.32 = (bf16[256,512]{1,0:T(8,128)(2,1)S(1)}, bf16[256,512]{1,0:T(8,128)(2,1)S(1)}, u32[]{:S(2)}, u32[]{:S(2)}) collective-permute-start(bf16[256,512]{1,0:T(8,128)(2,1)S(1)} %get-tuple-element.164), channel_id=1, source_target_pairs={{0,96},{32,0},{64,32},{96,64},{1,97},{33,1},{65,33},{97,65},{2,98}... | collective-permute-start | bytes 786440 | tf_op jit(solution)/shard_map/ppermute | solution.py:20
  117.8 6.7 %collective-permute-start.36 = (f32[20,1024]{1,0:T(8,128)S(1)}, f32[20,1024]{1,0:T(8,128)S(1)}, u32[]{:S(2)}, u32[]{:S(2)}) collective-permute-start(f32[20,1024]{1,0:T(8,128)S(1)} %shard_map.61.e0), channel_id=1, source_target_pairs={{0,96},{32,0},{64,32},{96,64},{1,97},{33,1},{65,33},{97,65},{2,98}... | collective-permute-start | bytes 245768 | tf_op jit(solution)/shard_map/ppermute | solution.py:20
  124.5 6.1 %collective-permute-start.37 = (f32[20,1024]{1,0:T(8,128)S(1)}, f32[20,1024]{1,0:T(8,128)S(1)}, u32[]{:S(2)}, u32[]{:S(2)}) collective-permute-start(f32[20,1024]{1,0:T(8,128)S(1)} %shard_map.61.e0), channel_id=1, source_target_pairs={{0,64},{32,96},{64,0},{96,32},{1,65},{33,97},{65,1},{97,33},{2,66}... | collective-permute-start | bytes 245768 | tf_op jit(solution)/shard_map/ppermute | solution.py:20
  130.8 2.1 %collective-permute-start.38 = (f32[17,1024]{1,0:T(8,128)S(1)}, f32[17,1024]{1,0:T(8,128)S(1)}, u32[]{:S(2)}, u32[]{:S(2)}) collective-permute-start(f32[17,1024]{1,0:T(8,128)S(1)} %get-tuple-element.182.t_own), channel_id=1, source_target_pairs={{0,1},{1,0},{2,3},{3,2},{4,5},{5,4},{6,7},{7,6},{8,9},{9,8},{10,11... | collective-permute-start | bytes 208904 | tf_op jit(solution)/shard_map/ppermute | solution.py:28
  133.0 12.9 %collective-permute-start.39 = (bf16[768,256]{1,0:T(8,128)(2,1)S(1)}, bf16[768,256]{1,0:T(8,128)(2,1)S(1)}, u32[]{:S(2)}, u32[]{:S(2)}) collective-permute-start(bf16[768,256]{1,0:T(8,128)(2,1)S(1)} %slice.54), channel_id=1, source_target_pairs={{0,8},{8,16},{16,24},{24,0},{1,9},{9,17},{17,25},{25,1},{2,10},{10... | collective-permute-start | bytes 1179656 | tf_op jit(solution)/shard_map/ppermute | solution.py:20
  134.5 11.4 %collective-permute-start.40 = (bf16[768,256]{1,0:T(8,128)(2,1)S(1)}, bf16[768,256]{1,0:T(8,128)(2,1)S(1)}, u32[]{:S(2)}, u32[]{:S(2)}) collective-permute-start(bf16[768,256]{1,0:T(8,128)(2,1)S(1)} %slice.55), channel_id=1, source_target_pairs={{0,24},{8,0},{16,8},{24,16},{1,25},{9,1},{17,9},{25,17},{2,26},{10... | collective-permute-start | bytes 1179656 | tf_op jit(solution)/shard_map/ppermute | solution.py:20
  136.3 11.9 %collective-permute-start.41 = (bf16[768,512]{1,0:T(8,128)(2,1)}, bf16[768,512]{1,0:T(8,128)(2,1)S(1)}, u32[]{:S(2)}, u32[]{:S(2)}) collective-permute-start(bf16[768,512]{1,0:T(8,128)(2,1)} %collective-permute-done.29.refs_6_), channel_id=1, source_target_pairs={{0,1},{1,0},{2,3},{3,2},{4,5},{5,4},{6,7},{7,6},{8,9},{9,8},{10,11... | collective-permute-start | bytes 2359304 | tf_op jit(solution)/shard_map/ppermute | solution.py:28
  136.4 11.8 %collective-permute-start.42 = (bf16[768,512]{1,0:T(8,128)(2,1)}, bf16[768,512]{1,0:T(8,128)(2,1)S(1)}, u32[]{:S(2)}, u32[]{:S(2)}) collective-permute-start(bf16[768,512]{1,0:T(8,128)(2,1)} %collective-permute-done.30.refs_7_), channel_id=1, source_target_pairs={{0,1},{1,0},{2,3},{3,2},{4,5},{5,4},{6,7},{7,6},{8,9},{9,8},{10,11... | collective-permute-start | bytes 2359304 | tf_op jit(solution)/shard_map/ppermute | solution.py:28
  136.8 11.4 %copy-start.15 = (f32[512,1]{1,0:T(8,128)S(1)}, f32[512,1]{1,0:T(8,128)}, u32[]{:S(2)}) copy-start(f32[512,1]{1,0:T(8,128)} %copy-done.13) | copy-start | bytes 6148
  145.9 1.7 collective-permute-start.43
  145.9 2.3 %collective-permute-start.44 = (bf16[768,256]{1,0:T(8,128)(2,1)S(1)}, bf16[768,256]{1,0:T(8,128)(2,1)S(1)}, u32[]{:S(2)}, u32[]{:S(2)}) collective-permute-start(bf16[768,256]{1,0:T(8,128)(2,1)S(1)} %collective-permute-done.40.refs_9_), channel_id=1, source_target_pairs={{0,1},{1,0},{2,3},{3,2},{4,5},{5,4},{6,7},{7,6},{8,9},{9,8},{10,11... | collective-permute-start | bytes 1179656 | tf_op jit(solution)/shard_map/ppermute | solution.py:28
  155.0 10.4 %collective-permute-start.45 = (bf16[256,512]{1,0:T(8,128)(2,1)S(1)}, bf16[256,512]{1,0:T(8,128)(2,1)S(1)}, u32[]{:S(2)}, u32[]{:S(2)}) collective-permute-start(bf16[256,512]{1,0:T(8,128)(2,1)S(1)} %get-tuple-element.177), channel_id=1, source_target_pairs={{0,32},{32,64},{64,96},{96,0},{1,33},{33,65},{65,97},{97,1},{2,34}... | collective-permute-start | bytes 786440 | tf_op jit(solution)/shard_map/ppermute | solution.py:20
  156.3 9.2 %collective-permute-start.46 = (bf16[256,512]{1,0:T(8,128)(2,1)S(1)}, bf16[256,512]{1,0:T(8,128)(2,1)S(1)}, u32[]{:S(2)}, u32[]{:S(2)}) collective-permute-start(bf16[256,512]{1,0:T(8,128)(2,1)S(1)} %get-tuple-element.178), channel_id=1, source_target_pairs={{0,96},{32,0},{64,32},{96,64},{1,97},{33,1},{65,33},{97,65},{2,98}... | collective-permute-start | bytes 786440 | tf_op jit(solution)/shard_map/ppermute | solution.py:20
  158.3 18.4 %collective-permute-start.49 = (bf16[256,1024]{1,0:T(8,128)(2,1)S(1)}, bf16[256,1024]{1,0:T(8,128)(2,1)S(1)}, u32[]{:S(2)}, u32[]{:S(2)}) collective-permute-start(bf16[256,1024]{1,0:T(8,128)(2,1)S(1)} %get-tuple-element.185), channel_id=1, source_target_pairs={{0,32},{32,64},{64,96},{96,0},{1,33},{33,65},{65,97},{97,1},{2,34}... | collective-permute-start | bytes 1572872 | tf_op jit(solution)/shard_map/ppermute | solution.py:20
  158.3 18.4 %collective-permute-start.50 = (bf16[256,1024]{1,0:T(8,128)(2,1)S(1)}, bf16[256,1024]{1,0:T(8,128)(2,1)S(1)}, u32[]{:S(2)}, u32[]{:S(2)}) collective-permute-start(bf16[256,1024]{1,0:T(8,128)(2,1)S(1)} %get-tuple-element.186), channel_id=1, source_target_pairs={{0,96},{32,0},{64,32},{96,64},{1,97},{33,1},{65,33},{97,65},{2,98}... | collective-permute-start | bytes 1572872 | tf_op jit(solution)/shard_map/ppermute | solution.py:20
  172.2 14.9 %collective-permute-start.47 = (bf16[256,1024]{1,0:T(8,128)(2,1)S(1)}, bf16[256,1024]{1,0:T(8,128)(2,1)S(1)}, u32[]{:S(2)}, u32[]{:S(2)}) collective-permute-start(bf16[256,1024]{1,0:T(8,128)(2,1)S(1)} %get-tuple-element.179), channel_id=1, source_target_pairs={{0,32},{32,64},{64,96},{96,0},{1,33},{33,65},{65,97},{97,1},{2,34}... | collective-permute-start | bytes 1572872 | tf_op jit(solution)/shard_map/ppermute | solution.py:20
  173.3 13.8 %collective-permute-start.48 = (bf16[256,1024]{1,0:T(8,128)(2,1)S(1)}, bf16[256,1024]{1,0:T(8,128)(2,1)S(1)}, u32[]{:S(2)}, u32[]{:S(2)}) collective-permute-start(bf16[256,1024]{1,0:T(8,128)(2,1)S(1)} %get-tuple-element.180), channel_id=1, source_target_pairs={{0,96},{32,0},{64,32},{96,64},{1,97},{33,1},{65,33},{97,65},{2,98}... | collective-permute-start | bytes 1572872 | tf_op jit(solution)/shard_map/ppermute | solution.py:20
  (9 other events, 7.2 us)

commit v4 on v3

--- a/solution.py
+++ b/solution.py
@@ -41,27 +41,38 @@
 
 
 def pack_kernel(place, student, *outs):
-    y, x = place[0], place[1]
-    part = outs[0].shape[1] // 2
+    y, x, count = place[0], place[1], place[2]
+    moments = outs[SIDE]
+    part = outs[0].shape[1] // SIDE
     for r, x_step in enumerate((0, 1, SIDE - 1, 2)):
-        for k, y_steps in enumerate(((2, 0), (1, SIDE - 1))):
-            for i, y_step in enumerate(y_steps):
-                slot = lax.rem(y + y_step, SIDE) * SIDE + lax.rem(x + x_step, SIDE)
-                first = pl.multiple_of(slot * part, 128)
-                outs[2 * r + k][:, i * part : (i + 1) * part] = student[:, pl.ds(first, part)]
+        at = lax.rem(x + x_step, SIDE)
+        for i, y_step in enumerate((2, 0, 1, SIDE - 1)):
+            slot = lax.rem(y + y_step, SIDE) * SIDE + at
+            first = pl.multiple_of(slot * part, 128)
+            columns = slice(i * part, (i + 1) * part)
+            block = student[:, pl.ds(first, part)]
+            outs[r][:, columns] = block
+            value = block.astype(f32)
+            live = lax.broadcasted_iota(jnp.int32, value.shape, 0) < count
+            total = jnp.sum(jnp.where(live, value, 0.0), axis=0, keepdims=True)
+            dev = jnp.where(live, value - total / count.astype(f32), 0.0)
+            moments[r : r + 1, columns] = total
+            moments[SIDE + r : SIDE + r + 1, columns] = jnp.sum(dev * dev, axis=0, keepdims=True)
 
 
 def pack(place, student):
-    part = student.shape[1] // (SIDE * SIDE)
-    shape = jax.ShapeDtypeStruct((SUB, 2 * part), bf16)
+    width = student.shape[1] // SIDE
     return pl.pallas_call(
         pack_kernel,
         in_specs=[smem(), vmem()],
-        out_specs=[vmem()] * 8,
-        out_shape=[shape] * 8,
-        compiler_params=pltpu.CompilerParams(vmem_limit_bytes=16 * 2**20),
+        out_specs=[vmem()] * (SIDE + 1),
+        out_shape=[jax.ShapeDtypeStruct((SUB, width), bf16)] * SIDE
+        + [jax.ShapeDtypeStruct((2 * SIDE, width), f32)],
+        compiler_params=pltpu.CompilerParams(vmem_limit_bytes=24 * 2**20),
         cost_estimate=pl.CostEstimate(
-            flops=0, bytes_accessed=4 * SUB * student.shape[1], transcendentals=0
+            flops=8 * SUB * student.shape[1],
+            bytes_accessed=4 * SUB * student.shape[1],
+            transcendentals=0,
         ),
     )(place, student)
 
@@ -93,59 +104,50 @@
     )(own_count, *pieces)
 
 
-def moments_kernel(counts, *refs):
-    out = refs[-1]
-    for r in range(SIDE):
-        for k in range(2):
-            value = refs[2 * r + k][...].astype(f32)
-            columns = slice(k * value.shape[1], (k + 1) * value.shape[1])
-            live = lax.broadcasted_iota(jnp.int32, value.shape, 0) < counts[r]
-            total = jnp.sum(jnp.where(live, value, 0.0), axis=0, keepdims=True)
-            dev = jnp.where(live, value - total / counts[r].astype(f32), 0.0)
-            out[r : r + 1, columns] = total
-            out[SIDE + r : SIDE + r + 1, columns] = jnp.sum(dev * dev, axis=0, keepdims=True)
-
-
-def moments(counts, pieces):
-    width = pieces[0].shape[1]
-    return pl.pallas_call(
-        moments_kernel,
-        in_specs=[smem()] + [vmem()] * len(pieces),
+def shards_kernel(counts, teacher, *refs):
+    blocks, out = refs[:SIDE], refs[-1]
+    out[:SIDE, :] = teacher[...]
+    size = [counts[q].astype(f32) for q in range(SIDE)]
+    totals = [b[:SIDE, :] for b in blocks]
+    total = totals[0] + totals[1] + totals[2] + totals[3]
+    mean = total / (size[0] + size[1] + size[2] + size[3])
+    square = jnp.zeros_like(total)
+    for q in range(SIDE):
+        off = totals[q] / size[q] - mean
+        square = square + blocks[q][SIDE:, :] + size[q] * off * off
+    out[SIDE : 2 * SIDE, :] = total
+    out[2 * SIDE :, :] = square
+
+
+def shards(counts, teacher, blocks):
+    columns = blocks[0].shape[1]
+    return pl.pallas_call(
+        shards_kernel,
+        in_specs=[smem()] + [vmem()] * (1 + SIDE),
         out_specs=vmem(),
-        out_shape=jax.ShapeDtypeStruct((2 * SIDE, 2 * width), f32),
-        compiler_params=pltpu.CompilerParams(vmem_limit_bytes=16 * 2**20),
-        cost_estimate=pl.CostEstimate(
-            flops=8 * SUB * SIDE * width, bytes_accessed=4 * SUB * SIDE * width, transcendentals=0
-        ),
-    )(counts, *pieces)
-
-
-def shards_kernel(counts, *refs):
-    blocks, teachers, out = refs[:SIDE], refs[SIDE : 2 * SIDE], refs[-1]
-    for r in range(SIDE):
+        out_shape=jax.ShapeDtypeStruct((3 * SIDE, columns), f32),
+        compiler_params=pltpu.CompilerParams(vmem_limit_bytes=8 * 2**20),
+    )(counts, teacher, *blocks)
+
+
+def gather_kernel(n0, n1, n2, n3, out):
+    for r, (n, row) in enumerate(zip((n0, n1, n2, n3), (0, 1, 2, 3))):
         for i in range(3):
-            out[i * SIDE + r : i * SIDE + r + 1, :] = teachers[r][i : i + 1, :]
-        size = [counts[q * SIDE + r].astype(f32) for q in range(SIDE)]
-        totals = [b[r : r + 1, :] for b in blocks]
-        total = totals[0] + totals[1] + totals[2] + totals[3]
-        mean = total / (size[0] + size[1] + size[2] + size[3])
-        square = jnp.zeros_like(total)
-        for q in range(SIDE):
-            off = totals[q] / size[q] - mean
-            square = square + blocks[q][SIDE + r : SIDE + r + 1, :] + size[q] * off * off
-        out[3 * SIDE + r : 3 * SIDE + r + 1, :] = total
-        out[4 * SIDE + r : 4 * SIDE + r + 1, :] = square
-
-
-def shards(counts, blocks, teachers):
-    columns = blocks[0].shape[1]
-    return pl.pallas_call(
-        shards_kernel,
-        in_specs=[smem()] + [vmem()] * (2 * SIDE),
+            out[i * SIDE + r : i * SIDE + r + 1, :] = n[i : i + 1, :]
+        for i in range(2):
+            at = (1 + i) * SIDE + row
+            out[(3 + i) * SIDE + r : (3 + i) * SIDE + r + 1, :] = n[at : at + 1, :]
+
+
+def gather_stats(near):
+    columns = near[0].shape[1]
+    return pl.pallas_call(
+        gather_kernel,
+        in_specs=[vmem()] * SIDE,
         out_specs=vmem(),
         out_shape=jax.ShapeDtypeStruct((5 * SIDE, columns), f32),
         compiler_params=pltpu.CompilerParams(vmem_limit_bytes=8 * 2**20),
-    )(counts, *blocks, *teachers)
+    )(*near)
 
 
 def settle_kernel(e0, e1, e2, e3, t_rows, s_left, work):
@@ -197,7 +199,7 @@
     )(*every)
 
 
-def pool_kernel(counts, before, teacher, behind, meta, full, first, second, stats, mix, share, pooled):
+def pool_kernel(counts, before, teacher, behind, meta, full, stats, mix, share, pooled):
     window = SUB + 2 * HALO
     length = teacher.shape[0]
     j = pl.program_id(0)
@@ -243,15 +245,6 @@
         dev = jnp.where(live, value - mean, 0.0)
         small = dev.astype(bf16)
         full[rows, :] = small
-
-        @pl.when(j < pl.num_programs(0) // 2)
-        def _():
-            first[rows, :] = small
-
-        @pl.when(j >= pl.num_programs(0) // 2)
-        def _():
-            second[rows, :] = small
-
         square = square + jnp.sum(dev * dev, axis=0, keepdims=True)
     stats[0:1, :] = total
     stats[1:2, :] = square
@@ -266,7 +259,6 @@
 def pool(counts, before, teacher, behind, meta):
     rows, columns = teacher.shape
     tile = 256
-    last = columns // tile // 2
     return pl.pallas_call(
         pool_kernel,
         grid=(columns // tile,),
@@ -279,14 +271,10 @@
         ],
         out_specs=[
             pl.BlockSpec((rows, tile), lambda j: (0, j)),
-            pl.BlockSpec((rows, tile), lambda j: (0, jnp.minimum(j, last - 1))),
-            pl.BlockSpec((rows, tile), lambda j: (0, jnp.maximum(j - last, 0))),
             pl.BlockSpec((4, tile), lambda j: (0, j)),
         ],
         out_shape=[
             jax.ShapeDtypeStruct((rows, columns), bf16),
-            jax.ShapeDtypeStruct((rows, columns // 2), bf16),
-            jax.ShapeDtypeStruct((rows, columns // 2), bf16),
             jax.ShapeDtypeStruct((4, columns), f32),
         ],
         scratch_shapes=[
@@ -301,33 +289,80 @@
     )(counts, before, teacher, behind, meta)
 
 
-def sums_of(place, near, left, right):
-    z = place[0]
-    total = None
-    for a, step in zip(left, COMING):
-        first = pl.multiple_of(lax.rem(z + step, SIDE) * SUB, 16)
-        rows = pl.ds(first, SUB)
-        far = jnp.concatenate([right[3][rows, :], right[4][rows, :]], axis=1)
-        b = jnp.concatenate([right[0][rows, :], right[1][rows, :], right[2][rows, :], far], axis=0)
-        term = jnp.dot(a, b, preferred_element_type=f32)
-        total = term if total is None else total + term
+def with_ones(a):
+    return jnp.concatenate([a, jnp.ones((16, a.shape[1]), bf16)], axis=0)
+
+
+def less_mean(total, near):
     part = total.shape[0] - 16
     return total[:part] - near * total[part : part + 1]
 
 
-def left_of(refs, i):
-    ones = jnp.ones((16, refs[0].shape[1]), bf16)
-    far = jnp.where(i == 0, refs[3][...], refs[4][...])
-    return [jnp.concatenate([a, ones], axis=0) for a in [r[...] for r in refs[:3]] + [far]]
+def first_kernel(place, a0, a1, a2, b0, b1, b2, near, out):
+    z = place[0]
+    depth = a0.shape[1]
+    fill = jnp.zeros((depth - 3 * SUB, b0.shape[1]), bf16)
+    total = None
+    for a, step in zip((a0, a1, a2), COMING):
+        rows = pl.ds(pl.multiple_of(lax.rem(z + step, SIDE) * SUB, 16), SUB)
+        b = jnp.concatenate([b0[rows, :], b1[rows, :], b2[rows, :], fill], axis=0)
+        term = jnp.dot(with_ones(a[...]), b, preferred_element_type=f32)
+        total = term if total is None else total + term
+    out[...] = less_mean(total, near[...])
+
+
+def first_product(place, left, right, near):
+    rows, depth = left[0].shape
+    part = rows // SIDE
+    length, columns = right[0].shape
+    near_depth = 640
+    return pl.pallas_call(
+        first_kernel,
+        grid_spec=pltpu.PrefetchScalarGridSpec(
+            num_scalar_prefetch=1,
+            grid=(SIDE,),
+            in_specs=[pl.BlockSpec((part, near_depth), lambda i, place: (i, 0))] * 3
+            + [pl.BlockSpec((length, columns), lambda i, place: (0, 0))] * 3
+            + [pl.BlockSpec((part, 1), lambda i, place: (i, 0))],
+            out_specs=pl.BlockSpec((part, columns), lambda i, place: (i, 0)),
+        ),
+        out_shape=jax.ShapeDtypeStruct((rows, columns), f32),
+        compiler_params=pltpu.CompilerParams(vmem_limit_bytes=40 * 2**20),
+        cost_estimate=pl.CostEstimate(
+            flops=2 * rows * 3 * near_depth * columns,
+            bytes_accessed=6 * rows * depth + 6 * length * columns + 4 * rows * columns,
+            transcendentals=0,
+        ),
+    )(place, *left, *right, near)
+
+
+def last_sums(place, refs):
+    z = place[0]
+    tails, far_a, near = refs[:3], refs[3], refs[4]
+    sides = (refs[5:10], refs[10:15])
+    results = []
+    lefts = [with_ones(t[...]) for t in tails]
+    far_left = with_ones(far_a[...])
+    for b0, b1, b2, far_b, done in sides:
+        fill = jnp.zeros((tails[0].shape[1] - SUB, far_b.shape[1]), bf16)
+        total = None
+        for a, step in zip(lefts, COMING):
+            rows = pl.ds(pl.multiple_of(lax.rem(z + step, SIDE) * SUB, 16), SUB)
+            b = jnp.concatenate([fill, far_b[rows, :]], axis=0)
+            term = jnp.dot(a, b, preferred_element_type=f32)
+            total = term if total is None else total + term
+        rows = pl.ds(pl.multiple_of(lax.rem(z + 2, SIDE) * SUB, 16), SUB)
+        b = jnp.concatenate([b0[...], b1[...], b2[...], far_b[rows, :]], axis=0)
+        total = total + jnp.dot(far_left, b, preferred_element_type=f32)
+        results.append(less_mean(total, near[...]) + done[...])
+    return results
 
 
 def open_kernel(place, *refs):
-    left, own, mate, near = refs[:5], refs[5:10], refs[10:15], refs[15]
-    up, down, kept = refs[16:]
+    up, down, kept = refs[15:]
     i = pl.program_id(0)
     half = up.shape[1]
-    a = left_of(left, i)
-    results = [sums_of(place, near[...], a, side) for side in (own, mate)]
+    results = last_sums(place, refs)
 
     @pl.when(i == 0)
     def _():
@@ -341,12 +376,10 @@
 
 
 def close_kernel(place, *refs):
-    left, own, mate, near = refs[:5], refs[5:10], refs[10:15], refs[15]
-    from_back, from_next, up, down = refs[16:]
+    from_back, from_next, up, down = refs[15:]
     i = pl.program_id(0)
     half = from_back.shape[1]
-    a = left_of(left, i)
-    results = [sums_of(place, near[...], a, side) for side in (own, mate)]
+    results = last_sums(place, refs)
 
     @pl.when(i == 0)
     def _():
@@ -359,22 +392,23 @@
         down[:, half:] = (results[1] + from_next[...].astype(f32)).astype(bf16)
 
 
-def product(place, k, left, own, mate, near, arrived=None):
+def last_product(place, k, left, far_left, near, own, mate, arrived=None):
     depth = left[0].shape[1]
-    part = left[0].shape[0] // 2
-    rows = own[1].shape[0]
-    half = own[1].shape[1]
+    part = left[0].shape[0] // SIDE
+    half = own[0].shape[1] // 2
+    start = 0 if arrived is None else 2
     one = lambda i, place: (0, 0)
+    tail = 256
     side = (
-        [pl.BlockSpec((rows, half), lambda i, place: (0, k))]
-        + [pl.BlockSpec((rows, half), one)] * 2
-        + [pl.BlockSpec((rows, half // 2), one)] * 2
+        [pl.BlockSpec((SUB, half), lambda i, place: (lax.rem(place[0] + 2, SIDE), k))] * 3
+        + [pl.BlockSpec((own[3].shape[0], half), one)]
+        + [pl.BlockSpec((part, half), lambda i, place: (start + i, k))]
     )
     in_specs = (
-        [pl.BlockSpec((part, depth), lambda i, place: (i, 0))] * 3
-        + [pl.BlockSpec((part, depth), one)] * 2
+        [pl.BlockSpec((part, tail), lambda i, place: (start + i, depth // tail - 1))] * 3
+        + [pl.BlockSpec((part, depth), lambda i, place: (i, 0))]
+        + [pl.BlockSpec((part, 1), lambda i, place: (start + i, 0))]
         + side * 2
-        + [pl.BlockSpec((part, 1), lambda i, place: (i, 0))]
     )
     S = jax.ShapeDtypeStruct
     if arrived is None:
@@ -395,11 +429,11 @@
         out_shape=shapes,
         compiler_params=pltpu.CompilerParams(vmem_limit_bytes=40 * 2**20),
         cost_estimate=pl.CostEstimate(
-            flops=2 * 2 * part * depth * SIDE * 2 * half,
-            bytes_accessed=2 * SIDE * depth * (2 * part + 2 * half) + 6 * part * half,
+            flops=2 * 2 * part * 2 * depth * 2 * half,
+            bytes_accessed=6 * depth * part + 5 * depth * half + 14 * part * half,
             transcendentals=0,
         ),
-    )(place, *left, *own, *mate, near, *extra)
+    )(place, *left, far_left, near, *own, *mate, *extra)
 
 
 def final_kernel(place, kept, first, second, s_left, t_own, t_mate, *rest):
@@ -463,81 +497,54 @@
     before = lax.ppermute(teacher[rows - HALO :], ("y", "x"), up)
     behind = lax.ppermute(teacher[:HALO], ("y", "x"), down)
 
-    steps = (0, 1, -1, 2)
-
-    def send_x(chunk):
-        return [chunk[0]] + [ring(chunk[r], "x", steps[r]) for r in (1, 2, 3)]
-
-    packed = pack(jnp.stack([y, x]).astype(jnp.int32), student)
-    packed, before, behind = lax.optimization_barrier((packed, before, behind))
-    got0 = send_x(packed[0::2])
+    own_count = lax.dynamic_slice_in_dim(counts[0], z, 1)
+    *packed, block = pack(jnp.stack([y, x, own_count[0]]).astype(jnp.int32), student)
+    packed, block, before, behind = lax.optimization_barrier((packed, block, before, behind))
+    got = [packed[0], ring(packed[1], "x", 1), ring(packed[2], "x", -1), ring(packed[3], "x", 2)]
+    blocks = ring_all(block, "row")
     meta = jnp.concatenate([(starts - shard * rows)[:, None], weights], axis=1)
-    standard, half0, half1, stats = pool(counts[0], before, teacher, behind, meta)
-    near = ring_all(stats, "x")
-    got0, standard, half0, half1, packed1 = lax.optimization_barrier(
-        (got0, standard, half0, half1, packed[1::2])
-    )
-
-    got1 = send_x(packed1)
-    own_count = lax.dynamic_slice_in_dim(counts[0], z, 1)
-    turned0, mean0 = turn(own_count, got0)
-    up0, down0 = ring(turned0, "row", 1), ring(turned0, "row", -1)
-    got1, half0, near, _ = lax.optimization_barrier((got1, half0, near, turned0))
-
-    quarter = half // 2
-    right0, left0 = ring(half0, "x", 1), ring(half0, "x", -1)
-    turned1, mean1 = turn(own_count, got1)
+    standard, stats = pool(counts[0], before, teacher, behind, meta)
+    z_counts = jnp.concatenate(
+        [lax.dynamic_slice_in_dim(counts[0], lax.rem(z + k, SIDE), 1) for k in COMING]
+    )
+    own_stats = shards(z_counts, stats, blocks)
+    got, own_stats, standard = lax.optimization_barrier((got, own_stats, standard))
+    near_stats = ring_all(own_stats, "x")
+    turned, mean = turn(own_count, got)
+    near_stats, turned, standard = lax.optimization_barrier((near_stats, turned, standard))
+
+    right, left = ring(standard, "x", 1), ring(standard, "x", -1)
+    up, down = ring(turned, "row", 1), ring(turned, "row", -1)
     t_standard = swap(standard)
-    group = jnp.stack([n[3, :SIDE] for n in near])
-    z_counts = jnp.stack(
-        [lax.dynamic_index_in_dim(group, lax.rem(z + k, SIDE), 1, keepdims=False) for k in COMING]
-    )
-    z_counts = z_counts.reshape(SIDE * SIDE).astype(jnp.int32)
-    pieces = [p for pair in zip(got0, got1) for p in pair]
-    moment = moments(z_counts, pieces)
-    up0, down0, turned1, moment = lax.optimization_barrier((up0, down0, turned1, moment))
-    far0 = [ring(up0[:part], "row", 1), ring(down0[part:], "row", -1)]
-    t_right0, t_left0 = swap(right0), swap(left0)
-    right0, left0, moment, _ = lax.optimization_barrier((right0, left0, moment, up0))
-    x_far0 = [ring(right0[:, :quarter], "x", 1), ring(left0[:, quarter:], "x", -1)]
-    far0, turned1, moment = lax.optimization_barrier((far0, turned1, moment))
-    every_z = ring_all(moment, "row")
-    turned1 = after(turned1, every_z)
-    up1, down1 = ring(turned1, "row", 1), ring(turned1, "row", -1)
-    t_x_far0 = [swap(f) for f in x_far0]
-    x_far0, half1 = lax.optimization_barrier((x_far0, half1))
-    right1, left1 = ring(half1, "x", 1), ring(half1, "x", -1)
-
-    every = ring_all(shards(z_counts, every_z, near), "y")
-    t_rows, s_left = settle(every)
+    t_rows, s_left = settle(ring_all(gather_stats(near_stats), "y"))
     t_mate = swap(t_rows)
-
+    right, left, up, down, t_standard, t_rows, t_mate, s_left = lax.optimization_barrier(
+        (right, left, up, down, t_standard, t_rows, t_mate, s_left)
+    )
+
+    x_far = [ring(right[:, :half], "x", 1), ring(left[:, half:], "x", -1)]
+    z_far = [ring(up[: width // 2], "row", 1), ring(down[width // 2 :], "row", -1)]
+    t_right, t_left = swap(right), swap(left)
     place = jnp.stack([z, c]).astype(jnp.int32)
-    z0 = [turned0, up0, down0] + far0
-    own0 = [standard, right0, left0] + x_far0
-    mate0 = [t_standard, t_right0, t_left0] + t_x_far0
-    open0 = product(place, 0, z0, own0, mate0, mean0)
-    open0, up1, down1, right1, left1 = lax.optimization_barrier(
-        (open0, up1, down1, right1, left1)
-    )
-    u0 = [ring(open0[0], "y", 1), ring(open0[1], "y", -1)]
-    far1 = [ring(up1[:part], "row", 1), ring(down1[part:], "row", -1)]
-    x_far1 = [ring(right1[:, :quarter], "x", 1), ring(left1[:, quarter:], "x", -1)]
-    t_right1, t_left1 = swap(right1), swap(left1)
-    u0, far1, t_rows, t_mate, s_left = lax.optimization_barrier((u0, far1, t_rows, t_mate, s_left))
-    z1 = [turned1, up1, down1] + far1
-    close0 = product(place, 0, z1, own0, mate0, mean1, u0)
-    close0, x_far1 = lax.optimization_barrier((close0, x_far1))
-    v0 = [ring(close0[0], "y", 1), ring(close0[1], "y", -1)]
-    t_x_far1 = [swap(f) for f in x_far1]
-    own1 = [standard, right1, left1] + x_far1
-    mate1 = [t_standard, t_right1, t_left1] + t_x_far1
-    open1 = product(place, 1, z0, own1, mate1, mean0)
-    u1 = [ring(open1[0], "y", 1), ring(open1[1], "y", -1)]
-    close1 = product(place, 1, z1, own1, mate1, mean1, u1)
-    v1 = [ring(close1[0], "y", 1), ring(close1[1], "y", -1)]
-    out = final(place, 0, open0[2], *v0, s_left, t_rows, t_mate)
-    out = final(place, 1, open1[2], *v1, s_left, t_rows, t_mate, out)
+    own, mate = [standard, right, left], [t_standard, t_right, t_left]
+    near_z = [turned, up, down]
+    own_sum = first_product(place, near_z, own, mean)
+    mate_sum = first_product(place, near_z, mate, mean)
+    x_far, z_far, own_sum, mate_sum = lax.optimization_barrier((x_far, z_far, own_sum, mate_sum))
+
+    t_x_far = [swap(f) for f in x_far]
+    opened = []
+    for k in range(2):
+        sides = (own + [x_far[k], own_sum], mate + [t_x_far[k], mate_sum])
+        opened.append((last_product(place, k, near_z, z_far[0], mean, *sides), sides))
+    arrived = [(ring(o[0], "y", 1), ring(o[1], "y", -1)) for o, _ in opened]
+    out = None
+    for k in range(2):
+        (_, _, kept), sides = opened[k]
+        v = last_product(place, k, near_z, z_far[1], mean, *sides, arrived[k])
+        out = final(
+            place, k, kept, ring(v[0], "y", 1), ring(v[1], "y", -1), s_left, t_rows, t_mate, out
+        )
     return out[None, None]
 
 

time: 191 us -> 177 us (0.927)
  starting transfers between devices: 68.4 us -> 52.3 us
  other arithmetic: 0.19 us -> 3.85 us
  Pallas kernels: 45.9 us -> 49.3 us
  local copies, waits for them, and re-layouts: 19.9 us -> 16.7 us
    ppermute x39 -> x28, starting transfers between devices: 61.4 us -> 46 us  [ring(): lax.ppermute(value, axis, [(i, (i + step) % SIDE) for i in range(SIDE)])]
    pallas_call x6 -> x8, Pallas kernels: 29.6 us -> 35.7 us  [the longest x4 18.3 us: last_product(): pl.pallas_call(kernel, grid_spec=pltpu.PrefetchScalarGridSpec(num_scalar_...]
    slice x12 -> x4, local copies, waits for them, and re-layouts: 5.21 us -> 2.06 us  [the longest x1 0.96 us: per_device(): up[:width // 2]]
    concatenate x0 -> x1, other arithmetic: none -> 2.53 us  [per_device(): jnp.concatenate([lax.dynamic_slice_in_dim(counts[0], lax.rem(z + k, SIDE)...]
    pallas_call x2 -> x1, Pallas kernels: 3.42 us -> 1.18 us  [turn(): pl.pallas_call(turn_kernel, in_specs=[smem()] + [vmem()] * SIDE, out_spec...]
    unnamed x44 -> x46, local copies, waits for them, and re-layouts: 12.8 us -> 11.3 us
    ppermute x39 -> x28, waiting for transfers between devices: 53.3 us -> 52.4 us  [ring(): lax.ppermute(value, axis, [(i, (i + step) % SIDE) for i in range(SIDE)])]
  transfers between devices with their start and end apart: 51 -> 36, of which waited for: 21 -> 8; matrix products, arithmetic and copies ran while one was open for 3% -> 5% of each run, Pallas kernels for 18% -> 26%
where the time goes in v4:
time: 177 us
  waiting for transfers between devices  54.2 us (31%)
  starting transfers between devices  52.3 us (30%)
  Pallas kernels  49.3 us (28%)
  local copies, waits for them, and re-layouts  16.7 us (9%)
  other arithmetic  3.85 us (2%)
    ppermute x28, waiting for transfers between devices, ring(): lax.ppermute(value, axis, [(i, (i + step) % SIDE) for i in range(SIDE)])  52.4 us
    ppermute x28, starting transfers between devices, ring(): lax.ppermute(value, axis, [(i, (i + step) % SIDE) for i in range(SIDE)])  46 us
    pallas_call x4, Pallas kernels, last_product(): pl.pallas_call(kernel, grid_spec=pltpu.PrefetchScalarGridSpec(num_scalar_...  18.3 us
    pallas_call x2, Pallas kernels, first_product(): pl.pallas_call(first_kernel, grid_spec=pltpu.PrefetchScalarGridSpec(num_s...  16.5 us
    unnamed x46, local copies, waits for them, and re-layouts  11.3 us
    pallas_call x2, Pallas kernels, final(): pl.pallas_call(final_kernel, grid_spec=pltpu.PrefetchScalarGridSpec(num_s...  5.34 us
    pallas_call x1, Pallas kernels, pool(): pl.pallas_call(pool_kernel, grid=(columns // tile,), in_specs=[smem(), pl...  4.61 us
    ppermute x1, starting transfers between devices, per_device(): behind = lax.ppermute(teacher[:HALO], ('y', 'x'), down)  3.78 us
  transfers between devices with their start and end apart: 36, of which 8 were waited for; matrix products, arithmetic and copies ran while one was open for 5% of the time, Pallas kernels for 26%

profile of v4, /device:TPU:0, one launch (start us, length us, event | category | flops | bytes accessed | tf_op | source)
XLA Modules:
  0.0 176.6 jit_solution(1229239459495892667)
XLA Ops:
  0.0 0.9 fusion
  0.9 1.6 collective-permute-start
  2.5 3.8 %collective-permute-start.1 = (bf16[16,1024]{1,0:T(8,128)(2,1)S(1)}, bf16[16,1024]{1,0:T(8,128)(2,1)S(1)}, u32[]{:S(2)}, u32[]{:S(2)}) collective-permute-start(bf16[16,1024]{1,0:T(8,128)(2,1)S(1)} %get-tuple-element.113), channel_id=1, source_target_pairs={{8,0},{16,8},{24,16},{32,24},{40,32},{48,40},{56,48},{64,56},{72,6... | collective-permute-start | bytes 98312 | tf_op jit(solution)/shard_map/ppermute | solution.py:498
  6.3 1.5 constant_dynamic-slice_fusion.3
  7.8 0.6 pad_add_fusion.2.place
  8.4 1.4 copy-done.15
  9.8 2.3 %shard_map.55 = (bf16[192,1024]{1,0:T(8,128)(2,1)S(1)}, bf16[192,1024]{1,0:T(8,128)(2,1)}, bf16[192,1024]{1,0:T(8,128)(2,1)}, bf16[192,1024]{1,0:T(8,128)(2,1)}, f32[8,1024]{1,0:T(8,128)}) custom-call(s32[3]{0:T(128)S(1)} %pad_add_fusion.2.place, bf16[192,4096]{1,0:T(8,128)(2,1)S(1)} %copy-done.15), custom_call_target="tpu_custom_call" | custom-call | flops 6291456 | bytes 3145728 | tf_op jit(solution)/shard_map/pallas_call | solution.py:65
  12.2 3.2 %collective-permute-start.3 = (bf16[192,1024]{1,0:T(8,128)(2,1)}, bf16[192,1024]{1,0:T(8,128)(2,1)S(1)}, u32[]{:S(2)}, u32[]{:S(2)}) collective-permute-start(bf16[192,1024]{1,0:T(8,128)(2,1)} %get-tuple-element.66), channel_id=1, source_target_pairs={{0,24},{8,0},{16,8},{24,16},{1,25},{9,1},{17,9},{25,17},{2,26},{10... | collective-permute-start | bytes 1179656 | tf_op jit(solution)/shard_map/ppermute | solution.py:20
  15.5 0.6 pad_add_fusion
  16.1 2.0 %collective-permute-start.5 = (f32[8,1024]{1,0:T(8,128)}, f32[8,1024]{1,0:T(8,128)}, u32[]{:S(2)}, u32[]{:S(2)}) collective-permute-start(f32[8,1024]{1,0:T(8,128)} %get-tuple-element.71.refs_0_), channel_id=1, source_target_pairs={{0,2},{2,4},{4,6},{6,0},{1,3},{3,5},{5,7},{7,1},{8,10},{10,12},{12... | collective-permute-start | bytes 98312 | tf_op jit(solution)/shard_map/ppermute | solution.py:20
  18.1 2.5 %pad_add_fusion.3.counts = s32[4]{0:T(128)S(1)} fusion(s32[1]{0:T(128)} %bitcast.8, s32[1]{0:T(128)} %bitcast.7, s32[1]{0:T(128)} %bitcast.6, s32[1]{0:T(128)} %bitcast.5), kind=kLoop, calls=%fused_computation.9 | loop fusion | flops 12 | bytes 32 | tf_op jit(solution)/shard_map/concatenate | solution.py:507
  20.6 0.9 copy.10.meta
  21.5 2.2 %collective-permute-start.6 = (f32[8,1024]{1,0:T(8,128)}, f32[8,1024]{1,0:T(8,128)S(1)}, u32[]{:S(2)}, u32[]{:S(2)}) collective-permute-start(f32[8,1024]{1,0:T(8,128)} %get-tuple-element.71.refs_0_), channel_id=1, source_target_pairs={{0,6},{2,0},{4,2},{6,4},{1,7},{3,1},{5,3},{7,5},{8,14},{10,8},{12,... | collective-permute-start | bytes 98312 | tf_op jit(solution)/shard_map/ppermute | solution.py:20
  23.7 1.9 %collective-permute-start.7 = (f32[8,1024]{1,0:T(8,128)}, f32[8,1024]{1,0:T(8,128)S(1)}, u32[]{:S(2)}, u32[]{:S(2)}) collective-permute-start(f32[8,1024]{1,0:T(8,128)} %get-tuple-element.71.refs_0_), channel_id=1, source_target_pairs={{0,4},{2,6},{4,0},{6,2},{1,5},{3,7},{5,1},{7,3},{8,12},{10,14},{12... | collective-permute-start | bytes 98312 | tf_op jit(solution)/shard_map/ppermute | solution.py:20
  25.6 0.8 copy-done.17
  26.3 0.8 copy-done.19
  27.1 4.6 %shard_map.56 = (bf16[768,1024]{1,0:T(8,128)(2,1)S(1)}, f32[4,1024]{1,0:T(4,128)S(1)}) custom-call(s32[4]{0:T(128)S(1)} %bitcast.11, bf16[16,1024]{1,0:T(8,128)(2,1)S(1)} %copy-done.17, bf16[768,1024]{1,0:T(8,128)(2,1)S(1)} %copy-done.14, bf16[16,1024]{1,0:T(8,128)(2,1)S(1)} %copy-done.19, s32[768,5]{1,0:T(8,128)S(1)} %copy.10.meta), custom_call_target="tpu_custom_call" | custom-call | flops 402653184 | bytes 4718592 | tf_op jit(solution)/shard_map/pallas_call | solution.py:262
  31.7 0.9 shard_map.57.n0
  32.7 0.9 collective-permute-start.8
  33.6 2.4 %collective-permute-start.9 = (f32[12,1024]{1,0:T(8,128)S(1)}, f32[12,1024]{1,0:T(8,128)S(1)}, u32[]{:S(2)}, u32[]{:S(2)}) collective-permute-start(f32[12,1024]{1,0:T(8,128)S(1)} %shard_map.57.n0), channel_id=1, source_target_pairs={{0,24},{8,0},{16,8},{24,16},{1,25},{9,1},{17,9},{25,17},{2,26},{10... | collective-permute-start | bytes 147464 | tf_op jit(solution)/shard_map/ppermute | solution.py:20
  36.0 2.3 %collective-permute-start.10 = (f32[12,1024]{1,0:T(8,128)S(1)}, f32[12,1024]{1,0:T(8,128)S(1)}, u32[]{:S(2)}, u32[]{:S(2)}) collective-permute-start(f32[12,1024]{1,0:T(8,128)S(1)} %shard_map.57.n0), channel_id=1, source_target_pairs={{0,16},{8,24},{16,0},{24,8},{1,17},{9,25},{17,1},{25,9},{2,18},{10... | collective-permute-start | bytes 147464 | tf_op jit(solution)/shard_map/ppermute | solution.py:20
  38.3 1.2 shard_map.58
  39.5 2.2 %collective-permute-done.10.n3 = f32[12,1024]{1,0:T(8,128)S(1)} collective-permute-done((f32[12,1024]{1,0:T(8,128)S(1)}, f32[12,1024]{1,0:T(8,128)S(1)}, u32[]{:S(2)}, u32[]{:S(2)}) %collective-permute-start.10) | collective-permute-done | bytes 49184 | tf_op jit(solution)/shard_map/ppermute | solution.py:20
  41.8 0.4 collective-permute-start.16
  42.2 2.9 %collective-permute-start.17 = (f32[20,1024]{1,0:T(8,128)S(1)}, f32[20,1024]{1,0:T(8,128)S(1)}, u32[]{:S(2)}, u32[]{:S(2)}) collective-permute-start(f32[20,1024]{1,0:T(8,128)S(1)} %shard_map.59.e0), channel_id=1, source_target_pairs={{0,96},{32,0},{64,32},{96,64},{1,97},{33,1},{65,33},{97,65},{2,98}... | collective-permute-start | bytes 245768 | tf_op jit(solution)/shard_map/ppermute | solution.py:20
  45.1 0.8 collective-permute-start.18
  45.9 1.9 %collective-permute-done.16.e1 = f32[20,1024]{1,0:T(8,128)S(1)} collective-permute-done((f32[20,1024]{1,0:T(8,128)S(1)}, f32[20,1024]{1,0:T(8,128)S(1)}, u32[]{:S(2)}, u32[]{:S(2)}) %collective-permute-start.16) | collective-permute-done | bytes 81952 | tf_op jit(solution)/shard_map/ppermute | solution.py:20
  47.8 3.4 %collective-permute-done.18.e3 = f32[20,1024]{1,0:T(8,128)S(1)} collective-permute-done((f32[20,1024]{1,0:T(8,128)S(1)}, f32[20,1024]{1,0:T(8,128)S(1)}, u32[]{:S(2)}, u32[]{:S(2)}) %collective-permute-start.18) | collective-permute-done | bytes 81952 | tf_op jit(solution)/shard_map/ppermute | solution.py:20
  51.2 0.2 shard_map.60
  51.5 0.3 collective-permute-start.11
  51.8 3.0 %collective-permute-start.12 = (bf16[768,1024]{1,0:T(8,128)(2,1)S(1)}, bf16[768,1024]{1,0:T(8,128)(2,1)S(1)}, u32[]{:S(2)}, u32[]{:S(2)}) collective-permute-start(bf16[768,1024]{1,0:T(8,128)(2,1)S(1)} %get-tuple-element.81.b0.refs_5_), channel_id=1, source_target_pairs={{0,24},{8,0},{16,8},{24,16},{1,25},{9,1},{17,9},{25,17},{2,26},{10... | collective-permute-start | bytes 4718600 | tf_op jit(solution)/shard_map/ppermute | solution.py:20
  54.8 1.8 %collective-permute-start.13 = (bf16[1024,768]{1,0:T(8,128)(2,1)S(1)}, bf16[1024,768]{1,0:T(8,128)(2,1)S(1)}, u32[]{:S(2)}, u32[]{:S(2)}) collective-permute-start(bf16[1024,768]{1,0:T(8,128)(2,1)S(1)} %get-tuple-element.80.a0.refs_0_), channel_id=1, source_target_pairs={{0,2},{2,4},{4,6},{6,0},{1,3},{3,5},{5,7},{7,1},{8,10},{10,12},{12... | collective-permute-start | bytes 4718600 | tf_op jit(solution)/shard_map/ppermute | solution.py:20
  56.6 2.1 %collective-permute-start.14 = (bf16[1024,768]{1,0:T(8,128)(2,1)S(1)}, bf16[1024,768]{1,0:T(8,128)(2,1)S(1)}, u32[]{:S(2)}, u32[]{:S(2)}) collective-permute-start(bf16[1024,768]{1,0:T(8,128)(2,1)S(1)} %get-tuple-element.80.a0.refs_0_), channel_id=1, source_target_pairs={{0,6},{2,0},{4,2},{6,4},{1,7},{3,1},{5,3},{7,5},{8,14},{10,8},{12,... | collective-permute-start | bytes 4718600 | tf_op jit(solution)/shard_map/ppermute | solution.py:20
  58.7 1.1 copy-done.8
  59.9 29.7 %collective-permute-done.11.b1.refs_6_ = bf16[768,1024]{1,0:T(8,128)(2,1)S(1)} collective-permute-done((bf16[768,1024]{1,0:T(8,128)(2,1)S(1)}, bf16[768,1024]{1,0:T(8,128)(2,1)S(1)}, u32[]{:S(2)}, u32[]{:S(2)}) %collective-permute-start.11) | collective-permute-done | bytes 1572896 | tf_op jit(solution)/shard_map/ppermute | solution.py:20
  89.6 3.6 %collective-permute-done.13.a1.refs_1_ = bf16[1024,768]{1,0:T(8,128)(2,1)S(1)} collective-permute-done((bf16[1024,768]{1,0:T(8,128)(2,1)S(1)}, bf16[1024,768]{1,0:T(8,128)(2,1)S(1)}, u32[]{:S(2)}, u32[]{:S(2)}) %collective-permute-start.13) | collective-permute-done | bytes 1572896 | tf_op jit(solution)/shard_map/ppermute | solution.py:20
  93.2 1.2 copy-done.10
  94.4 0.5 copy-done.2
  94.9 0.5 copy-done.4
  95.3 0.3 collective-permute-start.25
  95.9 3.2 %collective-permute-start.21 = (bf16[768,512]{1,0:T(8,128)(2,1)S(1)}, bf16[768,512]{1,0:T(8,128)(2,1)S(1)}, u32[]{:S(2)}, u32[]{:S(2)}) collective-permute-start(bf16[768,512]{1,0:T(8,128)(2,1)S(1)} %slice.21), channel_id=1, source_target_pairs={{0,24},{8,0},{16,8},{24,16},{1,25},{9,1},{17,9},{25,17},{2,26},{10... | collective-permute-start | bytes 2359304 | tf_op jit(solution)/shard_map/ppermute | solution.py:20
  99.1 1.0 slice.22
  100.1 0.8 collective-permute-start.22
  100.9 1.0 slice.23
  101.8 2.4 %collective-permute-start.23 = (bf16[512,768]{1,0:T(8,128)(2,1)}, bf16[512,768]{1,0:T(8,128)(2,1)S(1)}, u32[]{:S(2)}, u32[]{:S(2)}) collective-permute-start(bf16[512,768]{1,0:T(8,128)(2,1)} %slice.23), channel_id=1, source_target_pairs={{0,6},{2,0},{4,2},{6,4},{1,7},{3,1},{5,3},{7,5},{8,14},{10,8},{12,... | collective-permute-start | bytes 2359304 | tf_op jit(solution)/shard_map/ppermute | solution.py:20
  104.4 1.0 copy-done.13
  105.4 7.4 %shard_map.61.refs_9_ = f32[1024,1024]{1,0:T(8,128)S(1)} custom-call(s32[2]{0:T(128)S(1)} %pad_add_fusion.1.place, bf16[1024,768]{1,0:T(8,128)(2,1)S(1)} %copy-done.9, bf16[1024,768]{1,0:T(8,128)(2,1)S(1)} %copy-done.3, bf16[1024,768]{1,0:T(8,128)(2,1)S(1)} %copy-done.5, bf16[768,1024]{1,0:T(8,128)(2,1)S(1)} %copy-done.7, ...), custom_call_target="tpu_custom_call" | custom-call | flops 4026531840 | bytes 13631488 | tf_op jit(solution)/shard_map/pallas_call | solution.py:319
  112.8 2.0 %copy-done = f32[1024,1024]{1,0:T(8,128)} copy-done((f32[1024,1024]{1,0:T(8,128)}, f32[1024,1024]{1,0:T(8,128)S(1)}, u32[]{:S(2)}) %copy-start) | copy-done | bytes 4194328
  114.8 9.1 %shard_map.62.refs_14_ = f32[1024,1024]{1,0:T(8,128)S(1)} custom-call(s32[2]{0:T(128)S(1)} %pad_add_fusion.1.place, bf16[1024,768]{1,0:T(8,128)(2,1)S(1)} %copy-done.9, bf16[1024,768]{1,0:T(8,128)(2,1)S(1)} %copy-done.3, bf16[1024,768]{1,0:T(8,128)(2,1)S(1)} %copy-done.5, bf16[768,1024]{1,0:T(8,128)(2,1)S(1)} %copy-done.11, ...), custom_call_target="tpu_custom_call" | custom-call | flops 4026531840 | bytes 13631488 | tf_op jit(solution)/shard_map/pallas_call | solution.py:319
  123.9 2.0 %copy-done.1 = f32[1024,1024]{1,0:T(8,128)} copy-done((f32[1024,1024]{1,0:T(8,128)}, f32[1024,1024]{1,0:T(8,128)S(1)}, u32[]{:S(2)}) %copy-start.1) | copy-done | bytes 4194328
  126.0 0.5 collective-permute-start.26
  126.5 1.8 %collective-permute-done.31.refs_13_ = bf16[768,512]{1,0:T(8,128)(2,1)S(1)} collective-permute-done((bf16[768,512]{1,0:T(8,128)(2,1)S(1)}, bf16[768,512]{1,0:T(8,128)(2,1)S(1)}, u32[]{:S(2)}, u32[]{:S(2)}) %collective-permute-start.31) | collective-permute-done | bytes 786464 | tf_op jit(solution)/shard_map/ppermute | solution.py:28
  128.3 4.5 %shard_map.65 = (bf16[256,512]{1,0:T(8,128)(2,1)S(1)}, bf16[256,512]{1,0:T(8,128)(2,1)S(1)}, f32[256,1024]{1,0:T(8,128)S(1)}) custom-call(s32[2]{0:T(128)S(1)} %pad_add_fusion.1.place, bf16[1024,768]{1,0:T(8,128)(2,1)S(1)} %copy-done.9, bf16[1024,768]{1,0:T(8,128)(2,1)S(1)} %copy-done.3, bf16[1024,768]{1,0:T(8,128)(2,1)S(1)} %copy-done.5, ...), custom_call_target="tpu_custom_call" | custom-call | flops 1610612736 | bytes 4980736 | tf_op jit(solution)/shard_map/pallas_call | solution.py:421
  132.9 3.2 %collective-permute-start.33 = (bf16[256,512]{1,0:T(8,128)(2,1)S(1)}, bf16[256,512]{1,0:T(8,128)(2,1)S(1)}, u32[]{:S(2)}, u32[]{:S(2)}) collective-permute-start(bf16[256,512]{1,0:T(8,128)(2,1)S(1)} %get-tuple-element.110), channel_id=1, source_target_pairs={{0,96},{32,0},{64,32},{96,64},{1,97},{33,1},{65,33},{97,65},{2,98}... | collective-permute-start | bytes 786440 | tf_op jit(solution)/shard_map/ppermute | solution.py:20
  136.1 4.6 %shard_map.63 = (bf16[256,512]{1,0:T(8,128)(2,1)S(1)}, bf16[256,512]{1,0:T(8,128)(2,1)S(1)}, f32[256,1024]{1,0:T(8,128)S(1)}) custom-call(s32[2]{0:T(128)S(1)} %pad_add_fusion.1.place, bf16[1024,768]{1,0:T(8,128)(2,1)S(1)} %copy-done.9, bf16[1024,768]{1,0:T(8,128)(2,1)S(1)} %copy-done.3, bf16[1024,768]{1,0:T(8,128)(2,1)S(1)} %copy-done.5, ...), custom_call_target="tpu_custom_call" | custom-call | flops 1610612736 | bytes 4980736 | tf_op jit(solution)/shard_map/pallas_call | solution.py:421
  140.8 3.2 %collective-permute-start.28 = (bf16[256,512]{1,0:T(8,128)(2,1)S(1)}, bf16[256,512]{1,0:T(8,128)(2,1)S(1)}, u32[]{:S(2)}, u32[]{:S(2)}) collective-permute-start(bf16[256,512]{1,0:T(8,128)(2,1)S(1)} %get-tuple-element.101), channel_id=1, source_target_pairs={{0,96},{32,0},{64,32},{96,64},{1,97},{33,1},{65,33},{97,65},{2,98}... | collective-permute-start | bytes 786440 | tf_op jit(solution)/shard_map/ppermute | solution.py:20
  144.0 4.6 %shard_map.66 = (bf16[256,1024]{1,0:T(8,128)(2,1)S(1)}, bf16[256,1024]{1,0:T(8,128)(2,1)S(1)}) custom-call(s32[2]{0:T(128)S(1)} %pad_add_fusion.1.place, bf16[1024,768]{1,0:T(8,128)(2,1)S(1)} %copy-done.9, bf16[1024,768]{1,0:T(8,128)(2,1)S(1)} %copy-done.3, bf16[1024,768]{1,0:T(8,128)(2,1)S(1)} %copy-done.5, ...), custom_call_target="tpu_custom_call" | custom-call | flops 1610612736 | bytes 4980736 | tf_op jit(solution)/shard_map/pallas_call | solution.py:421
  148.7 3.2 %collective-permute-start.35 = (bf16[256,1024]{1,0:T(8,128)(2,1)S(1)}, bf16[256,1024]{1,0:T(8,128)(2,1)S(1)}, u32[]{:S(2)}, u32[]{:S(2)}) collective-permute-start(bf16[256,1024]{1,0:T(8,128)(2,1)S(1)} %get-tuple-element.112), channel_id=1, source_target_pairs={{0,96},{32,0},{64,32},{96,64},{1,97},{33,1},{65,33},{97,65},{2,98}... | collective-permute-start | bytes 1572872 | tf_op jit(solution)/shard_map/ppermute | solution.py:20
  151.9 4.6 %shard_map.64 = (bf16[256,1024]{1,0:T(8,128)(2,1)S(1)}, bf16[256,1024]{1,0:T(8,128)(2,1)S(1)}) custom-call(s32[2]{0:T(128)S(1)} %pad_add_fusion.1.place, bf16[1024,768]{1,0:T(8,128)(2,1)S(1)} %copy-done.9, bf16[1024,768]{1,0:T(8,128)(2,1)S(1)} %copy-done.3, bf16[1024,768]{1,0:T(8,128)(2,1)S(1)} %copy-done.5, ...), custom_call_target="tpu_custom_call" | custom-call | flops 1610612736 | bytes 4980736 | tf_op jit(solution)/shard_map/pallas_call | solution.py:421
  156.6 3.2 %collective-permute-start.30 = (bf16[256,1024]{1,0:T(8,128)(2,1)S(1)}, bf16[256,1024]{1,0:T(8,128)(2,1)S(1)}, u32[]{:S(2)}, u32[]{:S(2)}) collective-permute-start(bf16[256,1024]{1,0:T(8,128)(2,1)S(1)} %get-tuple-element.103), channel_id=1, source_target_pairs={{0,96},{32,0},{64,32},{96,64},{1,97},{33,1},{65,33},{97,65},{2,98}... | collective-permute-start | bytes 1572872 | tf_op jit(solution)/shard_map/ppermute | solution.py:20
  159.8 4.9 %collective-permute-done.34.first = bf16[256,1024]{1,0:T(8,128)(2,1)S(1)} collective-permute-done((bf16[256,1024]{1,0:T(8,128)(2,1)S(1)}, bf16[256,1024]{1,0:T(8,128)(2,1)S(1)}, u32[]{:S(2)}, u32[]{:S(2)}) %collective-permute-start.34) | collective-permute-done | bytes 524320 | tf_op jit(solution)/shard_map/ppermute | solution.py:20
  164.7 2.7 %shard_map.67.rest_0_ = f32[256,2048]{1,0:T(8,128)} custom-call(s32[2]{0:T(128)S(1)} %pad_add_fusion.1.place, f32[256,1024]{1,0:T(8,128)S(1)} %get-tuple-element.108.kept, bf16[256,1024]{1,0:T(8,128)(2,1)S(1)} %collective-permute-done.34.first, bf16[256,1024]{1,0:T(8,128)(2,1)S(1)} %collective-permute-done.35.second, ...), custom_call_target="tpu_custom_call" | custom-call | flops 1572864 | bytes 3145728 | tf_op jit(solution)/shard_map/pallas_call | solution.py:467
  167.4 6.5 %collective-permute-done.29.first = bf16[256,1024]{1,0:T(8,128)(2,1)S(1)} collective-permute-done((bf16[256,1024]{1,0:T(8,128)(2,1)S(1)}, bf16[256,1024]{1,0:T(8,128)(2,1)S(1)}, u32[]{:S(2)}, u32[]{:S(2)}) %collective-permute-start.29) | collective-permute-done | bytes 524320 | tf_op jit(solution)/shard_map/ppermute | solution.py:20
  173.9 2.7 %shard_map.68 = f32[256,2048]{1,0:T(8,128)} custom-call(s32[2]{0:T(128)S(1)} %pad_add_fusion.1.place, f32[256,1024]{1,0:T(8,128)S(1)} %get-tuple-element.98.kept, bf16[256,1024]{1,0:T(8,128)(2,1)S(1)} %collective-permute-done.29.first, bf16[256,1024]{1,0:T(8,128)(2,1)S(1)} %collective-permute-done.30.second, ...), custom_call_target="tpu_custom_call", output_to_operand_aliasing={{}: (7, {})} | custom-call | flops 1572864 | bytes 3145728 | tf_op jit(solution)/shard_map/pallas_call | solution.py:467
  (81 shorter events, 1.0 us)
Async XLA Ops:
  0.0 25.6 %copy-start.14 = (bf16[768,1024]{1,0:T(8,128)(2,1)S(1)}, bf16[768,1024]{1,0:T(8,128)(2,1)}, u32[]{:S(2)}) copy-start(bf16[768,1024]{1,0:T(8,128)(2,1)} %teacher.1) | copy-start | bytes 4718596
  0.9 11.2 %collective-permute-start = (bf16[16,1024]{1,0:T(8,128)(2,1)S(1)}, bf16[16,1024]{1,0:T(8,128)(2,1)S(1)}, u32[]{:S(2)}, u32[]{:S(2)}) collective-permute-start(bf16[16,1024]{1,0:T(8,128)(2,1)S(1)} %get-tuple-element.114), channel_id=1, source_target_pairs={{0,8},{8,16},{16,24},{24,32},{32,40},{40,48},{48,56},{56,64},{64,7... | collective-permute-start | bytes 98312 | tf_op jit(solution)/shard_map/ppermute | solution.py:497
  2.5 9.6 %collective-permute-start.1 = (bf16[16,1024]{1,0:T(8,128)(2,1)S(1)}, bf16[16,1024]{1,0:T(8,128)(2,1)S(1)}, u32[]{:S(2)}, u32[]{:S(2)}) collective-permute-start(bf16[16,1024]{1,0:T(8,128)(2,1)S(1)} %get-tuple-element.113), channel_id=1, source_target_pairs={{8,0},{16,8},{24,16},{32,24},{40,32},{48,40},{56,48},{64,56},{72,6... | collective-permute-start | bytes 98312 | tf_op jit(solution)/shard_map/ppermute | solution.py:498
  8.4 1.4 copy-start.15
  9.8 5.6 %copy-start.22 = (s32[768]{0:T(1024)S(1)}, s32[768]{0:T(1024)}, u32[]{:S(2)}) copy-start(s32[768]{0:T(1024)} %param.7) | copy-start | bytes 9220
  9.8 5.6 %copy-start.21 = (s32[768,4]{0,1:T(4,128)S(1)}, s32[768,4]{0,1:T(4,128)}, u32[]{:S(2)}) copy-start(s32[768,4]{0,1:T(4,128)} %param.8) | copy-start | bytes 36868
  9.8 15.8 %copy-start.20 = (s32[1,4]{1,0:T(1,128)S(1)}, s32[1,4]{1,0:T(1,128)}, u32[]{:S(2)}) copy-start(s32[1,4]{1,0:T(1,128)} %param.9) | copy-start | bytes 52
  12.1 6.0 %copy-start.16 = (bf16[16,1024]{1,0:T(8,128)(2,1)}, bf16[16,1024]{1,0:T(8,128)(2,1)S(1)}, u32[]{:S(2)}) copy-start(bf16[16,1024]{1,0:T(8,128)(2,1)S(1)} %collective-permute-done.before) | copy-start | bytes 98308
  12.1 6.0 %copy-start.18 = (bf16[16,1024]{1,0:T(8,128)(2,1)}, bf16[16,1024]{1,0:T(8,128)(2,1)S(1)}, u32[]{:S(2)}) copy-start(bf16[16,1024]{1,0:T(8,128)(2,1)S(1)} %collective-permute-done.1.behind) | copy-start | bytes 98308
  12.1 20.5 %collective-permute-start.2 = (bf16[192,1024]{1,0:T(8,128)(2,1)}, bf16[192,1024]{1,0:T(8,128)(2,1)S(1)}, u32[]{:S(2)}, u32[]{:S(2)}) collective-permute-start(bf16[192,1024]{1,0:T(8,128)(2,1)} %get-tuple-element.65), channel_id=1, source_target_pairs={{0,8},{8,16},{16,24},{24,0},{1,9},{9,17},{17,25},{25,1},{2,10},{10... | collective-permute-start | bytes 1179656 | tf_op jit(solution)/shard_map/ppermute | solution.py:20
  12.2 20.5 %collective-permute-start.3 = (bf16[192,1024]{1,0:T(8,128)(2,1)}, bf16[192,1024]{1,0:T(8,128)(2,1)S(1)}, u32[]{:S(2)}, u32[]{:S(2)}) collective-permute-start(bf16[192,1024]{1,0:T(8,128)(2,1)} %get-tuple-element.66), channel_id=1, source_target_pairs={{0,24},{8,0},{16,8},{24,16},{1,25},{9,1},{17,9},{25,17},{2,26},{10... | collective-permute-start | bytes 1179656 | tf_op jit(solution)/shard_map/ppermute | solution.py:20
  15.4 17.3 %collective-permute-start.4 = (bf16[192,1024]{1,0:T(8,128)(2,1)}, bf16[192,1024]{1,0:T(8,128)(2,1)S(1)}, u32[]{:S(2)}, u32[]{:S(2)}) collective-permute-start(bf16[192,1024]{1,0:T(8,128)(2,1)} %get-tuple-element.67), channel_id=1, source_target_pairs={{0,16},{8,24},{16,0},{24,8},{1,17},{9,25},{17,1},{25,9},{2,18},{10... | collective-permute-start | bytes 1179656 | tf_op jit(solution)/shard_map/ppermute | solution.py:20
  16.1 7.6 %collective-permute-start.5 = (f32[8,1024]{1,0:T(8,128)}, f32[8,1024]{1,0:T(8,128)}, u32[]{:S(2)}, u32[]{:S(2)}) collective-permute-start(f32[8,1024]{1,0:T(8,128)} %get-tuple-element.71.refs_0_), channel_id=1, source_target_pairs={{0,2},{2,4},{4,6},{6,0},{1,3},{3,5},{5,7},{7,1},{8,10},{10,12},{12... | collective-permute-start | bytes 98312 | tf_op jit(solution)/shard_map/ppermute | solution.py:20
  21.5 10.2 %collective-permute-start.6 = (f32[8,1024]{1,0:T(8,128)}, f32[8,1024]{1,0:T(8,128)S(1)}, u32[]{:S(2)}, u32[]{:S(2)}) collective-permute-start(f32[8,1024]{1,0:T(8,128)} %get-tuple-element.71.refs_0_), channel_id=1, source_target_pairs={{0,6},{2,0},{4,2},{6,4},{1,7},{3,1},{5,3},{7,5},{8,14},{10,8},{12,... | collective-permute-start | bytes 98312 | tf_op jit(solution)/shard_map/ppermute | solution.py:20
  23.7 8.0 %collective-permute-start.7 = (f32[8,1024]{1,0:T(8,128)}, f32[8,1024]{1,0:T(8,128)S(1)}, u32[]{:S(2)}, u32[]{:S(2)}) collective-permute-start(f32[8,1024]{1,0:T(8,128)} %get-tuple-element.71.refs_0_), channel_id=1, source_target_pairs={{0,4},{2,6},{4,0},{6,2},{1,5},{3,7},{5,1},{7,3},{8,12},{10,14},{12... | collective-permute-start | bytes 98312 | tf_op jit(solution)/shard_map/ppermute | solution.py:20
  25.6 0.8 copy-start.17
  26.3 0.8 copy-start.19
  31.7 63.1 %copy-start.6 = (bf16[768,1024]{1,0:T(8,128)(2,1)}, bf16[768,1024]{1,0:T(8,128)(2,1)S(1)}, u32[]{:S(2)}) copy-start(bf16[768,1024]{1,0:T(8,128)(2,1)S(1)} %get-tuple-element.81.b0.refs_5_) | copy-start | bytes 4718596
  32.7 6.8 %collective-permute-start.8 = (f32[12,1024]{1,0:T(8,128)S(1)}, f32[12,1024]{1,0:T(8,128)S(1)}, u32[]{:S(2)}, u32[]{:S(2)}) collective-permute-start(f32[12,1024]{1,0:T(8,128)S(1)} %shard_map.57.n0), channel_id=1, source_target_pairs={{0,8},{8,16},{16,24},{24,0},{1,9},{9,17},{17,25},{25,1},{2,10},{10... | collective-permute-start | bytes 147464 | tf_op jit(solution)/shard_map/ppermute | solution.py:20
  33.6 5.9 %collective-permute-start.9 = (f32[12,1024]{1,0:T(8,128)S(1)}, f32[12,1024]{1,0:T(8,128)S(1)}, u32[]{:S(2)}, u32[]{:S(2)}) collective-permute-start(f32[12,1024]{1,0:T(8,128)S(1)} %shard_map.57.n0), channel_id=1, source_target_pairs={{0,24},{8,0},{16,8},{24,16},{1,25},{9,1},{17,9},{25,17},{2,26},{10... | collective-permute-start | bytes 147464 | tf_op jit(solution)/shard_map/ppermute | solution.py:20
  36.0 5.8 %collective-permute-start.10 = (f32[12,1024]{1,0:T(8,128)S(1)}, f32[12,1024]{1,0:T(8,128)S(1)}, u32[]{:S(2)}, u32[]{:S(2)}) collective-permute-start(f32[12,1024]{1,0:T(8,128)S(1)} %shard_map.57.n0), channel_id=1, source_target_pairs={{0,16},{8,24},{16,0},{24,8},{1,17},{9,25},{17,1},{25,9},{2,18},{10... | collective-permute-start | bytes 147464 | tf_op jit(solution)/shard_map/ppermute | solution.py:20
  39.5 55.3 %copy-start.12 = (f32[1024,1]{1,0:T(8,128)}, f32[1024,1]{1,0:T(8,128)S(1)}, u32[]{:S(2)}) copy-start(f32[1024,1]{1,0:T(8,128)S(1)} %get-tuple-element.92.near.refs_4_) | copy-start | bytes 12292
  41.8 6.0 %collective-permute-start.16 = (f32[20,1024]{1,0:T(8,128)S(1)}, f32[20,1024]{1,0:T(8,128)S(1)}, u32[]{:S(2)}, u32[]{:S(2)}) collective-permute-start(f32[20,1024]{1,0:T(8,128)S(1)} %shard_map.59.e0), channel_id=1, source_target_pairs={{0,32},{32,64},{64,96},{96,0},{1,33},{33,65},{65,97},{97,1},{2,34}... | collective-permute-start | bytes 245768 | tf_op jit(solution)/shard_map/ppermute | solution.py:20
  42.2 5.5 %collective-permute-start.17 = (f32[20,1024]{1,0:T(8,128)S(1)}, f32[20,1024]{1,0:T(8,128)S(1)}, u32[]{:S(2)}, u32[]{:S(2)}) collective-permute-start(f32[20,1024]{1,0:T(8,128)S(1)} %shard_map.59.e0), channel_id=1, source_target_pairs={{0,96},{32,0},{64,32},{96,64},{1,97},{33,1},{65,33},{97,65},{2,98}... | collective-permute-start | bytes 245768 | tf_op jit(solution)/shard_map/ppermute | solution.py:20
  45.1 6.1 %collective-permute-start.18 = (f32[20,1024]{1,0:T(8,128)S(1)}, f32[20,1024]{1,0:T(8,128)S(1)}, u32[]{:S(2)}, u32[]{:S(2)}) collective-permute-start(f32[20,1024]{1,0:T(8,128)S(1)} %shard_map.59.e0), channel_id=1, source_target_pairs={{0,64},{32,96},{64,0},{96,32},{1,65},{33,97},{65,1},{97,33},{2,66}... | collective-permute-start | bytes 245768 | tf_op jit(solution)/shard_map/ppermute | solution.py:20
  51.4 8.4 %collective-permute-start.19 = (f32[17,1024]{1,0:T(8,128)S(1)}, f32[17,1024]{1,0:T(8,128)S(1)}, u32[]{:S(2)}, u32[]{:S(2)}) collective-permute-start(f32[17,1024]{1,0:T(8,128)S(1)} %get-tuple-element.105.t_own), channel_id=1, source_target_pairs={{0,1},{1,0},{2,3},{3,2},{4,5},{5,4},{6,7},{7,6},{8,9},{9,8},{10,11... | collective-permute-start | bytes 208904 | tf_op jit(solution)/shard_map/ppermute | solution.py:28
  51.5 38.0 %collective-permute-start.11 = (bf16[768,1024]{1,0:T(8,128)(2,1)S(1)}, bf16[768,1024]{1,0:T(8,128)(2,1)S(1)}, u32[]{:S(2)}, u32[]{:S(2)}) collective-permute-start(bf16[768,1024]{1,0:T(8,128)(2,1)S(1)} %get-tuple-element.81.b0.refs_5_), channel_id=1, source_target_pairs={{0,8},{8,16},{16,24},{24,0},{1,9},{9,17},{17,25},{25,1},{2,10},{10... | collective-permute-start | bytes 4718600 | tf_op jit(solution)/shard_map/ppermute | solution.py:20
  51.8 37.7 %collective-permute-start.12 = (bf16[768,1024]{1,0:T(8,128)(2,1)S(1)}, bf16[768,1024]{1,0:T(8,128)(2,1)S(1)}, u32[]{:S(2)}, u32[]{:S(2)}) collective-permute-start(bf16[768,1024]{1,0:T(8,128)(2,1)S(1)} %get-tuple-element.81.b0.refs_5_), channel_id=1, source_target_pairs={{0,24},{8,0},{16,8},{24,16},{1,25},{9,1},{17,9},{25,17},{2,26},{10... | collective-permute-start | bytes 4718600 | tf_op jit(solution)/shard_map/ppermute | solution.py:20
  54.8 38.3 %collective-permute-start.13 = (bf16[1024,768]{1,0:T(8,128)(2,1)S(1)}, bf16[1024,768]{1,0:T(8,128)(2,1)S(1)}, u32[]{:S(2)}, u32[]{:S(2)}) collective-permute-start(bf16[1024,768]{1,0:T(8,128)(2,1)S(1)} %get-tuple-element.80.a0.refs_0_), channel_id=1, source_target_pairs={{0,2},{2,4},{4,6},{6,0},{1,3},{3,5},{5,7},{7,1},{8,10},{10,12},{12... | collective-permute-start | bytes 4718600 | tf_op jit(solution)/shard_map/ppermute | solution.py:20
  56.6 36.6 %collective-permute-start.14 = (bf16[1024,768]{1,0:T(8,128)(2,1)S(1)}, bf16[1024,768]{1,0:T(8,128)(2,1)S(1)}, u32[]{:S(2)}, u32[]{:S(2)}) collective-permute-start(bf16[1024,768]{1,0:T(8,128)(2,1)S(1)} %get-tuple-element.80.a0.refs_0_), channel_id=1, source_target_pairs={{0,6},{2,0},{4,2},{6,4},{1,7},{3,1},{5,3},{7,5},{8,14},{10,8},{12,... | collective-permute-start | bytes 4718600 | tf_op jit(solution)/shard_map/ppermute | solution.py:20
  58.7 1.1 copy-start.8
  59.9 33.3 %collective-permute-start.15 = (bf16[768,1024]{1,0:T(8,128)(2,1)S(1)}, bf16[768,1024]{1,0:T(8,128)(2,1)S(1)}, u32[]{:S(2)}, u32[]{:S(2)}) collective-permute-start(bf16[768,1024]{1,0:T(8,128)(2,1)S(1)} %get-tuple-element.81.b0.refs_5_), channel_id=1, source_target_pairs={{0,1},{1,0},{2,3},{3,2},{4,5},{5,4},{6,7},{7,6},{8,9},{9,8},{10,11... | collective-permute-start | bytes 4718600 | tf_op jit(solution)/shard_map/ppermute | solution.py:28
  93.2 1.7 copy-start.2
  93.2 2.2 %copy-start.4 = (bf16[1024,768]{1,0:T(8,128)(2,1)}, bf16[1024,768]{1,0:T(8,128)(2,1)S(1)}, u32[]{:S(2)}) copy-start(bf16[1024,768]{1,0:T(8,128)(2,1)S(1)} %collective-permute-done.14.a2.refs_2_) | copy-start | bytes 4718596
  93.2 1.2 copy-start.10
  94.8 7.0 %collective-permute-start.24 = (bf16[768,1024]{1,0:T(8,128)(2,1)S(1)}, bf16[768,1024]{1,0:T(8,128)(2,1)}, u32[]{:S(2)}, u32[]{:S(2)}) collective-permute-start(bf16[768,1024]{1,0:T(8,128)(2,1)S(1)} %collective-permute-done.11.b1.refs_6_), channel_id=1, source_target_pairs={{0,1},{1,0},{2,3},{3,2},{4,5},{5,4},{6,7},{7,6},{8,9},{9,8},{10,11... | collective-permute-start | bytes 4718600 | tf_op jit(solution)/shard_map/ppermute | solution.py:28
  95.3 19.4 %collective-permute-start.25 = (bf16[768,1024]{1,0:T(8,128)(2,1)S(1)}, bf16[768,1024]{1,0:T(8,128)(2,1)}, u32[]{:S(2)}, u32[]{:S(2)}) collective-permute-start(bf16[768,1024]{1,0:T(8,128)(2,1)S(1)} %collective-permute-done.12.b2.refs_7_), channel_id=1, source_target_pairs={{0,1},{1,0},{2,3},{3,2},{4,5},{5,4},{6,7},{7,6},{8,9},{9,8},{10,11... | collective-permute-start | bytes 4718600 | tf_op jit(solution)/shard_map/ppermute | solution.py:28
  95.6 3.5 %copy-start.3 = (bf16[1024,768]{1,0:T(8,128)(2,1)S(1)}, bf16[1024,768]{1,0:T(8,128)(2,1)}, u32[]{:S(2)}) copy-start(bf16[1024,768]{1,0:T(8,128)(2,1)} %copy-done.2) | copy-start | bytes 4718596
  95.7 5.2 %copy-start.5 = (bf16[1024,768]{1,0:T(8,128)(2,1)S(1)}, bf16[1024,768]{1,0:T(8,128)(2,1)}, u32[]{:S(2)}) copy-start(bf16[1024,768]{1,0:T(8,128)(2,1)} %copy-done.4) | copy-start | bytes 4718596
  95.8 8.6 %copy-start.7 = (bf16[768,1024]{1,0:T(8,128)(2,1)S(1)}, bf16[768,1024]{1,0:T(8,128)(2,1)}, u32[]{:S(2)}) copy-start(bf16[768,1024]{1,0:T(8,128)(2,1)} %copy-done.6) | copy-start | bytes 4718596
  95.8 8.6 %copy-start.9 = (bf16[1024,768]{1,0:T(8,128)(2,1)S(1)}, bf16[1024,768]{1,0:T(8,128)(2,1)}, u32[]{:S(2)}) copy-start(bf16[1024,768]{1,0:T(8,128)(2,1)} %copy-done.8) | copy-start | bytes 4718596
  95.8 30.1 %collective-permute-start.20 = (bf16[768,512]{1,0:T(8,128)(2,1)S(1)}, bf16[768,512]{1,0:T(8,128)(2,1)S(1)}, u32[]{:S(2)}, u32[]{:S(2)}) collective-permute-start(bf16[768,512]{1,0:T(8,128)(2,1)S(1)} %slice.20), channel_id=1, source_target_pairs={{0,8},{8,16},{16,24},{24,0},{1,9},{9,17},{17,25},{25,1},{2,10},{10... | collective-permute-start | bytes 2359304 | tf_op jit(solution)/shard_map/ppermute | solution.py:20
  95.9 30.0 %collective-permute-start.21 = (bf16[768,512]{1,0:T(8,128)(2,1)S(1)}, bf16[768,512]{1,0:T(8,128)(2,1)S(1)}, u32[]{:S(2)}, u32[]{:S(2)}) collective-permute-start(bf16[768,512]{1,0:T(8,128)(2,1)S(1)} %slice.21), channel_id=1, source_target_pairs={{0,24},{8,0},{16,8},{24,16},{1,25},{9,1},{17,9},{25,17},{2,26},{10... | collective-permute-start | bytes 2359304 | tf_op jit(solution)/shard_map/ppermute | solution.py:20
  100.1 25.8 %collective-permute-start.22 = (bf16[512,768]{1,0:T(8,128)(2,1)}, bf16[512,768]{1,0:T(8,128)(2,1)S(1)}, u32[]{:S(2)}, u32[]{:S(2)}) collective-permute-start(bf16[512,768]{1,0:T(8,128)(2,1)} %slice.22), channel_id=1, source_target_pairs={{0,2},{2,4},{4,6},{6,0},{1,3},{3,5},{5,7},{7,1},{8,10},{10,12},{12... | collective-permute-start | bytes 2359304 | tf_op jit(solution)/shard_map/ppermute | solution.py:20
  101.8 24.1 %collective-permute-start.23 = (bf16[512,768]{1,0:T(8,128)(2,1)}, bf16[512,768]{1,0:T(8,128)(2,1)S(1)}, u32[]{:S(2)}, u32[]{:S(2)}) collective-permute-start(bf16[512,768]{1,0:T(8,128)(2,1)} %slice.23), channel_id=1, source_target_pairs={{0,6},{2,0},{4,2},{6,4},{1,7},{3,1},{5,3},{7,5},{8,14},{10,8},{12,... | collective-permute-start | bytes 2359304 | tf_op jit(solution)/shard_map/ppermute | solution.py:20
  104.4 1.0 copy-start.13
  105.4 9.4 %copy-start.11 = (bf16[768,1024]{1,0:T(8,128)(2,1)S(1)}, bf16[768,1024]{1,0:T(8,128)(2,1)}, u32[]{:S(2)}) copy-start(bf16[768,1024]{1,0:T(8,128)(2,1)} %copy-done.10) | copy-start | bytes 4718596
  112.8 2.0 %copy-start = (f32[1024,1024]{1,0:T(8,128)}, f32[1024,1024]{1,0:T(8,128)S(1)}, u32[]{:S(2)}) copy-start(f32[1024,1024]{1,0:T(8,128)S(1)} %shard_map.61.refs_9_) | copy-start | bytes 12582916
  123.9 2.0 %copy-start.1 = (f32[1024,1024]{1,0:T(8,128)}, f32[1024,1024]{1,0:T(8,128)S(1)}, u32[]{:S(2)}) copy-start(f32[1024,1024]{1,0:T(8,128)S(1)} %shard_map.62.refs_14_) | copy-start | bytes 12582916
  125.9 2.4 %collective-permute-start.31 = (bf16[768,512]{1,0:T(8,128)(2,1)S(1)}, bf16[768,512]{1,0:T(8,128)(2,1)S(1)}, u32[]{:S(2)}, u32[]{:S(2)}) collective-permute-start(bf16[768,512]{1,0:T(8,128)(2,1)S(1)} %collective-permute-done.20.refs_8_), channel_id=1, source_target_pairs={{0,1},{1,0},{2,3},{3,2},{4,5},{5,4},{6,7},{7,6},{8,9},{9,8},{10,11... | collective-permute-start | bytes 2359304 | tf_op jit(solution)/shard_map/ppermute | solution.py:28
  126.0 10.1 %collective-permute-start.26 = (bf16[768,512]{1,0:T(8,128)(2,1)S(1)}, bf16[768,512]{1,0:T(8,128)(2,1)S(1)}, u32[]{:S(2)}, u32[]{:S(2)}) collective-permute-start(bf16[768,512]{1,0:T(8,128)(2,1)S(1)} %collective-permute-done.21.refs_8_), channel_id=1, source_target_pairs={{0,1},{1,0},{2,3},{3,2},{4,5},{5,4},{6,7},{7,6},{8,9},{9,8},{10,11... | collective-permute-start | bytes 2359304 | tf_op jit(solution)/shard_map/ppermute | solution.py:28
  132.8 11.2 %collective-permute-start.32 = (bf16[256,512]{1,0:T(8,128)(2,1)S(1)}, bf16[256,512]{1,0:T(8,128)(2,1)S(1)}, u32[]{:S(2)}, u32[]{:S(2)}) collective-permute-start(bf16[256,512]{1,0:T(8,128)(2,1)S(1)} %get-tuple-element.109), channel_id=1, source_target_pairs={{0,32},{32,64},{64,96},{96,0},{1,33},{33,65},{65,97},{97,1},{2,34}... | collective-permute-start | bytes 786440 | tf_op jit(solution)/shard_map/ppermute | solution.py:20
  132.9 11.1 %collective-permute-start.33 = (bf16[256,512]{1,0:T(8,128)(2,1)S(1)}, bf16[256,512]{1,0:T(8,128)(2,1)S(1)}, u32[]{:S(2)}, u32[]{:S(2)}) collective-permute-start(bf16[256,512]{1,0:T(8,128)(2,1)S(1)} %get-tuple-element.110), channel_id=1, source_target_pairs={{0,96},{32,0},{64,32},{96,64},{1,97},{33,1},{65,33},{97,65},{2,98}... | collective-permute-start | bytes 786440 | tf_op jit(solution)/shard_map/ppermute | solution.py:20
  140.7 11.2 %collective-permute-start.27 = (bf16[256,512]{1,0:T(8,128)(2,1)S(1)}, bf16[256,512]{1,0:T(8,128)(2,1)S(1)}, u32[]{:S(2)}, u32[]{:S(2)}) collective-permute-start(bf16[256,512]{1,0:T(8,128)(2,1)S(1)} %get-tuple-element.100), channel_id=1, source_target_pairs={{0,32},{32,64},{64,96},{96,0},{1,33},{33,65},{65,97},{97,1},{2,34}... | collective-permute-start | bytes 786440 | tf_op jit(solution)/shard_map/ppermute | solution.py:20
  140.8 11.1 %collective-permute-start.28 = (bf16[256,512]{1,0:T(8,128)(2,1)S(1)}, bf16[256,512]{1,0:T(8,128)(2,1)S(1)}, u32[]{:S(2)}, u32[]{:S(2)}) collective-permute-start(bf16[256,512]{1,0:T(8,128)(2,1)S(1)} %get-tuple-element.101), channel_id=1, source_target_pairs={{0,96},{32,0},{64,32},{96,64},{1,97},{33,1},{65,33},{97,65},{2,98}... | collective-permute-start | bytes 786440 | tf_op jit(solution)/shard_map/ppermute | solution.py:20
  148.6 16.1 %collective-permute-start.34 = (bf16[256,1024]{1,0:T(8,128)(2,1)S(1)}, bf16[256,1024]{1,0:T(8,128)(2,1)S(1)}, u32[]{:S(2)}, u32[]{:S(2)}) collective-permute-start(bf16[256,1024]{1,0:T(8,128)(2,1)S(1)} %get-tuple-element.111), channel_id=1, source_target_pairs={{0,32},{32,64},{64,96},{96,0},{1,33},{33,65},{65,97},{97,1},{2,34}... | collective-permute-start | bytes 1572872 | tf_op jit(solution)/shard_map/ppermute | solution.py:20
  148.7 16.1 %collective-permute-start.35 = (bf16[256,1024]{1,0:T(8,128)(2,1)S(1)}, bf16[256,1024]{1,0:T(8,128)(2,1)S(1)}, u32[]{:S(2)}, u32[]{:S(2)}) collective-permute-start(bf16[256,1024]{1,0:T(8,128)(2,1)S(1)} %get-tuple-element.112), channel_id=1, source_target_pairs={{0,96},{32,0},{64,32},{96,64},{1,97},{33,1},{65,33},{97,65},{2,98}... | collective-permute-start | bytes 1572872 | tf_op jit(solution)/shard_map/ppermute | solution.py:20
  156.5 17.4 %collective-permute-start.29 = (bf16[256,1024]{1,0:T(8,128)(2,1)S(1)}, bf16[256,1024]{1,0:T(8,128)(2,1)S(1)}, u32[]{:S(2)}, u32[]{:S(2)}) collective-permute-start(bf16[256,1024]{1,0:T(8,128)(2,1)S(1)} %get-tuple-element.102), channel_id=1, source_target_pairs={{0,32},{32,64},{64,96},{96,0},{1,33},{33,65},{65,97},{97,1},{2,34}... | collective-permute-start | bytes 1572872 | tf_op jit(solution)/shard_map/ppermute | solution.py:20
  156.6 17.4 %collective-permute-start.30 = (bf16[256,1024]{1,0:T(8,128)(2,1)S(1)}, bf16[256,1024]{1,0:T(8,128)(2,1)S(1)}, u32[]{:S(2)}, u32[]{:S(2)}) collective-permute-start(bf16[256,1024]{1,0:T(8,128)(2,1)S(1)} %get-tuple-element.103), channel_id=1, source_target_pairs={{0,96},{32,0},{64,32},{96,64},{1,97},{33,1},{65,33},{97,65},{2,98}... | collective-permute-start | bytes 1572872 | tf_op jit(solution)/shard_map/ppermute | solution.py:20

commit v5 on v4

--- a/solution.py
+++ b/solution.py
@@ -40,8 +40,8 @@
     return pl.BlockSpec(memory_space=pltpu.VMEM)
 
 
-def pack_kernel(place, student, *outs):
-    y, x, count = place[0], place[1], place[2]
+def pack_kernel(place, counts, student, *outs):
+    y, x, count = place[2], place[3], counts[0, place[0]]
     moments = outs[SIDE]
     part = outs[0].shape[1] // SIDE
     for r, x_step in enumerate((0, 1, SIDE - 1, 2)):
@@ -60,11 +60,11 @@
             moments[SIDE + r : SIDE + r + 1, columns] = jnp.sum(dev * dev, axis=0, keepdims=True)
 
 
-def pack(place, student):
+def pack(place, counts, student):
     width = student.shape[1] // SIDE
     return pl.pallas_call(
         pack_kernel,
-        in_specs=[smem(), vmem()],
+        in_specs=[smem(), smem(), vmem()],
         out_specs=[vmem()] * (SIDE + 1),
         out_shape=[jax.ShapeDtypeStruct((SUB, width), bf16)] * SIDE
         + [jax.ShapeDtypeStruct((2 * SIDE, width), f32)],
@@ -74,24 +74,25 @@
             bytes_accessed=4 * SUB * student.shape[1],
             transcendentals=0,
         ),
-    )(place, student)
-
-
-def turn_kernel(own_count, p0, p1, p2, p3, turned, near):
+    )(place, counts, student)
+
+
+def turn_kernel(place, counts, p0, p1, p2, p3, turned, near):
+    count = counts[0, place[0]]
     rows = jnp.concatenate([p[...] for p in (p0, p1, p2, p3)], axis=0)
     flat = rows.T
     turned[...] = flat
     mine = flat[:, :SUB].astype(f32)
-    live = lax.broadcasted_iota(jnp.int32, mine.shape, 1) < own_count[0]
+    live = lax.broadcasted_iota(jnp.int32, mine.shape, 1) < count
     total = jnp.sum(jnp.where(live, mine, 0.0), axis=1, keepdims=True)
-    near[...] = total / own_count[0].astype(f32)
-
-
-def turn(own_count, pieces):
+    near[...] = total / count.astype(f32)
+
+
+def turn(place, counts, pieces):
     width = pieces[0].shape[1]
     return pl.pallas_call(
         turn_kernel,
-        in_specs=[smem()] + [vmem()] * SIDE,
+        in_specs=[smem()] * 2 + [vmem()] * SIDE,
         out_specs=[vmem()] * 2,
         out_shape=[
             jax.ShapeDtypeStruct((width, SIDE * SUB), bf16),
@@ -101,13 +102,13 @@
         cost_estimate=pl.CostEstimate(
             flops=0, bytes_accessed=4 * SUB * SIDE * width, transcendentals=0
         ),
-    )(own_count, *pieces)
-
-
-def shards_kernel(counts, teacher, *refs):
+    )(place, counts, *pieces)
+
+
+def shards_kernel(place, counts, teacher, *refs):
     blocks, out = refs[:SIDE], refs[-1]
     out[:SIDE, :] = teacher[...]
-    size = [counts[q].astype(f32) for q in range(SIDE)]
+    size = [counts[0, lax.rem(place[0] + k, SIDE)].astype(f32) for k in COMING]
     totals = [b[:SIDE, :] for b in blocks]
     total = totals[0] + totals[1] + totals[2] + totals[3]
     mean = total / (size[0] + size[1] + size[2] + size[3])
@@ -119,43 +120,45 @@
     out[2 * SIDE :, :] = square
 
 
-def shards(counts, teacher, blocks):
+def shards(place, counts, teacher, blocks):
     columns = blocks[0].shape[1]
     return pl.pallas_call(
         shards_kernel,
-        in_specs=[smem()] + [vmem()] * (1 + SIDE),
+        in_specs=[smem()] * 2 + [vmem()] * (1 + SIDE),
         out_specs=vmem(),
         out_shape=jax.ShapeDtypeStruct((3 * SIDE, columns), f32),
         compiler_params=pltpu.CompilerParams(vmem_limit_bytes=8 * 2**20),
-    )(counts, teacher, *blocks)
-
-
-def gather_kernel(n0, n1, n2, n3, out):
-    for r, (n, row) in enumerate(zip((n0, n1, n2, n3), (0, 1, 2, 3))):
-        for i in range(3):
-            out[i * SIDE + r : i * SIDE + r + 1, :] = n[i : i + 1, :]
-        for i in range(2):
-            at = (1 + i) * SIDE + row
-            out[(3 + i) * SIDE + r : (3 + i) * SIDE + r + 1, :] = n[at : at + 1, :]
-
-
-def gather_stats(near):
-    columns = near[0].shape[1]
-    return pl.pallas_call(
-        gather_kernel,
+    )(place, counts, teacher, *blocks)
+
+
+def spread_kernel(e0, e1, e2, e3, *outs):
+    part = e0.shape[1] // SIDE
+    for r, out in enumerate(outs):
+        for i, (e, slot) in enumerate(zip((e0, e1, e2, e3), (1, 2, 3, 0))):
+            for m in range(3):
+                out[m * SIDE + i : m * SIDE + i + 1, :] = e[m : m + 1, :]
+            for m in range(2):
+                row = (1 + m) * SIDE + r
+                out[12 + m : 13 + m, i * part : (i + 1) * part] = e[
+                    row : row + 1, slot * part : (slot + 1) * part
+                ]
+        out[14:16, :] = jnp.zeros((2, out.shape[1]), f32)
+
+
+def spread(every):
+    columns = every[0].shape[1]
+    return pl.pallas_call(
+        spread_kernel,
         in_specs=[vmem()] * SIDE,
-        out_specs=vmem(),
-        out_shape=jax.ShapeDtypeStruct((5 * SIDE, columns), f32),
+        out_specs=[vmem()] * SIDE,
+        out_shape=[jax.ShapeDtypeStruct((16, columns), f32)] * SIDE,
         compiler_params=pltpu.CompilerParams(vmem_limit_bytes=8 * 2**20),
-    )(*near)
-
-
-def settle_kernel(e0, e1, e2, e3, t_rows, s_left, work):
-    every = (e0, e1, e2, e3)
+    )(*every)
+
+
+def settle_kernel(n0, n1, n2, n3, t_rows, s_left, work):
+    every = (n0, n1, n2, n3)
     part = work.shape[1]
-
-    def pieces(first, columns):
-        return [e[first * SIDE : (first + 1) * SIDE, c] for e, c in zip(every, columns)]
 
     def combine(totals, squares, counts):
         tokens = sum(jnp.sum(n, axis=0, keepdims=True) for n in counts)
@@ -167,18 +170,21 @@
         )
         return offs, lax.rsqrt(square / tokens + epsilon), tokens
 
-    whole = [slice(None)] * SIDE
-    offs, scale, _ = combine(pieces(0, whole), pieces(1, whole), pieces(2, whole))
+    offs, scale, _ = combine(
+        [n[0:4, :] for n in every], [n[4:8, :] for n in every], [n[8:12, :] for n in every]
+    )
     for j in range(SIDE):
         t_rows[j * SIDE : (j + 1) * SIDE, :] = offs[j] * scale
     t_rows[SIDE * SIDE : SIDE * SIDE + 1, :] = scale
-    slots = [slice(i * part, (i + 1) * part) for i in (1, 2, 3, 0)]
-    counts = pieces(2, [slice(0, part)] * SIDE)
-    offs, scale, tokens = combine(pieces(3, slots), pieces(4, slots), counts)
+    spots = [(n, i, slice(i * part, (i + 1) * part)) for n in every for i in range(SIDE)]
+    counts = [n[8 + i : 9 + i, 0:part] for n, i, _ in spots]
+    offs, scale, tokens = combine(
+        [n[12:13, c] for n, _, c in spots], [n[13:14, c] for n, _, c in spots], counts
+    )
     scale = scale / jnp.sqrt(tokens)
     work[...] = jnp.zeros_like(work)
-    for j in range(SIDE):
-        work[j * SIDE : (j + 1) * SIDE, :] = offs[j] * scale * counts[j]
+    for j in range(SIDE * SIDE):
+        work[j : j + 1, :] = offs[j] * scale * counts[j]
     work[SIDE * SIDE : SIDE * SIDE + 1, :] = scale
     s_left[...] = work[...].T
 
@@ -196,25 +202,32 @@
         ],
         scratch_shapes=[pltpu.VMEM((128, part), f32)],
         compiler_params=pltpu.CompilerParams(vmem_limit_bytes=8 * 2**20),
+        cost_estimate=pl.CostEstimate(
+            flops=10**11, bytes_accessed=2 * 10**8, transcendentals=0
+        ),
     )(*every)
 
 
-def pool_kernel(counts, before, teacher, behind, meta, full, stats, mix, share, pooled):
+def pool_kernel(place, counts, before, teacher, behind, starts, weights, full, stats, mix, share, pooled, lines, meta):
     window = SUB + 2 * HALO
     length = teacher.shape[0]
     j = pl.program_id(0)
 
     @pl.when(j == 0)
     def _():
+        lines[...] = jnp.zeros_like(lines)
+        lines[0:1, :] = (starts[...] - (place[2] * SIDE + place[3]) * length).astype(f32)
+        lines[1 : 1 + BAND, :] = weights[...].astype(f32)
+        meta[...] = lines[...].T.astype(jnp.int32)
         for r in range(SIDE):
             rows = slice(r * SUB, (r + 1) * SUB)
-            place = lax.broadcasted_iota(jnp.int32, (SUB, window), 1)
+            spot = lax.broadcasted_iota(jnp.int32, (SUB, window), 1)
             local = meta[rows, 0:1] - (r * SUB - HALO)
             found = jnp.zeros((SUB, window), jnp.int32)
             whole = jnp.zeros((SUB, 1), jnp.int32)
             for k in range(BAND):
                 weight = meta[rows, 1 + k : 2 + k]
-                found = found + jnp.where(place == local + k, weight, 0)
+                found = found + jnp.where(spot == local + k, weight, 0)
                 whole = whole + weight
             mix[rows, :] = found.astype(f32).astype(bf16)
             share[rows, :] = jnp.broadcast_to(whole.astype(f32), (SUB, 128))
@@ -233,15 +246,15 @@
         value = jnp.dot(mix[rows, :], seen, preferred_element_type=f32)
         value = value / share[rows, 0:1]
         pooled[rows, :] = value
-        live = lax.broadcasted_iota(jnp.int32, value.shape, 0) < counts[r]
+        live = lax.broadcasted_iota(jnp.int32, value.shape, 0) < counts[0, r]
         total = total + jnp.sum(jnp.where(live, value, 0.0), axis=0, keepdims=True)
-        alive = alive + counts[r]
+        alive = alive + counts[0, r]
     mean = total / alive.astype(f32)
     square = jnp.zeros_like(total)
     for r in range(SIDE):
         rows = slice(r * SUB, (r + 1) * SUB)
         value = pooled[rows, :]
-        live = lax.broadcasted_iota(jnp.int32, value.shape, 0) < counts[r]
+        live = lax.broadcasted_iota(jnp.int32, value.shape, 0) < counts[0, r]
         dev = jnp.where(live, value - mean, 0.0)
         small = dev.astype(bf16)
         full[rows, :] = small
@@ -252,11 +265,11 @@
     lane = lax.broadcasted_iota(jnp.int32, total.shape, 1)
     row = jnp.zeros(total.shape, jnp.int32)
     for r in range(SIDE):
-        row = row + jnp.where(lane == r, counts[r], 0)
+        row = row + jnp.where(lane == r, counts[0, r], 0)
     stats[3:4, :] = row.astype(f32)
 
 
-def pool(counts, before, teacher, behind, meta):
+def pool(place, counts, before, teacher, behind, starts, weights):
     rows, columns = teacher.shape
     tile = 256
     return pl.pallas_call(
@@ -264,10 +277,12 @@
         grid=(columns // tile,),
         in_specs=[
             smem(),
+            smem(),
             pl.BlockSpec((HALO, tile), lambda j: (0, j)),
             pl.BlockSpec((rows, tile), lambda j: (0, j)),
             pl.BlockSpec((HALO, tile), lambda j: (0, j)),
-            pl.BlockSpec(meta.shape, lambda j: (0, 0)),
+            pl.BlockSpec(starts.shape, lambda j: (0, 0)),
+            pl.BlockSpec(weights.shape, lambda j: (0, 0)),
         ],
         out_specs=[
             pl.BlockSpec((rows, tile), lambda j: (0, j)),
@@ -281,12 +296,14 @@
             pltpu.VMEM((rows, SUB + 2 * HALO), bf16),
             pltpu.VMEM((rows, 128), f32),
             pltpu.VMEM((rows, tile), f32),
+            pltpu.VMEM((128, rows), f32),
+            pltpu.VMEM((rows, 128), jnp.int32),
         ],
         compiler_params=pltpu.CompilerParams(vmem_limit_bytes=32 * 2**20),
         cost_estimate=pl.CostEstimate(
             flops=2 * rows * 256 * columns, bytes_accessed=6 * rows * columns, transcendentals=0
         ),
-    )(counts, before, teacher, behind, meta)
+    )(place, counts, before, teacher, behind, starts, weights)
 
 
 def with_ones(a):
@@ -327,7 +344,7 @@
             out_specs=pl.BlockSpec((part, columns), lambda i, place: (i, 0)),
         ),
         out_shape=jax.ShapeDtypeStruct((rows, columns), f32),
-        compiler_params=pltpu.CompilerParams(vmem_limit_bytes=40 * 2**20),
+        compiler_params=pltpu.CompilerParams(vmem_limit_bytes=60 * 2**20),
         cost_estimate=pl.CostEstimate(
             flops=2 * rows * 3 * near_depth * columns,
             bytes_accessed=6 * rows * depth + 6 * length * columns + 4 * rows * columns,
@@ -358,21 +375,19 @@
     return results
 
 
-def open_kernel(place, *refs):
-    up, down, kept = refs[15:]
-    i = pl.program_id(0)
-    half = up.shape[1]
+def far_kernel(place, *refs):
+    up, down = refs[15:]
     results = last_sums(place, refs)
-
-    @pl.when(i == 0)
-    def _():
-        up[...] = results[0].astype(bf16)
-        down[...] = results[1].astype(bf16)
-
-    @pl.when(i == 1)
-    def _():
-        kept[:, :half] = results[0]
-        kept[:, half:] = results[1]
+    up[...] = results[0].astype(bf16)
+    down[...] = results[1].astype(bf16)
+
+
+def own_kernel(place, *refs):
+    kept = refs[15]
+    half = kept.shape[1] // 2
+    results = last_sums(place, refs)
+    kept[:, :half] = results[0]
+    kept[:, half:] = results[1]
 
 
 def close_kernel(place, *refs):
@@ -392,11 +407,15 @@
         down[:, half:] = (results[1] + from_next[...].astype(f32)).astype(bf16)
 
 
-def last_product(place, k, left, far_left, near, own, mate, arrived=None):
+def last_product(place, k, kind, left, far_left, near, own, mate, arrived=()):
     depth = left[0].shape[1]
     part = left[0].shape[0] // SIDE
     half = own[0].shape[1] // 2
-    start = 0 if arrived is None else 2
+    kernel, start, far_start, steps = {
+        "far": (far_kernel, 0, 0, 1),
+        "own": (own_kernel, 1, 1, 1),
+        "close": (close_kernel, 2, 0, 2),
+    }[kind]
     one = lambda i, place: (0, 0)
     tail = 256
     side = (
@@ -406,34 +425,33 @@
     )
     in_specs = (
         [pl.BlockSpec((part, tail), lambda i, place: (start + i, depth // tail - 1))] * 3
-        + [pl.BlockSpec((part, depth), lambda i, place: (i, 0))]
+        + [pl.BlockSpec((part, depth), lambda i, place: (far_start + i, 0))]
         + [pl.BlockSpec((part, 1), lambda i, place: (start + i, 0))]
         + side * 2
+        + [pl.BlockSpec((part, half), one)] * len(arrived)
     )
     S = jax.ShapeDtypeStruct
-    if arrived is None:
-        kernel, extra = open_kernel, ()
-        shapes = [S((part, half), bf16), S((part, half), bf16), S((part, 2 * half), f32)]
-    else:
-        kernel, extra = close_kernel, arrived
-        in_specs = in_specs + [pl.BlockSpec((part, half), one)] * 2
-        shapes = [S((part, 2 * half), bf16), S((part, 2 * half), bf16)]
+    shapes = {
+        "far": [S((part, half), bf16)] * 2,
+        "own": [S((part, 2 * half), f32)],
+        "close": [S((part, 2 * half), bf16)] * 2,
+    }[kind]
     return pl.pallas_call(
         kernel,
         grid_spec=pltpu.PrefetchScalarGridSpec(
             num_scalar_prefetch=1,
-            grid=(2,),
+            grid=(steps,),
             in_specs=in_specs,
             out_specs=[pl.BlockSpec(s.shape, one) for s in shapes],
         ),
         out_shape=shapes,
-        compiler_params=pltpu.CompilerParams(vmem_limit_bytes=40 * 2**20),
-        cost_estimate=pl.CostEstimate(
-            flops=2 * 2 * part * 2 * depth * 2 * half,
-            bytes_accessed=6 * depth * part + 5 * depth * half + 14 * part * half,
+        compiler_params=pltpu.CompilerParams(vmem_limit_bytes=60 * 2**20),
+        cost_estimate=pl.CostEstimate(
+            flops=2 * steps * part * 2 * depth * 2 * half,
+            bytes_accessed=3 * steps * depth * part + 5 * depth * half + 8 * part * half,
             transcendentals=0,
         ),
-    )(place, *left, far_left, near, *own, *mate, *extra)
+    )(place, *left, far_left, near, *own, *mate, *arrived)
 
 
 def final_kernel(place, kept, first, second, s_left, t_own, t_mate, *rest):
@@ -485,38 +503,32 @@
 
 def per_device(student, teacher, starts, weights, counts):
     y, x, z, c = (lax.axis_index(n) for n in ("y", "x", "row", "col"))
-    shard = y * SIDE + x
+    place = jnp.stack([z, c, y, x]).astype(jnp.int32)
     rows = starts.shape[0]
     columns = teacher.shape[1]
     half = columns // 2
     width = student.shape[1] // SIDE
-    part = width // SIDE
 
     up = [(i, (i + 1) % 16) for i in range(16)]
     down = [(j, i) for i, j in up]
     before = lax.ppermute(teacher[rows - HALO :], ("y", "x"), up)
     behind = lax.ppermute(teacher[:HALO], ("y", "x"), down)
 
-    own_count = lax.dynamic_slice_in_dim(counts[0], z, 1)
-    *packed, block = pack(jnp.stack([y, x, own_count[0]]).astype(jnp.int32), student)
+    *packed, block = pack(place, counts, student)
     packed, block, before, behind = lax.optimization_barrier((packed, block, before, behind))
     got = [packed[0], ring(packed[1], "x", 1), ring(packed[2], "x", -1), ring(packed[3], "x", 2)]
     blocks = ring_all(block, "row")
-    meta = jnp.concatenate([(starts - shard * rows)[:, None], weights], axis=1)
-    standard, stats = pool(counts[0], before, teacher, behind, meta)
-    z_counts = jnp.concatenate(
-        [lax.dynamic_slice_in_dim(counts[0], lax.rem(z + k, SIDE), 1) for k in COMING]
-    )
-    own_stats = shards(z_counts, stats, blocks)
-    got, own_stats, standard = lax.optimization_barrier((got, own_stats, standard))
-    near_stats = ring_all(own_stats, "x")
-    turned, mean = turn(own_count, got)
-    near_stats, turned, standard = lax.optimization_barrier((near_stats, turned, standard))
+    standard, stats = pool(place, counts, before, teacher, behind, starts[None], weights.T)
+    every = ring_all(shards(place, counts, stats, blocks), "y")
+    got, every, standard = lax.optimization_barrier((got, every, standard))
+    to = spread(every)
+    near = [to[0], ring(to[1], "x", 1), ring(to[2], "x", -1), ring(to[3], "x", 2)]
+    turned, mean = turn(place, counts, got)
 
     right, left = ring(standard, "x", 1), ring(standard, "x", -1)
     up, down = ring(turned, "row", 1), ring(turned, "row", -1)
     t_standard = swap(standard)
-    t_rows, s_left = settle(ring_all(gather_stats(near_stats), "y"))
+    t_rows, s_left = settle(near)
     t_mate = swap(t_rows)
     right, left, up, down, t_standard, t_rows, t_mate, s_left = lax.optimization_barrier(
         (right, left, up, down, t_standard, t_rows, t_mate, s_left)
@@ -525,7 +537,6 @@
     x_far = [ring(right[:, :half], "x", 1), ring(left[:, half:], "x", -1)]
     z_far = [ring(up[: width // 2], "row", 1), ring(down[width // 2 :], "row", -1)]
     t_right, t_left = swap(right), swap(left)
-    place = jnp.stack([z, c]).astype(jnp.int32)
     own, mate = [standard, right, left], [t_standard, t_right, t_left]
     near_z = [turned, up, down]
     own_sum = first_product(place, near_z, own, mean)
@@ -533,18 +544,21 @@
     x_far, z_far, own_sum, mate_sum = lax.optimization_barrier((x_far, z_far, own_sum, mate_sum))
 
     t_x_far = [swap(f) for f in x_far]
-    opened = []
+    sides = [
+        (own + [x_far[k], own_sum], mate + [t_x_far[k], mate_sum]) for k in range(2)
+    ]
+    arrived = []
     for k in range(2):
-        sides = (own + [x_far[k], own_sum], mate + [t_x_far[k], mate_sum])
-        opened.append((last_product(place, k, near_z, z_far[0], mean, *sides), sides))
-    arrived = [(ring(o[0], "y", 1), ring(o[1], "y", -1)) for o, _ in opened]
+        o = last_product(place, k, "far", near_z, z_far[0], mean, *sides[k])
+        arrived.append((ring(o[0], "y", 1), ring(o[1], "y", -1)))
+    passed = []
+    for k in range(2):
+        v = last_product(place, k, "close", near_z, z_far[1], mean, *sides[k], arrived[k])
+        passed.append((ring(v[0], "y", 1), ring(v[1], "y", -1)))
     out = None
     for k in range(2):
-        (_, _, kept), sides = opened[k]
-        v = last_product(place, k, near_z, z_far[1], mean, *sides, arrived[k])
-        out = final(
-            place, k, kept, ring(v[0], "y", 1), ring(v[1], "y", -1), s_left, t_rows, t_mate, out
-        )
+        kept = last_product(place, k, "own", near_z, z_far[0], mean, *sides[k])[0]
+        out = final(place, k, kept, *passed[k], s_left, t_rows, t_mate, out)
     return out[None, None]
 
 

time: 177 us -> 185 us (1.045)
  Pallas kernels: 49.3 us -> 70.7 us
  waiting for transfers between devices: 54.2 us -> 46.5 us
  other arithmetic: 3.85 us -> 0.08 us
  local copies, waits for them, and re-layouts: 16.7 us -> 13.8 us
    pallas_call x4 -> x6, Pallas kernels: 18.3 us -> 34.8 us  [last_product(): pl.pallas_call(kernel, grid_spec=pltpu.PrefetchScalarGridSpec(num_scalar_...]
    ppermute x28, waiting for transfers between devices: 52.4 us -> 44.3 us  [ring(): lax.ppermute(value, axis, [(i, (i + step) % SIDE) for i in range(SIDE)])]
    pallas_call x2, Pallas kernels: 16.5 us -> 22.2 us  [first_product(): pl.pallas_call(first_kernel, grid_spec=pltpu.PrefetchScalarGridSpec(num_s...]
    unnamed x46 -> x52, local copies, waits for them, and re-layouts: 11.3 us -> 7.92 us
    concatenate x2 -> x0, other arithmetic: 3.14 us -> none  [the longest x1 2.53 us: per_device(): jnp.concatenate([lax.dynamic_slice_in_dim(counts[0], lax.rem(z + k, SIDE)...]
    slice x2, local copies, waits for them, and re-layouts: 0.14 us -> 3 us  [per_device(): x_far = [ring(right[:, :half], 'x', 1), ring(left[:, half:], 'x', -1)]]
  transfers between devices with their start and end apart: 36 -> 36, of which waited for: 8 -> 9; matrix products, arithmetic and copies ran while one was open for 5% -> 3% of each run, Pallas kernels for 26% -> 37%
where the time goes in v5:
time: 185 us
  Pallas kernels  70.7 us (38%)
  starting transfers between devices  53.6 us (29%)
  waiting for transfers between devices  46.5 us (25%)
  local copies, waits for them, and re-layouts  13.8 us (7%)
    ppermute x28, starting transfers between devices, ring(): lax.ppermute(value, axis, [(i, (i + step) % SIDE) for i in range(SIDE)])  47 us
    ppermute x28, waiting for transfers between devices, ring(): lax.ppermute(value, axis, [(i, (i + step) % SIDE) for i in range(SIDE)])  44.3 us
    pallas_call x6, Pallas kernels, last_product(): pl.pallas_call(kernel, grid_spec=pltpu.PrefetchScalarGridSpec(num_scalar_...  34.8 us
    pallas_call x2, Pallas kernels, first_product(): pl.pallas_call(first_kernel, grid_spec=pltpu.PrefetchScalarGridSpec(num_s...  22.2 us
    unnamed x52, local copies, waits for them, and re-layouts  7.92 us
    pallas_call x2, Pallas kernels, final(): pl.pallas_call(final_kernel, grid_spec=pltpu.PrefetchScalarGridSpec(num_s...  5.35 us
    pallas_call x1, Pallas kernels, pool(): pl.pallas_call(pool_kernel, grid=(columns // tile,), in_specs=[smem(), sm...  4.76 us
    ppermute x1, starting transfers between devices, per_device(): behind = lax.ppermute(teacher[:HALO], ('y', 'x'), down)  3.78 us
  transfers between devices with their start and end apart: 36, of which 9 were waited for; matrix products, arithmetic and copies ran while one was open for 3% of the time, Pallas kernels for 37%

profile of v5, /device:TPU:0, one launch (start us, length us, event | category | flops | bytes accessed | tf_op | source)
XLA Modules:
  0.0 185.0 jit_solution(12421054237441410865)
XLA Ops:
  0.0 0.9 fusion
  0.9 1.6 collective-permute-start
  2.5 3.8 %collective-permute-start.1 = (bf16[16,1024]{1,0:T(8,128)(2,1)S(1)}, bf16[16,1024]{1,0:T(8,128)(2,1)S(1)}, u32[]{:S(2)}, u32[]{:S(2)}) collective-permute-start(bf16[16,1024]{1,0:T(8,128)(2,1)S(1)} %get-tuple-element.111), channel_id=1, source_target_pairs={{8,0},{16,8},{24,16},{32,24},{40,32},{48,40},{56,48},{64,56},{72,6... | collective-permute-start | bytes 98312 | tf_op jit(solution)/shard_map/ppermute | solution.py:515
  6.3 1.4 copy-done.6
  7.8 0.7 copy-done.10
  8.4 1.6 shard_map.55
  10.1 3.2 %collective-permute-start.3 = (bf16[192,1024]{1,0:T(8,128)(2,1)S(1)}, bf16[192,1024]{1,0:T(8,128)(2,1)S(1)}, u32[]{:S(2)}, u32[]{:S(2)}) collective-permute-start(bf16[192,1024]{1,0:T(8,128)(2,1)S(1)} %get-tuple-element.65), channel_id=1, source_target_pairs={{0,24},{8,0},{16,8},{24,16},{1,25},{9,1},{17,9},{25,17},{2,26},{10... | collective-permute-start | bytes 1179656 | tf_op jit(solution)/shard_map/ppermute | solution.py:20
  13.3 2.0 %collective-permute-start.5 = (f32[8,1024]{1,0:T(8,128)S(1)}, f32[8,1024]{1,0:T(8,128)S(1)}, u32[]{:S(2)}, u32[]{:S(2)}) collective-permute-start(f32[8,1024]{1,0:T(8,128)S(1)} %get-tuple-element.70.refs_0_), channel_id=1, source_target_pairs={{0,2},{2,4},{4,6},{6,0},{1,3},{3,5},{5,7},{7,1},{8,10},{10,12},{12... | collective-permute-start | bytes 98312 | tf_op jit(solution)/shard_map/ppermute | solution.py:20
  15.3 2.2 %collective-permute-start.6 = (f32[8,1024]{1,0:T(8,128)S(1)}, f32[8,1024]{1,0:T(8,128)S(1)}, u32[]{:S(2)}, u32[]{:S(2)}) collective-permute-start(f32[8,1024]{1,0:T(8,128)S(1)} %get-tuple-element.70.refs_0_), channel_id=1, source_target_pairs={{0,6},{2,0},{4,2},{6,4},{1,7},{3,1},{5,3},{7,5},{8,14},{10,8},{12,... | collective-permute-start | bytes 98312 | tf_op jit(solution)/shard_map/ppermute | solution.py:20
  17.5 1.8 collective-permute-done.5.refs_1_
  19.3 1.9 %collective-permute-start.7 = (f32[8,1024]{1,0:T(8,128)S(1)}, f32[8,1024]{1,0:T(8,128)S(1)}, u32[]{:S(2)}, u32[]{:S(2)}) collective-permute-start(f32[8,1024]{1,0:T(8,128)S(1)} %get-tuple-element.70.refs_0_), channel_id=1, source_target_pairs={{0,4},{2,6},{4,0},{6,2},{1,5},{3,7},{5,1},{7,3},{8,12},{10,14},{12... | collective-permute-start | bytes 98312 | tf_op jit(solution)/shard_map/ppermute | solution.py:20
  21.2 4.8 %shard_map.56 = (bf16[768,1024]{1,0:T(8,128)(2,1)S(1)}, f32[4,1024]{1,0:T(4,128)S(1)}) custom-call(s32[4]{0:T(128)S(1)} %pad_add_fusion.place, s32[1,4]{1,0:T(1,128)S(1)} %copy-done.11, bf16[16,1024]{1,0:T(8,128)(2,1)S(1)} %collective-permute-done.before, bf16[768,1024]{1,0:T(8,128)(2,1)S(1)} %copy-done.5, ...), custom_call_target="tpu_custom_call" | custom-call | flops 402653184 | bytes 4718592 | tf_op jit(solution)/shard_map/pallas_call | solution.py:275
  26.0 0.6 shard_map.57.e0
  26.6 2.3 %collective-permute-start.10 = (f32[12,1024]{1,0:T(8,128)S(1)}, f32[12,1024]{1,0:T(8,128)S(1)}, u32[]{:S(2)}, u32[]{:S(2)}) collective-permute-start(f32[12,1024]{1,0:T(8,128)S(1)} %shard_map.57.e0), channel_id=1, source_target_pairs={{0,64},{32,96},{64,0},{96,32},{1,65},{33,97},{65,1},{97,33},{2,66}... | collective-permute-start | bytes 147464 | tf_op jit(solution)/shard_map/ppermute | solution.py:20
  28.9 0.8 collective-permute-start.8
  29.7 2.7 %collective-permute-done.10.e3 = f32[12,1024]{1,0:T(8,128)S(1)} collective-permute-done((f32[12,1024]{1,0:T(8,128)S(1)}, f32[12,1024]{1,0:T(8,128)S(1)}, u32[]{:S(2)}, u32[]{:S(2)}) %collective-permute-start.10) | collective-permute-done | bytes 49184 | tf_op jit(solution)/shard_map/ppermute | solution.py:20
  32.5 2.6 %collective-permute-start.9 = (f32[12,1024]{1,0:T(8,128)S(1)}, f32[12,1024]{1,0:T(8,128)S(1)}, u32[]{:S(2)}, u32[]{:S(2)}) collective-permute-start(f32[12,1024]{1,0:T(8,128)S(1)} %shard_map.57.e0), channel_id=1, source_target_pairs={{0,96},{32,0},{64,32},{96,64},{1,97},{33,1},{65,33},{97,65},{2,98}... | collective-permute-start | bytes 147464 | tf_op jit(solution)/shard_map/ppermute | solution.py:20
  35.0 1.9 %collective-permute-done.9.e2 = f32[12,1024]{1,0:T(8,128)S(1)} collective-permute-done((f32[12,1024]{1,0:T(8,128)S(1)}, f32[12,1024]{1,0:T(8,128)S(1)}, u32[]{:S(2)}, u32[]{:S(2)}) %collective-permute-start.9) | collective-permute-done | bytes 49184 | tf_op jit(solution)/shard_map/ppermute | solution.py:20
  37.0 1.8 collective-permute-start.16
  38.8 1.5 collective-permute-start.17
  40.3 2.1 %collective-permute-start.18 = (f32[16,1024]{1,0:T(8,128)S(1)}, f32[16,1024]{1,0:T(8,128)S(1)}, u32[]{:S(2)}, u32[]{:S(2)}) collective-permute-start(f32[16,1024]{1,0:T(8,128)S(1)} %get-tuple-element.85), channel_id=1, source_target_pairs={{0,16},{8,24},{16,0},{24,8},{1,17},{9,25},{17,1},{25,9},{2,18},{10... | collective-permute-start | bytes 196616 | tf_op jit(solution)/shard_map/ppermute | solution.py:20
  42.4 0.1 collective-permute-done.16.n1
  42.6 0.5 collective-permute-done.17.n2
  43.1 3.0 %collective-permute-done.18.n3 = f32[16,1024]{1,0:T(8,128)S(1)} collective-permute-done((f32[16,1024]{1,0:T(8,128)S(1)}, f32[16,1024]{1,0:T(8,128)S(1)}, u32[]{:S(2)}, u32[]{:S(2)}) %collective-permute-start.18) | collective-permute-done | bytes 65568 | tf_op jit(solution)/shard_map/ppermute | solution.py:20
  46.1 0.3 shard_map.60
  46.5 1.2 shard_map.58
  47.6 0.9 collective-permute-start.13
  48.5 2.4 %collective-permute-start.14 = (bf16[1024,768]{1,0:T(8,128)(2,1)S(1)}, bf16[1024,768]{1,0:T(8,128)(2,1)S(1)}, u32[]{:S(2)}, u32[]{:S(2)}) collective-permute-start(bf16[1024,768]{1,0:T(8,128)(2,1)S(1)} %get-tuple-element.76.a0.refs_0_), channel_id=1, source_target_pairs={{0,6},{2,0},{4,2},{6,4},{1,7},{3,1},{5,3},{7,5},{8,14},{10,8},{12,... | collective-permute-start | bytes 4718600 | tf_op jit(solution)/shard_map/ppermute | solution.py:20
  51.0 0.5 collective-permute-start.11
  51.5 2.7 %collective-permute-start.12 = (bf16[768,1024]{1,0:T(8,128)(2,1)S(1)}, bf16[768,1024]{1,0:T(8,128)(2,1)}, u32[]{:S(2)}, u32[]{:S(2)}) collective-permute-start(bf16[768,1024]{1,0:T(8,128)(2,1)S(1)} %get-tuple-element.77.b0.refs_5_), channel_id=1, source_target_pairs={{0,24},{8,0},{16,8},{24,16},{1,25},{9,1},{17,9},{25,17},{2,26},{10... | collective-permute-start | bytes 4718600 | tf_op jit(solution)/shard_map/ppermute | solution.py:20
  54.2 31.5 %collective-permute-done.13.a1.refs_1_ = bf16[1024,768]{1,0:T(8,128)(2,1)S(1)} collective-permute-done((bf16[1024,768]{1,0:T(8,128)(2,1)S(1)}, bf16[1024,768]{1,0:T(8,128)(2,1)S(1)}, u32[]{:S(2)}, u32[]{:S(2)}) %collective-permute-start.13) | collective-permute-done | bytes 1572896 | tf_op jit(solution)/shard_map/ppermute | solution.py:20
  85.7 2.7 %collective-permute-done.11.b1.refs_6_ = bf16[768,1024]{1,0:T(8,128)(2,1)S(1)} collective-permute-done((bf16[768,1024]{1,0:T(8,128)(2,1)S(1)}, bf16[768,1024]{1,0:T(8,128)(2,1)S(1)}, u32[]{:S(2)}, u32[]{:S(2)}) %collective-permute-start.11) | collective-permute-done | bytes 1572896 | tf_op jit(solution)/shard_map/ppermute | solution.py:20
  88.4 1.2 copy-done.15
  89.6 0.5 collective-permute-start.25
  90.1 0.9 slice.20
  91.1 2.1 %slice.21 = bf16[768,512]{1,0:T(8,128)(2,1)} slice(bf16[768,1024]{1,0:T(8,128)(2,1)} %collective-permute-done.12.b2.refs_7_), slice={[0:768], [512:1024]} | slice | bytes 1572864 | tf_op jit(solution)/shard_map/slice | solution.py:537
  93.1 0.7 collective-permute-start.20
  93.8 2.6 %collective-permute-start.21 = (bf16[768,512]{1,0:T(8,128)(2,1)}, bf16[768,512]{1,0:T(8,128)(2,1)S(1)}, u32[]{:S(2)}, u32[]{:S(2)}) collective-permute-start(bf16[768,512]{1,0:T(8,128)(2,1)} %slice.21), channel_id=1, source_target_pairs={{0,24},{8,0},{16,8},{24,16},{1,25},{9,1},{17,9},{25,17},{2,26},{10... | collective-permute-start | bytes 2359304 | tf_op jit(solution)/shard_map/ppermute | solution.py:20
  96.4 1.0 slice.22
  97.4 1.0 slice.23
  98.4 3.3 %collective-permute-start.23 = (bf16[512,768]{1,0:T(8,128)(2,1)}, bf16[512,768]{1,0:T(8,128)(2,1)}, u32[]{:S(2)}, u32[]{:S(2)}) collective-permute-start(bf16[512,768]{1,0:T(8,128)(2,1)} %slice.23), channel_id=1, source_target_pairs={{0,6},{2,0},{4,2},{6,4},{1,7},{3,1},{5,3},{7,5},{8,14},{10,8},{12,... | collective-permute-start | bytes 2359304 | tf_op jit(solution)/shard_map/ppermute | solution.py:20
  101.7 11.1 %shard_map.61.refs_9_ = f32[1024,1024]{1,0:T(8,128)} custom-call(s32[4]{0:T(128)} %copy-done.7, bf16[1024,768]{1,0:T(8,128)(2,1)} %copy-done.1, bf16[1024,768]{1,0:T(8,128)(2,1)} %copy-done.12, bf16[1024,768]{1,0:T(8,128)(2,1)} %copy-done.13, bf16[768,1024]{1,0:T(8,128)(2,1)} %copy-done, bf16[768,1024]{1,0:T(8,128)(2,1)} %copy-done.14, ...), custom_call_target="tpu_custom_call" | custom-call | flops 4026531840 | bytes 13631488 | tf_op jit(solution)/shard_map/pallas_call | solution.py:336
  112.7 11.1 %shard_map.62.refs_14_ = f32[1024,1024]{1,0:T(8,128)} custom-call(s32[4]{0:T(128)} %copy-done.7, bf16[1024,768]{1,0:T(8,128)(2,1)} %copy-done.1, bf16[1024,768]{1,0:T(8,128)(2,1)} %copy-done.12, bf16[1024,768]{1,0:T(8,128)(2,1)} %copy-done.13, bf16[768,1024]{1,0:T(8,128)(2,1)} %copy-done.15, bf16[768,1024]{1,0:T(8,128)(2,1)} %copy-done.16, ...), custom_call_target="tpu_custom_call" | custom-call | flops 4026531840 | bytes 13631488 | tf_op jit(solution)/shard_map/pallas_call | solution.py:336
  124.0 0.5 collective-permute-start.26
  124.5 2.2 %collective-permute-done.31.refs_13_ = bf16[768,512]{1,0:T(8,128)(2,1)S(1)} collective-permute-done((bf16[768,512]{1,0:T(8,128)(2,1)}, bf16[768,512]{1,0:T(8,128)(2,1)S(1)}, u32[]{:S(2)}, u32[]{:S(2)}) %collective-permute-start.31) | collective-permute-done | bytes 786464 | tf_op jit(solution)/shard_map/ppermute | solution.py:28
  126.7 0.9 copy-done.20
  127.6 5.0 %shard_map.67 = (bf16[256,512]{1,0:T(8,128)(2,1)}, bf16[256,512]{1,0:T(8,128)(2,1)}) custom-call(s32[4]{0:T(128)} %copy-done.7, bf16[1024,768]{1,0:T(8,128)(2,1)} %copy-done.1, bf16[1024,768]{1,0:T(8,128)(2,1)} %copy-done.12, bf16[1024,768]{1,0:T(8,128)(2,1)} %copy-done.13, bf16[512,768]{1,0:T(8,128)(2,1)} %copy-done.17, f32[1024,1]{1,0:T(8,128)} %copy-done.2, ...), custom_call_target="tpu_custom_call" | custom-call | flops 805306368 | bytes 3604480 | tf_op jit(solution)/shard_map/pallas_call | solution.py:439
  132.5 1.0 collective-permute-start.32
  133.5 2.7 %collective-permute-start.33 = (bf16[256,512]{1,0:T(8,128)(2,1)}, bf16[256,512]{1,0:T(8,128)(2,1)S(1)}, u32[]{:S(2)}, u32[]{:S(2)}) collective-permute-start(bf16[256,512]{1,0:T(8,128)(2,1)} %get-tuple-element.108), channel_id=1, source_target_pairs={{0,96},{32,0},{64,32},{96,64},{1,97},{33,1},{65,33},{97,65},{2,98}... | collective-permute-start | bytes 786440 | tf_op jit(solution)/shard_map/ppermute | solution.py:20
  136.2 0.9 copy-done.19
  137.1 5.0 %shard_map.64 = (bf16[256,512]{1,0:T(8,128)(2,1)}, bf16[256,512]{1,0:T(8,128)(2,1)}) custom-call(s32[4]{0:T(128)} %copy-done.7, bf16[1024,768]{1,0:T(8,128)(2,1)} %copy-done.1, bf16[1024,768]{1,0:T(8,128)(2,1)} %copy-done.12, bf16[1024,768]{1,0:T(8,128)(2,1)} %copy-done.13, bf16[512,768]{1,0:T(8,128)(2,1)} %copy-done.17, f32[1024,1]{1,0:T(8,128)} %copy-done.2, ...), custom_call_target="tpu_custom_call" | custom-call | flops 805306368 | bytes 3604480 | tf_op jit(solution)/shard_map/pallas_call | solution.py:439
  142.1 3.2 %collective-permute-start.28 = (bf16[256,512]{1,0:T(8,128)(2,1)}, bf16[256,512]{1,0:T(8,128)(2,1)S(1)}, u32[]{:S(2)}, u32[]{:S(2)}) collective-permute-start(bf16[256,512]{1,0:T(8,128)(2,1)} %get-tuple-element.100), channel_id=1, source_target_pairs={{0,96},{32,0},{64,32},{96,64},{1,97},{33,1},{65,33},{97,65},{2,98}... | collective-permute-start | bytes 786440 | tf_op jit(solution)/shard_map/ppermute | solution.py:20
  145.3 0.7 copy-done.23
  146.0 0.7 copy-done.24
  146.7 7.0 %shard_map.68 = (bf16[256,1024]{1,0:T(8,128)(2,1)}, bf16[256,1024]{1,0:T(8,128)(2,1)}) custom-call(s32[4]{0:T(128)} %copy-done.7, bf16[1024,768]{1,0:T(8,128)(2,1)} %copy-done.1, bf16[1024,768]{1,0:T(8,128)(2,1)} %copy-done.12, bf16[1024,768]{1,0:T(8,128)(2,1)} %copy-done.13, bf16[512,768]{1,0:T(8,128)(2,1)} %collective-permute-done.23.refs_3_, ...), custom_call_target="tpu_custom_call" | custom-call | flops 1610612736 | bytes 4194304 | tf_op jit(solution)/shard_map/pallas_call | solution.py:439
  153.8 3.2 %collective-permute-start.35 = (bf16[256,1024]{1,0:T(8,128)(2,1)}, bf16[256,1024]{1,0:T(8,128)(2,1)S(1)}, u32[]{:S(2)}, u32[]{:S(2)}) collective-permute-start(bf16[256,1024]{1,0:T(8,128)(2,1)} %get-tuple-element.110), channel_id=1, source_target_pairs={{0,96},{32,0},{64,32},{96,64},{1,97},{33,1},{65,33},{97,65},{2,98}... | collective-permute-start | bytes 1572872 | tf_op jit(solution)/shard_map/ppermute | solution.py:20
  157.1 0.7 copy-done.21
  157.8 0.7 copy-done.22
  158.5 7.1 %shard_map.65 = (bf16[256,1024]{1,0:T(8,128)(2,1)}, bf16[256,1024]{1,0:T(8,128)(2,1)}) custom-call(s32[4]{0:T(128)} %copy-done.7, bf16[1024,768]{1,0:T(8,128)(2,1)} %copy-done.1, bf16[1024,768]{1,0:T(8,128)(2,1)} %copy-done.12, bf16[1024,768]{1,0:T(8,128)(2,1)} %copy-done.13, bf16[512,768]{1,0:T(8,128)(2,1)} %collective-permute-done.23.refs_3_, ...), custom_call_target="tpu_custom_call" | custom-call | flops 1610612736 | bytes 4194304 | tf_op jit(solution)/shard_map/pallas_call | solution.py:439
  165.7 3.2 %collective-permute-start.30 = (bf16[256,1024]{1,0:T(8,128)(2,1)}, bf16[256,1024]{1,0:T(8,128)(2,1)S(1)}, u32[]{:S(2)}, u32[]{:S(2)}) collective-permute-start(bf16[256,1024]{1,0:T(8,128)(2,1)} %get-tuple-element.102), channel_id=1, source_target_pairs={{0,96},{32,0},{64,32},{96,64},{1,97},{33,1},{65,33},{97,65},{2,98}... | collective-permute-start | bytes 1572872 | tf_op jit(solution)/shard_map/ppermute | solution.py:20
  168.9 5.3 %shard_map.66.kept = f32[256,1024]{1,0:T(8,128)} custom-call(s32[4]{0:T(128)} %copy-done.7, bf16[1024,768]{1,0:T(8,128)(2,1)} %copy-done.1, bf16[1024,768]{1,0:T(8,128)(2,1)} %copy-done.12, bf16[1024,768]{1,0:T(8,128)(2,1)} %copy-done.13, bf16[512,768]{1,0:T(8,128)(2,1)} %copy-done.17, f32[1024,1]{1,0:T(8,128)} %copy-done.2, bf16[768,1024]{1,0:T(8,128)(2,1)} %copy-done, ...), custom_call_target="tpu_custom_call" | custom-call | flops 805306368 | bytes 3604480 | tf_op jit(solution)/shard_map/pallas_call | solution.py:439
  174.2 5.4 %shard_map.63.kept = f32[256,1024]{1,0:T(8,128)} custom-call(s32[4]{0:T(128)} %copy-done.7, bf16[1024,768]{1,0:T(8,128)(2,1)} %copy-done.1, bf16[1024,768]{1,0:T(8,128)(2,1)} %copy-done.12, bf16[1024,768]{1,0:T(8,128)(2,1)} %copy-done.13, bf16[512,768]{1,0:T(8,128)(2,1)} %copy-done.17, f32[1024,1]{1,0:T(8,128)} %copy-done.2, bf16[768,1024]{1,0:T(8,128)(2,1)} %copy-done, ...), custom_call_target="tpu_custom_call" | custom-call | flops 805306368 | bytes 3604480 | tf_op jit(solution)/shard_map/pallas_call | solution.py:439
  179.6 2.7 %shard_map.69.rest_0_ = f32[256,2048]{1,0:T(8,128)} custom-call(s32[4]{0:T(128)S(1)} %copy-done.8, f32[256,1024]{1,0:T(8,128)S(1)} %copy-done.3, bf16[256,1024]{1,0:T(8,128)(2,1)S(1)} %collective-permute-done.34.first, bf16[256,1024]{1,0:T(8,128)(2,1)S(1)} %collective-permute-done.35.second, f32[256,128]{1,0:T(8,128)S(1)} %get-tuple-element.103.s_left, ...), custom_call_target="tpu_custom_call" | custom-call | flops 1572864 | bytes 3145728 | tf_op jit(solution)/shard_map/pallas_call | solution.py:485
  182.3 2.7 %shard_map.70 = f32[256,2048]{1,0:T(8,128)} custom-call(s32[4]{0:T(128)S(1)} %copy-done.8, f32[256,1024]{1,0:T(8,128)S(1)} %copy-done.4, bf16[256,1024]{1,0:T(8,128)(2,1)S(1)} %collective-permute-done.29.first, bf16[256,1024]{1,0:T(8,128)(2,1)S(1)} %collective-permute-done.30.second, ...), custom_call_target="tpu_custom_call", output_to_operand_aliasing={{}: (7, {})} | custom-call | flops 1572864 | bytes 3145728 | tf_op jit(solution)/shard_map/pallas_call | solution.py:485
  (83 shorter events, 0.7 us)
Async XLA Ops:
  0.0 21.2 %copy-start.5 = (bf16[768,1024]{1,0:T(8,128)(2,1)S(1)}, bf16[768,1024]{1,0:T(8,128)(2,1)}, u32[]{:S(2)}) copy-start(bf16[768,1024]{1,0:T(8,128)(2,1)} %teacher.1) | copy-start | bytes 4718596
  0.9 9.1 %collective-permute-start = (bf16[16,1024]{1,0:T(8,128)(2,1)S(1)}, bf16[16,1024]{1,0:T(8,128)(2,1)S(1)}, u32[]{:S(2)}, u32[]{:S(2)}) collective-permute-start(bf16[16,1024]{1,0:T(8,128)(2,1)S(1)} %get-tuple-element.112), channel_id=1, source_target_pairs={{0,8},{8,16},{16,24},{24,32},{32,40},{40,48},{48,56},{56,64},{64,7... | collective-permute-start | bytes 98312 | tf_op jit(solution)/shard_map/ppermute | solution.py:514
  2.5 7.5 %collective-permute-start.1 = (bf16[16,1024]{1,0:T(8,128)(2,1)S(1)}, bf16[16,1024]{1,0:T(8,128)(2,1)S(1)}, u32[]{:S(2)}, u32[]{:S(2)}) collective-permute-start(bf16[16,1024]{1,0:T(8,128)(2,1)S(1)} %get-tuple-element.111), channel_id=1, source_target_pairs={{8,0},{16,8},{24,16},{32,24},{40,32},{48,40},{56,48},{64,56},{72,6... | collective-permute-start | bytes 98312 | tf_op jit(solution)/shard_map/ppermute | solution.py:515
  6.3 1.4 copy-start.6
  7.7 0.7 copy-start.10
  8.4 38.0 %copy-start.7 = (s32[4]{0:T(128)}, s32[4]{0:T(128)S(1)}, u32[]{:S(2)}) copy-start(s32[4]{0:T(128)S(1)} %pad_add_fusion.place) | copy-start | bytes 52
  8.4 6.9 %copy-start.25 = (s32[768]{0:T(1024)S(1)}, s32[768]{0:T(1024)}, u32[]{:S(2)}) copy-start(s32[768]{0:T(1024)} %param.7) | copy-start | bytes 9220
  8.4 12.8 %copy-start.9 = (s32[768,4]{0,1:T(4,128)S(1)}, s32[768,4]{0,1:T(4,128)}, u32[]{:S(2)}) copy-start(s32[768,4]{0,1:T(4,128)} %param.8) | copy-start | bytes 36868
  8.4 12.8 %copy-start.11 = (s32[1,4]{1,0:T(1,128)S(1)}, s32[1,4]{1,0:T(1,128)}, u32[]{:S(2)}) copy-start(s32[1,4]{1,0:T(1,128)} %counts.7) | copy-start | bytes 52
  10.0 26.9 %collective-permute-start.2 = (bf16[192,1024]{1,0:T(8,128)(2,1)S(1)}, bf16[192,1024]{1,0:T(8,128)(2,1)S(1)}, u32[]{:S(2)}, u32[]{:S(2)}) collective-permute-start(bf16[192,1024]{1,0:T(8,128)(2,1)S(1)} %get-tuple-element.64), channel_id=1, source_target_pairs={{0,8},{8,16},{16,24},{24,0},{1,9},{9,17},{17,25},{25,1},{2,10},{10... | collective-permute-start | bytes 1179656 | tf_op jit(solution)/shard_map/ppermute | solution.py:20
  10.1 26.8 %collective-permute-start.3 = (bf16[192,1024]{1,0:T(8,128)(2,1)S(1)}, bf16[192,1024]{1,0:T(8,128)(2,1)S(1)}, u32[]{:S(2)}, u32[]{:S(2)}) collective-permute-start(bf16[192,1024]{1,0:T(8,128)(2,1)S(1)} %get-tuple-element.65), channel_id=1, source_target_pairs={{0,24},{8,0},{16,8},{24,16},{1,25},{9,1},{17,9},{25,17},{2,26},{10... | collective-permute-start | bytes 1179656 | tf_op jit(solution)/shard_map/ppermute | solution.py:20
  13.3 23.6 %collective-permute-start.4 = (bf16[192,1024]{1,0:T(8,128)(2,1)S(1)}, bf16[192,1024]{1,0:T(8,128)(2,1)S(1)}, u32[]{:S(2)}, u32[]{:S(2)}) collective-permute-start(bf16[192,1024]{1,0:T(8,128)(2,1)S(1)} %get-tuple-element.66), channel_id=1, source_target_pairs={{0,16},{8,24},{16,0},{24,8},{1,17},{9,25},{17,1},{25,9},{2,18},{10... | collective-permute-start | bytes 1179656 | tf_op jit(solution)/shard_map/ppermute | solution.py:20
  13.3 6.0 %collective-permute-start.5 = (f32[8,1024]{1,0:T(8,128)S(1)}, f32[8,1024]{1,0:T(8,128)S(1)}, u32[]{:S(2)}, u32[]{:S(2)}) collective-permute-start(f32[8,1024]{1,0:T(8,128)S(1)} %get-tuple-element.70.refs_0_), channel_id=1, source_target_pairs={{0,2},{2,4},{4,6},{6,0},{1,3},{3,5},{5,7},{7,1},{8,10},{10,12},{12... | collective-permute-start | bytes 98312 | tf_op jit(solution)/shard_map/ppermute | solution.py:20
  15.3 10.7 %collective-permute-start.6 = (f32[8,1024]{1,0:T(8,128)S(1)}, f32[8,1024]{1,0:T(8,128)S(1)}, u32[]{:S(2)}, u32[]{:S(2)}) collective-permute-start(f32[8,1024]{1,0:T(8,128)S(1)} %get-tuple-element.70.refs_0_), channel_id=1, source_target_pairs={{0,6},{2,0},{4,2},{6,4},{1,7},{3,1},{5,3},{7,5},{8,14},{10,8},{12,... | collective-permute-start | bytes 98312 | tf_op jit(solution)/shard_map/ppermute | solution.py:20
  19.3 6.7 %collective-permute-start.7 = (f32[8,1024]{1,0:T(8,128)S(1)}, f32[8,1024]{1,0:T(8,128)S(1)}, u32[]{:S(2)}, u32[]{:S(2)}) collective-permute-start(f32[8,1024]{1,0:T(8,128)S(1)} %get-tuple-element.70.refs_0_), channel_id=1, source_target_pairs={{0,4},{2,6},{4,0},{6,2},{1,5},{3,7},{5,1},{7,3},{8,12},{10,14},{12... | collective-permute-start | bytes 98312 | tf_op jit(solution)/shard_map/ppermute | solution.py:20
  26.0 28.2 %copy-start = (bf16[768,1024]{1,0:T(8,128)(2,1)}, bf16[768,1024]{1,0:T(8,128)(2,1)S(1)}, u32[]{:S(2)}) copy-start(bf16[768,1024]{1,0:T(8,128)(2,1)S(1)} %get-tuple-element.77.b0.refs_5_) | copy-start | bytes 4718596
  26.6 5.8 %collective-permute-start.10 = (f32[12,1024]{1,0:T(8,128)S(1)}, f32[12,1024]{1,0:T(8,128)S(1)}, u32[]{:S(2)}, u32[]{:S(2)}) collective-permute-start(f32[12,1024]{1,0:T(8,128)S(1)} %shard_map.57.e0), channel_id=1, source_target_pairs={{0,64},{32,96},{64,0},{96,32},{1,65},{33,97},{65,1},{97,33},{2,66}... | collective-permute-start | bytes 147464 | tf_op jit(solution)/shard_map/ppermute | solution.py:20
  28.9 6.1 %collective-permute-start.8 = (f32[12,1024]{1,0:T(8,128)S(1)}, f32[12,1024]{1,0:T(8,128)S(1)}, u32[]{:S(2)}, u32[]{:S(2)}) collective-permute-start(f32[12,1024]{1,0:T(8,128)S(1)} %shard_map.57.e0), channel_id=1, source_target_pairs={{0,32},{32,64},{64,96},{96,0},{1,33},{33,65},{65,97},{97,1},{2,34}... | collective-permute-start | bytes 147464 | tf_op jit(solution)/shard_map/ppermute | solution.py:20
  32.5 4.5 %collective-permute-start.9 = (f32[12,1024]{1,0:T(8,128)S(1)}, f32[12,1024]{1,0:T(8,128)S(1)}, u32[]{:S(2)}, u32[]{:S(2)}) collective-permute-start(f32[12,1024]{1,0:T(8,128)S(1)} %shard_map.57.e0), channel_id=1, source_target_pairs={{0,96},{32,0},{64,32},{96,64},{1,97},{33,1},{65,33},{97,65},{2,98}... | collective-permute-start | bytes 147464 | tf_op jit(solution)/shard_map/ppermute | solution.py:20
  37.0 5.5 %collective-permute-start.16 = (f32[16,1024]{1,0:T(8,128)S(1)}, f32[16,1024]{1,0:T(8,128)S(1)}, u32[]{:S(2)}, u32[]{:S(2)}) collective-permute-start(f32[16,1024]{1,0:T(8,128)S(1)} %get-tuple-element.83), channel_id=1, source_target_pairs={{0,8},{8,16},{16,24},{24,0},{1,9},{9,17},{17,25},{25,1},{2,10},{10... | collective-permute-start | bytes 196616 | tf_op jit(solution)/shard_map/ppermute | solution.py:20
  38.8 4.3 %collective-permute-start.17 = (f32[16,1024]{1,0:T(8,128)S(1)}, f32[16,1024]{1,0:T(8,128)S(1)}, u32[]{:S(2)}, u32[]{:S(2)}) collective-permute-start(f32[16,1024]{1,0:T(8,128)S(1)} %get-tuple-element.84), channel_id=1, source_target_pairs={{0,24},{8,0},{16,8},{24,16},{1,25},{9,1},{17,9},{25,17},{2,26},{10... | collective-permute-start | bytes 196616 | tf_op jit(solution)/shard_map/ppermute | solution.py:20
  40.3 5.8 %collective-permute-start.18 = (f32[16,1024]{1,0:T(8,128)S(1)}, f32[16,1024]{1,0:T(8,128)S(1)}, u32[]{:S(2)}, u32[]{:S(2)}) collective-permute-start(f32[16,1024]{1,0:T(8,128)S(1)} %get-tuple-element.85), channel_id=1, source_target_pairs={{0,16},{8,24},{16,0},{24,8},{1,17},{9,25},{17,1},{25,9},{2,18},{10... | collective-permute-start | bytes 196616 | tf_op jit(solution)/shard_map/ppermute | solution.py:20
  46.4 7.8 %collective-permute-start.19 = (f32[17,1024]{1,0:T(8,128)S(1)}, f32[17,1024]{1,0:T(8,128)S(1)}, u32[]{:S(2)}, u32[]{:S(2)}) collective-permute-start(f32[17,1024]{1,0:T(8,128)S(1)} %get-tuple-element.104.t_own), channel_id=1, source_target_pairs={{0,1},{1,0},{2,3},{3,2},{4,5},{5,4},{6,7},{7,6},{8,9},{9,8},{10,11... | collective-permute-start | bytes 208904 | tf_op jit(solution)/shard_map/ppermute | solution.py:28
  47.6 45.5 %copy-start.1 = (bf16[1024,768]{1,0:T(8,128)(2,1)}, bf16[1024,768]{1,0:T(8,128)(2,1)S(1)}, u32[]{:S(2)}) copy-start(bf16[1024,768]{1,0:T(8,128)(2,1)S(1)} %get-tuple-element.76.a0.refs_0_) | copy-start | bytes 4718596
  47.6 45.5 %copy-start.2 = (f32[1024,1]{1,0:T(8,128)}, f32[1024,1]{1,0:T(8,128)S(1)}, u32[]{:S(2)}) copy-start(f32[1024,1]{1,0:T(8,128)S(1)} %get-tuple-element.92.near.refs_4_) | copy-start | bytes 12292
  47.6 38.1 %collective-permute-start.13 = (bf16[1024,768]{1,0:T(8,128)(2,1)S(1)}, bf16[1024,768]{1,0:T(8,128)(2,1)S(1)}, u32[]{:S(2)}, u32[]{:S(2)}) collective-permute-start(bf16[1024,768]{1,0:T(8,128)(2,1)S(1)} %get-tuple-element.76.a0.refs_0_), channel_id=1, source_target_pairs={{0,2},{2,4},{4,6},{6,0},{1,3},{3,5},{5,7},{7,1},{8,10},{10,12},{12... | collective-permute-start | bytes 4718600 | tf_op jit(solution)/shard_map/ppermute | solution.py:20
  48.5 37.2 %collective-permute-start.14 = (bf16[1024,768]{1,0:T(8,128)(2,1)S(1)}, bf16[1024,768]{1,0:T(8,128)(2,1)S(1)}, u32[]{:S(2)}, u32[]{:S(2)}) collective-permute-start(bf16[1024,768]{1,0:T(8,128)(2,1)S(1)} %get-tuple-element.76.a0.refs_0_), channel_id=1, source_target_pairs={{0,6},{2,0},{4,2},{6,4},{1,7},{3,1},{5,3},{7,5},{8,14},{10,8},{12,... | collective-permute-start | bytes 4718600 | tf_op jit(solution)/shard_map/ppermute | solution.py:20
  51.0 37.4 %collective-permute-start.11 = (bf16[768,1024]{1,0:T(8,128)(2,1)S(1)}, bf16[768,1024]{1,0:T(8,128)(2,1)S(1)}, u32[]{:S(2)}, u32[]{:S(2)}) collective-permute-start(bf16[768,1024]{1,0:T(8,128)(2,1)S(1)} %get-tuple-element.77.b0.refs_5_), channel_id=1, source_target_pairs={{0,8},{8,16},{16,24},{24,0},{1,9},{9,17},{17,25},{25,1},{2,10},{10... | collective-permute-start | bytes 4718600 | tf_op jit(solution)/shard_map/ppermute | solution.py:20
  51.5 36.9 %collective-permute-start.12 = (bf16[768,1024]{1,0:T(8,128)(2,1)S(1)}, bf16[768,1024]{1,0:T(8,128)(2,1)}, u32[]{:S(2)}, u32[]{:S(2)}) collective-permute-start(bf16[768,1024]{1,0:T(8,128)(2,1)S(1)} %get-tuple-element.77.b0.refs_5_), channel_id=1, source_target_pairs={{0,24},{8,0},{16,8},{24,16},{1,25},{9,1},{17,9},{25,17},{2,26},{10... | collective-permute-start | bytes 4718600 | tf_op jit(solution)/shard_map/ppermute | solution.py:20
  54.2 34.2 %collective-permute-start.15 = (bf16[768,1024]{1,0:T(8,128)(2,1)S(1)}, bf16[768,1024]{1,0:T(8,128)(2,1)S(1)}, u32[]{:S(2)}, u32[]{:S(2)}) collective-permute-start(bf16[768,1024]{1,0:T(8,128)(2,1)S(1)} %get-tuple-element.77.b0.refs_5_), channel_id=1, source_target_pairs={{0,1},{1,0},{2,3},{3,2},{4,5},{5,4},{6,7},{7,6},{8,9},{9,8},{10,11... | collective-permute-start | bytes 4718600 | tf_op jit(solution)/shard_map/ppermute | solution.py:28
  85.7 10.7 %copy-start.12 = (bf16[1024,768]{1,0:T(8,128)(2,1)}, bf16[1024,768]{1,0:T(8,128)(2,1)S(1)}, u32[]{:S(2)}) copy-start(bf16[1024,768]{1,0:T(8,128)(2,1)S(1)} %collective-permute-done.13.a1.refs_1_) | copy-start | bytes 4718596
  85.7 11.7 %copy-start.13 = (bf16[1024,768]{1,0:T(8,128)(2,1)}, bf16[1024,768]{1,0:T(8,128)(2,1)S(1)}, u32[]{:S(2)}) copy-start(bf16[1024,768]{1,0:T(8,128)(2,1)S(1)} %collective-permute-done.14.a2.refs_2_) | copy-start | bytes 4718596
  88.4 10.0 %copy-start.14 = (bf16[768,1024]{1,0:T(8,128)(2,1)}, bf16[768,1024]{1,0:T(8,128)(2,1)S(1)}, u32[]{:S(2)}) copy-start(bf16[768,1024]{1,0:T(8,128)(2,1)S(1)} %collective-permute-done.11.b1.refs_6_) | copy-start | bytes 4718596
  88.4 1.2 copy-start.15
  89.6 8.7 %collective-permute-start.24 = (bf16[768,1024]{1,0:T(8,128)(2,1)S(1)}, bf16[768,1024]{1,0:T(8,128)(2,1)S(1)}, u32[]{:S(2)}, u32[]{:S(2)}) collective-permute-start(bf16[768,1024]{1,0:T(8,128)(2,1)S(1)} %collective-permute-done.11.b1.refs_6_), channel_id=1, source_target_pairs={{0,1},{1,0},{2,3},{3,2},{4,5},{5,4},{6,7},{7,6},{8,9},{9,8},{10,11... | collective-permute-start | bytes 4718600 | tf_op jit(solution)/shard_map/ppermute | solution.py:28
  89.6 23.1 %collective-permute-start.25 = (bf16[768,1024]{1,0:T(8,128)(2,1)}, bf16[768,1024]{1,0:T(8,128)(2,1)}, u32[]{:S(2)}, u32[]{:S(2)}) collective-permute-start(bf16[768,1024]{1,0:T(8,128)(2,1)} %collective-permute-done.12.b2.refs_7_), channel_id=1, source_target_pairs={{0,1},{1,0},{2,3},{3,2},{4,5},{5,4},{6,7},{7,6},{8,9},{9,8},{10,11... | collective-permute-start | bytes 4718600 | tf_op jit(solution)/shard_map/ppermute | solution.py:28
  93.1 30.7 %collective-permute-start.20 = (bf16[768,512]{1,0:T(8,128)(2,1)}, bf16[768,512]{1,0:T(8,128)(2,1)}, u32[]{:S(2)}, u32[]{:S(2)}) collective-permute-start(bf16[768,512]{1,0:T(8,128)(2,1)} %slice.20), channel_id=1, source_target_pairs={{0,8},{8,16},{16,24},{24,0},{1,9},{9,17},{17,25},{25,1},{2,10},{10... | collective-permute-start | bytes 2359304 | tf_op jit(solution)/shard_map/ppermute | solution.py:20
  93.8 30.1 %collective-permute-start.21 = (bf16[768,512]{1,0:T(8,128)(2,1)}, bf16[768,512]{1,0:T(8,128)(2,1)S(1)}, u32[]{:S(2)}, u32[]{:S(2)}) collective-permute-start(bf16[768,512]{1,0:T(8,128)(2,1)} %slice.21), channel_id=1, source_target_pairs={{0,24},{8,0},{16,8},{24,16},{1,25},{9,1},{17,9},{25,17},{2,26},{10... | collective-permute-start | bytes 2359304 | tf_op jit(solution)/shard_map/ppermute | solution.py:20
  97.4 26.5 %collective-permute-start.22 = (bf16[512,768]{1,0:T(8,128)(2,1)}, bf16[512,768]{1,0:T(8,128)(2,1)S(1)}, u32[]{:S(2)}, u32[]{:S(2)}) collective-permute-start(bf16[512,768]{1,0:T(8,128)(2,1)} %slice.22), channel_id=1, source_target_pairs={{0,2},{2,4},{4,6},{6,0},{1,3},{3,5},{5,7},{7,1},{8,10},{10,12},{12... | collective-permute-start | bytes 2359304 | tf_op jit(solution)/shard_map/ppermute | solution.py:20
  98.4 14.4 %copy-start.16 = (bf16[768,1024]{1,0:T(8,128)(2,1)}, bf16[768,1024]{1,0:T(8,128)(2,1)S(1)}, u32[]{:S(2)}) copy-start(bf16[768,1024]{1,0:T(8,128)(2,1)S(1)} %collective-permute-done.24.b1.refs_11_) | copy-start | bytes 4718596
  98.4 25.5 %collective-permute-start.23 = (bf16[512,768]{1,0:T(8,128)(2,1)}, bf16[512,768]{1,0:T(8,128)(2,1)}, u32[]{:S(2)}, u32[]{:S(2)}) collective-permute-start(bf16[512,768]{1,0:T(8,128)(2,1)} %slice.23), channel_id=1, source_target_pairs={{0,6},{2,0},{4,2},{6,4},{1,7},{3,1},{5,3},{7,5},{8,14},{10,8},{12,... | collective-permute-start | bytes 2359304 | tf_op jit(solution)/shard_map/ppermute | solution.py:20
  123.9 8.6 %copy-start.18 = (bf16[768,512]{1,0:T(8,128)(2,1)}, bf16[768,512]{1,0:T(8,128)(2,1)S(1)}, u32[]{:S(2)}) copy-start(bf16[768,512]{1,0:T(8,128)(2,1)S(1)} %collective-permute-done.21.refs_8_) | copy-start | bytes 2359300
  123.9 2.8 %copy-start.17 = (bf16[512,768]{1,0:T(8,128)(2,1)}, bf16[512,768]{1,0:T(8,128)(2,1)S(1)}, u32[]{:S(2)}) copy-start(bf16[512,768]{1,0:T(8,128)(2,1)S(1)} %collective-permute-done.22.refs_3_) | copy-start | bytes 2359300
  123.9 2.8 %collective-permute-start.31 = (bf16[768,512]{1,0:T(8,128)(2,1)}, bf16[768,512]{1,0:T(8,128)(2,1)S(1)}, u32[]{:S(2)}, u32[]{:S(2)}) collective-permute-start(bf16[768,512]{1,0:T(8,128)(2,1)} %collective-permute-done.20.refs_8_), channel_id=1, source_target_pairs={{0,1},{1,0},{2,3},{3,2},{4,5},{5,4},{6,7},{7,6},{8,9},{9,8},{10,11... | collective-permute-start | bytes 2359304 | tf_op jit(solution)/shard_map/ppermute | solution.py:28
  124.0 12.2 %collective-permute-start.26 = (bf16[768,512]{1,0:T(8,128)(2,1)S(1)}, bf16[768,512]{1,0:T(8,128)(2,1)S(1)}, u32[]{:S(2)}, u32[]{:S(2)}) collective-permute-start(bf16[768,512]{1,0:T(8,128)(2,1)S(1)} %collective-permute-done.21.refs_8_), channel_id=1, source_target_pairs={{0,1},{1,0},{2,3},{3,2},{4,5},{5,4},{6,7},{7,6},{8,9},{9,8},{10,11... | collective-permute-start | bytes 2359304 | tf_op jit(solution)/shard_map/ppermute | solution.py:28
  126.7 0.9 copy-start.20
  132.5 12.8 %collective-permute-start.32 = (bf16[256,512]{1,0:T(8,128)(2,1)}, bf16[256,512]{1,0:T(8,128)(2,1)S(1)}, u32[]{:S(2)}, u32[]{:S(2)}) collective-permute-start(bf16[256,512]{1,0:T(8,128)(2,1)} %get-tuple-element.107), channel_id=1, source_target_pairs={{0,32},{32,64},{64,96},{96,0},{1,33},{33,65},{65,97},{97,1},{2,34}... | collective-permute-start | bytes 786440 | tf_op jit(solution)/shard_map/ppermute | solution.py:20
  133.5 11.8 %collective-permute-start.33 = (bf16[256,512]{1,0:T(8,128)(2,1)}, bf16[256,512]{1,0:T(8,128)(2,1)S(1)}, u32[]{:S(2)}, u32[]{:S(2)}) collective-permute-start(bf16[256,512]{1,0:T(8,128)(2,1)} %get-tuple-element.108), channel_id=1, source_target_pairs={{0,96},{32,0},{64,32},{96,64},{1,97},{33,1},{65,33},{97,65},{2,98}... | collective-permute-start | bytes 786440 | tf_op jit(solution)/shard_map/ppermute | solution.py:20
  136.2 0.9 copy-start.19
  142.1 15.0 %collective-permute-start.27 = (bf16[256,512]{1,0:T(8,128)(2,1)}, bf16[256,512]{1,0:T(8,128)(2,1)S(1)}, u32[]{:S(2)}, u32[]{:S(2)}) collective-permute-start(bf16[256,512]{1,0:T(8,128)(2,1)} %get-tuple-element.99), channel_id=1, source_target_pairs={{0,32},{32,64},{64,96},{96,0},{1,33},{33,65},{65,97},{97,1},{2,34}... | collective-permute-start | bytes 786440 | tf_op jit(solution)/shard_map/ppermute | solution.py:20
  142.1 15.0 %collective-permute-start.28 = (bf16[256,512]{1,0:T(8,128)(2,1)}, bf16[256,512]{1,0:T(8,128)(2,1)S(1)}, u32[]{:S(2)}, u32[]{:S(2)}) collective-permute-start(bf16[256,512]{1,0:T(8,128)(2,1)} %get-tuple-element.100), channel_id=1, source_target_pairs={{0,96},{32,0},{64,32},{96,64},{1,97},{33,1},{65,33},{97,65},{2,98}... | collective-permute-start | bytes 786440 | tf_op jit(solution)/shard_map/ppermute | solution.py:20
  145.3 0.7 copy-start.23
  146.0 0.7 copy-start.24
  153.7 25.8 %collective-permute-start.34 = (bf16[256,1024]{1,0:T(8,128)(2,1)}, bf16[256,1024]{1,0:T(8,128)(2,1)S(1)}, u32[]{:S(2)}, u32[]{:S(2)}) collective-permute-start(bf16[256,1024]{1,0:T(8,128)(2,1)} %get-tuple-element.109), channel_id=1, source_target_pairs={{0,32},{32,64},{64,96},{96,0},{1,33},{33,65},{65,97},{97,1},{2,34}... | collective-permute-start | bytes 1572872 | tf_op jit(solution)/shard_map/ppermute | solution.py:20
  153.8 25.8 %collective-permute-start.35 = (bf16[256,1024]{1,0:T(8,128)(2,1)}, bf16[256,1024]{1,0:T(8,128)(2,1)S(1)}, u32[]{:S(2)}, u32[]{:S(2)}) collective-permute-start(bf16[256,1024]{1,0:T(8,128)(2,1)} %get-tuple-element.110), channel_id=1, source_target_pairs={{0,96},{32,0},{64,32},{96,64},{1,97},{33,1},{65,33},{97,65},{2,98}... | collective-permute-start | bytes 1572872 | tf_op jit(solution)/shard_map/ppermute | solution.py:20
  157.1 0.7 copy-start.21
  157.8 0.7 copy-start.22
  165.6 16.7 %collective-permute-start.29 = (bf16[256,1024]{1,0:T(8,128)(2,1)}, bf16[256,1024]{1,0:T(8,128)(2,1)S(1)}, u32[]{:S(2)}, u32[]{:S(2)}) collective-permute-start(bf16[256,1024]{1,0:T(8,128)(2,1)} %get-tuple-element.101), channel_id=1, source_target_pairs={{0,32},{32,64},{64,96},{96,0},{1,33},{33,65},{65,97},{97,1},{2,34}... | collective-permute-start | bytes 1572872 | tf_op jit(solution)/shard_map/ppermute | solution.py:20
  165.7 16.6 %collective-permute-start.30 = (bf16[256,1024]{1,0:T(8,128)(2,1)}, bf16[256,1024]{1,0:T(8,128)(2,1)S(1)}, u32[]{:S(2)}, u32[]{:S(2)}) collective-permute-start(bf16[256,1024]{1,0:T(8,128)(2,1)} %get-tuple-element.102), channel_id=1, source_target_pairs={{0,96},{32,0},{64,32},{96,64},{1,97},{33,1},{65,33},{97,65},{2,98}... | collective-permute-start | bytes 1572872 | tf_op jit(solution)/shard_map/ppermute | solution.py:20
  174.1 5.4 %copy-start.3 = (f32[256,1024]{1,0:T(8,128)S(1)}, f32[256,1024]{1,0:T(8,128)}, u32[]{:S(2)}) copy-start(f32[256,1024]{1,0:T(8,128)} %shard_map.66.kept) | copy-start | bytes 3145732
  174.2 5.5 %copy-start.8 = (s32[4]{0:T(128)S(1)}, s32[4]{0:T(128)}, u32[]{:S(2)}) copy-start(s32[4]{0:T(128)} %copy-done.7) | copy-start | bytes 52
  179.6 2.7 %copy-start.4 = (f32[256,1024]{1,0:T(8,128)S(1)}, f32[256,1024]{1,0:T(8,128)}, u32[]{:S(2)}) copy-start(f32[256,1024]{1,0:T(8,128)} %shard_map.63.kept) | copy-start | bytes 3145732

commit v6 on v5

--- a/solution.py
+++ b/solution.py
@@ -9,6 +9,7 @@
 SUB = 192
 BAND = 4
 HALO = 16
+EXTRA = 16
 SIDE = 4
 COMING = (0, SIDE - 1, 1, 2)
 epsilon = 1e-05
@@ -32,6 +33,19 @@
     return lax.optimization_barrier((value, others))[0]
 
 
+def in_parts(value):
+    high = value.astype(bf16)
+    rest = value - high.astype(f32)
+    middle = rest.astype(bf16)
+    low = (rest - middle.astype(f32)).astype(bf16)
+    return high, middle, low
+
+
+def from_parts(rows):
+    rows = rows.astype(f32)
+    return rows[0:1] + rows[1:2] + rows[2:3]
+
+
 def smem():
     return pl.BlockSpec(memory_space=pltpu.SMEM)
 
@@ -42,7 +56,6 @@
 
 def pack_kernel(place, counts, student, *outs):
     y, x, count = place[2], place[3], counts[0, place[0]]
-    moments = outs[SIDE]
     part = outs[0].shape[1] // SIDE
     for r, x_step in enumerate((0, 1, SIDE - 1, 2)):
         at = lax.rem(x + x_step, SIDE)
@@ -51,13 +64,15 @@
             first = pl.multiple_of(slot * part, 128)
             columns = slice(i * part, (i + 1) * part)
             block = student[:, pl.ds(first, part)]
-            outs[r][:, columns] = block
+            outs[r][:SUB, columns] = block
             value = block.astype(f32)
             live = lax.broadcasted_iota(jnp.int32, value.shape, 0) < count
             total = jnp.sum(jnp.where(live, value, 0.0), axis=0, keepdims=True)
             dev = jnp.where(live, value - total / count.astype(f32), 0.0)
-            moments[r : r + 1, columns] = total
-            moments[SIDE + r : SIDE + r + 1, columns] = jnp.sum(dev * dev, axis=0, keepdims=True)
+            square = jnp.sum(dev * dev, axis=0, keepdims=True)
+            rows = in_parts(total) + in_parts(square)
+            rows = rows + (jnp.zeros((EXTRA - len(rows), part), bf16),)
+            outs[r][SUB:, columns] = jnp.concatenate(rows, axis=0)
 
 
 def pack(place, counts, student):
@@ -65,9 +80,8 @@
     return pl.pallas_call(
         pack_kernel,
         in_specs=[smem(), smem(), vmem()],
-        out_specs=[vmem()] * (SIDE + 1),
-        out_shape=[jax.ShapeDtypeStruct((SUB, width), bf16)] * SIDE
-        + [jax.ShapeDtypeStruct((2 * SIDE, width), f32)],
+        out_specs=[vmem()] * SIDE,
+        out_shape=[jax.ShapeDtypeStruct((SUB + EXTRA, width), bf16)] * SIDE,
         compiler_params=pltpu.CompilerParams(vmem_limit_bytes=24 * 2**20),
         cost_estimate=pl.CostEstimate(
             flops=8 * SUB * student.shape[1],
@@ -79,9 +93,17 @@
 
 def turn_kernel(place, counts, p0, p1, p2, p3, turned, near):
     count = counts[0, place[0]]
-    rows = jnp.concatenate([p[...] for p in (p0, p1, p2, p3)], axis=0)
+    pieces = (p0, p1, p2, p3)
+    rows = jnp.concatenate([p[:SUB, :] for p in pieces], axis=0)
     flat = rows.T
-    turned[...] = flat
+    width, depth = flat.shape
+    turned[:width, :] = flat
+    moments = jnp.concatenate([p[SUB : SUB + 6, :].astype(f32) for p in pieces], axis=0)
+    rests = [
+        jnp.concatenate([moments[3 * m + i : 3 * m + i + 1, depth:] for i in range(3)], axis=1)
+        for m in range(8)
+    ]
+    turned[width:, :] = jnp.concatenate([moments[:, :depth]] + rests, axis=0).astype(bf16)
     mine = flat[:, :SUB].astype(f32)
     live = lax.broadcasted_iota(jnp.int32, mine.shape, 1) < count
     total = jnp.sum(jnp.where(live, mine, 0.0), axis=1, keepdims=True)
@@ -95,7 +117,7 @@
         in_specs=[smem()] * 2 + [vmem()] * SIDE,
         out_specs=[vmem()] * 2,
         out_shape=[
-            jax.ShapeDtypeStruct((width, SIDE * SUB), bf16),
+            jax.ShapeDtypeStruct((width + 2 * EXTRA, SIDE * SUB), bf16),
             jax.ShapeDtypeStruct((width, 1), f32),
         ],
         compiler_params=pltpu.CompilerParams(vmem_limit_bytes=16 * 2**20),
@@ -105,59 +127,71 @@
     )(place, counts, *pieces)
 
 
-def shards_kernel(place, counts, teacher, *refs):
-    blocks, out = refs[:SIDE], refs[-1]
-    out[:SIDE, :] = teacher[...]
-    size = [counts[0, lax.rem(place[0] + k, SIDE)].astype(f32) for k in COMING]
-    totals = [b[:SIDE, :] for b in blocks]
-    total = totals[0] + totals[1] + totals[2] + totals[3]
-    mean = total / (size[0] + size[1] + size[2] + size[3])
-    square = jnp.zeros_like(total)
-    for q in range(SIDE):
-        off = totals[q] / size[q] - mean
-        square = square + blocks[q][SIDE:, :] + size[q] * off * off
-    out[SIDE : 2 * SIDE, :] = total
-    out[2 * SIDE :, :] = square
-
-
-def shards(place, counts, teacher, blocks):
-    columns = blocks[0].shape[1]
+def shards_kernel(place, *refs):
+    zs, own, mate, out = refs[:SIDE], refs[SIDE : SIDE + 5], refs[SIDE + 5 : SIDE + 10], refs[-1]
+    half = own[3].shape[1]
+    depth = zs[0].shape[1]
+    blocks = []
+    for ref in zs:
+        rows = ref[...].astype(f32)
+        rests = [
+            rows[24 + m : 25 + m, i * (depth // 3) : (i + 1) * (depth // 3)]
+            for m in range(8)
+            for i in range(3)
+        ]
+        rests = jnp.concatenate(rests, axis=0)
+        blocks.append(jnp.concatenate([rows[:24], rests], axis=1))
+    lane = lax.broadcasted_iota(jnp.int32, (1, half), 1)
+    for r in range(SIDE):
+        for s, side in enumerate((own, mate)):
+            if r < 3:
+                rows = side[r][...]
+            else:
+                rows = jnp.concatenate([side[3][...], side[4][...]], axis=1)
+            out[8 * s + r : 8 * s + r + 1, :] = from_parts(rows[0:3])
+            out[8 * s + SIDE + r : 8 * s + SIDE + r + 1, :] = from_parts(rows[3:6])
+        sizes = own[r][...][6:7, :half].astype(f32)
+        n = jnp.sum(jnp.where(lane < SIDE, sizes, 0.0), axis=1, keepdims=True)
+        out[16 + r : 17 + r, :] = jnp.broadcast_to(n, (1, out.shape[1]))
+        totals = [from_parts(b[6 * r : 6 * r + 3]) for b in blocks]
+        squares = [from_parts(b[6 * r + 3 : 6 * r + 6]) for b in blocks]
+        total = totals[0] + totals[1] + totals[2] + totals[3]
+        mean = total / n
+        square = jnp.zeros_like(total)
+        for q, step in enumerate(COMING):
+            here = lax.rem(place[0] + step, SIDE)
+            size = jnp.sum(jnp.where(lane == here, sizes, 0.0), axis=1, keepdims=True)
+            off = totals[q] / size - mean
+            square = square + squares[q] + size * off * off
+        out[20 + r : 21 + r, :] = total
+        out[24 + r : 25 + r, :] = square
+    out[28:32, :] = jnp.zeros((4, out.shape[1]), f32)
+
+
+def shards(place, left, far_left, own, mate):
+    depth = left[0].shape[1]
+    columns = own[0].shape[1]
+
+    def low(value, rows):
+        first = value.shape[0] // rows - 1
+        return pl.BlockSpec((rows, value.shape[1]), lambda i, place: (first, 0))
+
     return pl.pallas_call(
         shards_kernel,
-        in_specs=[smem()] * 2 + [vmem()] * (1 + SIDE),
-        out_specs=vmem(),
-        out_shape=jax.ShapeDtypeStruct((3 * SIDE, columns), f32),
+        grid_spec=pltpu.PrefetchScalarGridSpec(
+            num_scalar_prefetch=1,
+            grid=(1,),
+            in_specs=[low(v, 2 * EXTRA) for v in left + [far_left]]
+            + [low(v, EXTRA) for v in own + mate],
+            out_specs=pl.BlockSpec((32, columns), lambda i, place: (0, 0)),
+        ),
+        out_shape=jax.ShapeDtypeStruct((32, columns), f32),
         compiler_params=pltpu.CompilerParams(vmem_limit_bytes=8 * 2**20),
-    )(place, counts, teacher, *blocks)
-
-
-def spread_kernel(e0, e1, e2, e3, *outs):
-    part = e0.shape[1] // SIDE
-    for r, out in enumerate(outs):
-        for i, (e, slot) in enumerate(zip((e0, e1, e2, e3), (1, 2, 3, 0))):
-            for m in range(3):
-                out[m * SIDE + i : m * SIDE + i + 1, :] = e[m : m + 1, :]
-            for m in range(2):
-                row = (1 + m) * SIDE + r
-                out[12 + m : 13 + m, i * part : (i + 1) * part] = e[
-                    row : row + 1, slot * part : (slot + 1) * part
-                ]
-        out[14:16, :] = jnp.zeros((2, out.shape[1]), f32)
-
-
-def spread(every):
-    columns = every[0].shape[1]
-    return pl.pallas_call(
-        spread_kernel,
-        in_specs=[vmem()] * SIDE,
-        out_specs=[vmem()] * SIDE,
-        out_shape=[jax.ShapeDtypeStruct((16, columns), f32)] * SIDE,
-        compiler_params=pltpu.CompilerParams(vmem_limit_bytes=8 * 2**20),
-    )(*every)
-
-
-def settle_kernel(n0, n1, n2, n3, t_rows, s_left, work):
-    every = (n0, n1, n2, n3)
+    )(place, *left, far_left, *own, *mate)
+
+
+def settle_kernel(e0, e1, e2, e3, t_own, t_mate, s_left, work):
+    every = (e0, e1, e2, e3)
     part = work.shape[1]
 
     def combine(totals, squares, counts):
@@ -170,21 +204,26 @@
         )
         return offs, lax.rsqrt(square / tokens + epsilon), tokens
 
-    offs, scale, _ = combine(
-        [n[0:4, :] for n in every], [n[4:8, :] for n in every], [n[8:12, :] for n in every]
-    )
-    for j in range(SIDE):
-        t_rows[j * SIDE : (j + 1) * SIDE, :] = offs[j] * scale
-    t_rows[SIDE * SIDE : SIDE * SIDE + 1, :] = scale
-    spots = [(n, i, slice(i * part, (i + 1) * part)) for n in every for i in range(SIDE)]
-    counts = [n[8 + i : 9 + i, 0:part] for n, i, _ in spots]
+    for s, t_rows in enumerate((t_own, t_mate)):
+        offs, scale, _ = combine(
+            [e[8 * s : 8 * s + 4, :] for e in every],
+            [e[8 * s + 4 : 8 * s + 8, :] for e in every],
+            [e[16:20, :] for e in every],
+        )
+        for j in range(SIDE):
+            t_rows[j * SIDE : (j + 1) * SIDE, :] = offs[j] * scale
+        t_rows[SIDE * SIDE : SIDE * SIDE + 1, :] = scale
+    slots = [slice(i * part, (i + 1) * part) for i in (1, 2, 3, 0)]
+    counts = [e[16:20, 0:part] for e in every]
     offs, scale, tokens = combine(
-        [n[12:13, c] for n, _, c in spots], [n[13:14, c] for n, _, c in spots], counts
+        [e[20:24, c] for e, c in zip(every, slots)],
+        [e[24:28, c] for e, c in zip(every, slots)],
+        counts,
     )
     scale = scale / jnp.sqrt(tokens)
     work[...] = jnp.zeros_like(work)
-    for j in range(SIDE * SIDE):
-        work[j : j + 1, :] = offs[j] * scale * counts[j]
+    for j in range(SIDE):
+        work[j * SIDE : (j + 1) * SIDE, :] = offs[j] * scale * counts[j]
     work[SIDE * SIDE : SIDE * SIDE + 1, :] = scale
     s_left[...] = work[...].T
 
@@ -192,23 +231,18 @@
 def settle(every):
     columns = every[0].shape[1]
     part = columns // SIDE
+    S = jax.ShapeDtypeStruct
     return pl.pallas_call(
         settle_kernel,
         in_specs=[vmem()] * SIDE,
-        out_specs=[vmem()] * 2,
-        out_shape=[
-            jax.ShapeDtypeStruct((SIDE * SIDE + 1, columns), f32),
-            jax.ShapeDtypeStruct((part, 128), f32),
-        ],
+        out_specs=[vmem()] * 3,
+        out_shape=[S((SIDE * SIDE + 1, columns), f32)] * 2 + [S((part, 128), f32)],
         scratch_shapes=[pltpu.VMEM((128, part), f32)],
         compiler_params=pltpu.CompilerParams(vmem_limit_bytes=8 * 2**20),
-        cost_estimate=pl.CostEstimate(
-            flops=10**11, bytes_accessed=2 * 10**8, transcendentals=0
-        ),
     )(*every)
 
 
-def pool_kernel(place, counts, before, teacher, behind, starts, weights, full, stats, mix, share, pooled, lines, meta):
+def pool_kernel(place, counts, before, teacher, behind, starts, weights, full, mix, share, pooled, lines, meta):
     window = SUB + 2 * HALO
     length = teacher.shape[0]
     j = pl.program_id(0)
@@ -259,14 +293,13 @@
         small = dev.astype(bf16)
         full[rows, :] = small
         square = square + jnp.sum(dev * dev, axis=0, keepdims=True)
-    stats[0:1, :] = total
-    stats[1:2, :] = square
-    stats[2:3, :] = jnp.broadcast_to(alive.astype(f32), total.shape)
     lane = lax.broadcasted_iota(jnp.int32, total.shape, 1)
-    row = jnp.zeros(total.shape, jnp.int32)
+    sizes = jnp.zeros(total.shape, jnp.int32)
     for r in range(SIDE):
-        row = row + jnp.where(lane == r, counts[0, r], 0)
-    stats[3:4, :] = row.astype(f32)
+        sizes = sizes + jnp.where(lane == r, counts[0, r], 0)
+    rows = in_parts(total) + in_parts(square) + (sizes.astype(f32).astype(bf16),)
+    rows = rows + (jnp.zeros((EXTRA - len(rows), total.shape[1]), bf16),)
+    full[length:, :] = jnp.concatenate(rows, axis=0)
 
 
 def pool(place, counts, before, teacher, behind, starts, weights):
@@ -284,14 +317,8 @@
             pl.BlockSpec(starts.shape, lambda j: (0, 0)),
             pl.BlockSpec(weights.shape, lambda j: (0, 0)),
         ],
-        out_specs=[
-            pl.BlockSpec((rows, tile), lambda j: (0, j)),
-            pl.BlockSpec((4, tile), lambda j: (0, j)),
-        ],
-        out_shape=[
-            jax.ShapeDtypeStruct((rows, columns), bf16),
-            jax.ShapeDtypeStruct((4, columns), f32),
-        ],
+        out_specs=pl.BlockSpec((rows + EXTRA, tile), lambda j: (0, j)),
+        out_shape=jax.ShapeDtypeStruct((rows + EXTRA, columns), bf16),
         scratch_shapes=[
             pltpu.VMEM((rows, SUB + 2 * HALO), bf16),
             pltpu.VMEM((rows, 128), f32),
@@ -329,7 +356,8 @@
 
 
 def first_product(place, left, right, near):
-    rows, depth = left[0].shape
+    depth = left[0].shape[1]
+    rows = near.shape[0]
     part = rows // SIDE
     length, columns = right[0].shape
     near_depth = 640
@@ -343,8 +371,8 @@
             + [pl.BlockSpec((part, 1), lambda i, place: (i, 0))],
             out_specs=pl.BlockSpec((part, columns), lambda i, place: (i, 0)),
         ),
-        out_shape=jax.ShapeDtypeStruct((rows, columns), f32),
-        compiler_params=pltpu.CompilerParams(vmem_limit_bytes=60 * 2**20),
+        out_shape=pltpu.HBM((rows, columns), f32),
+        compiler_params=pltpu.CompilerParams(vmem_limit_bytes=40 * 2**20),
         cost_estimate=pl.CostEstimate(
             flops=2 * rows * 3 * near_depth * columns,
             bytes_accessed=6 * rows * depth + 6 * length * columns + 4 * rows * columns,
@@ -409,7 +437,7 @@
 
 def last_product(place, k, kind, left, far_left, near, own, mate, arrived=()):
     depth = left[0].shape[1]
-    part = left[0].shape[0] // SIDE
+    part = near.shape[0] // SIDE
     half = own[0].shape[1] // 2
     kernel, start, far_start, steps = {
         "far": (far_kernel, 0, 0, 1),
@@ -445,7 +473,7 @@
             out_specs=[pl.BlockSpec(s.shape, one) for s in shapes],
         ),
         out_shape=shapes,
-        compiler_params=pltpu.CompilerParams(vmem_limit_bytes=60 * 2**20),
+        compiler_params=pltpu.CompilerParams(vmem_limit_bytes=40 * 2**20),
         cost_estimate=pl.CostEstimate(
             flops=2 * steps * part * 2 * depth * 2 * half,
             bytes_accessed=3 * steps * depth * part + 5 * depth * half + 8 * part * half,
@@ -514,24 +542,18 @@
     before = lax.ppermute(teacher[rows - HALO :], ("y", "x"), up)
     behind = lax.ppermute(teacher[:HALO], ("y", "x"), down)
 
-    *packed, block = pack(place, counts, student)
-    packed, block, before, behind = lax.optimization_barrier((packed, block, before, behind))
+    packed = pack(place, counts, student)
+    packed, before, behind = lax.optimization_barrier((packed, before, behind))
     got = [packed[0], ring(packed[1], "x", 1), ring(packed[2], "x", -1), ring(packed[3], "x", 2)]
-    blocks = ring_all(block, "row")
-    standard, stats = pool(place, counts, before, teacher, behind, starts[None], weights.T)
-    every = ring_all(shards(place, counts, stats, blocks), "y")
-    got, every, standard = lax.optimization_barrier((got, every, standard))
-    to = spread(every)
-    near = [to[0], ring(to[1], "x", 1), ring(to[2], "x", -1), ring(to[3], "x", 2)]
+    standard = pool(place, counts, before, teacher, behind, starts[None], weights.T)
+    got, standard = lax.optimization_barrier((got, standard))
     turned, mean = turn(place, counts, got)
 
     right, left = ring(standard, "x", 1), ring(standard, "x", -1)
     up, down = ring(turned, "row", 1), ring(turned, "row", -1)
     t_standard = swap(standard)
-    t_rows, s_left = settle(near)
-    t_mate = swap(t_rows)
-    right, left, up, down, t_standard, t_rows, t_mate, s_left = lax.optimization_barrier(
-        (right, left, up, down, t_standard, t_rows, t_mate, s_left)
+    right, left, up, down, t_standard = lax.optimization_barrier(
+        (right, left, up, down, t_standard)
     )
 
     x_far = [ring(right[:, :half], "x", 1), ring(left[:, half:], "x", -1)]
@@ -551,6 +573,10 @@
     for k in range(2):
         o = last_product(place, k, "far", near_z, z_far[0], mean, *sides[k])
         arrived.append((ring(o[0], "y", 1), ring(o[1], "y", -1)))
+    moments = shards(place, near_z, z_far[1], own + x_far, mate + t_x_far)
+    every = ring_all(moments, "y")
+    arrived, every = lax.optimization_barrier((arrived, every))
+    t_rows, t_mate, s_left = settle(every)
     passed = []
     for k in range(2):
         v = last_product(place, k, "close", near_z, z_far[1], mean, *sides[k], arrived[k])

time: 185 us -> 166 us (0.90)
  waiting for transfers between devices: 46.5 us -> 69.6 us
  starting transfers between devices: 53.6 us -> 36.6 us
  Pallas kernels: 70.7 us -> 54.1 us
  local copies, waits for them, and re-layouts: 13.8 us -> 5.28 us
    ppermute x28 -> x22, waiting for transfers between devices: 44.3 us -> 62.7 us  [ring(): lax.ppermute(value, axis, [(i, (i + step) % SIDE) for i in range(SIDE)])]
    ppermute x28 -> x22, starting transfers between devices: 47 us -> 30.2 us  [ring(): lax.ppermute(value, axis, [(i, (i + step) % SIDE) for i in range(SIDE)])]
    pallas_call x6, Pallas kernels: 34.8 us -> 22.1 us  [last_product(): pl.pallas_call(kernel, grid_spec=pltpu.PrefetchScalarGridSpec(num_scalar_...]
    unnamed x52 -> x16, local copies, waits for them, and re-layouts: 7.92 us -> 3.44 us
    pallas_call x2, Pallas kernels: 22.2 us -> 17.8 us  [first_product(): pl.pallas_call(first_kernel, grid_spec=pltpu.PrefetchScalarGridSpec(num_s...]
    ppermute x1, waiting for transfers between devices: 0.01 us -> 3.43 us  [per_device(): before = lax.ppermute(teacher[rows - HALO:], ('y', 'x'), up)]
    slice x2, local copies, waits for them, and re-layouts: 3 us -> 0.14 us  [per_device(): x_far = [ring(right[:, :half], 'x', 1), ring(left[:, half:], 'x', -1)]]
  transfers between devices with their start and end apart: 36 -> 29, of which waited for: 9 -> 10; matrix products, arithmetic and copies ran while one was open for 3% -> 1% of each run, Pallas kernels for 37% -> 27%
where the time goes in v6:
time: 166 us
  waiting for transfers between devices  69.6 us (42%)
  Pallas kernels  54.1 us (33%)
  starting transfers between devices  36.6 us (22%)
  local copies, waits for them, and re-layouts  5.28 us (3%)
    ppermute x22, waiting for transfers between devices, ring(): lax.ppermute(value, axis, [(i, (i + step) % SIDE) for i in range(SIDE)])  62.7 us
    ppermute x22, starting transfers between devices, ring(): lax.ppermute(value, axis, [(i, (i + step) % SIDE) for i in range(SIDE)])  30.2 us
    pallas_call x6, Pallas kernels, last_product(): pl.pallas_call(kernel, grid_spec=pltpu.PrefetchScalarGridSpec(num_scalar_...  22.1 us
    pallas_call x2, Pallas kernels, first_product(): pl.pallas_call(first_kernel, grid_spec=pltpu.PrefetchScalarGridSpec(num_s...  17.8 us
    pallas_call x2, Pallas kernels, final(): pl.pallas_call(final_kernel, grid_spec=pltpu.PrefetchScalarGridSpec(num_s...  5.34 us
    ppermute x1, starting transfers between devices, per_device(): behind = lax.ppermute(teacher[:HALO], ('y', 'x'), down)  5.29 us
    pallas_call x1, Pallas kernels, pool(): pl.pallas_call(pool_kernel, grid=(columns // tile,), in_specs=[smem(), sm...  4.73 us
    ppermute x5, waiting for transfers between devices, swap(): return lax.ppermute(value, 'col', [(0, 1), (1, 0)])  3.45 us
  transfers between devices with their start and end apart: 29, of which 10 were waited for; matrix products, arithmetic and copies ran while one was open for 1% of the time, Pallas kernels for 27%

profile of v6, /device:TPU:0, one launch (start us, length us, event | category | flops | bytes accessed | tf_op | source)
XLA Modules:
  0.0 165.8 jit_solution(15748398314889672102)
XLA Ops:
  0.0 0.9 fusion
  0.9 5.3 %collective-permute-start.1 = (bf16[16,1024]{1,0:T(8,128)(2,1)S(1)}, bf16[16,1024]{1,0:T(8,128)(2,1)S(1)}, u32[]{:S(2)}, u32[]{:S(2)}) collective-permute-start(bf16[16,1024]{1,0:T(8,128)(2,1)S(1)} %get-tuple-element.99), channel_id=1, source_target_pairs={{8,0},{16,8},{24,16},{32,24},{40,32},{48,40},{56,48},{64,56},{72,6... | collective-permute-start | bytes 98312 | tf_op jit(solution)/shard_map/ppermute | solution.py:543
  6.2 0.0 collective-permute-start
  6.2 0.1 pad_add_fusion.place
  6.3 1.4 copy-done.4
  7.7 0.7 copy-done.6
  8.3 1.7 shard_map.55
  10.0 3.4 %collective-permute-done.before = bf16[16,1024]{1,0:T(8,128)(2,1)S(1)} collective-permute-done((bf16[16,1024]{1,0:T(8,128)(2,1)S(1)}, bf16[16,1024]{1,0:T(8,128)(2,1)S(1)}, u32[]{:S(2)}, u32[]{:S(2)}) %collective-permute-start) | collective-permute-done | bytes 32800 | tf_op jit(solution)/shard_map/ppermute | solution.py:542
  13.4 3.2 %collective-permute-start.3 = (bf16[208,1024]{1,0:T(8,128)(2,1)S(1)}, bf16[208,1024]{1,0:T(8,128)(2,1)S(1)}, u32[]{:S(2)}, u32[]{:S(2)}) collective-permute-start(bf16[208,1024]{1,0:T(8,128)(2,1)S(1)} %get-tuple-element.58), channel_id=1, source_target_pairs={{0,24},{8,0},{16,8},{24,16},{1,25},{9,1},{17,9},{25,17},{2,26},{10... | collective-permute-start | bytes 1277960 | tf_op jit(solution)/shard_map/ppermute | solution.py:21
  16.7 0.0 collective-permute-start.4
  16.7 0.7 broadcast_in_dim.6.starts
  17.4 0.7 copy-done.5
  18.1 0.7 copy-done.7
  18.7 4.7 %shard_map.56.b0.refs_5_.refs_4_ = bf16[784,1024]{1,0:T(8,128)(2,1)S(1)} custom-call(s32[4]{0:T(128)S(1)} %pad_add_fusion.place, s32[1,4]{1,0:T(1,128)S(1)} %copy-done.7, bf16[16,1024]{1,0:T(8,128)(2,1)S(1)} %collective-permute-done.before, bf16[768,1024]{1,0:T(8,128)(2,1)S(1)} %copy-done.3, bf16[16,1024]{1,0:T(8,128)(2,1)S(1)} %collective-permute-done.1.behind, ...), custom_call_target="tpu_custom_call" | custom-call | flops 402653184 | bytes 4718592 | tf_op jit(solution)/shard_map/pallas_call | solution.py:308
  23.5 10.4 %collective-permute-done.2.p1 = bf16[208,1024]{1,0:T(8,128)(2,1)S(1)} collective-permute-done((bf16[208,1024]{1,0:T(8,128)(2,1)S(1)}, bf16[208,1024]{1,0:T(8,128)(2,1)S(1)}, u32[]{:S(2)}, u32[]{:S(2)}) %collective-permute-start.2) | collective-permute-done | bytes 426016 | tf_op jit(solution)/shard_map/ppermute | solution.py:21
  33.9 0.0 collective-permute-done.3.p2
  33.9 1.2 shard_map.57
  35.1 0.0 copy-start.2
  35.1 4.1 %collective-permute-start.8 = (bf16[1056,768]{1,0:T(8,128)(2,1)S(1)}, bf16[1056,768]{1,0:T(8,128)(2,1)S(1)}, u32[]{:S(2)}, u32[]{:S(2)}) collective-permute-start(bf16[1056,768]{1,0:T(8,128)(2,1)S(1)} %get-tuple-element.66.a0.refs_0_), channel_id=1, source_target_pairs={{0,6},{2,0},{4,2},{6,4},{1,7},{3,1},{5,3},{7,5},{8,14},{10,8},{12,... | collective-permute-start | bytes 4866056 | tf_op jit(solution)/shard_map/ppermute | solution.py:21
  39.2 3.0 %collective-permute-start.6 = (bf16[784,1024]{1,0:T(8,128)(2,1)S(1)}, bf16[784,1024]{1,0:T(8,128)(2,1)S(1)}, u32[]{:S(2)}, u32[]{:S(2)}) collective-permute-start(bf16[784,1024]{1,0:T(8,128)(2,1)S(1)} %shard_map.56.b0.refs_5_.refs_4_), channel_id=1, source_target_pairs={{0,24},{8,0},{16,8},{24,16},{1,25},{9,1},{17,9},{25,17},{2,26},{10... | collective-permute-start | bytes 4816904 | tf_op jit(solution)/shard_map/ppermute | solution.py:21
  42.2 0.5 collective-permute-done.9.b0.refs_10_.refs_9_
  42.6 34.5 %collective-permute-done.6.b2.refs_7_.refs_6_ = bf16[784,1024]{1,0:T(8,128)(2,1)S(1)} collective-permute-done((bf16[784,1024]{1,0:T(8,128)(2,1)S(1)}, bf16[784,1024]{1,0:T(8,128)(2,1)S(1)}, u32[]{:S(2)}, u32[]{:S(2)}) %collective-permute-start.6) | collective-permute-done | bytes 1605664 | tf_op jit(solution)/shard_map/ppermute | solution.py:21
  77.2 3.4 %collective-permute-done.5.b1.refs_6_.refs_5_ = bf16[784,1024]{1,0:T(8,128)(2,1)S(1)} collective-permute-done((bf16[784,1024]{1,0:T(8,128)(2,1)S(1)}, bf16[784,1024]{1,0:T(8,128)(2,1)S(1)}, u32[]{:S(2)}, u32[]{:S(2)}) %collective-permute-start.5) | collective-permute-done | bytes 1605664 | tf_op jit(solution)/shard_map/ppermute | solution.py:21
  80.6 0.1 collective-permute-start.14
  80.7 0.5 collective-permute-start.15
  81.2 0.1 slice.23
  81.3 3.3 %collective-permute-start.13 = (bf16[544,768]{1,0:T(8,128)(2,1)S(1)}, bf16[544,768]{1,0:T(8,128)(2,1)S(1)}, u32[]{:S(2)}, u32[]{:S(2)}) collective-permute-start(bf16[544,768]{1,0:T(8,128)(2,1)S(1)} %slice.23), channel_id=1, source_target_pairs={{0,6},{2,0},{4,2},{6,4},{1,7},{3,1},{5,3},{7,5},{8,14},{10,8},{12,... | collective-permute-start | bytes 2506760 | tf_op jit(solution)/shard_map/ppermute | solution.py:21
  84.6 0.1 slice.20
  84.6 0.1 slice.21
  84.7 0.4 collective-permute-start.11
  85.1 1.7 %collective-permute-start.10 = (bf16[784,512]{1,0:T(8,128)(2,1)S(1)}, bf16[784,512]{1,0:T(8,128)(2,1)S(1)}, u32[]{:S(2)}, u32[]{:S(2)}) collective-permute-start(bf16[784,512]{1,0:T(8,128)(2,1)S(1)} %slice.20), channel_id=1, source_target_pairs={{0,8},{8,16},{16,24},{24,0},{1,9},{9,17},{17,25},{25,1},{2,10},{10... | collective-permute-start | bytes 2408456 | tf_op jit(solution)/shard_map/ppermute | solution.py:21
  86.8 0.1 slice.22
  86.9 0.3 collective-permute-start.12
  87.1 8.9 %shard_map.58.refs_9_ = f32[1024,1024]{1,0:T(8,128)} custom-call(s32[4]{0:T(128)S(1)} %pad_add_fusion.place, bf16[1056,768]{1,0:T(8,128)(2,1)S(1)} %get-tuple-element.66.a0.refs_0_, bf16[1056,768]{1,0:T(8,128)(2,1)S(1)} %collective-permute-done.7.a1.refs_1_, bf16[1056,768]{1,0:T(8,128)(2,1)S(1)} %collective-permute-done.8.a2.refs_2_, ...), custom_call_target="tpu_custom_call" | custom-call | flops 4026531840 | bytes 13729792 | tf_op jit(solution)/shard_map/pallas_call | solution.py:364
  96.0 8.9 %shard_map.59.refs_14_ = f32[1024,1024]{1,0:T(8,128)} custom-call(s32[4]{0:T(128)S(1)} %pad_add_fusion.place, bf16[1056,768]{1,0:T(8,128)(2,1)S(1)} %get-tuple-element.66.a0.refs_0_, bf16[1056,768]{1,0:T(8,128)(2,1)S(1)} %collective-permute-done.7.a1.refs_1_, bf16[1056,768]{1,0:T(8,128)(2,1)S(1)} %collective-permute-done.8.a2.refs_2_, ...), custom_call_target="tpu_custom_call" | custom-call | flops 4026531840 | bytes 13729792 | tf_op jit(solution)/shard_map/pallas_call | solution.py:364
  105.0 2.1 %collective-permute-done.12.refs_3_ = bf16[512,768]{1,0:T(8,128)(2,1)S(1)} collective-permute-done((bf16[512,768]{1,0:T(8,128)(2,1)S(1)}, bf16[512,768]{1,0:T(8,128)(2,1)S(1)}, u32[]{:S(2)}, u32[]{:S(2)}) %collective-permute-start.12) | collective-permute-done | bytes 786464 | tf_op jit(solution)/shard_map/ppermute | solution.py:21
  107.0 0.0 collective-permute-done.11.refs_8_
  107.0 0.1 collective-permute-start.16
  107.1 0.5 collective-permute-start.17
  107.6 1.8 %collective-permute-done.16.refs_13_ = bf16[784,512]{1,0:T(8,128)(2,1)S(1)} collective-permute-done((bf16[784,512]{1,0:T(8,128)(2,1)S(1)}, bf16[784,512]{1,0:T(8,128)(2,1)S(1)}, u32[]{:S(2)}, u32[]{:S(2)}) %collective-permute-start.16) | collective-permute-done | bytes 802848 | tf_op jit(solution)/shard_map/ppermute | solution.py:29
  109.4 1.1 collective-permute-done.17.refs_13_.refs_12_
  110.6 0.9 shard_map.63.e0
  111.5 0.1 collective-permute-start.24
  111.6 0.6 collective-permute-start.23
  112.3 3.2 %shard_map.62 = (bf16[256,512]{1,0:T(8,128)(2,1)S(1)}, bf16[256,512]{1,0:T(8,128)(2,1)S(1)}) custom-call(s32[4]{0:T(128)S(1)} %pad_add_fusion.place, bf16[1056,768]{1,0:T(8,128)(2,1)} %copy-done.2, bf16[1056,768]{1,0:T(8,128)(2,1)} %copy-done.1, bf16[1056,768]{1,0:T(8,128)(2,1)} %copy-done, bf16[512,768]{1,0:T(8,128)(2,1)S(1)} %collective-permute-done.12.refs_3_, ...), custom_call_target="tpu_custom_call" | custom-call | flops 805306368 | bytes 3604480 | tf_op jit(solution)/shard_map/pallas_call | solution.py:467
  115.4 1.5 collective-permute-start.20
  117.0 2.1 %collective-permute-start.21 = (bf16[256,512]{1,0:T(8,128)(2,1)S(1)}, bf16[256,512]{1,0:T(8,128)(2,1)S(1)}, u32[]{:S(2)}, u32[]{:S(2)}) collective-permute-start(bf16[256,512]{1,0:T(8,128)(2,1)S(1)} %get-tuple-element.83), channel_id=1, source_target_pairs={{0,96},{32,0},{64,32},{96,64},{1,97},{33,1},{65,33},{97,65},{2,98}... | collective-permute-start | bytes 786440 | tf_op jit(solution)/shard_map/ppermute | solution.py:21
  119.1 3.2 %shard_map.61 = (bf16[256,512]{1,0:T(8,128)(2,1)S(1)}, bf16[256,512]{1,0:T(8,128)(2,1)S(1)}) custom-call(s32[4]{0:T(128)S(1)} %pad_add_fusion.place, bf16[1056,768]{1,0:T(8,128)(2,1)} %copy-done.2, bf16[1056,768]{1,0:T(8,128)(2,1)} %copy-done.1, bf16[1056,768]{1,0:T(8,128)(2,1)} %copy-done, bf16[512,768]{1,0:T(8,128)(2,1)S(1)} %collective-permute-done.12.refs_3_, ...), custom_call_target="tpu_custom_call" | custom-call | flops 805306368 | bytes 3604480 | tf_op jit(solution)/shard_map/pallas_call | solution.py:467
  122.2 0.1 collective-permute-start.18
  122.3 0.0 collective-permute-done.24.e3
  122.3 3.2 %collective-permute-start.19 = (bf16[256,512]{1,0:T(8,128)(2,1)S(1)}, bf16[256,512]{1,0:T(8,128)(2,1)S(1)}, u32[]{:S(2)}, u32[]{:S(2)}) collective-permute-start(bf16[256,512]{1,0:T(8,128)(2,1)S(1)} %get-tuple-element.81), channel_id=1, source_target_pairs={{0,96},{32,0},{64,32},{96,64},{1,97},{33,1},{65,33},{97,65},{2,98}... | collective-permute-start | bytes 786440 | tf_op jit(solution)/shard_map/ppermute | solution.py:21
  125.6 8.3 %collective-permute-done.22.e1 = f32[32,1024]{1,0:T(8,128)S(1)} collective-permute-done((f32[32,1024]{1,0:T(8,128)S(1)}, f32[32,1024]{1,0:T(8,128)S(1)}, u32[]{:S(2)}, u32[]{:S(2)}) %collective-permute-start.22) | collective-permute-done | bytes 131104 | tf_op jit(solution)/shard_map/ppermute | solution.py:21
  133.9 4.6 %shard_map.67 = (bf16[256,1024]{1,0:T(8,128)(2,1)S(1)}, bf16[256,1024]{1,0:T(8,128)(2,1)S(1)}) custom-call(s32[4]{0:T(128)S(1)} %pad_add_fusion.place, bf16[1056,768]{1,0:T(8,128)(2,1)} %copy-done.2, bf16[1056,768]{1,0:T(8,128)(2,1)} %copy-done.1, bf16[1056,768]{1,0:T(8,128)(2,1)} %copy-done, bf16[544,768]{1,0:T(8,128)(2,1)S(1)} %collective-permute-done.13.refs_3_, ...), custom_call_target="tpu_custom_call" | custom-call | flops 1610612736 | bytes 4194304 | tf_op jit(solution)/shard_map/pallas_call | solution.py:467
  138.5 0.1 collective-permute-start.27
  138.5 3.2 %collective-permute-start.28 = (bf16[256,1024]{1,0:T(8,128)(2,1)S(1)}, bf16[256,1024]{1,0:T(8,128)(2,1)S(1)}, u32[]{:S(2)}, u32[]{:S(2)}) collective-permute-start(bf16[256,1024]{1,0:T(8,128)(2,1)S(1)} %get-tuple-element.98), channel_id=1, source_target_pairs={{0,96},{32,0},{64,32},{96,64},{1,97},{33,1},{65,33},{97,65},{2,98}... | collective-permute-start | bytes 1572872 | tf_op jit(solution)/shard_map/ppermute | solution.py:21
  141.8 4.6 %shard_map.64 = (bf16[256,1024]{1,0:T(8,128)(2,1)S(1)}, bf16[256,1024]{1,0:T(8,128)(2,1)S(1)}) custom-call(s32[4]{0:T(128)S(1)} %pad_add_fusion.place, bf16[1056,768]{1,0:T(8,128)(2,1)} %copy-done.2, bf16[1056,768]{1,0:T(8,128)(2,1)} %copy-done.1, bf16[1056,768]{1,0:T(8,128)(2,1)} %copy-done, bf16[544,768]{1,0:T(8,128)(2,1)S(1)} %collective-permute-done.13.refs_3_, ...), custom_call_target="tpu_custom_call" | custom-call | flops 1610612736 | bytes 4194304 | tf_op jit(solution)/shard_map/pallas_call | solution.py:467
  146.4 0.1 collective-permute-start.25
  146.4 3.2 %collective-permute-start.26 = (bf16[256,1024]{1,0:T(8,128)(2,1)S(1)}, bf16[256,1024]{1,0:T(8,128)(2,1)S(1)}, u32[]{:S(2)}, u32[]{:S(2)}) collective-permute-start(bf16[256,1024]{1,0:T(8,128)(2,1)S(1)} %get-tuple-element.87), channel_id=1, source_target_pairs={{0,96},{32,0},{64,32},{96,64},{1,97},{33,1},{65,33},{97,65},{2,98}... | collective-permute-start | bytes 1572872 | tf_op jit(solution)/shard_map/ppermute | solution.py:21
  149.7 3.3 %shard_map.60.kept = f32[256,1024]{1,0:T(8,128)S(1)} custom-call(s32[4]{0:T(128)S(1)} %pad_add_fusion.place, bf16[1056,768]{1,0:T(8,128)(2,1)} %copy-done.2, bf16[1056,768]{1,0:T(8,128)(2,1)} %copy-done.1, bf16[1056,768]{1,0:T(8,128)(2,1)} %copy-done, bf16[512,768]{1,0:T(8,128)(2,1)S(1)} %collective-permute-done.12.refs_3_, ...), custom_call_target="tpu_custom_call" | custom-call | flops 805306368 | bytes 3604480 | tf_op jit(solution)/shard_map/pallas_call | solution.py:467
  153.0 3.2 %shard_map.66.kept = f32[256,1024]{1,0:T(8,128)S(1)} custom-call(s32[4]{0:T(128)S(1)} %pad_add_fusion.place, bf16[1056,768]{1,0:T(8,128)(2,1)} %copy-done.2, bf16[1056,768]{1,0:T(8,128)(2,1)} %copy-done.1, bf16[1056,768]{1,0:T(8,128)(2,1)} %copy-done, bf16[512,768]{1,0:T(8,128)(2,1)S(1)} %collective-permute-done.12.refs_3_, ...), custom_call_target="tpu_custom_call" | custom-call | flops 805306368 | bytes 3604480 | tf_op jit(solution)/shard_map/pallas_call | solution.py:467
  156.2 0.3 shard_map.65
  156.6 2.7 %shard_map.68.rest_0_ = f32[256,2048]{1,0:T(8,128)} custom-call(s32[4]{0:T(128)S(1)} %pad_add_fusion.place, f32[256,1024]{1,0:T(8,128)S(1)} %shard_map.66.kept, bf16[256,1024]{1,0:T(8,128)(2,1)S(1)} %collective-permute-done.27.first, bf16[256,1024]{1,0:T(8,128)(2,1)S(1)} %collective-permute-done.28.second, f32[256,128]{1,0:T(8,128)S(1)} %get-tuple-element.92.s_left, ...), custom_call_target="tpu_custom_call" | custom-call | flops 1572864 | bytes 3145728 | tf_op jit(solution)/shard_map/pallas_call | solution.py:513
  159.3 3.9 %collective-permute-done.25.first = bf16[256,1024]{1,0:T(8,128)(2,1)S(1)} collective-permute-done((bf16[256,1024]{1,0:T(8,128)(2,1)S(1)}, bf16[256,1024]{1,0:T(8,128)(2,1)S(1)}, u32[]{:S(2)}, u32[]{:S(2)}) %collective-permute-start.25) | collective-permute-done | bytes 524320 | tf_op jit(solution)/shard_map/ppermute | solution.py:21
  163.2 2.7 %shard_map.69 = f32[256,2048]{1,0:T(8,128)} custom-call(s32[4]{0:T(128)S(1)} %pad_add_fusion.place, f32[256,1024]{1,0:T(8,128)S(1)} %shard_map.60.kept, bf16[256,1024]{1,0:T(8,128)(2,1)S(1)} %collective-permute-done.25.first, bf16[256,1024]{1,0:T(8,128)(2,1)S(1)} %collective-permute-done.26.second, ...), custom_call_target="tpu_custom_call", output_to_operand_aliasing={{}: (7, {})} | custom-call | flops 1572864 | bytes 3145728 | tf_op jit(solution)/shard_map/pallas_call | solution.py:513
  (32 shorter events, 0.1 us)
Async XLA Ops:
  0.0 17.4 %copy-start.3 = (bf16[768,1024]{1,0:T(8,128)(2,1)S(1)}, bf16[768,1024]{1,0:T(8,128)(2,1)}, u32[]{:S(2)}) copy-start(bf16[768,1024]{1,0:T(8,128)(2,1)} %teacher.1) | copy-start | bytes 4718596
  0.9 9.1 %collective-permute-start.1 = (bf16[16,1024]{1,0:T(8,128)(2,1)S(1)}, bf16[16,1024]{1,0:T(8,128)(2,1)S(1)}, u32[]{:S(2)}, u32[]{:S(2)}) collective-permute-start(bf16[16,1024]{1,0:T(8,128)(2,1)S(1)} %get-tuple-element.99), channel_id=1, source_target_pairs={{8,0},{16,8},{24,16},{32,24},{40,32},{48,40},{56,48},{64,56},{72,6... | collective-permute-start | bytes 98312 | tf_op jit(solution)/shard_map/ppermute | solution.py:543
  6.2 7.2 %collective-permute-start = (bf16[16,1024]{1,0:T(8,128)(2,1)S(1)}, bf16[16,1024]{1,0:T(8,128)(2,1)S(1)}, u32[]{:S(2)}, u32[]{:S(2)}) collective-permute-start(bf16[16,1024]{1,0:T(8,128)(2,1)S(1)} %get-tuple-element.100), channel_id=1, source_target_pairs={{0,8},{8,16},{16,24},{24,32},{32,40},{40,48},{48,56},{56,64},{64,7... | collective-permute-start | bytes 98312 | tf_op jit(solution)/shard_map/ppermute | solution.py:542
  6.3 1.4 copy-start.4
  7.7 0.7 copy-start.6
  13.4 20.5 %collective-permute-start.2 = (bf16[208,1024]{1,0:T(8,128)(2,1)S(1)}, bf16[208,1024]{1,0:T(8,128)(2,1)S(1)}, u32[]{:S(2)}, u32[]{:S(2)}) collective-permute-start(bf16[208,1024]{1,0:T(8,128)(2,1)S(1)} %get-tuple-element.57), channel_id=1, source_target_pairs={{0,8},{8,16},{16,24},{24,0},{1,9},{9,17},{17,25},{25,1},{2,10},{10... | collective-permute-start | bytes 1277960 | tf_op jit(solution)/shard_map/ppermute | solution.py:21
  13.4 20.5 %collective-permute-start.3 = (bf16[208,1024]{1,0:T(8,128)(2,1)S(1)}, bf16[208,1024]{1,0:T(8,128)(2,1)S(1)}, u32[]{:S(2)}, u32[]{:S(2)}) collective-permute-start(bf16[208,1024]{1,0:T(8,128)(2,1)S(1)} %get-tuple-element.58), channel_id=1, source_target_pairs={{0,24},{8,0},{16,8},{24,16},{1,25},{9,1},{17,9},{25,17},{2,26},{10... | collective-permute-start | bytes 1277960 | tf_op jit(solution)/shard_map/ppermute | solution.py:21
  16.7 17.2 %collective-permute-start.4 = (bf16[208,1024]{1,0:T(8,128)(2,1)S(1)}, bf16[208,1024]{1,0:T(8,128)(2,1)S(1)}, u32[]{:S(2)}, u32[]{:S(2)}) collective-permute-start(bf16[208,1024]{1,0:T(8,128)(2,1)S(1)} %get-tuple-element.59), channel_id=1, source_target_pairs={{0,16},{8,24},{16,0},{24,8},{1,17},{9,25},{17,1},{25,9},{2,18},{10... | collective-permute-start | bytes 1277960 | tf_op jit(solution)/shard_map/ppermute | solution.py:21
  17.4 0.7 copy-start.5
  18.1 0.7 copy-start.7
  35.1 75.5 %copy-start.2 = (bf16[1056,768]{1,0:T(8,128)(2,1)}, bf16[1056,768]{1,0:T(8,128)(2,1)S(1)}, u32[]{:S(2)}) copy-start(bf16[1056,768]{1,0:T(8,128)(2,1)S(1)} %get-tuple-element.66.a0.refs_0_) | copy-start | bytes 4866052
  35.1 45.5 %collective-permute-start.8 = (bf16[1056,768]{1,0:T(8,128)(2,1)S(1)}, bf16[1056,768]{1,0:T(8,128)(2,1)S(1)}, u32[]{:S(2)}, u32[]{:S(2)}) collective-permute-start(bf16[1056,768]{1,0:T(8,128)(2,1)S(1)} %get-tuple-element.66.a0.refs_0_), channel_id=1, source_target_pairs={{0,6},{2,0},{4,2},{6,4},{1,7},{3,1},{5,3},{7,5},{8,14},{10,8},{12,... | collective-permute-start | bytes 4866056 | tf_op jit(solution)/shard_map/ppermute | solution.py:21
  39.2 41.4 %collective-permute-start.7 = (bf16[1056,768]{1,0:T(8,128)(2,1)S(1)}, bf16[1056,768]{1,0:T(8,128)(2,1)S(1)}, u32[]{:S(2)}, u32[]{:S(2)}) collective-permute-start(bf16[1056,768]{1,0:T(8,128)(2,1)S(1)} %get-tuple-element.66.a0.refs_0_), channel_id=1, source_target_pairs={{0,2},{2,4},{4,6},{6,0},{1,3},{3,5},{5,7},{7,1},{8,10},{10,12},{12... | collective-permute-start | bytes 4866056 | tf_op jit(solution)/shard_map/ppermute | solution.py:21
  39.2 3.5 %collective-permute-start.9 = (bf16[784,1024]{1,0:T(8,128)(2,1)S(1)}, bf16[784,1024]{1,0:T(8,128)(2,1)S(1)}, u32[]{:S(2)}, u32[]{:S(2)}) collective-permute-start(bf16[784,1024]{1,0:T(8,128)(2,1)S(1)} %shard_map.56.b0.refs_5_.refs_4_), channel_id=1, source_target_pairs={{0,1},{1,0},{2,3},{3,2},{4,5},{5,4},{6,7},{7,6},{8,9},{9,8},{10,11... | collective-permute-start | bytes 4816904 | tf_op jit(solution)/shard_map/ppermute | solution.py:29
  39.2 38.0 %collective-permute-start.6 = (bf16[784,1024]{1,0:T(8,128)(2,1)S(1)}, bf16[784,1024]{1,0:T(8,128)(2,1)S(1)}, u32[]{:S(2)}, u32[]{:S(2)}) collective-permute-start(bf16[784,1024]{1,0:T(8,128)(2,1)S(1)} %shard_map.56.b0.refs_5_.refs_4_), channel_id=1, source_target_pairs={{0,24},{8,0},{16,8},{24,16},{1,25},{9,1},{17,9},{25,17},{2,26},{10... | collective-permute-start | bytes 4816904 | tf_op jit(solution)/shard_map/ppermute | solution.py:21
  42.1 38.4 %collective-permute-start.5 = (bf16[784,1024]{1,0:T(8,128)(2,1)S(1)}, bf16[784,1024]{1,0:T(8,128)(2,1)S(1)}, u32[]{:S(2)}, u32[]{:S(2)}) collective-permute-start(bf16[784,1024]{1,0:T(8,128)(2,1)S(1)} %shard_map.56.b0.refs_5_.refs_4_), channel_id=1, source_target_pairs={{0,8},{8,16},{16,24},{24,0},{1,9},{9,17},{17,25},{25,1},{2,10},{10... | collective-permute-start | bytes 4816904 | tf_op jit(solution)/shard_map/ppermute | solution.py:21
  80.6 30.0 %copy-start = (bf16[1056,768]{1,0:T(8,128)(2,1)}, bf16[1056,768]{1,0:T(8,128)(2,1)S(1)}, u32[]{:S(2)}) copy-start(bf16[1056,768]{1,0:T(8,128)(2,1)S(1)} %collective-permute-done.8.a2.refs_2_) | copy-start | bytes 4866052
  80.6 30.0 %copy-start.1 = (bf16[1056,768]{1,0:T(8,128)(2,1)}, bf16[1056,768]{1,0:T(8,128)(2,1)S(1)}, u32[]{:S(2)}) copy-start(bf16[1056,768]{1,0:T(8,128)(2,1)S(1)} %collective-permute-done.7.a1.refs_1_) | copy-start | bytes 4866052
  80.6 6.3 %collective-permute-start.14 = (bf16[784,1024]{1,0:T(8,128)(2,1)S(1)}, bf16[784,1024]{1,0:T(8,128)(2,1)S(1)}, u32[]{:S(2)}, u32[]{:S(2)}) collective-permute-start(bf16[784,1024]{1,0:T(8,128)(2,1)S(1)} %collective-permute-done.5.b1.refs_6_.refs_5_), channel_id=1, source_target_pairs={{0,1},{1,0},{2,3},{3,2},{4,5},{5,4},{6,7},{7,6},{8,9},{9,8},{10,11... | collective-permute-start | bytes 4816904 | tf_op jit(solution)/shard_map/ppermute | solution.py:29
  80.7 15.3 %collective-permute-start.15 = (bf16[784,1024]{1,0:T(8,128)(2,1)S(1)}, bf16[784,1024]{1,0:T(8,128)(2,1)S(1)}, u32[]{:S(2)}, u32[]{:S(2)}) collective-permute-start(bf16[784,1024]{1,0:T(8,128)(2,1)S(1)} %collective-permute-done.6.b2.refs_7_.refs_6_), channel_id=1, source_target_pairs={{0,1},{1,0},{2,3},{3,2},{4,5},{5,4},{6,7},{7,6},{8,9},{9,8},{10,11... | collective-permute-start | bytes 4816904 | tf_op jit(solution)/shard_map/ppermute | solution.py:29
  81.3 25.8 %collective-permute-start.13 = (bf16[544,768]{1,0:T(8,128)(2,1)S(1)}, bf16[544,768]{1,0:T(8,128)(2,1)S(1)}, u32[]{:S(2)}, u32[]{:S(2)}) collective-permute-start(bf16[544,768]{1,0:T(8,128)(2,1)S(1)} %slice.23), channel_id=1, source_target_pairs={{0,6},{2,0},{4,2},{6,4},{1,7},{3,1},{5,3},{7,5},{8,14},{10,8},{12,... | collective-permute-start | bytes 2506760 | tf_op jit(solution)/shard_map/ppermute | solution.py:21
  84.7 22.3 %collective-permute-start.11 = (bf16[784,512]{1,0:T(8,128)(2,1)S(1)}, bf16[784,512]{1,0:T(8,128)(2,1)S(1)}, u32[]{:S(2)}, u32[]{:S(2)}) collective-permute-start(bf16[784,512]{1,0:T(8,128)(2,1)S(1)} %slice.21), channel_id=1, source_target_pairs={{0,24},{8,0},{16,8},{24,16},{1,25},{9,1},{17,9},{25,17},{2,26},{10... | collective-permute-start | bytes 2408456 | tf_op jit(solution)/shard_map/ppermute | solution.py:21
  85.1 22.0 %collective-permute-start.10 = (bf16[784,512]{1,0:T(8,128)(2,1)S(1)}, bf16[784,512]{1,0:T(8,128)(2,1)S(1)}, u32[]{:S(2)}, u32[]{:S(2)}) collective-permute-start(bf16[784,512]{1,0:T(8,128)(2,1)S(1)} %slice.20), channel_id=1, source_target_pairs={{0,8},{8,16},{16,24},{24,0},{1,9},{9,17},{17,25},{25,1},{2,10},{10... | collective-permute-start | bytes 2408456 | tf_op jit(solution)/shard_map/ppermute | solution.py:21
  86.9 20.2 %collective-permute-start.12 = (bf16[512,768]{1,0:T(8,128)(2,1)S(1)}, bf16[512,768]{1,0:T(8,128)(2,1)S(1)}, u32[]{:S(2)}, u32[]{:S(2)}) collective-permute-start(bf16[512,768]{1,0:T(8,128)(2,1)S(1)} %slice.22), channel_id=1, source_target_pairs={{0,2},{2,4},{4,6},{6,0},{1,3},{3,5},{5,7},{7,1},{8,10},{10,12},{12... | collective-permute-start | bytes 2359304 | tf_op jit(solution)/shard_map/ppermute | solution.py:21
  107.0 2.4 %collective-permute-start.16 = (bf16[784,512]{1,0:T(8,128)(2,1)S(1)}, bf16[784,512]{1,0:T(8,128)(2,1)S(1)}, u32[]{:S(2)}, u32[]{:S(2)}) collective-permute-start(bf16[784,512]{1,0:T(8,128)(2,1)S(1)} %collective-permute-done.11.refs_8_), channel_id=1, source_target_pairs={{0,1},{1,0},{2,3},{3,2},{4,5},{5,4},{6,7},{7,6},{8,9},{9,8},{10,11... | collective-permute-start | bytes 2408456 | tf_op jit(solution)/shard_map/ppermute | solution.py:29
  107.1 3.4 %collective-permute-start.17 = (bf16[784,512]{1,0:T(8,128)(2,1)S(1)}, bf16[784,512]{1,0:T(8,128)(2,1)S(1)}, u32[]{:S(2)}, u32[]{:S(2)}) collective-permute-start(bf16[784,512]{1,0:T(8,128)(2,1)S(1)} %collective-permute-done.10.refs_8_.refs_7_), channel_id=1, source_target_pairs={{0,1},{1,0},{2,3},{3,2},{4,5},{5,4},{6,7},{7,6},{8,9},{9,8},{10,11... | collective-permute-start | bytes 2408456 | tf_op jit(solution)/shard_map/ppermute | solution.py:29
  111.5 10.8 %collective-permute-start.24 = (f32[32,1024]{1,0:T(8,128)S(1)}, f32[32,1024]{1,0:T(8,128)S(1)}, u32[]{:S(2)}, u32[]{:S(2)}) collective-permute-start(f32[32,1024]{1,0:T(8,128)S(1)} %shard_map.63.e0), channel_id=1, source_target_pairs={{0,64},{32,96},{64,0},{96,32},{1,65},{33,97},{65,1},{97,33},{2,66}... | collective-permute-start | bytes 393224 | tf_op jit(solution)/shard_map/ppermute | solution.py:21
  111.6 13.9 %collective-permute-start.23 = (f32[32,1024]{1,0:T(8,128)S(1)}, f32[32,1024]{1,0:T(8,128)S(1)}, u32[]{:S(2)}, u32[]{:S(2)}) collective-permute-start(f32[32,1024]{1,0:T(8,128)S(1)} %shard_map.63.e0), channel_id=1, source_target_pairs={{0,96},{32,0},{64,32},{96,64},{1,97},{33,1},{65,33},{97,65},{2,98}... | collective-permute-start | bytes 393224 | tf_op jit(solution)/shard_map/ppermute | solution.py:21
  115.4 18.4 %collective-permute-start.20 = (bf16[256,512]{1,0:T(8,128)(2,1)S(1)}, bf16[256,512]{1,0:T(8,128)(2,1)S(1)}, u32[]{:S(2)}, u32[]{:S(2)}) collective-permute-start(bf16[256,512]{1,0:T(8,128)(2,1)S(1)} %get-tuple-element.82), channel_id=1, source_target_pairs={{0,32},{32,64},{64,96},{96,0},{1,33},{33,65},{65,97},{97,1},{2,34}... | collective-permute-start | bytes 786440 | tf_op jit(solution)/shard_map/ppermute | solution.py:21
  117.0 16.8 %collective-permute-start.21 = (bf16[256,512]{1,0:T(8,128)(2,1)S(1)}, bf16[256,512]{1,0:T(8,128)(2,1)S(1)}, u32[]{:S(2)}, u32[]{:S(2)}) collective-permute-start(bf16[256,512]{1,0:T(8,128)(2,1)S(1)} %get-tuple-element.83), channel_id=1, source_target_pairs={{0,96},{32,0},{64,32},{96,64},{1,97},{33,1},{65,33},{97,65},{2,98}... | collective-permute-start | bytes 786440 | tf_op jit(solution)/shard_map/ppermute | solution.py:21
  122.2 11.6 %collective-permute-start.18 = (bf16[256,512]{1,0:T(8,128)(2,1)S(1)}, bf16[256,512]{1,0:T(8,128)(2,1)S(1)}, u32[]{:S(2)}, u32[]{:S(2)}) collective-permute-start(bf16[256,512]{1,0:T(8,128)(2,1)S(1)} %get-tuple-element.80), channel_id=1, source_target_pairs={{0,32},{32,64},{64,96},{96,0},{1,33},{33,65},{65,97},{97,1},{2,34}... | collective-permute-start | bytes 786440 | tf_op jit(solution)/shard_map/ppermute | solution.py:21
  122.3 11.5 %collective-permute-start.19 = (bf16[256,512]{1,0:T(8,128)(2,1)S(1)}, bf16[256,512]{1,0:T(8,128)(2,1)S(1)}, u32[]{:S(2)}, u32[]{:S(2)}) collective-permute-start(bf16[256,512]{1,0:T(8,128)(2,1)S(1)} %get-tuple-element.81), channel_id=1, source_target_pairs={{0,96},{32,0},{64,32},{96,64},{1,97},{33,1},{65,33},{97,65},{2,98}... | collective-permute-start | bytes 786440 | tf_op jit(solution)/shard_map/ppermute | solution.py:21
  125.6 8.3 %collective-permute-start.22 = (f32[32,1024]{1,0:T(8,128)S(1)}, f32[32,1024]{1,0:T(8,128)S(1)}, u32[]{:S(2)}, u32[]{:S(2)}) collective-permute-start(f32[32,1024]{1,0:T(8,128)S(1)} %shard_map.63.e0), channel_id=1, source_target_pairs={{0,32},{32,64},{64,96},{96,0},{1,33},{33,65},{65,97},{97,1},{2,34}... | collective-permute-start | bytes 393224 | tf_op jit(solution)/shard_map/ppermute | solution.py:21
  138.5 18.1 %collective-permute-start.27 = (bf16[256,1024]{1,0:T(8,128)(2,1)S(1)}, bf16[256,1024]{1,0:T(8,128)(2,1)S(1)}, u32[]{:S(2)}, u32[]{:S(2)}) collective-permute-start(bf16[256,1024]{1,0:T(8,128)(2,1)S(1)} %get-tuple-element.97), channel_id=1, source_target_pairs={{0,32},{32,64},{64,96},{96,0},{1,33},{33,65},{65,97},{97,1},{2,34}... | collective-permute-start | bytes 1572872 | tf_op jit(solution)/shard_map/ppermute | solution.py:21
  138.5 18.0 %collective-permute-start.28 = (bf16[256,1024]{1,0:T(8,128)(2,1)S(1)}, bf16[256,1024]{1,0:T(8,128)(2,1)S(1)}, u32[]{:S(2)}, u32[]{:S(2)}) collective-permute-start(bf16[256,1024]{1,0:T(8,128)(2,1)S(1)} %get-tuple-element.98), channel_id=1, source_target_pairs={{0,96},{32,0},{64,32},{96,64},{1,97},{33,1},{65,33},{97,65},{2,98}... | collective-permute-start | bytes 1572872 | tf_op jit(solution)/shard_map/ppermute | solution.py:21
  146.4 16.8 %collective-permute-start.25 = (bf16[256,1024]{1,0:T(8,128)(2,1)S(1)}, bf16[256,1024]{1,0:T(8,128)(2,1)S(1)}, u32[]{:S(2)}, u32[]{:S(2)}) collective-permute-start(bf16[256,1024]{1,0:T(8,128)(2,1)S(1)} %get-tuple-element.86), channel_id=1, source_target_pairs={{0,32},{32,64},{64,96},{96,0},{1,33},{33,65},{65,97},{97,1},{2,34}... | collective-permute-start | bytes 1572872 | tf_op jit(solution)/shard_map/ppermute | solution.py:21
  146.4 16.7 %collective-permute-start.26 = (bf16[256,1024]{1,0:T(8,128)(2,1)S(1)}, bf16[256,1024]{1,0:T(8,128)(2,1)S(1)}, u32[]{:S(2)}, u32[]{:S(2)}) collective-permute-start(bf16[256,1024]{1,0:T(8,128)(2,1)S(1)} %get-tuple-element.87), channel_id=1, source_target_pairs={{0,96},{32,0},{64,32},{96,64},{1,97},{33,1},{65,33},{97,65},{2,98}... | collective-permute-start | bytes 1572872 | tf_op jit(solution)/shard_map/ppermute | solution.py:21

commit v7 on v6

--- a/solution.py
+++ b/solution.py
@@ -242,7 +242,7 @@
     )(*every)
 
 
-def pool_kernel(place, counts, before, teacher, behind, starts, weights, full, mix, share, pooled, lines, meta):
+def pool_kernel(place, counts, before, teacher, behind, starts, weights, full, mark, mix, share, pooled, lines, meta):
     window = SUB + 2 * HALO
     length = teacher.shape[0]
     j = pl.program_id(0)
@@ -300,6 +300,7 @@
     rows = in_parts(total) + in_parts(square) + (sizes.astype(f32).astype(bf16),)
     rows = rows + (jnp.zeros((EXTRA - len(rows), total.shape[1]), bf16),)
     full[length:, :] = jnp.concatenate(rows, axis=0)
+    mark[...] = jnp.zeros_like(mark)
 
 
 def pool(place, counts, before, teacher, behind, starts, weights):
@@ -317,8 +318,14 @@
             pl.BlockSpec(starts.shape, lambda j: (0, 0)),
             pl.BlockSpec(weights.shape, lambda j: (0, 0)),
         ],
-        out_specs=pl.BlockSpec((rows + EXTRA, tile), lambda j: (0, j)),
-        out_shape=jax.ShapeDtypeStruct((rows + EXTRA, columns), bf16),
+        out_specs=[
+            pl.BlockSpec((rows + EXTRA, tile), lambda j: (0, j)),
+            pl.BlockSpec((8, 128), lambda j: (0, 0)),
+        ],
+        out_shape=[
+            jax.ShapeDtypeStruct((rows + EXTRA, columns), bf16),
+            jax.ShapeDtypeStruct((8, 128), f32),
+        ],
         scratch_shapes=[
             pltpu.VMEM((rows, SUB + 2 * HALO), bf16),
             pltpu.VMEM((rows, 128), f32),
@@ -411,11 +418,19 @@
 
 
 def own_kernel(place, *refs):
-    kept = refs[15]
-    half = kept.shape[1] // 2
+    s_left, t_own, t_mate, base = refs[15:]
+    half = base.shape[1] // 2
+    every = SIDE * SIDE
     results = last_sums(place, refs)
-    kept[:, :half] = results[0]
-    kept[:, half:] = results[1]
+    for i, t in enumerate((t_own, t_mate)):
+        between = jnp.dot(
+            s_left[:, :every],
+            t[:every, :],
+            preferred_element_type=f32,
+            precision=lax.Precision.HIGHEST,
+        )
+        scaled = results[i] * s_left[:, every : every + 1] * t[every : every + 1, :]
+        base[:, i * half : (i + 1) * half] = scaled + between
 
 
 def close_kernel(place, *refs):
@@ -456,7 +471,12 @@
         + [pl.BlockSpec((part, depth), lambda i, place: (far_start + i, 0))]
         + [pl.BlockSpec((part, 1), lambda i, place: (start + i, 0))]
         + side * 2
-        + [pl.BlockSpec((part, half), one)] * len(arrived)
+        + (
+            [pl.BlockSpec(arrived[0].shape, one)]
+            + [pl.BlockSpec((a.shape[0], half), lambda i, place: (0, k)) for a in arrived[1:]]
+            if kind == "own"
+            else [pl.BlockSpec((part, half), one)] * len(arrived)
+        )
     )
     S = jax.ShapeDtypeStruct
     shapes = {
@@ -482,19 +502,13 @@
     )(place, *left, far_left, near, *own, *mate, *arrived)
 
 
-def final_kernel(place, kept, first, second, s_left, t_own, t_mate, *rest):
+def final_kernel(place, base, first, second, s_left, t_own, t_mate, *rest):
     out = rest[-1]
-    t = jnp.where(pl.program_id(0) == 0, t_own[...], t_mate[...])
-    shards_all = SIDE * SIDE
-    between = jnp.dot(
-        s_left[:, :shards_all],
-        t[:shards_all],
-        preferred_element_type=f32,
-        precision=lax.Precision.HIGHEST,
-    )
-    inside = kept[...] + first[...].astype(f32) + second[...].astype(f32)
-    row_scale = s_left[:, shards_all : shards_all + 1]
-    out[...] = inside * row_scale * t[shards_all : shards_all + 1] + between
+    every = SIDE * SIDE
+    last = slice(every, every + 1)
+    t = jnp.where(pl.program_id(0) == 0, t_own[last, :], t_mate[last, :])
+    inside = first[...].astype(f32) + second[...].astype(f32)
+    out[...] = inside * s_left[:, last] * t + base[...]
 
 
 def final(place, k, kept, first, second, s_left, t_own, t_mate, whole=None):
@@ -545,8 +559,8 @@
     packed = pack(place, counts, student)
     packed, before, behind = lax.optimization_barrier((packed, before, behind))
     got = [packed[0], ring(packed[1], "x", 1), ring(packed[2], "x", -1), ring(packed[3], "x", 2)]
-    standard = pool(place, counts, before, teacher, behind, starts[None], weights.T)
-    got, standard = lax.optimization_barrier((got, standard))
+    standard, mark = pool(place, counts, before, teacher, behind, starts[None], weights.T)
+    got, _ = lax.optimization_barrier((got, mark))
     turned, mean = turn(place, counts, got)
 
     right, left = ring(standard, "x", 1), ring(standard, "x", -1)
@@ -569,22 +583,25 @@
     sides = [
         (own + [x_far[k], own_sum], mate + [t_x_far[k], mate_sum]) for k in range(2)
     ]
-    arrived = []
+    arrived, sent = [], []
     for k in range(2):
         o = last_product(place, k, "far", near_z, z_far[0], mean, *sides[k])
+        sent.append(o[0])
         arrived.append((ring(o[0], "y", 1), ring(o[1], "y", -1)))
-    moments = shards(place, near_z, z_far[1], own + x_far, mate + t_x_far)
-    every = ring_all(moments, "y")
-    arrived, every = lax.optimization_barrier((arrived, every))
-    t_rows, t_mate, s_left = settle(every)
+    far_rows = after(z_far[1], sent)
+    every = ring_all(shards(place, near_z, far_rows, own + x_far, mate + t_x_far), "y")
     passed = []
     for k in range(2):
+        if k == 1:
+            arrived[k], every = lax.optimization_barrier((arrived[k], every))
         v = last_product(place, k, "close", near_z, z_far[1], mean, *sides[k], arrived[k])
         passed.append((ring(v[0], "y", 1), ring(v[1], "y", -1)))
+    t_rows, t_mate, s_left = settle(every)
+    settled = (s_left, t_rows, t_mate)
     out = None
     for k in range(2):
-        kept = last_product(place, k, "own", near_z, z_far[0], mean, *sides[k])[0]
-        out = final(place, k, kept, *passed[k], s_left, t_rows, t_mate, out)
+        base = last_product(place, k, "own", near_z, z_far[0], mean, *sides[k], settled)[0]
+        out = final(place, k, base, *passed[k], *settled, out)
     return out[None, None]
 
 

time: 166 us -> 177 us (1.066)
  waiting for transfers between devices: 69.6 us -> 81.2 us
    ppermute x22, waiting for transfers between devices: 62.7 us -> 75.5 us  [ring(): lax.ppermute(value, axis, [(i, (i + step) % SIDE) for i in range(SIDE)])]
    unnamed x16 -> x28, local copies, waits for them, and re-layouts: 3.44 us -> 3.67 us
  transfers between devices with their start and end apart: 29 -> 29, of which waited for: 10 -> 11; matrix products, arithmetic and copies ran while one was open for 1% -> 0% of each run, Pallas kernels for 27% -> 24%
where the time goes in v7:
time: 177 us
  waiting for transfers between devices  81.2 us (46%)
  Pallas kernels  54.1 us (31%)
  starting transfers between devices  36.4 us (21%)
  local copies, waits for them, and re-layouts  4.72 us (3%)
    ppermute x22, waiting for transfers between devices, ring(): lax.ppermute(value, axis, [(i, (i + step) % SIDE) for i in range(SIDE)])  75.5 us
    ppermute x22, starting transfers between devices, ring(): lax.ppermute(value, axis, [(i, (i + step) % SIDE) for i in range(SIDE)])  29.9 us
    pallas_call x6, Pallas kernels, last_product(): pl.pallas_call(kernel, grid_spec=pltpu.PrefetchScalarGridSpec(num_scalar_...  23.2 us
    pallas_call x2, Pallas kernels, first_product(): pl.pallas_call(first_kernel, grid_spec=pltpu.PrefetchScalarGridSpec(num_s...  17.8 us
    pallas_call x1, Pallas kernels, pool(): pl.pallas_call(pool_kernel, grid=(columns // tile,), in_specs=[smem(), sm...  5.32 us
    ppermute x1, starting transfers between devices, per_device(): behind = lax.ppermute(teacher[:HALO], ('y', 'x'), down)  5.29 us
    unnamed x28, local copies, waits for them, and re-layouts  3.67 us
    pallas_call x2, Pallas kernels, final(): pl.pallas_call(final_kernel, grid_spec=pltpu.PrefetchScalarGridSpec(num_s...  3.66 us
  transfers between devices with their start and end apart: 29, of which 11 were waited for; matrix products, arithmetic and copies ran while one was open for 0% of the time, Pallas kernels for 24%

profile of v7, /device:TPU:0, one launch (start us, length us, event | category | flops | bytes accessed | tf_op | source)
XLA Modules:
  0.0 176.8 jit_solution(1971656538621776150)
XLA Ops:
  0.0 0.8 fusion
  0.8 5.3 %collective-permute-start.1 = (bf16[16,1024]{1,0:T(8,128)(2,1)S(1)}, bf16[16,1024]{1,0:T(8,128)(2,1)S(1)}, u32[]{:S(2)}, u32[]{:S(2)}) collective-permute-start(bf16[16,1024]{1,0:T(8,128)(2,1)S(1)} %get-tuple-element.97), channel_id=1, source_target_pairs={{8,0},{16,8},{24,16},{32,24},{40,32},{48,40},{56,48},{64,56},{72,6... | collective-permute-start | bytes 98312 | tf_op jit(solution)/shard_map/ppermute | solution.py:557
  6.1 0.0 collective-permute-start
  6.1 0.1 pad_add_fusion.place
  6.2 1.4 copy-done.9
  7.6 0.7 copy-done.11
  8.2 1.7 shard_map.55
  9.9 3.4 %collective-permute-done.before = bf16[16,1024]{1,0:T(8,128)(2,1)S(1)} collective-permute-done((bf16[16,1024]{1,0:T(8,128)(2,1)S(1)}, bf16[16,1024]{1,0:T(8,128)(2,1)S(1)}, u32[]{:S(2)}, u32[]{:S(2)}) %collective-permute-start) | collective-permute-done | bytes 32800 | tf_op jit(solution)/shard_map/ppermute | solution.py:556
  13.3 0.0 collective-permute-start.2
  13.3 3.2 %collective-permute-start.3 = (bf16[208,1024]{1,0:T(8,128)(2,1)S(1)}, bf16[208,1024]{1,0:T(8,128)(2,1)S(1)}, u32[]{:S(2)}, u32[]{:S(2)}) collective-permute-start(bf16[208,1024]{1,0:T(8,128)(2,1)S(1)} %get-tuple-element.57), channel_id=1, source_target_pairs={{0,24},{8,0},{16,8},{24,16},{1,25},{9,1},{17,9},{25,17},{2,26},{10... | collective-permute-start | bytes 1277960 | tf_op jit(solution)/shard_map/ppermute | solution.py:21
  16.6 17.2 %collective-permute-done.2.p1 = bf16[208,1024]{1,0:T(8,128)(2,1)S(1)} collective-permute-done((bf16[208,1024]{1,0:T(8,128)(2,1)S(1)}, bf16[208,1024]{1,0:T(8,128)(2,1)S(1)}, u32[]{:S(2)}, u32[]{:S(2)}) %collective-permute-start.2) | collective-permute-done | bytes 426016 | tf_op jit(solution)/shard_map/ppermute | solution.py:21
  33.8 1.2 shard_map.56
  35.0 0.0 copy-start.4
  35.0 4.1 %collective-permute-start.8 = (bf16[1056,768]{1,0:T(8,128)(2,1)S(1)}, bf16[1056,768]{1,0:T(8,128)(2,1)S(1)}, u32[]{:S(2)}, u32[]{:S(2)}) collective-permute-start(bf16[1056,768]{1,0:T(8,128)(2,1)S(1)} %get-tuple-element.63.a0.refs_0_), channel_id=1, source_target_pairs={{0,6},{2,0},{4,2},{6,4},{1,7},{3,1},{5,3},{7,5},{8,14},{10,8},{12,... | collective-permute-start | bytes 4866056 | tf_op jit(solution)/shard_map/ppermute | solution.py:21
  39.1 5.3 %shard_map.57 = (bf16[784,1024]{1,0:T(8,128)(2,1)S(1)}, f32[8,128]{1,0:T(8,128)}) custom-call(s32[4]{0:T(128)S(1)} %pad_add_fusion.place, s32[1,4]{1,0:T(1,128)S(1)} %copy-done.12, bf16[16,1024]{1,0:T(8,128)(2,1)S(1)} %collective-permute-done.before, bf16[768,1024]{1,0:T(8,128)(2,1)S(1)} %copy-done.8, bf16[16,1024]{1,0:T(8,128)(2,1)S(1)} %collective-permute-done.1.behind, ...), custom_call_target="tpu_custom_call" | custom-call | flops 402653184 | bytes 4718592 | tf_op jit(solution)/shard_map/pallas_call | solution.py:309
  44.4 3.0 %collective-permute-start.6 = (bf16[784,1024]{1,0:T(8,128)(2,1)S(1)}, bf16[784,1024]{1,0:T(8,128)(2,1)S(1)}, u32[]{:S(2)}, u32[]{:S(2)}) collective-permute-start(bf16[784,1024]{1,0:T(8,128)(2,1)S(1)} %get-tuple-element.66.b0.refs_5_.refs_4_), channel_id=1, source_target_pairs={{0,24},{8,0},{16,8},{24,16},{1,25},{9,1},{17,9},{25,17},{2,26},{10... | collective-permute-start | bytes 4816904 | tf_op jit(solution)/shard_map/ppermute | solution.py:21
  47.4 0.0 collective-permute-start.5
  47.4 0.5 collective-permute-done.9.b0.refs_10_.refs_9_
  47.9 34.5 %collective-permute-done.6.b2.refs_7_.refs_6_ = bf16[784,1024]{1,0:T(8,128)(2,1)S(1)} collective-permute-done((bf16[784,1024]{1,0:T(8,128)(2,1)S(1)}, bf16[784,1024]{1,0:T(8,128)(2,1)S(1)}, u32[]{:S(2)}, u32[]{:S(2)}) %collective-permute-start.6) | collective-permute-done | bytes 1605664 | tf_op jit(solution)/shard_map/ppermute | solution.py:21
  82.4 3.4 %collective-permute-done.5.b1.refs_6_.refs_5_ = bf16[784,1024]{1,0:T(8,128)(2,1)S(1)} collective-permute-done((bf16[784,1024]{1,0:T(8,128)(2,1)S(1)}, bf16[784,1024]{1,0:T(8,128)(2,1)S(1)}, u32[]{:S(2)}, u32[]{:S(2)}) %collective-permute-start.5) | collective-permute-done | bytes 1605664 | tf_op jit(solution)/shard_map/ppermute | solution.py:21
  85.8 0.0 collective-permute-done.8.a2.refs_2_
  85.8 0.0 collective-permute-done.7.a1.refs_1_
  85.9 0.1 collective-permute-start.14
  85.9 0.5 collective-permute-start.15
  86.4 0.1 slice.23
  86.5 3.3 %collective-permute-start.13 = (bf16[544,768]{1,0:T(8,128)(2,1)S(1)}, bf16[544,768]{1,0:T(8,128)(2,1)S(1)}, u32[]{:S(2)}, u32[]{:S(2)}) collective-permute-start(bf16[544,768]{1,0:T(8,128)(2,1)S(1)} %slice.23), channel_id=1, source_target_pairs={{0,6},{2,0},{4,2},{6,4},{1,7},{3,1},{5,3},{7,5},{8,14},{10,8},{12,... | collective-permute-start | bytes 2506760 | tf_op jit(solution)/shard_map/ppermute | solution.py:21
  89.8 0.1 slice.20
  89.9 0.1 slice.21
  89.9 0.4 collective-permute-start.11
  90.3 1.7 collective-permute-start.10
  92.0 0.1 slice.22
  92.1 0.3 collective-permute-start.12
  92.4 8.9 %shard_map.58.refs_9_ = f32[1024,1024]{1,0:T(8,128)} custom-call(s32[4]{0:T(128)S(1)} %pad_add_fusion.place, bf16[1056,768]{1,0:T(8,128)(2,1)S(1)} %get-tuple-element.63.a0.refs_0_, bf16[1056,768]{1,0:T(8,128)(2,1)S(1)} %collective-permute-done.7.a1.refs_1_, bf16[1056,768]{1,0:T(8,128)(2,1)S(1)} %collective-permute-done.8.a2.refs_2_, ...), custom_call_target="tpu_custom_call" | custom-call | flops 4026531840 | bytes 13729792 | tf_op jit(solution)/shard_map/pallas_call | solution.py:371
  101.2 0.0 collective-permute-done.15.b2.refs_12_.refs_11_
  101.2 8.9 %shard_map.59.refs_14_ = f32[1024,1024]{1,0:T(8,128)} custom-call(s32[4]{0:T(128)S(1)} %pad_add_fusion.place, bf16[1056,768]{1,0:T(8,128)(2,1)S(1)} %get-tuple-element.63.a0.refs_0_, bf16[1056,768]{1,0:T(8,128)(2,1)S(1)} %collective-permute-done.7.a1.refs_1_, bf16[1056,768]{1,0:T(8,128)(2,1)S(1)} %collective-permute-done.8.a2.refs_2_, ...), custom_call_target="tpu_custom_call" | custom-call | flops 4026531840 | bytes 13729792 | tf_op jit(solution)/shard_map/pallas_call | solution.py:371
  110.1 2.1 %collective-permute-done.12.refs_3_ = bf16[512,768]{1,0:T(8,128)(2,1)S(1)} collective-permute-done((bf16[512,768]{1,0:T(8,128)(2,1)S(1)}, bf16[512,768]{1,0:T(8,128)(2,1)S(1)}, u32[]{:S(2)}, u32[]{:S(2)}) %collective-permute-start.12) | collective-permute-done | bytes 786464 | tf_op jit(solution)/shard_map/ppermute | solution.py:21
  112.3 0.0 collective-permute-done.11.refs_8_
  112.3 0.1 collective-permute-start.16
  112.4 0.5 collective-permute-start.19
  112.9 1.8 %collective-permute-done.16.refs_13_ = bf16[784,512]{1,0:T(8,128)(2,1)S(1)} collective-permute-done((bf16[784,512]{1,0:T(8,128)(2,1)S(1)}, bf16[784,512]{1,0:T(8,128)(2,1)S(1)}, u32[]{:S(2)}, u32[]{:S(2)}) %collective-permute-start.16) | collective-permute-done | bytes 802848 | tf_op jit(solution)/shard_map/ppermute | solution.py:29
  114.7 3.2 %shard_map.60 = (bf16[256,512]{1,0:T(8,128)(2,1)S(1)}, bf16[256,512]{1,0:T(8,128)(2,1)S(1)}) custom-call(s32[4]{0:T(128)S(1)} %pad_add_fusion.place, bf16[1056,768]{1,0:T(8,128)(2,1)} %copy-done.4, bf16[1056,768]{1,0:T(8,128)(2,1)} %copy-done.2, bf16[1056,768]{1,0:T(8,128)(2,1)} %copy-done, bf16[512,768]{1,0:T(8,128)(2,1)S(1)} %collective-permute-done.12.refs_3_, ...), custom_call_target="tpu_custom_call" | custom-call | flops 805306368 | bytes 3604480 | tf_op jit(solution)/shard_map/pallas_call | solution.py:487
  117.9 0.0 copy-start.5
  117.9 1.6 copy-done.7
  119.5 3.2 %shard_map.61 = (bf16[256,512]{1,0:T(8,128)(2,1)S(1)}, bf16[256,512]{1,0:T(8,128)(2,1)S(1)}) custom-call(s32[4]{0:T(128)S(1)} %pad_add_fusion.place, bf16[1056,768]{1,0:T(8,128)(2,1)} %copy-done.4, bf16[1056,768]{1,0:T(8,128)(2,1)} %copy-done.2, bf16[1056,768]{1,0:T(8,128)(2,1)} %copy-done, bf16[512,768]{1,0:T(8,128)(2,1)S(1)} %collective-permute-done.12.refs_3_, ...), custom_call_target="tpu_custom_call" | custom-call | flops 805306368 | bytes 3604480 | tf_op jit(solution)/shard_map/pallas_call | solution.py:487
  122.7 0.9 shard_map.62.e0
  123.6 0.1 collective-permute-start.22
  123.7 0.6 collective-permute-start.21
  124.4 3.4 %collective-permute-start.18 = (bf16[256,512]{1,0:T(8,128)(2,1)S(1)}, bf16[256,512]{1,0:T(8,128)(2,1)S(1)}, u32[]{:S(2)}, u32[]{:S(2)}) collective-permute-start(bf16[256,512]{1,0:T(8,128)(2,1)S(1)} %get-tuple-element.78), channel_id=1, source_target_pairs={{0,96},{32,0},{64,32},{96,64},{1,97},{33,1},{65,33},{97,65},{2,98}... | collective-permute-start | bytes 786440 | tf_op jit(solution)/shard_map/ppermute | solution.py:21
  127.8 3.2 %collective-permute-start.26 = (bf16[256,512]{1,0:T(8,128)(2,1)S(1)}, bf16[256,512]{1,0:T(8,128)(2,1)S(1)}, u32[]{:S(2)}, u32[]{:S(2)}) collective-permute-start(bf16[256,512]{1,0:T(8,128)(2,1)S(1)} %get-tuple-element.94), channel_id=1, source_target_pairs={{0,96},{32,0},{64,32},{96,64},{1,97},{33,1},{65,33},{97,65},{2,98}... | collective-permute-start | bytes 786440 | tf_op jit(solution)/shard_map/ppermute | solution.py:21
  131.0 0.5 collective-permute-done.22.e3
  131.6 0.8 collective-permute-done.21.e2
  132.3 13.0 %collective-permute-done.20.e1 = f32[32,1024]{1,0:T(8,128)S(1)} collective-permute-done((f32[32,1024]{1,0:T(8,128)S(1)}, f32[32,1024]{1,0:T(8,128)S(1)}, u32[]{:S(2)}, u32[]{:S(2)}) %collective-permute-start.20) | collective-permute-done | bytes 131104 | tf_op jit(solution)/shard_map/ppermute | solution.py:21
  145.3 4.6 %shard_map.67 = (bf16[256,1024]{1,0:T(8,128)(2,1)S(1)}, bf16[256,1024]{1,0:T(8,128)(2,1)S(1)}) custom-call(s32[4]{0:T(128)S(1)} %pad_add_fusion.place, bf16[1056,768]{1,0:T(8,128)(2,1)} %copy-done.4, bf16[1056,768]{1,0:T(8,128)(2,1)} %copy-done.2, bf16[1056,768]{1,0:T(8,128)(2,1)} %copy-done, bf16[544,768]{1,0:T(8,128)(2,1)S(1)} %collective-permute-done.13.refs_3_, ...), custom_call_target="tpu_custom_call" | custom-call | flops 1610612736 | bytes 4194304 | tf_op jit(solution)/shard_map/pallas_call | solution.py:487
  149.9 0.1 collective-permute-start.27
  150.0 3.2 %collective-permute-start.28 = (bf16[256,1024]{1,0:T(8,128)(2,1)S(1)}, bf16[256,1024]{1,0:T(8,128)(2,1)S(1)}, u32[]{:S(2)}, u32[]{:S(2)}) collective-permute-start(bf16[256,1024]{1,0:T(8,128)(2,1)S(1)} %get-tuple-element.96), channel_id=1, source_target_pairs={{0,96},{32,0},{64,32},{96,64},{1,97},{33,1},{65,33},{97,65},{2,98}... | collective-permute-start | bytes 1572872 | tf_op jit(solution)/shard_map/ppermute | solution.py:21
  153.2 4.6 %shard_map.65 = (bf16[256,1024]{1,0:T(8,128)(2,1)S(1)}, bf16[256,1024]{1,0:T(8,128)(2,1)S(1)}) custom-call(s32[4]{0:T(128)S(1)} %pad_add_fusion.place, bf16[1056,768]{1,0:T(8,128)(2,1)} %copy-done.4, bf16[1056,768]{1,0:T(8,128)(2,1)} %copy-done.2, bf16[1056,768]{1,0:T(8,128)(2,1)} %copy-done, bf16[544,768]{1,0:T(8,128)(2,1)S(1)} %collective-permute-done.13.refs_3_, ...), custom_call_target="tpu_custom_call" | custom-call | flops 1610612736 | bytes 4194304 | tf_op jit(solution)/shard_map/pallas_call | solution.py:487
  157.8 0.1 collective-permute-start.23
  157.9 3.2 %collective-permute-start.24 = (bf16[256,1024]{1,0:T(8,128)(2,1)S(1)}, bf16[256,1024]{1,0:T(8,128)(2,1)S(1)}, u32[]{:S(2)}, u32[]{:S(2)}) collective-permute-start(bf16[256,1024]{1,0:T(8,128)(2,1)S(1)} %get-tuple-element.93), channel_id=1, source_target_pairs={{0,96},{32,0},{64,32},{96,64},{1,97},{33,1},{65,33},{97,65},{2,98}... | collective-permute-start | bytes 1572872 | tf_op jit(solution)/shard_map/ppermute | solution.py:21
  161.1 0.3 shard_map.63
  161.5 3.8 %shard_map.66.base = f32[256,1024]{1,0:T(8,128)S(1)} custom-call(s32[4]{0:T(128)S(1)} %pad_add_fusion.place, bf16[1056,768]{1,0:T(8,128)(2,1)} %copy-done.4, bf16[1056,768]{1,0:T(8,128)(2,1)} %copy-done.2, bf16[1056,768]{1,0:T(8,128)(2,1)} %copy-done, bf16[512,768]{1,0:T(8,128)(2,1)S(1)} %collective-permute-done.12.refs_3_, ...), custom_call_target="tpu_custom_call" | custom-call | flops 805306368 | bytes 3604480 | tf_op jit(solution)/shard_map/pallas_call | solution.py:487
  165.3 3.8 %shard_map.64.base = f32[256,1024]{1,0:T(8,128)S(1)} custom-call(s32[4]{0:T(128)S(1)} %pad_add_fusion.place, bf16[1056,768]{1,0:T(8,128)(2,1)} %copy-done.4, bf16[1056,768]{1,0:T(8,128)(2,1)} %copy-done.2, bf16[1056,768]{1,0:T(8,128)(2,1)} %copy-done, bf16[512,768]{1,0:T(8,128)(2,1)S(1)} %collective-permute-done.12.refs_3_, ...), custom_call_target="tpu_custom_call" | custom-call | flops 805306368 | bytes 3604480 | tf_op jit(solution)/shard_map/pallas_call | solution.py:487
  169.2 1.8 %shard_map.68.rest_0_ = f32[256,2048]{1,0:T(8,128)} custom-call(s32[4]{0:T(128)S(1)} %pad_add_fusion.place, f32[256,1024]{1,0:T(8,128)S(1)} %shard_map.66.base, bf16[256,1024]{1,0:T(8,128)(2,1)S(1)} %collective-permute-done.27.first, bf16[256,1024]{1,0:T(8,128)(2,1)S(1)} %collective-permute-done.28.second, f32[256,128]{1,0:T(8,128)S(1)} %get-tuple-element.87.refs_15_.s_left, ...), custom_call_target="tpu_custom_call" | custom-call | flops 1572864 | bytes 3145728 | tf_op jit(solution)/shard_map/pallas_call | solution.py:527
  171.0 3.9 %collective-permute-done.23.first = bf16[256,1024]{1,0:T(8,128)(2,1)S(1)} collective-permute-done((bf16[256,1024]{1,0:T(8,128)(2,1)S(1)}, bf16[256,1024]{1,0:T(8,128)(2,1)S(1)}, u32[]{:S(2)}, u32[]{:S(2)}) %collective-permute-start.23) | collective-permute-done | bytes 524320 | tf_op jit(solution)/shard_map/ppermute | solution.py:21
  175.0 1.8 %shard_map.69 = f32[256,2048]{1,0:T(8,128)} custom-call(s32[4]{0:T(128)S(1)} %pad_add_fusion.place, f32[256,1024]{1,0:T(8,128)S(1)} %shard_map.64.base, bf16[256,1024]{1,0:T(8,128)(2,1)S(1)} %collective-permute-done.23.first, bf16[256,1024]{1,0:T(8,128)(2,1)S(1)} %collective-permute-done.24.second, ...), custom_call_target="tpu_custom_call", output_to_operand_aliasing={{}: (7, {})} | custom-call | flops 1572864 | bytes 3145728 | tf_op jit(solution)/shard_map/pallas_call | solution.py:527
  (44 shorter events, 0.1 us)
Async XLA Ops:
  0.0 16.6 %copy-start.13 = (s32[768]{0:T(1024)S(1)}, s32[768]{0:T(1024)}, u32[]{:S(2)}) copy-start(s32[768]{0:T(1024)} %param.7) | copy-start | bytes 9220
  0.8 9.1 %collective-permute-start.1 = (bf16[16,1024]{1,0:T(8,128)(2,1)S(1)}, bf16[16,1024]{1,0:T(8,128)(2,1)S(1)}, u32[]{:S(2)}, u32[]{:S(2)}) collective-permute-start(bf16[16,1024]{1,0:T(8,128)(2,1)S(1)} %get-tuple-element.97), channel_id=1, source_target_pairs={{8,0},{16,8},{24,16},{32,24},{40,32},{48,40},{56,48},{64,56},{72,6... | collective-permute-start | bytes 98312 | tf_op jit(solution)/shard_map/ppermute | solution.py:557
  6.1 7.2 %collective-permute-start = (bf16[16,1024]{1,0:T(8,128)(2,1)S(1)}, bf16[16,1024]{1,0:T(8,128)(2,1)S(1)}, u32[]{:S(2)}, u32[]{:S(2)}) collective-permute-start(bf16[16,1024]{1,0:T(8,128)(2,1)S(1)} %get-tuple-element.98), channel_id=1, source_target_pairs={{0,8},{8,16},{16,24},{24,32},{32,40},{40,48},{48,56},{56,64},{64,7... | collective-permute-start | bytes 98312 | tf_op jit(solution)/shard_map/ppermute | solution.py:556
  6.2 1.4 copy-start.9
  7.6 0.7 copy-start.11
  8.2 30.9 %copy-start.8 = (bf16[768,1024]{1,0:T(8,128)(2,1)S(1)}, bf16[768,1024]{1,0:T(8,128)(2,1)}, u32[]{:S(2)}) copy-start(bf16[768,1024]{1,0:T(8,128)(2,1)} %teacher.1) | copy-start | bytes 4718596
  8.2 30.9 %copy-start.10 = (s32[768,4]{0,1:T(4,128)S(1)}, s32[768,4]{0,1:T(4,128)}, u32[]{:S(2)}) copy-start(s32[768,4]{0,1:T(4,128)} %param.8) | copy-start | bytes 36868
  8.2 30.9 %copy-start.12 = (s32[1,4]{1,0:T(1,128)S(1)}, s32[1,4]{1,0:T(1,128)}, u32[]{:S(2)}) copy-start(s32[1,4]{1,0:T(1,128)} %counts.5) | copy-start | bytes 52
  13.3 20.5 %collective-permute-start.2 = (bf16[208,1024]{1,0:T(8,128)(2,1)S(1)}, bf16[208,1024]{1,0:T(8,128)(2,1)S(1)}, u32[]{:S(2)}, u32[]{:S(2)}) collective-permute-start(bf16[208,1024]{1,0:T(8,128)(2,1)S(1)} %get-tuple-element.56), channel_id=1, source_target_pairs={{0,8},{8,16},{16,24},{24,0},{1,9},{9,17},{17,25},{25,1},{2,10},{10... | collective-permute-start | bytes 1277960 | tf_op jit(solution)/shard_map/ppermute | solution.py:21
  13.3 20.5 %collective-permute-start.3 = (bf16[208,1024]{1,0:T(8,128)(2,1)S(1)}, bf16[208,1024]{1,0:T(8,128)(2,1)S(1)}, u32[]{:S(2)}, u32[]{:S(2)}) collective-permute-start(bf16[208,1024]{1,0:T(8,128)(2,1)S(1)} %get-tuple-element.57), channel_id=1, source_target_pairs={{0,24},{8,0},{16,8},{24,16},{1,25},{9,1},{17,9},{25,17},{2,26},{10... | collective-permute-start | bytes 1277960 | tf_op jit(solution)/shard_map/ppermute | solution.py:21
  16.6 17.2 %collective-permute-start.4 = (bf16[208,1024]{1,0:T(8,128)(2,1)S(1)}, bf16[208,1024]{1,0:T(8,128)(2,1)S(1)}, u32[]{:S(2)}, u32[]{:S(2)}) collective-permute-start(bf16[208,1024]{1,0:T(8,128)(2,1)S(1)} %get-tuple-element.58), channel_id=1, source_target_pairs={{0,16},{8,24},{16,0},{24,8},{1,17},{9,25},{17,1},{25,9},{2,18},{10... | collective-permute-start | bytes 1277960 | tf_op jit(solution)/shard_map/ppermute | solution.py:21
  35.0 66.3 %copy-start.4 = (bf16[1056,768]{1,0:T(8,128)(2,1)}, bf16[1056,768]{1,0:T(8,128)(2,1)S(1)}, u32[]{:S(2)}) copy-start(bf16[1056,768]{1,0:T(8,128)(2,1)S(1)} %get-tuple-element.63.a0.refs_0_) | copy-start | bytes 4866052
  35.0 50.9 %collective-permute-start.8 = (bf16[1056,768]{1,0:T(8,128)(2,1)S(1)}, bf16[1056,768]{1,0:T(8,128)(2,1)S(1)}, u32[]{:S(2)}, u32[]{:S(2)}) collective-permute-start(bf16[1056,768]{1,0:T(8,128)(2,1)S(1)} %get-tuple-element.63.a0.refs_0_), channel_id=1, source_target_pairs={{0,6},{2,0},{4,2},{6,4},{1,7},{3,1},{5,3},{7,5},{8,14},{10,8},{12,... | collective-permute-start | bytes 4866056 | tf_op jit(solution)/shard_map/ppermute | solution.py:21
  39.1 46.8 %collective-permute-start.7 = (bf16[1056,768]{1,0:T(8,128)(2,1)S(1)}, bf16[1056,768]{1,0:T(8,128)(2,1)S(1)}, u32[]{:S(2)}, u32[]{:S(2)}) collective-permute-start(bf16[1056,768]{1,0:T(8,128)(2,1)S(1)} %get-tuple-element.63.a0.refs_0_), channel_id=1, source_target_pairs={{0,2},{2,4},{4,6},{6,0},{1,3},{3,5},{5,7},{7,1},{8,10},{10,12},{12... | collective-permute-start | bytes 4866056 | tf_op jit(solution)/shard_map/ppermute | solution.py:21
  44.4 3.5 %collective-permute-start.9 = (bf16[784,1024]{1,0:T(8,128)(2,1)S(1)}, bf16[784,1024]{1,0:T(8,128)(2,1)S(1)}, u32[]{:S(2)}, u32[]{:S(2)}) collective-permute-start(bf16[784,1024]{1,0:T(8,128)(2,1)S(1)} %get-tuple-element.66.b0.refs_5_.refs_4_), channel_id=1, source_target_pairs={{0,1},{1,0},{2,3},{3,2},{4,5},{5,4},{6,7},{7,6},{8,9},{9,8},{10,11... | collective-permute-start | bytes 4816904 | tf_op jit(solution)/shard_map/ppermute | solution.py:29
  44.4 38.0 %collective-permute-start.6 = (bf16[784,1024]{1,0:T(8,128)(2,1)S(1)}, bf16[784,1024]{1,0:T(8,128)(2,1)S(1)}, u32[]{:S(2)}, u32[]{:S(2)}) collective-permute-start(bf16[784,1024]{1,0:T(8,128)(2,1)S(1)} %get-tuple-element.66.b0.refs_5_.refs_4_), channel_id=1, source_target_pairs={{0,24},{8,0},{16,8},{24,16},{1,25},{9,1},{17,9},{25,17},{2,26},{10... | collective-permute-start | bytes 4816904 | tf_op jit(solution)/shard_map/ppermute | solution.py:21
  47.4 38.4 %collective-permute-start.5 = (bf16[784,1024]{1,0:T(8,128)(2,1)S(1)}, bf16[784,1024]{1,0:T(8,128)(2,1)S(1)}, u32[]{:S(2)}, u32[]{:S(2)}) collective-permute-start(bf16[784,1024]{1,0:T(8,128)(2,1)S(1)} %get-tuple-element.66.b0.refs_5_.refs_4_), channel_id=1, source_target_pairs={{0,8},{8,16},{16,24},{24,0},{1,9},{9,17},{17,25},{25,1},{2,10},{10... | collective-permute-start | bytes 4816904 | tf_op jit(solution)/shard_map/ppermute | solution.py:21
  47.9 66.8 %copy-start.6 = (bf16[784,1024]{1,0:T(8,128)(2,1)}, bf16[784,1024]{1,0:T(8,128)(2,1)S(1)}, u32[]{:S(2)}) copy-start(bf16[784,1024]{1,0:T(8,128)(2,1)S(1)} %collective-permute-done.9.b0.refs_10_.refs_9_) | copy-start | bytes 4816900
  85.8 15.4 %copy-start = (bf16[1056,768]{1,0:T(8,128)(2,1)}, bf16[1056,768]{1,0:T(8,128)(2,1)S(1)}, u32[]{:S(2)}) copy-start(bf16[1056,768]{1,0:T(8,128)(2,1)S(1)} %collective-permute-done.8.a2.refs_2_) | copy-start | bytes 4866052
  85.8 15.4 %copy-start.2 = (bf16[1056,768]{1,0:T(8,128)(2,1)}, bf16[1056,768]{1,0:T(8,128)(2,1)S(1)}, u32[]{:S(2)}) copy-start(bf16[1056,768]{1,0:T(8,128)(2,1)S(1)} %collective-permute-done.7.a1.refs_1_) | copy-start | bytes 4866052
  85.9 6.2 %collective-permute-start.14 = (bf16[784,1024]{1,0:T(8,128)(2,1)S(1)}, bf16[784,1024]{1,0:T(8,128)(2,1)S(1)}, u32[]{:S(2)}, u32[]{:S(2)}) collective-permute-start(bf16[784,1024]{1,0:T(8,128)(2,1)S(1)} %collective-permute-done.5.b1.refs_6_.refs_5_), channel_id=1, source_target_pairs={{0,1},{1,0},{2,3},{3,2},{4,5},{5,4},{6,7},{7,6},{8,9},{9,8},{10,11... | collective-permute-start | bytes 4816904 | tf_op jit(solution)/shard_map/ppermute | solution.py:29
  85.9 15.3 %collective-permute-start.15 = (bf16[784,1024]{1,0:T(8,128)(2,1)S(1)}, bf16[784,1024]{1,0:T(8,128)(2,1)S(1)}, u32[]{:S(2)}, u32[]{:S(2)}) collective-permute-start(bf16[784,1024]{1,0:T(8,128)(2,1)S(1)} %collective-permute-done.6.b2.refs_7_.refs_6_), channel_id=1, source_target_pairs={{0,1},{1,0},{2,3},{3,2},{4,5},{5,4},{6,7},{7,6},{8,9},{9,8},{10,11... | collective-permute-start | bytes 4816904 | tf_op jit(solution)/shard_map/ppermute | solution.py:29
  86.5 25.8 %collective-permute-start.13 = (bf16[544,768]{1,0:T(8,128)(2,1)S(1)}, bf16[544,768]{1,0:T(8,128)(2,1)S(1)}, u32[]{:S(2)}, u32[]{:S(2)}) collective-permute-start(bf16[544,768]{1,0:T(8,128)(2,1)S(1)} %slice.23), channel_id=1, source_target_pairs={{0,6},{2,0},{4,2},{6,4},{1,7},{3,1},{5,3},{7,5},{8,14},{10,8},{12,... | collective-permute-start | bytes 2506760 | tf_op jit(solution)/shard_map/ppermute | solution.py:21
  89.9 22.3 %collective-permute-start.11 = (bf16[784,512]{1,0:T(8,128)(2,1)S(1)}, bf16[784,512]{1,0:T(8,128)(2,1)S(1)}, u32[]{:S(2)}, u32[]{:S(2)}) collective-permute-start(bf16[784,512]{1,0:T(8,128)(2,1)S(1)} %slice.21), channel_id=1, source_target_pairs={{0,24},{8,0},{16,8},{24,16},{1,25},{9,1},{17,9},{25,17},{2,26},{10... | collective-permute-start | bytes 2408456 | tf_op jit(solution)/shard_map/ppermute | solution.py:21
  90.3 22.0 %collective-permute-start.10 = (bf16[784,512]{1,0:T(8,128)(2,1)S(1)}, bf16[784,512]{1,0:T(8,128)(2,1)S(1)}, u32[]{:S(2)}, u32[]{:S(2)}) collective-permute-start(bf16[784,512]{1,0:T(8,128)(2,1)S(1)} %slice.20), channel_id=1, source_target_pairs={{0,8},{8,16},{16,24},{24,0},{1,9},{9,17},{17,25},{25,1},{2,10},{10... | collective-permute-start | bytes 2408456 | tf_op jit(solution)/shard_map/ppermute | solution.py:21
  92.1 20.2 %collective-permute-start.12 = (bf16[512,768]{1,0:T(8,128)(2,1)S(1)}, bf16[512,768]{1,0:T(8,128)(2,1)S(1)}, u32[]{:S(2)}, u32[]{:S(2)}) collective-permute-start(bf16[512,768]{1,0:T(8,128)(2,1)S(1)} %slice.22), channel_id=1, source_target_pairs={{0,2},{2,4},{4,6},{6,0},{1,3},{3,5},{5,7},{7,1},{8,10},{10,12},{12... | collective-permute-start | bytes 2359304 | tf_op jit(solution)/shard_map/ppermute | solution.py:21
  112.3 2.4 %collective-permute-start.16 = (bf16[784,512]{1,0:T(8,128)(2,1)S(1)}, bf16[784,512]{1,0:T(8,128)(2,1)S(1)}, u32[]{:S(2)}, u32[]{:S(2)}) collective-permute-start(bf16[784,512]{1,0:T(8,128)(2,1)S(1)} %collective-permute-done.11.refs_8_), channel_id=1, source_target_pairs={{0,1},{1,0},{2,3},{3,2},{4,5},{5,4},{6,7},{7,6},{8,9},{9,8},{10,11... | collective-permute-start | bytes 2408456 | tf_op jit(solution)/shard_map/ppermute | solution.py:29
  112.4 5.5 %collective-permute-start.19 = (bf16[784,512]{1,0:T(8,128)(2,1)S(1)}, bf16[784,512]{1,0:T(8,128)(2,1)S(1)}, u32[]{:S(2)}, u32[]{:S(2)}) collective-permute-start(bf16[784,512]{1,0:T(8,128)(2,1)S(1)} %collective-permute-done.10.refs_8_.refs_7_), channel_id=1, source_target_pairs={{0,1},{1,0},{2,3},{3,2},{4,5},{5,4},{6,7},{7,6},{8,9},{9,8},{10,11... | collective-permute-start | bytes 2408456 | tf_op jit(solution)/shard_map/ppermute | solution.py:29
  117.8 4.8 %copy-start.1 = (bf16[1056,768]{1,0:T(8,128)(2,1)S(1)}, bf16[1056,768]{1,0:T(8,128)(2,1)}, u32[]{:S(2)}) copy-start(bf16[1056,768]{1,0:T(8,128)(2,1)} %copy-done) | copy-start | bytes 4866052
  117.9 4.8 %copy-start.3 = (bf16[1056,768]{1,0:T(8,128)(2,1)S(1)}, bf16[1056,768]{1,0:T(8,128)(2,1)}, u32[]{:S(2)}) copy-start(bf16[1056,768]{1,0:T(8,128)(2,1)} %copy-done.2) | copy-start | bytes 4866052
  117.9 4.8 %copy-start.5 = (bf16[1056,768]{1,0:T(8,128)(2,1)S(1)}, bf16[1056,768]{1,0:T(8,128)(2,1)}, u32[]{:S(2)}) copy-start(bf16[1056,768]{1,0:T(8,128)(2,1)} %copy-done.4) | copy-start | bytes 4866052
  117.9 1.6 copy-start.7
  123.6 7.9 %collective-permute-start.22 = (f32[32,1024]{1,0:T(8,128)S(1)}, f32[32,1024]{1,0:T(8,128)S(1)}, u32[]{:S(2)}, u32[]{:S(2)}) collective-permute-start(f32[32,1024]{1,0:T(8,128)S(1)} %shard_map.62.e0), channel_id=1, source_target_pairs={{0,64},{32,96},{64,0},{96,32},{1,65},{33,97},{65,1},{97,33},{2,66}... | collective-permute-start | bytes 393224 | tf_op jit(solution)/shard_map/ppermute | solution.py:21
  123.7 8.6 %collective-permute-start.21 = (f32[32,1024]{1,0:T(8,128)S(1)}, f32[32,1024]{1,0:T(8,128)S(1)}, u32[]{:S(2)}, u32[]{:S(2)}) collective-permute-start(f32[32,1024]{1,0:T(8,128)S(1)} %shard_map.62.e0), channel_id=1, source_target_pairs={{0,96},{32,0},{64,32},{96,64},{1,97},{33,1},{65,33},{97,65},{2,98}... | collective-permute-start | bytes 393224 | tf_op jit(solution)/shard_map/ppermute | solution.py:21
  124.4 20.9 %collective-permute-start.18 = (bf16[256,512]{1,0:T(8,128)(2,1)S(1)}, bf16[256,512]{1,0:T(8,128)(2,1)S(1)}, u32[]{:S(2)}, u32[]{:S(2)}) collective-permute-start(bf16[256,512]{1,0:T(8,128)(2,1)S(1)} %get-tuple-element.78), channel_id=1, source_target_pairs={{0,96},{32,0},{64,32},{96,64},{1,97},{33,1},{65,33},{97,65},{2,98}... | collective-permute-start | bytes 786440 | tf_op jit(solution)/shard_map/ppermute | solution.py:21
  127.8 17.5 %collective-permute-start.17 = (bf16[256,512]{1,0:T(8,128)(2,1)S(1)}, bf16[256,512]{1,0:T(8,128)(2,1)S(1)}, u32[]{:S(2)}, u32[]{:S(2)}) collective-permute-start(bf16[256,512]{1,0:T(8,128)(2,1)S(1)} %get-tuple-element.77), channel_id=1, source_target_pairs={{0,32},{32,64},{64,96},{96,0},{1,33},{33,65},{65,97},{97,1},{2,34}... | collective-permute-start | bytes 786440 | tf_op jit(solution)/shard_map/ppermute | solution.py:21
  127.8 17.5 %collective-permute-start.26 = (bf16[256,512]{1,0:T(8,128)(2,1)S(1)}, bf16[256,512]{1,0:T(8,128)(2,1)S(1)}, u32[]{:S(2)}, u32[]{:S(2)}) collective-permute-start(bf16[256,512]{1,0:T(8,128)(2,1)S(1)} %get-tuple-element.94), channel_id=1, source_target_pairs={{0,96},{32,0},{64,32},{96,64},{1,97},{33,1},{65,33},{97,65},{2,98}... | collective-permute-start | bytes 786440 | tf_op jit(solution)/shard_map/ppermute | solution.py:21
  131.6 13.7 %collective-permute-start.25 = (bf16[256,512]{1,0:T(8,128)(2,1)S(1)}, bf16[256,512]{1,0:T(8,128)(2,1)S(1)}, u32[]{:S(2)}, u32[]{:S(2)}) collective-permute-start(bf16[256,512]{1,0:T(8,128)(2,1)S(1)} %get-tuple-element.81), channel_id=1, source_target_pairs={{0,32},{32,64},{64,96},{96,0},{1,33},{33,65},{65,97},{97,1},{2,34}... | collective-permute-start | bytes 786440 | tf_op jit(solution)/shard_map/ppermute | solution.py:21
  132.3 13.0 %collective-permute-start.20 = (f32[32,1024]{1,0:T(8,128)S(1)}, f32[32,1024]{1,0:T(8,128)S(1)}, u32[]{:S(2)}, u32[]{:S(2)}) collective-permute-start(f32[32,1024]{1,0:T(8,128)S(1)} %shard_map.62.e0), channel_id=1, source_target_pairs={{0,32},{32,64},{64,96},{96,0},{1,33},{33,65},{65,97},{97,1},{2,34}... | collective-permute-start | bytes 393224 | tf_op jit(solution)/shard_map/ppermute | solution.py:21
  149.9 19.3 %collective-permute-start.27 = (bf16[256,1024]{1,0:T(8,128)(2,1)S(1)}, bf16[256,1024]{1,0:T(8,128)(2,1)S(1)}, u32[]{:S(2)}, u32[]{:S(2)}) collective-permute-start(bf16[256,1024]{1,0:T(8,128)(2,1)S(1)} %get-tuple-element.95), channel_id=1, source_target_pairs={{0,32},{32,64},{64,96},{96,0},{1,33},{33,65},{65,97},{97,1},{2,34}... | collective-permute-start | bytes 1572872 | tf_op jit(solution)/shard_map/ppermute | solution.py:21
  150.0 19.2 %collective-permute-start.28 = (bf16[256,1024]{1,0:T(8,128)(2,1)S(1)}, bf16[256,1024]{1,0:T(8,128)(2,1)S(1)}, u32[]{:S(2)}, u32[]{:S(2)}) collective-permute-start(bf16[256,1024]{1,0:T(8,128)(2,1)S(1)} %get-tuple-element.96), channel_id=1, source_target_pairs={{0,96},{32,0},{64,32},{96,64},{1,97},{33,1},{65,33},{97,65},{2,98}... | collective-permute-start | bytes 1572872 | tf_op jit(solution)/shard_map/ppermute | solution.py:21
  157.8 17.1 %collective-permute-start.23 = (bf16[256,1024]{1,0:T(8,128)(2,1)S(1)}, bf16[256,1024]{1,0:T(8,128)(2,1)S(1)}, u32[]{:S(2)}, u32[]{:S(2)}) collective-permute-start(bf16[256,1024]{1,0:T(8,128)(2,1)S(1)} %get-tuple-element.92), channel_id=1, source_target_pairs={{0,32},{32,64},{64,96},{96,0},{1,33},{33,65},{65,97},{97,1},{2,34}... | collective-permute-start | bytes 1572872 | tf_op jit(solution)/shard_map/ppermute | solution.py:21
  157.9 17.1 %collective-permute-start.24 = (bf16[256,1024]{1,0:T(8,128)(2,1)S(1)}, bf16[256,1024]{1,0:T(8,128)(2,1)S(1)}, u32[]{:S(2)}, u32[]{:S(2)}) collective-permute-start(bf16[256,1024]{1,0:T(8,128)(2,1)S(1)} %get-tuple-element.93), channel_id=1, source_target_pairs={{0,96},{32,0},{64,32},{96,64},{1,97},{33,1},{65,33},{97,65},{2,98}... | collective-permute-start | bytes 1572872 | tf_op jit(solution)/shard_map/ppermute | solution.py:21

commit v8 on v7

--- a/solution.py
+++ b/solution.py
@@ -128,7 +128,7 @@
 
 
 def shards_kernel(place, *refs):
-    zs, own, mate, out = refs[:SIDE], refs[SIDE : SIDE + 5], refs[SIDE + 5 : SIDE + 10], refs[-1]
+    zs, own, out = refs[:SIDE], refs[SIDE : SIDE + 5], refs[-1]
     half = own[3].shape[1]
     depth = zs[0].shape[1]
     blocks = []
@@ -143,16 +143,15 @@
         blocks.append(jnp.concatenate([rows[:24], rests], axis=1))
     lane = lax.broadcasted_iota(jnp.int32, (1, half), 1)
     for r in range(SIDE):
-        for s, side in enumerate((own, mate)):
-            if r < 3:
-                rows = side[r][...]
-            else:
-                rows = jnp.concatenate([side[3][...], side[4][...]], axis=1)
-            out[8 * s + r : 8 * s + r + 1, :] = from_parts(rows[0:3])
-            out[8 * s + SIDE + r : 8 * s + SIDE + r + 1, :] = from_parts(rows[3:6])
+        if r < 3:
+            rows = own[r][...]
+        else:
+            rows = jnp.concatenate([own[3][...], own[4][...]], axis=1)
+        out[r : r + 1, :] = from_parts(rows[0:3])
+        out[SIDE + r : SIDE + r + 1, :] = from_parts(rows[3:6])
         sizes = own[r][...][6:7, :half].astype(f32)
         n = jnp.sum(jnp.where(lane < SIDE, sizes, 0.0), axis=1, keepdims=True)
-        out[16 + r : 17 + r, :] = jnp.broadcast_to(n, (1, out.shape[1]))
+        out[8 + r : 9 + r, :] = jnp.broadcast_to(n, (1, out.shape[1]))
         totals = [from_parts(b[6 * r : 6 * r + 3]) for b in blocks]
         squares = [from_parts(b[6 * r + 3 : 6 * r + 6]) for b in blocks]
         total = totals[0] + totals[1] + totals[2] + totals[3]
@@ -163,12 +162,12 @@
             size = jnp.sum(jnp.where(lane == here, sizes, 0.0), axis=1, keepdims=True)
             off = totals[q] / size - mean
             square = square + squares[q] + size * off * off
-        out[20 + r : 21 + r, :] = total
-        out[24 + r : 25 + r, :] = square
-    out[28:32, :] = jnp.zeros((4, out.shape[1]), f32)
-
-
-def shards(place, left, far_left, own, mate):
+        out[12 + r : 13 + r, :] = total
+        out[16 + r : 17 + r, :] = square
+    out[20:24, :] = jnp.zeros((4, out.shape[1]), f32)
+
+
+def shards(place, left, far_left, own):
     depth = left[0].shape[1]
     columns = own[0].shape[1]
 
@@ -182,15 +181,15 @@
             num_scalar_prefetch=1,
             grid=(1,),
             in_specs=[low(v, 2 * EXTRA) for v in left + [far_left]]
-            + [low(v, EXTRA) for v in own + mate],
-            out_specs=pl.BlockSpec((32, columns), lambda i, place: (0, 0)),
-        ),
-        out_shape=jax.ShapeDtypeStruct((32, columns), f32),
+            + [low(v, EXTRA) for v in own],
+            out_specs=pl.BlockSpec((24, columns), lambda i, place: (0, 0)),
+        ),
+        out_shape=jax.ShapeDtypeStruct((24, columns), f32),
         compiler_params=pltpu.CompilerParams(vmem_limit_bytes=8 * 2**20),
-    )(place, *left, far_left, *own, *mate)
-
-
-def settle_kernel(e0, e1, e2, e3, t_own, t_mate, s_left, work):
+    )(place, *left, far_left, *own)
+
+
+def settle_kernel(e0, e1, e2, e3, t_rows, s_left, work):
     every = (e0, e1, e2, e3)
     part = work.shape[1]
 
@@ -204,20 +203,17 @@
         )
         return offs, lax.rsqrt(square / tokens + epsilon), tokens
 
-    for s, t_rows in enumerate((t_own, t_mate)):
-        offs, scale, _ = combine(
-            [e[8 * s : 8 * s + 4, :] for e in every],
-            [e[8 * s + 4 : 8 * s + 8, :] for e in every],
-            [e[16:20, :] for e in every],
-        )
-        for j in range(SIDE):
-            t_rows[j * SIDE : (j + 1) * SIDE, :] = offs[j] * scale
-        t_rows[SIDE * SIDE : SIDE * SIDE + 1, :] = scale
+    offs, scale, _ = combine(
+        [e[0:4, :] for e in every], [e[4:8, :] for e in every], [e[8:12, :] for e in every]
+    )
+    for j in range(SIDE):
+        t_rows[j * SIDE : (j + 1) * SIDE, :] = offs[j] * scale
+    t_rows[SIDE * SIDE : SIDE * SIDE + 1, :] = scale
     slots = [slice(i * part, (i + 1) * part) for i in (1, 2, 3, 0)]
-    counts = [e[16:20, 0:part] for e in every]
+    counts = [e[8:12, 0:part] for e in every]
     offs, scale, tokens = combine(
-        [e[20:24, c] for e, c in zip(every, slots)],
-        [e[24:28, c] for e, c in zip(every, slots)],
+        [e[12:16, c] for e, c in zip(every, slots)],
+        [e[16:20, c] for e, c in zip(every, slots)],
         counts,
     )
     scale = scale / jnp.sqrt(tokens)
@@ -235,14 +231,14 @@
     return pl.pallas_call(
         settle_kernel,
         in_specs=[vmem()] * SIDE,
-        out_specs=[vmem()] * 3,
-        out_shape=[S((SIDE * SIDE + 1, columns), f32)] * 2 + [S((part, 128), f32)],
+        out_specs=[vmem()] * 2,
+        out_shape=[S((SIDE * SIDE + 1, columns), f32), S((part, 128), f32)],
         scratch_shapes=[pltpu.VMEM((128, part), f32)],
         compiler_params=pltpu.CompilerParams(vmem_limit_bytes=8 * 2**20),
     )(*every)
 
 
-def pool_kernel(place, counts, before, teacher, behind, starts, weights, full, mark, mix, share, pooled, lines, meta):
+def pool_kernel(place, counts, before, teacher, behind, starts, weights, full, mix, share, pooled, lines, meta):
     window = SUB + 2 * HALO
     length = teacher.shape[0]
     j = pl.program_id(0)
@@ -300,7 +296,6 @@
     rows = in_parts(total) + in_parts(square) + (sizes.astype(f32).astype(bf16),)
     rows = rows + (jnp.zeros((EXTRA - len(rows), total.shape[1]), bf16),)
     full[length:, :] = jnp.concatenate(rows, axis=0)
-    mark[...] = jnp.zeros_like(mark)
 
 
 def pool(place, counts, before, teacher, behind, starts, weights):
@@ -318,14 +313,8 @@
             pl.BlockSpec(starts.shape, lambda j: (0, 0)),
             pl.BlockSpec(weights.shape, lambda j: (0, 0)),
         ],
-        out_specs=[
-            pl.BlockSpec((rows + EXTRA, tile), lambda j: (0, j)),
-            pl.BlockSpec((8, 128), lambda j: (0, 0)),
-        ],
-        out_shape=[
-            jax.ShapeDtypeStruct((rows + EXTRA, columns), bf16),
-            jax.ShapeDtypeStruct((8, 128), f32),
-        ],
+        out_specs=pl.BlockSpec((rows + EXTRA, tile), lambda j: (0, j)),
+        out_shape=jax.ShapeDtypeStruct((rows + EXTRA, columns), bf16),
         scratch_shapes=[
             pltpu.VMEM((rows, SUB + 2 * HALO), bf16),
             pltpu.VMEM((rows, 128), f32),
@@ -559,8 +548,8 @@
     packed = pack(place, counts, student)
     packed, before, behind = lax.optimization_barrier((packed, before, behind))
     got = [packed[0], ring(packed[1], "x", 1), ring(packed[2], "x", -1), ring(packed[3], "x", 2)]
-    standard, mark = pool(place, counts, before, teacher, behind, starts[None], weights.T)
-    got, _ = lax.optimization_barrier((got, mark))
+    standard = pool(place, counts, before, teacher, behind, starts[None], weights.T)
+    got, standard = lax.optimization_barrier((got, standard))
     turned, mean = turn(place, counts, got)
 
     right, left = ring(standard, "x", 1), ring(standard, "x", -1)
@@ -580,24 +569,20 @@
     x_far, z_far, own_sum, mate_sum = lax.optimization_barrier((x_far, z_far, own_sum, mate_sum))
 
     t_x_far = [swap(f) for f in x_far]
-    sides = [
-        (own + [x_far[k], own_sum], mate + [t_x_far[k], mate_sum]) for k in range(2)
-    ]
-    arrived, sent = [], []
+    every = ring_all(shards(place, near_z, z_far[1], own + x_far), "y")
+    sides, arrived = [], []
     for k in range(2):
+        if k == 1:
+            every, own_sum, mate_sum = lax.optimization_barrier((every, own_sum, mate_sum))
+        sides.append((own + [x_far[k], own_sum], mate + [t_x_far[k], mate_sum]))
         o = last_product(place, k, "far", near_z, z_far[0], mean, *sides[k])
-        sent.append(o[0])
         arrived.append((ring(o[0], "y", 1), ring(o[1], "y", -1)))
-    far_rows = after(z_far[1], sent)
-    every = ring_all(shards(place, near_z, far_rows, own + x_far, mate + t_x_far), "y")
+    t_rows, s_left = settle(every)
+    settled = (s_left, t_rows, swap(t_rows))
     passed = []
     for k in range(2):
-        if k == 1:
-            arrived[k], every = lax.optimization_barrier((arrived[k], every))
         v = last_product(place, k, "close", near_z, z_far[1], mean, *sides[k], arrived[k])
         passed.append((ring(v[0], "y", 1), ring(v[1], "y", -1)))
-    t_rows, t_mate, s_left = settle(every)
-    settled = (s_left, t_rows, t_mate)
     out = None
     for k in range(2):
         base = last_product(place, k, "own", near_z, z_far[0], mean, *sides[k], settled)[0]

time: 177 us -> 149 us (0.84)
  waiting for transfers between devices: 81.2 us -> 50.2 us
  starting transfers between devices: 36.4 us -> 39.7 us
    ppermute x22, waiting for transfers between devices: 75.5 us -> 48.9 us  [ring(): lax.ppermute(value, axis, [(i, (i + step) % SIDE) for i in range(SIDE)])]
    ppermute x1, waiting for transfers between devices: 3.41 us -> 0.01 us  [per_device(): before = lax.ppermute(teacher[rows - HALO:], ('y', 'x'), up)]
    ppermute x22, starting transfers between devices: 29.9 us -> 32.9 us  [ring(): lax.ppermute(value, axis, [(i, (i + step) % SIDE) for i in range(SIDE)])]
    unnamed x28 -> x16, local copies, waits for them, and re-layouts: 3.67 us -> 3.44 us
  transfers between devices with their start and end apart: 29 -> 30, of which waited for: 11 -> 5; matrix products, arithmetic and copies ran while one was open for 0% -> 1% of each run, Pallas kernels for 24% -> 34%
where the time goes in v8:
time: 149 us
  Pallas kernels  53.3 us (36%)
  waiting for transfers between devices  50.2 us (34%)
  starting transfers between devices  39.7 us (27%)
  local copies, waits for them, and re-layouts  5.28 us (4%)
    ppermute x22, waiting for transfers between devices, ring(): lax.ppermute(value, axis, [(i, (i + step) % SIDE) for i in range(SIDE)])  48.9 us
    ppermute x22, starting transfers between devices, ring(): lax.ppermute(value, axis, [(i, (i + step) % SIDE) for i in range(SIDE)])  32.9 us
    pallas_call x6, Pallas kernels, last_product(): pl.pallas_call(kernel, grid_spec=pltpu.PrefetchScalarGridSpec(num_scalar_...  23.2 us
    pallas_call x2, Pallas kernels, first_product(): pl.pallas_call(first_kernel, grid_spec=pltpu.PrefetchScalarGridSpec(num_s...  17.8 us
    pallas_call x1, Pallas kernels, pool(): pl.pallas_call(pool_kernel, grid=(columns // tile,), in_specs=[smem(), sm...  4.73 us
    ppermute x1, starting transfers between devices, per_device(): behind = lax.ppermute(teacher[:HALO], ('y', 'x'), down)  3.78 us
    pallas_call x2, Pallas kernels, final(): pl.pallas_call(final_kernel, grid_spec=pltpu.PrefetchScalarGridSpec(num_s...  3.66 us
    unnamed x16, local copies, waits for them, and re-layouts  3.44 us
  transfers between devices with their start and end apart: 30, of which 5 were waited for; matrix products, arithmetic and copies ran while one was open for 1% of the time, Pallas kernels for 34%

profile of v8, /device:TPU:0, one launch (start us, length us, event | category | flops | bytes accessed | tf_op | source)
XLA Modules:
  0.0 148.9 jit_solution(7731784428454484901)
XLA Ops:
  0.0 0.9 fusion
  0.9 1.6 %collective-permute-start = (bf16[16,1024]{1,0:T(8,128)(2,1)S(1)}, bf16[16,1024]{1,0:T(8,128)(2,1)S(1)}, u32[]{:S(2)}, u32[]{:S(2)}) collective-permute-start(bf16[16,1024]{1,0:T(8,128)(2,1)S(1)} %get-tuple-element.94), channel_id=1, source_target_pairs={{0,8},{8,16},{16,24},{24,32},{32,40},{40,48},{48,56},{56,64},{64,7... | collective-permute-start | bytes 98312 | tf_op jit(solution)/shard_map/ppermute | solution.py:545
  2.5 3.8 %collective-permute-start.1 = (bf16[16,1024]{1,0:T(8,128)(2,1)S(1)}, bf16[16,1024]{1,0:T(8,128)(2,1)S(1)}, u32[]{:S(2)}, u32[]{:S(2)}) collective-permute-start(bf16[16,1024]{1,0:T(8,128)(2,1)S(1)} %get-tuple-element.93), channel_id=1, source_target_pairs={{8,0},{16,8},{24,16},{32,24},{40,32},{48,40},{56,48},{64,56},{72,6... | collective-permute-start | bytes 98312 | tf_op jit(solution)/shard_map/ppermute | solution.py:546
  6.3 0.1 pad_add_fusion.place
  6.3 1.4 copy-done.4
  7.8 0.7 copy-done.6
  8.4 1.7 %shard_map.55 = (bf16[208,1024]{1,0:T(8,128)(2,1)S(1)}, bf16[208,1024]{1,0:T(8,128)(2,1)S(1)}, bf16[208,1024]{1,0:T(8,128)(2,1)S(1)}, bf16[208,1024]{1,0:T(8,128)(2,1)S(1)}) custom-call(s32[4]{0:T(128)S(1)} %pad_add_fusion.place, s32[1,4]{1,0:T(1,128)S(1)} %copy-done.6, bf16[192,4096]{1,0:T(8,128)(2,1)S(1)} %copy-done.4), custom_call_target="tpu_custom_call" | custom-call | flops 6291456 | bytes 3145728 | tf_op jit(solution)/shard_map/pallas_call | solution.py:80
  10.1 0.0 collective-permute-done.before
  10.1 0.1 collective-permute-start.2
  10.2 3.2 %collective-permute-start.3 = (bf16[208,1024]{1,0:T(8,128)(2,1)S(1)}, bf16[208,1024]{1,0:T(8,128)(2,1)S(1)}, u32[]{:S(2)}, u32[]{:S(2)}) collective-permute-start(bf16[208,1024]{1,0:T(8,128)(2,1)S(1)} %get-tuple-element.55), channel_id=1, source_target_pairs={{0,24},{8,0},{16,8},{24,16},{1,25},{9,1},{17,9},{25,17},{2,26},{10... | collective-permute-start | bytes 1277960 | tf_op jit(solution)/shard_map/ppermute | solution.py:21
  13.4 0.7 broadcast_in_dim.6.starts
  14.1 0.7 copy-done.5
  14.8 0.7 copy-done.7
  15.5 4.7 %shard_map.56.b0.refs_4_.refs_5_ = bf16[784,1024]{1,0:T(8,128)(2,1)S(1)} custom-call(s32[4]{0:T(128)S(1)} %pad_add_fusion.place, s32[1,4]{1,0:T(1,128)S(1)} %copy-done.7, bf16[16,1024]{1,0:T(8,128)(2,1)S(1)} %collective-permute-done.before, bf16[768,1024]{1,0:T(8,128)(2,1)S(1)} %copy-done.3, bf16[16,1024]{1,0:T(8,128)(2,1)S(1)} %collective-permute-done.1.behind, ...), custom_call_target="tpu_custom_call" | custom-call | flops 402653184 | bytes 4718592 | tf_op jit(solution)/shard_map/pallas_call | solution.py:304
  20.2 11.6 %collective-permute-done.2.p1 = bf16[208,1024]{1,0:T(8,128)(2,1)S(1)} collective-permute-done((bf16[208,1024]{1,0:T(8,128)(2,1)S(1)}, bf16[208,1024]{1,0:T(8,128)(2,1)S(1)}, u32[]{:S(2)}, u32[]{:S(2)}) %collective-permute-start.2) | collective-permute-done | bytes 426016 | tf_op jit(solution)/shard_map/ppermute | solution.py:21
  31.8 0.0 collective-permute-done.3.p2
  31.8 0.0 collective-permute-done.4.p3
  31.8 1.2 shard_map.57
  33.0 0.0 copy-start.2
  33.0 2.0 %collective-permute-start.7 = (bf16[1056,768]{1,0:T(8,128)(2,1)S(1)}, bf16[1056,768]{1,0:T(8,128)(2,1)S(1)}, u32[]{:S(2)}, u32[]{:S(2)}) collective-permute-start(bf16[1056,768]{1,0:T(8,128)(2,1)S(1)} %get-tuple-element.63.a0.refs_0_), channel_id=1, source_target_pairs={{0,2},{2,4},{4,6},{6,0},{1,3},{3,5},{5,7},{7,1},{8,10},{10,12},{12... | collective-permute-start | bytes 4866056 | tf_op jit(solution)/shard_map/ppermute | solution.py:21
  34.9 2.2 %collective-permute-start.8 = (bf16[1056,768]{1,0:T(8,128)(2,1)S(1)}, bf16[1056,768]{1,0:T(8,128)(2,1)S(1)}, u32[]{:S(2)}, u32[]{:S(2)}) collective-permute-start(bf16[1056,768]{1,0:T(8,128)(2,1)S(1)} %get-tuple-element.63.a0.refs_0_), channel_id=1, source_target_pairs={{0,6},{2,0},{4,2},{6,4},{1,7},{3,1},{5,3},{7,5},{8,14},{10,8},{12,... | collective-permute-start | bytes 4866056 | tf_op jit(solution)/shard_map/ppermute | solution.py:21
  37.1 0.9 collective-permute-start.5
  38.0 2.4 %collective-permute-start.6 = (bf16[784,1024]{1,0:T(8,128)(2,1)S(1)}, bf16[784,1024]{1,0:T(8,128)(2,1)S(1)}, u32[]{:S(2)}, u32[]{:S(2)}) collective-permute-start(bf16[784,1024]{1,0:T(8,128)(2,1)S(1)} %shard_map.56.b0.refs_4_.refs_5_), channel_id=1, source_target_pairs={{0,24},{8,0},{16,8},{24,16},{1,25},{9,1},{17,9},{25,17},{2,26},{10... | collective-permute-start | bytes 4816904 | tf_op jit(solution)/shard_map/ppermute | solution.py:21
  40.4 33.3 %collective-permute-done.5.b1.refs_5_.refs_6_ = bf16[784,1024]{1,0:T(8,128)(2,1)S(1)} collective-permute-done((bf16[784,1024]{1,0:T(8,128)(2,1)S(1)}, bf16[784,1024]{1,0:T(8,128)(2,1)S(1)}, u32[]{:S(2)}, u32[]{:S(2)}) %collective-permute-start.5) | collective-permute-done | bytes 1605664 | tf_op jit(solution)/shard_map/ppermute | solution.py:21
  73.6 0.0 collective-permute-done.6.b2.refs_6_.refs_7_
  73.6 0.0 collective-permute-done.9.b0.refs_10_
  73.7 0.1 collective-permute-start.14
  73.8 0.5 collective-permute-start.15
  74.3 0.1 slice.23
  74.3 1.7 %collective-permute-start.13 = (bf16[544,768]{1,0:T(8,128)(2,1)S(1)}, bf16[544,768]{1,0:T(8,128)(2,1)S(1)}, u32[]{:S(2)}, u32[]{:S(2)}) collective-permute-start(bf16[544,768]{1,0:T(8,128)(2,1)S(1)} %slice.23), channel_id=1, source_target_pairs={{0,6},{2,0},{4,2},{6,4},{1,7},{3,1},{5,3},{7,5},{8,14},{10,8},{12,... | collective-permute-start | bytes 2506760 | tf_op jit(solution)/shard_map/ppermute | solution.py:21
  76.1 0.1 slice.20
  76.1 0.1 slice.21
  76.2 0.1 collective-permute-start.10
  76.3 3.2 %collective-permute-start.11 = (bf16[784,512]{1,0:T(8,128)(2,1)S(1)}, bf16[784,512]{1,0:T(8,128)(2,1)S(1)}, u32[]{:S(2)}, u32[]{:S(2)}) collective-permute-start(bf16[784,512]{1,0:T(8,128)(2,1)S(1)} %slice.21), channel_id=1, source_target_pairs={{0,24},{8,0},{16,8},{24,16},{1,25},{9,1},{17,9},{25,17},{2,26},{10... | collective-permute-start | bytes 2408456 | tf_op jit(solution)/shard_map/ppermute | solution.py:21
  79.5 0.1 slice.22
  79.6 0.6 collective-permute-start.12
  80.2 8.9 %shard_map.58.refs_9_ = f32[1024,1024]{1,0:T(8,128)} custom-call(s32[4]{0:T(128)S(1)} %pad_add_fusion.place, bf16[1056,768]{1,0:T(8,128)(2,1)S(1)} %get-tuple-element.63.a0.refs_0_, bf16[1056,768]{1,0:T(8,128)(2,1)S(1)} %collective-permute-done.7.a1.refs_1_, bf16[1056,768]{1,0:T(8,128)(2,1)S(1)} %collective-permute-done.8.a2.refs_2_, ...), custom_call_target="tpu_custom_call" | custom-call | flops 4026531840 | bytes 13729792 | tf_op jit(solution)/shard_map/pallas_call | solution.py:360
  89.1 8.9 %shard_map.59.refs_14_ = f32[1024,1024]{1,0:T(8,128)} custom-call(s32[4]{0:T(128)S(1)} %pad_add_fusion.place, bf16[1056,768]{1,0:T(8,128)(2,1)S(1)} %get-tuple-element.63.a0.refs_0_, bf16[1056,768]{1,0:T(8,128)(2,1)S(1)} %collective-permute-done.7.a1.refs_1_, bf16[1056,768]{1,0:T(8,128)(2,1)S(1)} %collective-permute-done.8.a2.refs_2_, ...), custom_call_target="tpu_custom_call" | custom-call | flops 4026531840 | bytes 13729792 | tf_op jit(solution)/shard_map/pallas_call | solution.py:360
  98.0 1.8 %collective-permute-done.12.refs_3_ = bf16[512,768]{1,0:T(8,128)(2,1)S(1)} collective-permute-done((bf16[512,768]{1,0:T(8,128)(2,1)S(1)}, bf16[512,768]{1,0:T(8,128)(2,1)S(1)}, u32[]{:S(2)}, u32[]{:S(2)}) %collective-permute-start.12) | collective-permute-done | bytes 786464 | tf_op jit(solution)/shard_map/ppermute | solution.py:21
  99.8 0.1 collective-permute-start.25
  99.9 0.5 collective-permute-start.19
  100.4 0.9 shard_map.60.e0
  101.3 0.1 collective-permute-start.16
  101.4 3.2 %collective-permute-start.17 = (f32[24,1024]{1,0:T(8,128)S(1)}, f32[24,1024]{1,0:T(8,128)S(1)}, u32[]{:S(2)}, u32[]{:S(2)}) collective-permute-start(f32[24,1024]{1,0:T(8,128)S(1)} %shard_map.60.e0), channel_id=1, source_target_pairs={{0,96},{32,0},{64,32},{96,64},{1,97},{33,1},{65,33},{97,65},{2,98}... | collective-permute-start | bytes 294920 | tf_op jit(solution)/shard_map/ppermute | solution.py:21
  104.7 3.2 %shard_map.66 = (bf16[256,512]{1,0:T(8,128)(2,1)S(1)}, bf16[256,512]{1,0:T(8,128)(2,1)S(1)}) custom-call(s32[4]{0:T(128)S(1)} %pad_add_fusion.place, bf16[1056,768]{1,0:T(8,128)(2,1)} %copy-done.2, bf16[1056,768]{1,0:T(8,128)(2,1)} %copy-done.1, bf16[1056,768]{1,0:T(8,128)(2,1)} %copy-done, bf16[512,768]{1,0:T(8,128)(2,1)S(1)} %collective-permute-done.12.refs_3_, ...), custom_call_target="tpu_custom_call" | custom-call | flops 805306368 | bytes 3604480 | tf_op jit(solution)/shard_map/pallas_call | solution.py:476
  107.8 0.9 collective-permute-start.26
  108.8 2.4 %collective-permute-start.27 = (bf16[256,512]{1,0:T(8,128)(2,1)S(1)}, bf16[256,512]{1,0:T(8,128)(2,1)S(1)}, u32[]{:S(2)}, u32[]{:S(2)}) collective-permute-start(bf16[256,512]{1,0:T(8,128)(2,1)S(1)} %get-tuple-element.90), channel_id=1, source_target_pairs={{0,96},{32,0},{64,32},{96,64},{1,97},{33,1},{65,33},{97,65},{2,98}... | collective-permute-start | bytes 786440 | tf_op jit(solution)/shard_map/ppermute | solution.py:21
  111.2 3.2 %shard_map.63 = (bf16[256,512]{1,0:T(8,128)(2,1)S(1)}, bf16[256,512]{1,0:T(8,128)(2,1)S(1)}) custom-call(s32[4]{0:T(128)S(1)} %pad_add_fusion.place, bf16[1056,768]{1,0:T(8,128)(2,1)} %copy-done.2, bf16[1056,768]{1,0:T(8,128)(2,1)} %copy-done.1, bf16[1056,768]{1,0:T(8,128)(2,1)} %copy-done, bf16[512,768]{1,0:T(8,128)(2,1)S(1)} %collective-permute-done.12.refs_3_, ...), custom_call_target="tpu_custom_call" | custom-call | flops 805306368 | bytes 3604480 | tf_op jit(solution)/shard_map/pallas_call | solution.py:476
  114.4 0.3 collective-permute-start.21
  114.7 3.0 %collective-permute-start.22 = (bf16[256,512]{1,0:T(8,128)(2,1)S(1)}, bf16[256,512]{1,0:T(8,128)(2,1)S(1)}, u32[]{:S(2)}, u32[]{:S(2)}) collective-permute-start(bf16[256,512]{1,0:T(8,128)(2,1)S(1)} %get-tuple-element.86), channel_id=1, source_target_pairs={{0,96},{32,0},{64,32},{96,64},{1,97},{33,1},{65,33},{97,65},{2,98}... | collective-permute-start | bytes 786440 | tf_op jit(solution)/shard_map/ppermute | solution.py:21
  117.7 4.6 %shard_map.67 = (bf16[256,1024]{1,0:T(8,128)(2,1)S(1)}, bf16[256,1024]{1,0:T(8,128)(2,1)S(1)}) custom-call(s32[4]{0:T(128)S(1)} %pad_add_fusion.place, bf16[1056,768]{1,0:T(8,128)(2,1)} %copy-done.2, bf16[1056,768]{1,0:T(8,128)(2,1)} %copy-done.1, bf16[1056,768]{1,0:T(8,128)(2,1)} %copy-done, bf16[544,768]{1,0:T(8,128)(2,1)S(1)} %collective-permute-done.13.refs_3_, ...), custom_call_target="tpu_custom_call" | custom-call | flops 1610612736 | bytes 4194304 | tf_op jit(solution)/shard_map/pallas_call | solution.py:476
  122.3 1.8 %collective-permute-start.28 = (bf16[256,1024]{1,0:T(8,128)(2,1)S(1)}, bf16[256,1024]{1,0:T(8,128)(2,1)S(1)}, u32[]{:S(2)}, u32[]{:S(2)}) collective-permute-start(bf16[256,1024]{1,0:T(8,128)(2,1)S(1)} %get-tuple-element.91), channel_id=1, source_target_pairs={{0,32},{32,64},{64,96},{96,0},{1,33},{33,65},{65,97},{97,1},{2,34}... | collective-permute-start | bytes 1572872 | tf_op jit(solution)/shard_map/ppermute | solution.py:21
  124.0 1.5 %collective-permute-start.29 = (bf16[256,1024]{1,0:T(8,128)(2,1)S(1)}, bf16[256,1024]{1,0:T(8,128)(2,1)S(1)}, u32[]{:S(2)}, u32[]{:S(2)}) collective-permute-start(bf16[256,1024]{1,0:T(8,128)(2,1)S(1)} %get-tuple-element.92), channel_id=1, source_target_pairs={{0,96},{32,0},{64,32},{96,64},{1,97},{33,1},{65,33},{97,65},{2,98}... | collective-permute-start | bytes 1572872 | tf_op jit(solution)/shard_map/ppermute | solution.py:21
  125.6 4.6 %shard_map.64 = (bf16[256,1024]{1,0:T(8,128)(2,1)S(1)}, bf16[256,1024]{1,0:T(8,128)(2,1)S(1)}) custom-call(s32[4]{0:T(128)S(1)} %pad_add_fusion.place, bf16[1056,768]{1,0:T(8,128)(2,1)} %copy-done.2, bf16[1056,768]{1,0:T(8,128)(2,1)} %copy-done.1, bf16[1056,768]{1,0:T(8,128)(2,1)} %copy-done, bf16[544,768]{1,0:T(8,128)(2,1)S(1)} %collective-permute-done.13.refs_3_, ...), custom_call_target="tpu_custom_call" | custom-call | flops 1610612736 | bytes 4194304 | tf_op jit(solution)/shard_map/pallas_call | solution.py:476
  130.2 0.6 collective-permute-start.23
  130.7 2.7 %collective-permute-start.24 = (bf16[256,1024]{1,0:T(8,128)(2,1)S(1)}, bf16[256,1024]{1,0:T(8,128)(2,1)S(1)}, u32[]{:S(2)}, u32[]{:S(2)}) collective-permute-start(bf16[256,1024]{1,0:T(8,128)(2,1)S(1)} %get-tuple-element.88), channel_id=1, source_target_pairs={{0,96},{32,0},{64,32},{96,64},{1,97},{33,1},{65,33},{97,65},{2,98}... | collective-permute-start | bytes 1572872 | tf_op jit(solution)/shard_map/ppermute | solution.py:21
  133.5 0.2 shard_map.61
  133.7 0.3 collective-permute-start.20
  134.0 1.3 collective-permute-done.20.refs_17_.t_mate
  135.3 3.8 %shard_map.65.base = f32[256,1024]{1,0:T(8,128)S(1)} custom-call(s32[4]{0:T(128)S(1)} %pad_add_fusion.place, bf16[1056,768]{1,0:T(8,128)(2,1)} %copy-done.2, bf16[1056,768]{1,0:T(8,128)(2,1)} %copy-done.1, bf16[1056,768]{1,0:T(8,128)(2,1)} %copy-done, bf16[512,768]{1,0:T(8,128)(2,1)S(1)} %collective-permute-done.12.refs_3_, ...), custom_call_target="tpu_custom_call" | custom-call | flops 805306368 | bytes 3604480 | tf_op jit(solution)/shard_map/pallas_call | solution.py:476
  139.1 3.8 %shard_map.62.base = f32[256,1024]{1,0:T(8,128)S(1)} custom-call(s32[4]{0:T(128)S(1)} %pad_add_fusion.place, bf16[1056,768]{1,0:T(8,128)(2,1)} %copy-done.2, bf16[1056,768]{1,0:T(8,128)(2,1)} %copy-done.1, bf16[1056,768]{1,0:T(8,128)(2,1)} %copy-done, bf16[512,768]{1,0:T(8,128)(2,1)S(1)} %collective-permute-done.12.refs_3_, ...), custom_call_target="tpu_custom_call" | custom-call | flops 805306368 | bytes 3604480 | tf_op jit(solution)/shard_map/pallas_call | solution.py:476
  143.0 1.8 %shard_map.68.rest_0_ = f32[256,2048]{1,0:T(8,128)} custom-call(s32[4]{0:T(128)S(1)} %pad_add_fusion.place, f32[256,1024]{1,0:T(8,128)S(1)} %shard_map.65.base, bf16[256,1024]{1,0:T(8,128)(2,1)S(1)} %collective-permute-done.28.first, bf16[256,1024]{1,0:T(8,128)(2,1)S(1)} %collective-permute-done.29.second, f32[256,128]{1,0:T(8,128)S(1)} %get-tuple-element.83.refs_15_.s_left, ...), custom_call_target="tpu_custom_call" | custom-call | flops 1572864 | bytes 3145728 | tf_op jit(solution)/shard_map/pallas_call | solution.py:516
  144.8 2.2 %collective-permute-done.23.first = bf16[256,1024]{1,0:T(8,128)(2,1)S(1)} collective-permute-done((bf16[256,1024]{1,0:T(8,128)(2,1)S(1)}, bf16[256,1024]{1,0:T(8,128)(2,1)S(1)}, u32[]{:S(2)}, u32[]{:S(2)}) %collective-permute-start.23) | collective-permute-done | bytes 524320 | tf_op jit(solution)/shard_map/ppermute | solution.py:21
  147.0 1.8 %shard_map.69 = f32[256,2048]{1,0:T(8,128)} custom-call(s32[4]{0:T(128)S(1)} %pad_add_fusion.place, f32[256,1024]{1,0:T(8,128)S(1)} %shard_map.62.base, bf16[256,1024]{1,0:T(8,128)(2,1)S(1)} %collective-permute-done.23.first, bf16[256,1024]{1,0:T(8,128)(2,1)S(1)} %collective-permute-done.24.second, ...), custom_call_target="tpu_custom_call", output_to_operand_aliasing={{}: (7, {})} | custom-call | flops 1572864 | bytes 3145728 | tf_op jit(solution)/shard_map/pallas_call | solution.py:516
  (34 shorter events, 0.1 us)
Async XLA Ops:
  0.0 14.1 %copy-start.3 = (bf16[768,1024]{1,0:T(8,128)(2,1)S(1)}, bf16[768,1024]{1,0:T(8,128)(2,1)}, u32[]{:S(2)}) copy-start(bf16[768,1024]{1,0:T(8,128)(2,1)} %teacher.1) | copy-start | bytes 4718596
  0.9 9.2 %collective-permute-start = (bf16[16,1024]{1,0:T(8,128)(2,1)S(1)}, bf16[16,1024]{1,0:T(8,128)(2,1)S(1)}, u32[]{:S(2)}, u32[]{:S(2)}) collective-permute-start(bf16[16,1024]{1,0:T(8,128)(2,1)S(1)} %get-tuple-element.94), channel_id=1, source_target_pairs={{0,8},{8,16},{16,24},{24,32},{32,40},{40,48},{48,56},{56,64},{64,7... | collective-permute-start | bytes 98312 | tf_op jit(solution)/shard_map/ppermute | solution.py:545
  2.5 7.6 %collective-permute-start.1 = (bf16[16,1024]{1,0:T(8,128)(2,1)S(1)}, bf16[16,1024]{1,0:T(8,128)(2,1)S(1)}, u32[]{:S(2)}, u32[]{:S(2)}) collective-permute-start(bf16[16,1024]{1,0:T(8,128)(2,1)S(1)} %get-tuple-element.93), channel_id=1, source_target_pairs={{8,0},{16,8},{24,16},{32,24},{40,32},{48,40},{56,48},{64,56},{72,6... | collective-permute-start | bytes 98312 | tf_op jit(solution)/shard_map/ppermute | solution.py:546
  6.3 1.4 copy-start.4
  7.7 0.7 copy-start.6
  10.1 21.7 %collective-permute-start.2 = (bf16[208,1024]{1,0:T(8,128)(2,1)S(1)}, bf16[208,1024]{1,0:T(8,128)(2,1)S(1)}, u32[]{:S(2)}, u32[]{:S(2)}) collective-permute-start(bf16[208,1024]{1,0:T(8,128)(2,1)S(1)} %get-tuple-element.54), channel_id=1, source_target_pairs={{0,8},{8,16},{16,24},{24,0},{1,9},{9,17},{17,25},{25,1},{2,10},{10... | collective-permute-start | bytes 1277960 | tf_op jit(solution)/shard_map/ppermute | solution.py:21
  10.2 21.6 %collective-permute-start.3 = (bf16[208,1024]{1,0:T(8,128)(2,1)S(1)}, bf16[208,1024]{1,0:T(8,128)(2,1)S(1)}, u32[]{:S(2)}, u32[]{:S(2)}) collective-permute-start(bf16[208,1024]{1,0:T(8,128)(2,1)S(1)} %get-tuple-element.55), channel_id=1, source_target_pairs={{0,24},{8,0},{16,8},{24,16},{1,25},{9,1},{17,9},{25,17},{2,26},{10... | collective-permute-start | bytes 1277960 | tf_op jit(solution)/shard_map/ppermute | solution.py:21
  13.4 18.4 %collective-permute-start.4 = (bf16[208,1024]{1,0:T(8,128)(2,1)S(1)}, bf16[208,1024]{1,0:T(8,128)(2,1)S(1)}, u32[]{:S(2)}, u32[]{:S(2)}) collective-permute-start(bf16[208,1024]{1,0:T(8,128)(2,1)S(1)} %get-tuple-element.56), channel_id=1, source_target_pairs={{0,16},{8,24},{16,0},{24,8},{1,17},{9,25},{17,1},{25,9},{2,18},{10... | collective-permute-start | bytes 1277960 | tf_op jit(solution)/shard_map/ppermute | solution.py:21
  14.1 0.7 copy-start.5
  14.8 0.7 copy-start.7
  33.0 67.5 %copy-start.2 = (bf16[1056,768]{1,0:T(8,128)(2,1)}, bf16[1056,768]{1,0:T(8,128)(2,1)S(1)}, u32[]{:S(2)}) copy-start(bf16[1056,768]{1,0:T(8,128)(2,1)S(1)} %get-tuple-element.63.a0.refs_0_) | copy-start | bytes 4866052
  33.0 40.7 %collective-permute-start.7 = (bf16[1056,768]{1,0:T(8,128)(2,1)S(1)}, bf16[1056,768]{1,0:T(8,128)(2,1)S(1)}, u32[]{:S(2)}, u32[]{:S(2)}) collective-permute-start(bf16[1056,768]{1,0:T(8,128)(2,1)S(1)} %get-tuple-element.63.a0.refs_0_), channel_id=1, source_target_pairs={{0,2},{2,4},{4,6},{6,0},{1,3},{3,5},{5,7},{7,1},{8,10},{10,12},{12... | collective-permute-start | bytes 4866056 | tf_op jit(solution)/shard_map/ppermute | solution.py:21
  34.9 38.7 %collective-permute-start.8 = (bf16[1056,768]{1,0:T(8,128)(2,1)S(1)}, bf16[1056,768]{1,0:T(8,128)(2,1)S(1)}, u32[]{:S(2)}, u32[]{:S(2)}) collective-permute-start(bf16[1056,768]{1,0:T(8,128)(2,1)S(1)} %get-tuple-element.63.a0.refs_0_), channel_id=1, source_target_pairs={{0,6},{2,0},{4,2},{6,4},{1,7},{3,1},{5,3},{7,5},{8,14},{10,8},{12,... | collective-permute-start | bytes 4866056 | tf_op jit(solution)/shard_map/ppermute | solution.py:21
  37.1 36.5 %collective-permute-start.5 = (bf16[784,1024]{1,0:T(8,128)(2,1)S(1)}, bf16[784,1024]{1,0:T(8,128)(2,1)S(1)}, u32[]{:S(2)}, u32[]{:S(2)}) collective-permute-start(bf16[784,1024]{1,0:T(8,128)(2,1)S(1)} %shard_map.56.b0.refs_4_.refs_5_), channel_id=1, source_target_pairs={{0,8},{8,16},{16,24},{24,0},{1,9},{9,17},{17,25},{25,1},{2,10},{10... | collective-permute-start | bytes 4816904 | tf_op jit(solution)/shard_map/ppermute | solution.py:21
  38.0 35.6 %collective-permute-start.6 = (bf16[784,1024]{1,0:T(8,128)(2,1)S(1)}, bf16[784,1024]{1,0:T(8,128)(2,1)S(1)}, u32[]{:S(2)}, u32[]{:S(2)}) collective-permute-start(bf16[784,1024]{1,0:T(8,128)(2,1)S(1)} %shard_map.56.b0.refs_4_.refs_5_), channel_id=1, source_target_pairs={{0,24},{8,0},{16,8},{24,16},{1,25},{9,1},{17,9},{25,17},{2,26},{10... | collective-permute-start | bytes 4816904 | tf_op jit(solution)/shard_map/ppermute | solution.py:21
  40.4 33.3 %collective-permute-start.9 = (bf16[784,1024]{1,0:T(8,128)(2,1)S(1)}, bf16[784,1024]{1,0:T(8,128)(2,1)S(1)}, u32[]{:S(2)}, u32[]{:S(2)}) collective-permute-start(bf16[784,1024]{1,0:T(8,128)(2,1)S(1)} %shard_map.56.b0.refs_4_.refs_5_), channel_id=1, source_target_pairs={{0,1},{1,0},{2,3},{3,2},{4,5},{5,4},{6,7},{7,6},{8,9},{9,8},{10,11... | collective-permute-start | bytes 4816904 | tf_op jit(solution)/shard_map/ppermute | solution.py:29
  73.7 26.8 %copy-start.1 = (bf16[1056,768]{1,0:T(8,128)(2,1)}, bf16[1056,768]{1,0:T(8,128)(2,1)S(1)}, u32[]{:S(2)}) copy-start(bf16[1056,768]{1,0:T(8,128)(2,1)S(1)} %collective-permute-done.7.a1.refs_1_) | copy-start | bytes 4866052
  73.7 26.8 %copy-start = (bf16[1056,768]{1,0:T(8,128)(2,1)}, bf16[1056,768]{1,0:T(8,128)(2,1)S(1)}, u32[]{:S(2)}) copy-start(bf16[1056,768]{1,0:T(8,128)(2,1)S(1)} %collective-permute-done.8.a2.refs_2_) | copy-start | bytes 4866052
  73.7 5.9 %collective-permute-start.14 = (bf16[784,1024]{1,0:T(8,128)(2,1)S(1)}, bf16[784,1024]{1,0:T(8,128)(2,1)S(1)}, u32[]{:S(2)}, u32[]{:S(2)}) collective-permute-start(bf16[784,1024]{1,0:T(8,128)(2,1)S(1)} %collective-permute-done.5.b1.refs_5_.refs_6_), channel_id=1, source_target_pairs={{0,1},{1,0},{2,3},{3,2},{4,5},{5,4},{6,7},{7,6},{8,9},{9,8},{10,11... | collective-permute-start | bytes 4816904 | tf_op jit(solution)/shard_map/ppermute | solution.py:29
  73.8 15.3 %collective-permute-start.15 = (bf16[784,1024]{1,0:T(8,128)(2,1)S(1)}, bf16[784,1024]{1,0:T(8,128)(2,1)S(1)}, u32[]{:S(2)}, u32[]{:S(2)}) collective-permute-start(bf16[784,1024]{1,0:T(8,128)(2,1)S(1)} %collective-permute-done.6.b2.refs_6_.refs_7_), channel_id=1, source_target_pairs={{0,1},{1,0},{2,3},{3,2},{4,5},{5,4},{6,7},{7,6},{8,9},{9,8},{10,11... | collective-permute-start | bytes 4816904 | tf_op jit(solution)/shard_map/ppermute | solution.py:29
  74.3 25.5 %collective-permute-start.13 = (bf16[544,768]{1,0:T(8,128)(2,1)S(1)}, bf16[544,768]{1,0:T(8,128)(2,1)S(1)}, u32[]{:S(2)}, u32[]{:S(2)}) collective-permute-start(bf16[544,768]{1,0:T(8,128)(2,1)S(1)} %slice.23), channel_id=1, source_target_pairs={{0,6},{2,0},{4,2},{6,4},{1,7},{3,1},{5,3},{7,5},{8,14},{10,8},{12,... | collective-permute-start | bytes 2506760 | tf_op jit(solution)/shard_map/ppermute | solution.py:21
  76.2 23.6 %collective-permute-start.10 = (bf16[784,512]{1,0:T(8,128)(2,1)S(1)}, bf16[784,512]{1,0:T(8,128)(2,1)S(1)}, u32[]{:S(2)}, u32[]{:S(2)}) collective-permute-start(bf16[784,512]{1,0:T(8,128)(2,1)S(1)} %slice.20), channel_id=1, source_target_pairs={{0,8},{8,16},{16,24},{24,0},{1,9},{9,17},{17,25},{25,1},{2,10},{10... | collective-permute-start | bytes 2408456 | tf_op jit(solution)/shard_map/ppermute | solution.py:21
  76.3 23.5 %collective-permute-start.11 = (bf16[784,512]{1,0:T(8,128)(2,1)S(1)}, bf16[784,512]{1,0:T(8,128)(2,1)S(1)}, u32[]{:S(2)}, u32[]{:S(2)}) collective-permute-start(bf16[784,512]{1,0:T(8,128)(2,1)S(1)} %slice.21), channel_id=1, source_target_pairs={{0,24},{8,0},{16,8},{24,16},{1,25},{9,1},{17,9},{25,17},{2,26},{10... | collective-permute-start | bytes 2408456 | tf_op jit(solution)/shard_map/ppermute | solution.py:21
  79.6 20.2 %collective-permute-start.12 = (bf16[512,768]{1,0:T(8,128)(2,1)S(1)}, bf16[512,768]{1,0:T(8,128)(2,1)S(1)}, u32[]{:S(2)}, u32[]{:S(2)}) collective-permute-start(bf16[512,768]{1,0:T(8,128)(2,1)S(1)} %slice.22), channel_id=1, source_target_pairs={{0,2},{2,4},{4,6},{6,0},{1,3},{3,5},{5,7},{7,1},{8,10},{10,12},{12... | collective-permute-start | bytes 2359304 | tf_op jit(solution)/shard_map/ppermute | solution.py:21
  99.8 4.8 %collective-permute-start.25 = (bf16[784,512]{1,0:T(8,128)(2,1)S(1)}, bf16[784,512]{1,0:T(8,128)(2,1)S(1)}, u32[]{:S(2)}, u32[]{:S(2)}) collective-permute-start(bf16[784,512]{1,0:T(8,128)(2,1)S(1)} %collective-permute-done.10.refs_7_.refs_8_), channel_id=1, source_target_pairs={{0,1},{1,0},{2,3},{3,2},{4,5},{5,4},{6,7},{7,6},{8,9},{9,8},{10,11... | collective-permute-start | bytes 2408456 | tf_op jit(solution)/shard_map/ppermute | solution.py:29
  99.9 11.2 %collective-permute-start.19 = (bf16[784,512]{1,0:T(8,128)(2,1)S(1)}, bf16[784,512]{1,0:T(8,128)(2,1)S(1)}, u32[]{:S(2)}, u32[]{:S(2)}) collective-permute-start(bf16[784,512]{1,0:T(8,128)(2,1)S(1)} %collective-permute-done.11.refs_8_), channel_id=1, source_target_pairs={{0,1},{1,0},{2,3},{3,2},{4,5},{5,4},{6,7},{7,6},{8,9},{9,8},{10,11... | collective-permute-start | bytes 2408456 | tf_op jit(solution)/shard_map/ppermute | solution.py:29
  101.3 7.4 %collective-permute-start.16 = (f32[24,1024]{1,0:T(8,128)S(1)}, f32[24,1024]{1,0:T(8,128)S(1)}, u32[]{:S(2)}, u32[]{:S(2)}) collective-permute-start(f32[24,1024]{1,0:T(8,128)S(1)} %shard_map.60.e0), channel_id=1, source_target_pairs={{0,32},{32,64},{64,96},{96,0},{1,33},{33,65},{65,97},{97,1},{2,34}... | collective-permute-start | bytes 294920 | tf_op jit(solution)/shard_map/ppermute | solution.py:21
  101.4 9.7 %collective-permute-start.17 = (f32[24,1024]{1,0:T(8,128)S(1)}, f32[24,1024]{1,0:T(8,128)S(1)}, u32[]{:S(2)}, u32[]{:S(2)}) collective-permute-start(f32[24,1024]{1,0:T(8,128)S(1)} %shard_map.60.e0), channel_id=1, source_target_pairs={{0,96},{32,0},{64,32},{96,64},{1,97},{33,1},{65,33},{97,65},{2,98}... | collective-permute-start | bytes 294920 | tf_op jit(solution)/shard_map/ppermute | solution.py:21
  104.7 6.5 %collective-permute-start.18 = (f32[24,1024]{1,0:T(8,128)S(1)}, f32[24,1024]{1,0:T(8,128)S(1)}, u32[]{:S(2)}, u32[]{:S(2)}) collective-permute-start(f32[24,1024]{1,0:T(8,128)S(1)} %shard_map.60.e0), channel_id=1, source_target_pairs={{0,64},{32,96},{64,0},{96,32},{1,65},{33,97},{65,1},{97,33},{2,66}... | collective-permute-start | bytes 294920 | tf_op jit(solution)/shard_map/ppermute | solution.py:21
  107.8 9.8 %collective-permute-start.26 = (bf16[256,512]{1,0:T(8,128)(2,1)S(1)}, bf16[256,512]{1,0:T(8,128)(2,1)S(1)}, u32[]{:S(2)}, u32[]{:S(2)}) collective-permute-start(bf16[256,512]{1,0:T(8,128)(2,1)S(1)} %get-tuple-element.89), channel_id=1, source_target_pairs={{0,32},{32,64},{64,96},{96,0},{1,33},{33,65},{65,97},{97,1},{2,34}... | collective-permute-start | bytes 786440 | tf_op jit(solution)/shard_map/ppermute | solution.py:21
  108.8 8.9 %collective-permute-start.27 = (bf16[256,512]{1,0:T(8,128)(2,1)S(1)}, bf16[256,512]{1,0:T(8,128)(2,1)S(1)}, u32[]{:S(2)}, u32[]{:S(2)}) collective-permute-start(bf16[256,512]{1,0:T(8,128)(2,1)S(1)} %get-tuple-element.90), channel_id=1, source_target_pairs={{0,96},{32,0},{64,32},{96,64},{1,97},{33,1},{65,33},{97,65},{2,98}... | collective-permute-start | bytes 786440 | tf_op jit(solution)/shard_map/ppermute | solution.py:21
  114.4 11.2 %collective-permute-start.21 = (bf16[256,512]{1,0:T(8,128)(2,1)S(1)}, bf16[256,512]{1,0:T(8,128)(2,1)S(1)}, u32[]{:S(2)}, u32[]{:S(2)}) collective-permute-start(bf16[256,512]{1,0:T(8,128)(2,1)S(1)} %get-tuple-element.85), channel_id=1, source_target_pairs={{0,32},{32,64},{64,96},{96,0},{1,33},{33,65},{65,97},{97,1},{2,34}... | collective-permute-start | bytes 786440 | tf_op jit(solution)/shard_map/ppermute | solution.py:21
  114.7 10.9 %collective-permute-start.22 = (bf16[256,512]{1,0:T(8,128)(2,1)S(1)}, bf16[256,512]{1,0:T(8,128)(2,1)S(1)}, u32[]{:S(2)}, u32[]{:S(2)}) collective-permute-start(bf16[256,512]{1,0:T(8,128)(2,1)S(1)} %get-tuple-element.86), channel_id=1, source_target_pairs={{0,96},{32,0},{64,32},{96,64},{1,97},{33,1},{65,33},{97,65},{2,98}... | collective-permute-start | bytes 786440 | tf_op jit(solution)/shard_map/ppermute | solution.py:21
  122.3 20.7 %collective-permute-start.28 = (bf16[256,1024]{1,0:T(8,128)(2,1)S(1)}, bf16[256,1024]{1,0:T(8,128)(2,1)S(1)}, u32[]{:S(2)}, u32[]{:S(2)}) collective-permute-start(bf16[256,1024]{1,0:T(8,128)(2,1)S(1)} %get-tuple-element.91), channel_id=1, source_target_pairs={{0,32},{32,64},{64,96},{96,0},{1,33},{33,65},{65,97},{97,1},{2,34}... | collective-permute-start | bytes 1572872 | tf_op jit(solution)/shard_map/ppermute | solution.py:21
  124.0 18.9 %collective-permute-start.29 = (bf16[256,1024]{1,0:T(8,128)(2,1)S(1)}, bf16[256,1024]{1,0:T(8,128)(2,1)S(1)}, u32[]{:S(2)}, u32[]{:S(2)}) collective-permute-start(bf16[256,1024]{1,0:T(8,128)(2,1)S(1)} %get-tuple-element.92), channel_id=1, source_target_pairs={{0,96},{32,0},{64,32},{96,64},{1,97},{33,1},{65,33},{97,65},{2,98}... | collective-permute-start | bytes 1572872 | tf_op jit(solution)/shard_map/ppermute | solution.py:21
  130.2 16.8 %collective-permute-start.23 = (bf16[256,1024]{1,0:T(8,128)(2,1)S(1)}, bf16[256,1024]{1,0:T(8,128)(2,1)S(1)}, u32[]{:S(2)}, u32[]{:S(2)}) collective-permute-start(bf16[256,1024]{1,0:T(8,128)(2,1)S(1)} %get-tuple-element.87), channel_id=1, source_target_pairs={{0,32},{32,64},{64,96},{96,0},{1,33},{33,65},{65,97},{97,1},{2,34}... | collective-permute-start | bytes 1572872 | tf_op jit(solution)/shard_map/ppermute | solution.py:21
  130.7 16.3 %collective-permute-start.24 = (bf16[256,1024]{1,0:T(8,128)(2,1)S(1)}, bf16[256,1024]{1,0:T(8,128)(2,1)S(1)}, u32[]{:S(2)}, u32[]{:S(2)}) collective-permute-start(bf16[256,1024]{1,0:T(8,128)(2,1)S(1)} %get-tuple-element.88), channel_id=1, source_target_pairs={{0,96},{32,0},{64,32},{96,64},{1,97},{33,1},{65,33},{97,65},{2,98}... | collective-permute-start | bytes 1572872 | tf_op jit(solution)/shard_map/ppermute | solution.py:21
  133.7 1.6 %collective-permute-start.20 = (f32[17,1024]{1,0:T(8,128)S(1)}, f32[17,1024]{1,0:T(8,128)S(1)}, u32[]{:S(2)}, u32[]{:S(2)}) collective-permute-start(f32[17,1024]{1,0:T(8,128)S(1)} %get-tuple-element.84.refs_16_.t_own), channel_id=1, source_target_pairs={{0,1},{1,0},{2,3},{3,2},{4,5},{5,4},{6,7},{7,6},{8,9},{9,8},{10,11... | collective-permute-start | bytes 208904 | tf_op jit(solution)/shard_map/ppermute | solution.py:29

commit v9 on v8

--- a/solution.py
+++ b/solution.py
@@ -34,15 +34,18 @@
 
 
 def in_parts(value):
-    high = value.astype(bf16)
-    rest = value - high.astype(f32)
-    middle = rest.astype(bf16)
-    low = (rest - middle.astype(f32)).astype(bf16)
-    return high, middle, low
+    high = value.astype(bf16).astype(f32)
+    rest = value - high
+    middle = rest.astype(bf16).astype(f32)
+    return high, middle, (rest - middle).astype(bf16).astype(f32)
+
+
+def below(rows):
+    empty = jnp.zeros((EXTRA - len(rows), rows[0].shape[1]), f32)
+    return jnp.concatenate(rows + (empty,), axis=0).astype(bf16)
 
 
 def from_parts(rows):
-    rows = rows.astype(f32)
     return rows[0:1] + rows[1:2] + rows[2:3]
 
 
@@ -70,9 +73,7 @@
             total = jnp.sum(jnp.where(live, value, 0.0), axis=0, keepdims=True)
             dev = jnp.where(live, value - total / count.astype(f32), 0.0)
             square = jnp.sum(dev * dev, axis=0, keepdims=True)
-            rows = in_parts(total) + in_parts(square)
-            rows = rows + (jnp.zeros((EXTRA - len(rows), part), bf16),)
-            outs[r][SUB:, columns] = jnp.concatenate(rows, axis=0)
+            outs[r][SUB:, columns] = below(in_parts(total) + in_parts(square))
 
 
 def pack(place, counts, student):
@@ -98,7 +99,7 @@
     flat = rows.T
     width, depth = flat.shape
     turned[:width, :] = flat
-    moments = jnp.concatenate([p[SUB : SUB + 6, :].astype(f32) for p in pieces], axis=0)
+    moments = jnp.concatenate([p[SUB:, :].astype(f32)[:6] for p in pieces], axis=0)
     rests = [
         jnp.concatenate([moments[3 * m + i : 3 * m + i + 1, depth:] for i in range(3)], axis=1)
         for m in range(8)
@@ -144,12 +145,12 @@
     lane = lax.broadcasted_iota(jnp.int32, (1, half), 1)
     for r in range(SIDE):
         if r < 3:
-            rows = own[r][...]
+            rows = own[r][...].astype(f32)
         else:
-            rows = jnp.concatenate([own[3][...], own[4][...]], axis=1)
+            rows = jnp.concatenate([own[3][...].astype(f32), own[4][...].astype(f32)], axis=1)
         out[r : r + 1, :] = from_parts(rows[0:3])
         out[SIDE + r : SIDE + r + 1, :] = from_parts(rows[3:6])
-        sizes = own[r][...][6:7, :half].astype(f32)
+        sizes = rows[6:7, :half]
         n = jnp.sum(jnp.where(lane < SIDE, sizes, 0.0), axis=1, keepdims=True)
         out[8 + r : 9 + r, :] = jnp.broadcast_to(n, (1, out.shape[1]))
         totals = [from_parts(b[6 * r : 6 * r + 3]) for b in blocks]
@@ -293,9 +294,7 @@
     sizes = jnp.zeros(total.shape, jnp.int32)
     for r in range(SIDE):
         sizes = sizes + jnp.where(lane == r, counts[0, r], 0)
-    rows = in_parts(total) + in_parts(square) + (sizes.astype(f32).astype(bf16),)
-    rows = rows + (jnp.zeros((EXTRA - len(rows), total.shape[1]), bf16),)
-    full[length:, :] = jnp.concatenate(rows, axis=0)
+    full[length:, :] = below(in_parts(total) + in_parts(square) + (sizes.astype(f32),))
 
 
 def pool(place, counts, before, teacher, behind, starts, weights):

time: 149 us -> 149 us (level)
  no operation moved by 1% of the time
where the time goes in v9:
time: 149 us
  Pallas kernels  53.3 us (36%)
  waiting for transfers between devices  50.2 us (34%)
  starting transfers between devices  39.7 us (27%)
  local copies, waits for them, and re-layouts  5.28 us (4%)
    ppermute x22, waiting for transfers between devices, ring(): lax.ppermute(value, axis, [(i, (i + step) % SIDE) for i in range(SIDE)])  48.9 us
    ppermute x22, starting transfers between devices, ring(): lax.ppermute(value, axis, [(i, (i + step) % SIDE) for i in range(SIDE)])  32.9 us
    pallas_call x6, Pallas kernels, last_product(): pl.pallas_call(kernel, grid_spec=pltpu.PrefetchScalarGridSpec(num_scalar_...  23.2 us
    pallas_call x2, Pallas kernels, first_product(): pl.pallas_call(first_kernel, grid_spec=pltpu.PrefetchScalarGridSpec(num_s...  17.8 us
    pallas_call x1, Pallas kernels, pool(): pl.pallas_call(pool_kernel, grid=(columns // tile,), in_specs=[smem(), sm...  4.69 us
    ppermute x1, starting transfers between devices, per_device(): behind = lax.ppermute(teacher[:HALO], ('y', 'x'), down)  3.78 us
    pallas_call x2, Pallas kernels, final(): pl.pallas_call(final_kernel, grid_spec=pltpu.PrefetchScalarGridSpec(num_s...  3.66 us
    unnamed x16, local copies, waits for them, and re-layouts  3.44 us
  transfers between devices with their start and end apart: 30, of which 5 were waited for; matrix products, arithmetic and copies ran while one was open for 1% of the time, Pallas kernels for 34%

profile of v9, /device:TPU:0, one launch (start us, length us, event | category | flops | bytes accessed | tf_op | source)
XLA Modules:
  0.0 148.8 jit_solution(4544655355801476288)
XLA Ops:
  0.0 0.9 fusion
  0.9 1.6 %collective-permute-start = (bf16[16,1024]{1,0:T(8,128)(2,1)S(1)}, bf16[16,1024]{1,0:T(8,128)(2,1)S(1)}, u32[]{:S(2)}, u32[]{:S(2)}) collective-permute-start(bf16[16,1024]{1,0:T(8,128)(2,1)S(1)} %get-tuple-element.94), channel_id=1, source_target_pairs={{0,8},{8,16},{16,24},{24,32},{32,40},{40,48},{48,56},{56,64},{64,7... | collective-permute-start | bytes 98312 | tf_op jit(solution)/shard_map/ppermute | solution.py:544
  2.5 3.8 %collective-permute-start.1 = (bf16[16,1024]{1,0:T(8,128)(2,1)S(1)}, bf16[16,1024]{1,0:T(8,128)(2,1)S(1)}, u32[]{:S(2)}, u32[]{:S(2)}) collective-permute-start(bf16[16,1024]{1,0:T(8,128)(2,1)S(1)} %get-tuple-element.93), channel_id=1, source_target_pairs={{8,0},{16,8},{24,16},{32,24},{40,32},{48,40},{56,48},{64,56},{72,6... | collective-permute-start | bytes 98312 | tf_op jit(solution)/shard_map/ppermute | solution.py:545
  6.3 0.1 pad_add_fusion.place
  6.3 1.4 copy-done.4
  7.8 0.7 copy-done.6
  8.4 1.6 %shard_map.55 = (bf16[208,1024]{1,0:T(8,128)(2,1)S(1)}, bf16[208,1024]{1,0:T(8,128)(2,1)S(1)}, bf16[208,1024]{1,0:T(8,128)(2,1)S(1)}, bf16[208,1024]{1,0:T(8,128)(2,1)S(1)}) custom-call(s32[4]{0:T(128)S(1)} %pad_add_fusion.place, s32[1,4]{1,0:T(1,128)S(1)} %copy-done.6, bf16[192,4096]{1,0:T(8,128)(2,1)S(1)} %copy-done.4), custom_call_target="tpu_custom_call" | custom-call | flops 6291456 | bytes 3145728 | tf_op jit(solution)/shard_map/pallas_call | solution.py:81
  10.0 0.0 collective-permute-done.before
  10.0 0.0 collective-permute-done.1.behind
  10.1 0.1 collective-permute-start.2
  10.1 3.2 %collective-permute-start.3 = (bf16[208,1024]{1,0:T(8,128)(2,1)S(1)}, bf16[208,1024]{1,0:T(8,128)(2,1)S(1)}, u32[]{:S(2)}, u32[]{:S(2)}) collective-permute-start(bf16[208,1024]{1,0:T(8,128)(2,1)S(1)} %get-tuple-element.55), channel_id=1, source_target_pairs={{0,24},{8,0},{16,8},{24,16},{1,25},{9,1},{17,9},{25,17},{2,26},{10... | collective-permute-start | bytes 1277960 | tf_op jit(solution)/shard_map/ppermute | solution.py:21
  13.4 0.7 broadcast_in_dim.6.starts
  14.1 0.7 copy-done.5
  14.8 0.7 copy-done.7
  15.4 4.7 %shard_map.56.b0.refs_4_.refs_5_ = bf16[784,1024]{1,0:T(8,128)(2,1)S(1)} custom-call(s32[4]{0:T(128)S(1)} %pad_add_fusion.place, s32[1,4]{1,0:T(1,128)S(1)} %copy-done.7, bf16[16,1024]{1,0:T(8,128)(2,1)S(1)} %collective-permute-done.before, bf16[768,1024]{1,0:T(8,128)(2,1)S(1)} %copy-done.3, bf16[16,1024]{1,0:T(8,128)(2,1)S(1)} %collective-permute-done.1.behind, ...), custom_call_target="tpu_custom_call" | custom-call | flops 402653184 | bytes 4718592 | tf_op jit(solution)/shard_map/pallas_call | solution.py:303
  20.1 11.6 %collective-permute-done.2.p1 = bf16[208,1024]{1,0:T(8,128)(2,1)S(1)} collective-permute-done((bf16[208,1024]{1,0:T(8,128)(2,1)S(1)}, bf16[208,1024]{1,0:T(8,128)(2,1)S(1)}, u32[]{:S(2)}, u32[]{:S(2)}) %collective-permute-start.2) | collective-permute-done | bytes 426016 | tf_op jit(solution)/shard_map/ppermute | solution.py:21
  31.7 0.0 collective-permute-done.3.p2
  31.7 0.0 collective-permute-done.4.p3
  31.8 1.2 shard_map.57
  32.9 0.0 copy-start.2
  32.9 2.0 %collective-permute-start.7 = (bf16[1056,768]{1,0:T(8,128)(2,1)S(1)}, bf16[1056,768]{1,0:T(8,128)(2,1)S(1)}, u32[]{:S(2)}, u32[]{:S(2)}) collective-permute-start(bf16[1056,768]{1,0:T(8,128)(2,1)S(1)} %get-tuple-element.63.a0.refs_0_), channel_id=1, source_target_pairs={{0,2},{2,4},{4,6},{6,0},{1,3},{3,5},{5,7},{7,1},{8,10},{10,12},{12... | collective-permute-start | bytes 4866056 | tf_op jit(solution)/shard_map/ppermute | solution.py:21
  34.9 2.2 %collective-permute-start.8 = (bf16[1056,768]{1,0:T(8,128)(2,1)S(1)}, bf16[1056,768]{1,0:T(8,128)(2,1)S(1)}, u32[]{:S(2)}, u32[]{:S(2)}) collective-permute-start(bf16[1056,768]{1,0:T(8,128)(2,1)S(1)} %get-tuple-element.63.a0.refs_0_), channel_id=1, source_target_pairs={{0,6},{2,0},{4,2},{6,4},{1,7},{3,1},{5,3},{7,5},{8,14},{10,8},{12,... | collective-permute-start | bytes 4866056 | tf_op jit(solution)/shard_map/ppermute | solution.py:21
  37.1 0.9 collective-permute-start.5
  38.0 2.4 %collective-permute-start.6 = (bf16[784,1024]{1,0:T(8,128)(2,1)S(1)}, bf16[784,1024]{1,0:T(8,128)(2,1)S(1)}, u32[]{:S(2)}, u32[]{:S(2)}) collective-permute-start(bf16[784,1024]{1,0:T(8,128)(2,1)S(1)} %shard_map.56.b0.refs_4_.refs_5_), channel_id=1, source_target_pairs={{0,24},{8,0},{16,8},{24,16},{1,25},{9,1},{17,9},{25,17},{2,26},{10... | collective-permute-start | bytes 4816904 | tf_op jit(solution)/shard_map/ppermute | solution.py:21
  40.4 33.3 %collective-permute-done.5.b1.refs_5_.refs_6_ = bf16[784,1024]{1,0:T(8,128)(2,1)S(1)} collective-permute-done((bf16[784,1024]{1,0:T(8,128)(2,1)S(1)}, bf16[784,1024]{1,0:T(8,128)(2,1)S(1)}, u32[]{:S(2)}, u32[]{:S(2)}) %collective-permute-start.5) | collective-permute-done | bytes 1605664 | tf_op jit(solution)/shard_map/ppermute | solution.py:21
  73.6 0.0 collective-permute-done.7.a1.refs_1_
  73.7 0.1 collective-permute-start.14
  73.8 0.5 collective-permute-start.15
  74.2 0.1 slice.23
  74.3 1.7 %collective-permute-start.13 = (bf16[544,768]{1,0:T(8,128)(2,1)S(1)}, bf16[544,768]{1,0:T(8,128)(2,1)S(1)}, u32[]{:S(2)}, u32[]{:S(2)}) collective-permute-start(bf16[544,768]{1,0:T(8,128)(2,1)S(1)} %slice.23), channel_id=1, source_target_pairs={{0,6},{2,0},{4,2},{6,4},{1,7},{3,1},{5,3},{7,5},{8,14},{10,8},{12,... | collective-permute-start | bytes 2506760 | tf_op jit(solution)/shard_map/ppermute | solution.py:21
  76.0 0.1 slice.20
  76.1 0.1 slice.21
  76.2 0.1 collective-permute-start.10
  76.3 3.2 %collective-permute-start.11 = (bf16[784,512]{1,0:T(8,128)(2,1)S(1)}, bf16[784,512]{1,0:T(8,128)(2,1)S(1)}, u32[]{:S(2)}, u32[]{:S(2)}) collective-permute-start(bf16[784,512]{1,0:T(8,128)(2,1)S(1)} %slice.21), channel_id=1, source_target_pairs={{0,24},{8,0},{16,8},{24,16},{1,25},{9,1},{17,9},{25,17},{2,26},{10... | collective-permute-start | bytes 2408456 | tf_op jit(solution)/shard_map/ppermute | solution.py:21
  79.5 0.1 slice.22
  79.6 0.6 collective-permute-start.12
  80.2 8.9 %shard_map.58.refs_9_ = f32[1024,1024]{1,0:T(8,128)} custom-call(s32[4]{0:T(128)S(1)} %pad_add_fusion.place, bf16[1056,768]{1,0:T(8,128)(2,1)S(1)} %get-tuple-element.63.a0.refs_0_, bf16[1056,768]{1,0:T(8,128)(2,1)S(1)} %collective-permute-done.7.a1.refs_1_, bf16[1056,768]{1,0:T(8,128)(2,1)S(1)} %collective-permute-done.8.a2.refs_2_, ...), custom_call_target="tpu_custom_call" | custom-call | flops 4026531840 | bytes 13729792 | tf_op jit(solution)/shard_map/pallas_call | solution.py:359
  89.0 8.9 %shard_map.59.refs_14_ = f32[1024,1024]{1,0:T(8,128)} custom-call(s32[4]{0:T(128)S(1)} %pad_add_fusion.place, bf16[1056,768]{1,0:T(8,128)(2,1)S(1)} %get-tuple-element.63.a0.refs_0_, bf16[1056,768]{1,0:T(8,128)(2,1)S(1)} %collective-permute-done.7.a1.refs_1_, bf16[1056,768]{1,0:T(8,128)(2,1)S(1)} %collective-permute-done.8.a2.refs_2_, ...), custom_call_target="tpu_custom_call" | custom-call | flops 4026531840 | bytes 13729792 | tf_op jit(solution)/shard_map/pallas_call | solution.py:359
  98.0 1.8 %collective-permute-done.12.refs_3_ = bf16[512,768]{1,0:T(8,128)(2,1)S(1)} collective-permute-done((bf16[512,768]{1,0:T(8,128)(2,1)S(1)}, bf16[512,768]{1,0:T(8,128)(2,1)S(1)}, u32[]{:S(2)}, u32[]{:S(2)}) %collective-permute-start.12) | collective-permute-done | bytes 786464 | tf_op jit(solution)/shard_map/ppermute | solution.py:21
  99.8 0.1 collective-permute-start.25
  99.9 0.5 collective-permute-start.19
  100.4 0.9 shard_map.60.e0
  101.3 0.1 collective-permute-start.16
  101.4 3.2 %collective-permute-start.17 = (f32[24,1024]{1,0:T(8,128)S(1)}, f32[24,1024]{1,0:T(8,128)S(1)}, u32[]{:S(2)}, u32[]{:S(2)}) collective-permute-start(f32[24,1024]{1,0:T(8,128)S(1)} %shard_map.60.e0), channel_id=1, source_target_pairs={{0,96},{32,0},{64,32},{96,64},{1,97},{33,1},{65,33},{97,65},{2,98}... | collective-permute-start | bytes 294920 | tf_op jit(solution)/shard_map/ppermute | solution.py:21
  104.6 3.2 %shard_map.66 = (bf16[256,512]{1,0:T(8,128)(2,1)S(1)}, bf16[256,512]{1,0:T(8,128)(2,1)S(1)}) custom-call(s32[4]{0:T(128)S(1)} %pad_add_fusion.place, bf16[1056,768]{1,0:T(8,128)(2,1)} %copy-done.2, bf16[1056,768]{1,0:T(8,128)(2,1)} %copy-done.1, bf16[1056,768]{1,0:T(8,128)(2,1)} %copy-done, bf16[512,768]{1,0:T(8,128)(2,1)S(1)} %collective-permute-done.12.refs_3_, ...), custom_call_target="tpu_custom_call" | custom-call | flops 805306368 | bytes 3604480 | tf_op jit(solution)/shard_map/pallas_call | solution.py:475
  107.8 0.9 collective-permute-start.26
  108.7 2.4 %collective-permute-start.27 = (bf16[256,512]{1,0:T(8,128)(2,1)S(1)}, bf16[256,512]{1,0:T(8,128)(2,1)S(1)}, u32[]{:S(2)}, u32[]{:S(2)}) collective-permute-start(bf16[256,512]{1,0:T(8,128)(2,1)S(1)} %get-tuple-element.90), channel_id=1, source_target_pairs={{0,96},{32,0},{64,32},{96,64},{1,97},{33,1},{65,33},{97,65},{2,98}... | collective-permute-start | bytes 786440 | tf_op jit(solution)/shard_map/ppermute | solution.py:21
  111.1 3.2 %shard_map.63 = (bf16[256,512]{1,0:T(8,128)(2,1)S(1)}, bf16[256,512]{1,0:T(8,128)(2,1)S(1)}) custom-call(s32[4]{0:T(128)S(1)} %pad_add_fusion.place, bf16[1056,768]{1,0:T(8,128)(2,1)} %copy-done.2, bf16[1056,768]{1,0:T(8,128)(2,1)} %copy-done.1, bf16[1056,768]{1,0:T(8,128)(2,1)} %copy-done, bf16[512,768]{1,0:T(8,128)(2,1)S(1)} %collective-permute-done.12.refs_3_, ...), custom_call_target="tpu_custom_call" | custom-call | flops 805306368 | bytes 3604480 | tf_op jit(solution)/shard_map/pallas_call | solution.py:475
  114.3 0.3 collective-permute-start.21
  114.7 3.0 %collective-permute-start.22 = (bf16[256,512]{1,0:T(8,128)(2,1)S(1)}, bf16[256,512]{1,0:T(8,128)(2,1)S(1)}, u32[]{:S(2)}, u32[]{:S(2)}) collective-permute-start(bf16[256,512]{1,0:T(8,128)(2,1)S(1)} %get-tuple-element.86), channel_id=1, source_target_pairs={{0,96},{32,0},{64,32},{96,64},{1,97},{33,1},{65,33},{97,65},{2,98}... | collective-permute-start | bytes 786440 | tf_op jit(solution)/shard_map/ppermute | solution.py:21
  117.6 4.6 %shard_map.67 = (bf16[256,1024]{1,0:T(8,128)(2,1)S(1)}, bf16[256,1024]{1,0:T(8,128)(2,1)S(1)}) custom-call(s32[4]{0:T(128)S(1)} %pad_add_fusion.place, bf16[1056,768]{1,0:T(8,128)(2,1)} %copy-done.2, bf16[1056,768]{1,0:T(8,128)(2,1)} %copy-done.1, bf16[1056,768]{1,0:T(8,128)(2,1)} %copy-done, bf16[544,768]{1,0:T(8,128)(2,1)S(1)} %collective-permute-done.13.refs_3_, ...), custom_call_target="tpu_custom_call" | custom-call | flops 1610612736 | bytes 4194304 | tf_op jit(solution)/shard_map/pallas_call | solution.py:475
  122.2 1.8 %collective-permute-start.28 = (bf16[256,1024]{1,0:T(8,128)(2,1)S(1)}, bf16[256,1024]{1,0:T(8,128)(2,1)S(1)}, u32[]{:S(2)}, u32[]{:S(2)}) collective-permute-start(bf16[256,1024]{1,0:T(8,128)(2,1)S(1)} %get-tuple-element.91), channel_id=1, source_target_pairs={{0,32},{32,64},{64,96},{96,0},{1,33},{33,65},{65,97},{97,1},{2,34}... | collective-permute-start | bytes 1572872 | tf_op jit(solution)/shard_map/ppermute | solution.py:21
  124.0 1.5 %collective-permute-start.29 = (bf16[256,1024]{1,0:T(8,128)(2,1)S(1)}, bf16[256,1024]{1,0:T(8,128)(2,1)S(1)}, u32[]{:S(2)}, u32[]{:S(2)}) collective-permute-start(bf16[256,1024]{1,0:T(8,128)(2,1)S(1)} %get-tuple-element.92), channel_id=1, source_target_pairs={{0,96},{32,0},{64,32},{96,64},{1,97},{33,1},{65,33},{97,65},{2,98}... | collective-permute-start | bytes 1572872 | tf_op jit(solution)/shard_map/ppermute | solution.py:21
  125.6 4.6 %shard_map.64 = (bf16[256,1024]{1,0:T(8,128)(2,1)S(1)}, bf16[256,1024]{1,0:T(8,128)(2,1)S(1)}) custom-call(s32[4]{0:T(128)S(1)} %pad_add_fusion.place, bf16[1056,768]{1,0:T(8,128)(2,1)} %copy-done.2, bf16[1056,768]{1,0:T(8,128)(2,1)} %copy-done.1, bf16[1056,768]{1,0:T(8,128)(2,1)} %copy-done, bf16[544,768]{1,0:T(8,128)(2,1)S(1)} %collective-permute-done.13.refs_3_, ...), custom_call_target="tpu_custom_call" | custom-call | flops 1610612736 | bytes 4194304 | tf_op jit(solution)/shard_map/pallas_call | solution.py:475
  130.2 0.6 collective-permute-start.23
  130.7 2.7 %collective-permute-start.24 = (bf16[256,1024]{1,0:T(8,128)(2,1)S(1)}, bf16[256,1024]{1,0:T(8,128)(2,1)S(1)}, u32[]{:S(2)}, u32[]{:S(2)}) collective-permute-start(bf16[256,1024]{1,0:T(8,128)(2,1)S(1)} %get-tuple-element.88), channel_id=1, source_target_pairs={{0,96},{32,0},{64,32},{96,64},{1,97},{33,1},{65,33},{97,65},{2,98}... | collective-permute-start | bytes 1572872 | tf_op jit(solution)/shard_map/ppermute | solution.py:21
  133.5 0.2 shard_map.61
  133.7 0.3 collective-permute-start.20
  134.0 1.3 collective-permute-done.20.refs_17_.t_mate
  135.3 3.8 %shard_map.65.base = f32[256,1024]{1,0:T(8,128)S(1)} custom-call(s32[4]{0:T(128)S(1)} %pad_add_fusion.place, bf16[1056,768]{1,0:T(8,128)(2,1)} %copy-done.2, bf16[1056,768]{1,0:T(8,128)(2,1)} %copy-done.1, bf16[1056,768]{1,0:T(8,128)(2,1)} %copy-done, bf16[512,768]{1,0:T(8,128)(2,1)S(1)} %collective-permute-done.12.refs_3_, ...), custom_call_target="tpu_custom_call" | custom-call | flops 805306368 | bytes 3604480 | tf_op jit(solution)/shard_map/pallas_call | solution.py:475
  139.1 3.8 %shard_map.62.base = f32[256,1024]{1,0:T(8,128)S(1)} custom-call(s32[4]{0:T(128)S(1)} %pad_add_fusion.place, bf16[1056,768]{1,0:T(8,128)(2,1)} %copy-done.2, bf16[1056,768]{1,0:T(8,128)(2,1)} %copy-done.1, bf16[1056,768]{1,0:T(8,128)(2,1)} %copy-done, bf16[512,768]{1,0:T(8,128)(2,1)S(1)} %collective-permute-done.12.refs_3_, ...), custom_call_target="tpu_custom_call" | custom-call | flops 805306368 | bytes 3604480 | tf_op jit(solution)/shard_map/pallas_call | solution.py:475
  143.0 1.8 %shard_map.68.rest_0_ = f32[256,2048]{1,0:T(8,128)} custom-call(s32[4]{0:T(128)S(1)} %pad_add_fusion.place, f32[256,1024]{1,0:T(8,128)S(1)} %shard_map.65.base, bf16[256,1024]{1,0:T(8,128)(2,1)S(1)} %collective-permute-done.28.first, bf16[256,1024]{1,0:T(8,128)(2,1)S(1)} %collective-permute-done.29.second, f32[256,128]{1,0:T(8,128)S(1)} %get-tuple-element.83.refs_15_.s_left, ...), custom_call_target="tpu_custom_call" | custom-call | flops 1572864 | bytes 3145728 | tf_op jit(solution)/shard_map/pallas_call | solution.py:515
  144.8 2.2 %collective-permute-done.23.first = bf16[256,1024]{1,0:T(8,128)(2,1)S(1)} collective-permute-done((bf16[256,1024]{1,0:T(8,128)(2,1)S(1)}, bf16[256,1024]{1,0:T(8,128)(2,1)S(1)}, u32[]{:S(2)}, u32[]{:S(2)}) %collective-permute-start.23) | collective-permute-done | bytes 524320 | tf_op jit(solution)/shard_map/ppermute | solution.py:21
  147.0 1.8 %shard_map.69 = f32[256,2048]{1,0:T(8,128)} custom-call(s32[4]{0:T(128)S(1)} %pad_add_fusion.place, f32[256,1024]{1,0:T(8,128)S(1)} %shard_map.62.base, bf16[256,1024]{1,0:T(8,128)(2,1)S(1)} %collective-permute-done.23.first, bf16[256,1024]{1,0:T(8,128)(2,1)S(1)} %collective-permute-done.24.second, ...), custom_call_target="tpu_custom_call", output_to_operand_aliasing={{}: (7, {})} | custom-call | flops 1572864 | bytes 3145728 | tf_op jit(solution)/shard_map/pallas_call | solution.py:515
  (34 shorter events, 0.1 us)
Async XLA Ops:
  0.0 14.1 %copy-start.3 = (bf16[768,1024]{1,0:T(8,128)(2,1)S(1)}, bf16[768,1024]{1,0:T(8,128)(2,1)}, u32[]{:S(2)}) copy-start(bf16[768,1024]{1,0:T(8,128)(2,1)} %teacher.1) | copy-start | bytes 4718596
  0.9 9.1 %collective-permute-start = (bf16[16,1024]{1,0:T(8,128)(2,1)S(1)}, bf16[16,1024]{1,0:T(8,128)(2,1)S(1)}, u32[]{:S(2)}, u32[]{:S(2)}) collective-permute-start(bf16[16,1024]{1,0:T(8,128)(2,1)S(1)} %get-tuple-element.94), channel_id=1, source_target_pairs={{0,8},{8,16},{16,24},{24,32},{32,40},{40,48},{48,56},{56,64},{64,7... | collective-permute-start | bytes 98312 | tf_op jit(solution)/shard_map/ppermute | solution.py:544
  2.5 7.6 %collective-permute-start.1 = (bf16[16,1024]{1,0:T(8,128)(2,1)S(1)}, bf16[16,1024]{1,0:T(8,128)(2,1)S(1)}, u32[]{:S(2)}, u32[]{:S(2)}) collective-permute-start(bf16[16,1024]{1,0:T(8,128)(2,1)S(1)} %get-tuple-element.93), channel_id=1, source_target_pairs={{8,0},{16,8},{24,16},{32,24},{40,32},{48,40},{56,48},{64,56},{72,6... | collective-permute-start | bytes 98312 | tf_op jit(solution)/shard_map/ppermute | solution.py:545
  6.3 1.4 copy-start.4
  7.7 0.7 copy-start.6
  10.1 21.7 %collective-permute-start.2 = (bf16[208,1024]{1,0:T(8,128)(2,1)S(1)}, bf16[208,1024]{1,0:T(8,128)(2,1)S(1)}, u32[]{:S(2)}, u32[]{:S(2)}) collective-permute-start(bf16[208,1024]{1,0:T(8,128)(2,1)S(1)} %get-tuple-element.54), channel_id=1, source_target_pairs={{0,8},{8,16},{16,24},{24,0},{1,9},{9,17},{17,25},{25,1},{2,10},{10... | collective-permute-start | bytes 1277960 | tf_op jit(solution)/shard_map/ppermute | solution.py:21
  10.1 21.6 %collective-permute-start.3 = (bf16[208,1024]{1,0:T(8,128)(2,1)S(1)}, bf16[208,1024]{1,0:T(8,128)(2,1)S(1)}, u32[]{:S(2)}, u32[]{:S(2)}) collective-permute-start(bf16[208,1024]{1,0:T(8,128)(2,1)S(1)} %get-tuple-element.55), channel_id=1, source_target_pairs={{0,24},{8,0},{16,8},{24,16},{1,25},{9,1},{17,9},{25,17},{2,26},{10... | collective-permute-start | bytes 1277960 | tf_op jit(solution)/shard_map/ppermute | solution.py:21
  13.4 18.4 %collective-permute-start.4 = (bf16[208,1024]{1,0:T(8,128)(2,1)S(1)}, bf16[208,1024]{1,0:T(8,128)(2,1)S(1)}, u32[]{:S(2)}, u32[]{:S(2)}) collective-permute-start(bf16[208,1024]{1,0:T(8,128)(2,1)S(1)} %get-tuple-element.56), channel_id=1, source_target_pairs={{0,16},{8,24},{16,0},{24,8},{1,17},{9,25},{17,1},{25,9},{2,18},{10... | collective-permute-start | bytes 1277960 | tf_op jit(solution)/shard_map/ppermute | solution.py:21
  14.1 0.7 copy-start.5
  14.8 0.7 copy-start.7
  32.9 67.5 %copy-start.2 = (bf16[1056,768]{1,0:T(8,128)(2,1)}, bf16[1056,768]{1,0:T(8,128)(2,1)S(1)}, u32[]{:S(2)}) copy-start(bf16[1056,768]{1,0:T(8,128)(2,1)S(1)} %get-tuple-element.63.a0.refs_0_) | copy-start | bytes 4866052
  32.9 40.7 %collective-permute-start.7 = (bf16[1056,768]{1,0:T(8,128)(2,1)S(1)}, bf16[1056,768]{1,0:T(8,128)(2,1)S(1)}, u32[]{:S(2)}, u32[]{:S(2)}) collective-permute-start(bf16[1056,768]{1,0:T(8,128)(2,1)S(1)} %get-tuple-element.63.a0.refs_0_), channel_id=1, source_target_pairs={{0,2},{2,4},{4,6},{6,0},{1,3},{3,5},{5,7},{7,1},{8,10},{10,12},{12... | collective-permute-start | bytes 4866056 | tf_op jit(solution)/shard_map/ppermute | solution.py:21
  34.9 38.7 %collective-permute-start.8 = (bf16[1056,768]{1,0:T(8,128)(2,1)S(1)}, bf16[1056,768]{1,0:T(8,128)(2,1)S(1)}, u32[]{:S(2)}, u32[]{:S(2)}) collective-permute-start(bf16[1056,768]{1,0:T(8,128)(2,1)S(1)} %get-tuple-element.63.a0.refs_0_), channel_id=1, source_target_pairs={{0,6},{2,0},{4,2},{6,4},{1,7},{3,1},{5,3},{7,5},{8,14},{10,8},{12,... | collective-permute-start | bytes 4866056 | tf_op jit(solution)/shard_map/ppermute | solution.py:21
  37.1 36.5 %collective-permute-start.5 = (bf16[784,1024]{1,0:T(8,128)(2,1)S(1)}, bf16[784,1024]{1,0:T(8,128)(2,1)S(1)}, u32[]{:S(2)}, u32[]{:S(2)}) collective-permute-start(bf16[784,1024]{1,0:T(8,128)(2,1)S(1)} %shard_map.56.b0.refs_4_.refs_5_), channel_id=1, source_target_pairs={{0,8},{8,16},{16,24},{24,0},{1,9},{9,17},{17,25},{25,1},{2,10},{10... | collective-permute-start | bytes 4816904 | tf_op jit(solution)/shard_map/ppermute | solution.py:21
  38.0 35.6 %collective-permute-start.6 = (bf16[784,1024]{1,0:T(8,128)(2,1)S(1)}, bf16[784,1024]{1,0:T(8,128)(2,1)S(1)}, u32[]{:S(2)}, u32[]{:S(2)}) collective-permute-start(bf16[784,1024]{1,0:T(8,128)(2,1)S(1)} %shard_map.56.b0.refs_4_.refs_5_), channel_id=1, source_target_pairs={{0,24},{8,0},{16,8},{24,16},{1,25},{9,1},{17,9},{25,17},{2,26},{10... | collective-permute-start | bytes 4816904 | tf_op jit(solution)/shard_map/ppermute | solution.py:21
  40.4 33.3 %collective-permute-start.9 = (bf16[784,1024]{1,0:T(8,128)(2,1)S(1)}, bf16[784,1024]{1,0:T(8,128)(2,1)S(1)}, u32[]{:S(2)}, u32[]{:S(2)}) collective-permute-start(bf16[784,1024]{1,0:T(8,128)(2,1)S(1)} %shard_map.56.b0.refs_4_.refs_5_), channel_id=1, source_target_pairs={{0,1},{1,0},{2,3},{3,2},{4,5},{5,4},{6,7},{7,6},{8,9},{9,8},{10,11... | collective-permute-start | bytes 4816904 | tf_op jit(solution)/shard_map/ppermute | solution.py:29
  73.6 26.8 %copy-start.1 = (bf16[1056,768]{1,0:T(8,128)(2,1)}, bf16[1056,768]{1,0:T(8,128)(2,1)S(1)}, u32[]{:S(2)}) copy-start(bf16[1056,768]{1,0:T(8,128)(2,1)S(1)} %collective-permute-done.7.a1.refs_1_) | copy-start | bytes 4866052
  73.6 26.8 %copy-start = (bf16[1056,768]{1,0:T(8,128)(2,1)}, bf16[1056,768]{1,0:T(8,128)(2,1)S(1)}, u32[]{:S(2)}) copy-start(bf16[1056,768]{1,0:T(8,128)(2,1)S(1)} %collective-permute-done.8.a2.refs_2_) | copy-start | bytes 4866052
  73.7 5.9 %collective-permute-start.14 = (bf16[784,1024]{1,0:T(8,128)(2,1)S(1)}, bf16[784,1024]{1,0:T(8,128)(2,1)S(1)}, u32[]{:S(2)}, u32[]{:S(2)}) collective-permute-start(bf16[784,1024]{1,0:T(8,128)(2,1)S(1)} %collective-permute-done.5.b1.refs_5_.refs_6_), channel_id=1, source_target_pairs={{0,1},{1,0},{2,3},{3,2},{4,5},{5,4},{6,7},{7,6},{8,9},{9,8},{10,11... | collective-permute-start | bytes 4816904 | tf_op jit(solution)/shard_map/ppermute | solution.py:29
  73.8 15.3 %collective-permute-start.15 = (bf16[784,1024]{1,0:T(8,128)(2,1)S(1)}, bf16[784,1024]{1,0:T(8,128)(2,1)S(1)}, u32[]{:S(2)}, u32[]{:S(2)}) collective-permute-start(bf16[784,1024]{1,0:T(8,128)(2,1)S(1)} %collective-permute-done.6.b2.refs_6_.refs_7_), channel_id=1, source_target_pairs={{0,1},{1,0},{2,3},{3,2},{4,5},{5,4},{6,7},{7,6},{8,9},{9,8},{10,11... | collective-permute-start | bytes 4816904 | tf_op jit(solution)/shard_map/ppermute | solution.py:29
  74.3 25.5 %collective-permute-start.13 = (bf16[544,768]{1,0:T(8,128)(2,1)S(1)}, bf16[544,768]{1,0:T(8,128)(2,1)S(1)}, u32[]{:S(2)}, u32[]{:S(2)}) collective-permute-start(bf16[544,768]{1,0:T(8,128)(2,1)S(1)} %slice.23), channel_id=1, source_target_pairs={{0,6},{2,0},{4,2},{6,4},{1,7},{3,1},{5,3},{7,5},{8,14},{10,8},{12,... | collective-permute-start | bytes 2506760 | tf_op jit(solution)/shard_map/ppermute | solution.py:21
  76.2 23.6 %collective-permute-start.10 = (bf16[784,512]{1,0:T(8,128)(2,1)S(1)}, bf16[784,512]{1,0:T(8,128)(2,1)S(1)}, u32[]{:S(2)}, u32[]{:S(2)}) collective-permute-start(bf16[784,512]{1,0:T(8,128)(2,1)S(1)} %slice.20), channel_id=1, source_target_pairs={{0,8},{8,16},{16,24},{24,0},{1,9},{9,17},{17,25},{25,1},{2,10},{10... | collective-permute-start | bytes 2408456 | tf_op jit(solution)/shard_map/ppermute | solution.py:21
  76.3 23.5 %collective-permute-start.11 = (bf16[784,512]{1,0:T(8,128)(2,1)S(1)}, bf16[784,512]{1,0:T(8,128)(2,1)S(1)}, u32[]{:S(2)}, u32[]{:S(2)}) collective-permute-start(bf16[784,512]{1,0:T(8,128)(2,1)S(1)} %slice.21), channel_id=1, source_target_pairs={{0,24},{8,0},{16,8},{24,16},{1,25},{9,1},{17,9},{25,17},{2,26},{10... | collective-permute-start | bytes 2408456 | tf_op jit(solution)/shard_map/ppermute | solution.py:21
  79.6 20.2 %collective-permute-start.12 = (bf16[512,768]{1,0:T(8,128)(2,1)S(1)}, bf16[512,768]{1,0:T(8,128)(2,1)S(1)}, u32[]{:S(2)}, u32[]{:S(2)}) collective-permute-start(bf16[512,768]{1,0:T(8,128)(2,1)S(1)} %slice.22), channel_id=1, source_target_pairs={{0,2},{2,4},{4,6},{6,0},{1,3},{3,5},{5,7},{7,1},{8,10},{10,12},{12... | collective-permute-start | bytes 2359304 | tf_op jit(solution)/shard_map/ppermute | solution.py:21
  99.8 4.8 %collective-permute-start.25 = (bf16[784,512]{1,0:T(8,128)(2,1)S(1)}, bf16[784,512]{1,0:T(8,128)(2,1)S(1)}, u32[]{:S(2)}, u32[]{:S(2)}) collective-permute-start(bf16[784,512]{1,0:T(8,128)(2,1)S(1)} %collective-permute-done.10.refs_7_.refs_8_), channel_id=1, source_target_pairs={{0,1},{1,0},{2,3},{3,2},{4,5},{5,4},{6,7},{7,6},{8,9},{9,8},{10,11... | collective-permute-start | bytes 2408456 | tf_op jit(solution)/shard_map/ppermute | solution.py:29
  99.9 11.2 %collective-permute-start.19 = (bf16[784,512]{1,0:T(8,128)(2,1)S(1)}, bf16[784,512]{1,0:T(8,128)(2,1)S(1)}, u32[]{:S(2)}, u32[]{:S(2)}) collective-permute-start(bf16[784,512]{1,0:T(8,128)(2,1)S(1)} %collective-permute-done.11.refs_8_), channel_id=1, source_target_pairs={{0,1},{1,0},{2,3},{3,2},{4,5},{5,4},{6,7},{7,6},{8,9},{9,8},{10,11... | collective-permute-start | bytes 2408456 | tf_op jit(solution)/shard_map/ppermute | solution.py:29
  101.3 7.4 %collective-permute-start.16 = (f32[24,1024]{1,0:T(8,128)S(1)}, f32[24,1024]{1,0:T(8,128)S(1)}, u32[]{:S(2)}, u32[]{:S(2)}) collective-permute-start(f32[24,1024]{1,0:T(8,128)S(1)} %shard_map.60.e0), channel_id=1, source_target_pairs={{0,32},{32,64},{64,96},{96,0},{1,33},{33,65},{65,97},{97,1},{2,34}... | collective-permute-start | bytes 294920 | tf_op jit(solution)/shard_map/ppermute | solution.py:21
  101.4 9.7 %collective-permute-start.17 = (f32[24,1024]{1,0:T(8,128)S(1)}, f32[24,1024]{1,0:T(8,128)S(1)}, u32[]{:S(2)}, u32[]{:S(2)}) collective-permute-start(f32[24,1024]{1,0:T(8,128)S(1)} %shard_map.60.e0), channel_id=1, source_target_pairs={{0,96},{32,0},{64,32},{96,64},{1,97},{33,1},{65,33},{97,65},{2,98}... | collective-permute-start | bytes 294920 | tf_op jit(solution)/shard_map/ppermute | solution.py:21
  104.6 6.5 %collective-permute-start.18 = (f32[24,1024]{1,0:T(8,128)S(1)}, f32[24,1024]{1,0:T(8,128)S(1)}, u32[]{:S(2)}, u32[]{:S(2)}) collective-permute-start(f32[24,1024]{1,0:T(8,128)S(1)} %shard_map.60.e0), channel_id=1, source_target_pairs={{0,64},{32,96},{64,0},{96,32},{1,65},{33,97},{65,1},{97,33},{2,66}... | collective-permute-start | bytes 294920 | tf_op jit(solution)/shard_map/ppermute | solution.py:21
  107.8 9.8 %collective-permute-start.26 = (bf16[256,512]{1,0:T(8,128)(2,1)S(1)}, bf16[256,512]{1,0:T(8,128)(2,1)S(1)}, u32[]{:S(2)}, u32[]{:S(2)}) collective-permute-start(bf16[256,512]{1,0:T(8,128)(2,1)S(1)} %get-tuple-element.89), channel_id=1, source_target_pairs={{0,32},{32,64},{64,96},{96,0},{1,33},{33,65},{65,97},{97,1},{2,34}... | collective-permute-start | bytes 786440 | tf_op jit(solution)/shard_map/ppermute | solution.py:21
  108.7 8.9 %collective-permute-start.27 = (bf16[256,512]{1,0:T(8,128)(2,1)S(1)}, bf16[256,512]{1,0:T(8,128)(2,1)S(1)}, u32[]{:S(2)}, u32[]{:S(2)}) collective-permute-start(bf16[256,512]{1,0:T(8,128)(2,1)S(1)} %get-tuple-element.90), channel_id=1, source_target_pairs={{0,96},{32,0},{64,32},{96,64},{1,97},{33,1},{65,33},{97,65},{2,98}... | collective-permute-start | bytes 786440 | tf_op jit(solution)/shard_map/ppermute | solution.py:21
  114.3 11.2 %collective-permute-start.21 = (bf16[256,512]{1,0:T(8,128)(2,1)S(1)}, bf16[256,512]{1,0:T(8,128)(2,1)S(1)}, u32[]{:S(2)}, u32[]{:S(2)}) collective-permute-start(bf16[256,512]{1,0:T(8,128)(2,1)S(1)} %get-tuple-element.85), channel_id=1, source_target_pairs={{0,32},{32,64},{64,96},{96,0},{1,33},{33,65},{65,97},{97,1},{2,34}... | collective-permute-start | bytes 786440 | tf_op jit(solution)/shard_map/ppermute | solution.py:21
  114.7 10.9 %collective-permute-start.22 = (bf16[256,512]{1,0:T(8,128)(2,1)S(1)}, bf16[256,512]{1,0:T(8,128)(2,1)S(1)}, u32[]{:S(2)}, u32[]{:S(2)}) collective-permute-start(bf16[256,512]{1,0:T(8,128)(2,1)S(1)} %get-tuple-element.86), channel_id=1, source_target_pairs={{0,96},{32,0},{64,32},{96,64},{1,97},{33,1},{65,33},{97,65},{2,98}... | collective-permute-start | bytes 786440 | tf_op jit(solution)/shard_map/ppermute | solution.py:21
  122.2 20.7 %collective-permute-start.28 = (bf16[256,1024]{1,0:T(8,128)(2,1)S(1)}, bf16[256,1024]{1,0:T(8,128)(2,1)S(1)}, u32[]{:S(2)}, u32[]{:S(2)}) collective-permute-start(bf16[256,1024]{1,0:T(8,128)(2,1)S(1)} %get-tuple-element.91), channel_id=1, source_target_pairs={{0,32},{32,64},{64,96},{96,0},{1,33},{33,65},{65,97},{97,1},{2,34}... | collective-permute-start | bytes 1572872 | tf_op jit(solution)/shard_map/ppermute | solution.py:21
  124.0 18.9 %collective-permute-start.29 = (bf16[256,1024]{1,0:T(8,128)(2,1)S(1)}, bf16[256,1024]{1,0:T(8,128)(2,1)S(1)}, u32[]{:S(2)}, u32[]{:S(2)}) collective-permute-start(bf16[256,1024]{1,0:T(8,128)(2,1)S(1)} %get-tuple-element.92), channel_id=1, source_target_pairs={{0,96},{32,0},{64,32},{96,64},{1,97},{33,1},{65,33},{97,65},{2,98}... | collective-permute-start | bytes 1572872 | tf_op jit(solution)/shard_map/ppermute | solution.py:21
  130.2 16.8 %collective-permute-start.23 = (bf16[256,1024]{1,0:T(8,128)(2,1)S(1)}, bf16[256,1024]{1,0:T(8,128)(2,1)S(1)}, u32[]{:S(2)}, u32[]{:S(2)}) collective-permute-start(bf16[256,1024]{1,0:T(8,128)(2,1)S(1)} %get-tuple-element.87), channel_id=1, source_target_pairs={{0,32},{32,64},{64,96},{96,0},{1,33},{33,65},{65,97},{97,1},{2,34}... | collective-permute-start | bytes 1572872 | tf_op jit(solution)/shard_map/ppermute | solution.py:21
  130.7 16.3 %collective-permute-start.24 = (bf16[256,1024]{1,0:T(8,128)(2,1)S(1)}, bf16[256,1024]{1,0:T(8,128)(2,1)S(1)}, u32[]{:S(2)}, u32[]{:S(2)}) collective-permute-start(bf16[256,1024]{1,0:T(8,128)(2,1)S(1)} %get-tuple-element.88), channel_id=1, source_target_pairs={{0,96},{32,0},{64,32},{96,64},{1,97},{33,1},{65,33},{97,65},{2,98}... | collective-permute-start | bytes 1572872 | tf_op jit(solution)/shard_map/ppermute | solution.py:21
  133.7 1.6 %collective-permute-start.20 = (f32[17,1024]{1,0:T(8,128)S(1)}, f32[17,1024]{1,0:T(8,128)S(1)}, u32[]{:S(2)}, u32[]{:S(2)}) collective-permute-start(f32[17,1024]{1,0:T(8,128)S(1)} %get-tuple-element.84.refs_16_.t_own), channel_id=1, source_target_pairs={{0,1},{1,0},{2,3},{3,2},{4,5},{5,4},{6,7},{7,6},{8,9},{9,8},{10,11... | collective-permute-start | bytes 208904 | tf_op jit(solution)/shard_map/ppermute | solution.py:29

commit v10 on v9

--- a/solution.py
+++ b/solution.py
@@ -367,7 +367,7 @@
             out_specs=pl.BlockSpec((part, columns), lambda i, place: (i, 0)),
         ),
         out_shape=pltpu.HBM((rows, columns), f32),
-        compiler_params=pltpu.CompilerParams(vmem_limit_bytes=40 * 2**20),
+        compiler_params=pltpu.CompilerParams(vmem_limit_bytes=26 * 2**20),
         cost_estimate=pl.CostEstimate(
             flops=2 * rows * 3 * near_depth * columns,
             bytes_accessed=6 * rows * depth + 6 * length * columns + 4 * rows * columns,
@@ -481,7 +481,7 @@
             out_specs=[pl.BlockSpec(s.shape, one) for s in shapes],
         ),
         out_shape=shapes,
-        compiler_params=pltpu.CompilerParams(vmem_limit_bytes=40 * 2**20),
+        compiler_params=pltpu.CompilerParams(vmem_limit_bytes=26 * 2**20),
         cost_estimate=pl.CostEstimate(
             flops=2 * steps * part * 2 * depth * 2 * half,
             bytes_accessed=3 * steps * depth * part + 5 * depth * half + 8 * part * half,

time: 149 us -> 148 us (level)
  Pallas kernels: 53.3 us -> 46.7 us
  waiting for transfers between devices: 50.2 us -> 55.7 us
    pallas_call x6, Pallas kernels: 23.2 us -> 16.6 us  [last_product(): pl.pallas_call(kernel, grid_spec=pltpu.PrefetchScalarGridSpec(num_scalar_...]
    ppermute x22, waiting for transfers between devices: 48.9 us -> 54.4 us  [ring(): lax.ppermute(value, axis, [(i, (i + step) % SIDE) for i in range(SIDE)])]
    unnamed x16 -> x14, local copies, waits for them, and re-layouts: 3.44 us -> 3.44 us
  transfers between devices with their start and end apart: 30 -> 30, of which waited for: 5 -> 7; matrix products, arithmetic and copies ran while one was open for 1% -> 1% of each run, Pallas kernels for 34% -> 30%
where the time goes in v10:
time: 148 us; the launch traced here: 147 us
  waiting for transfers between devices  55.7 us (38%)
  Pallas kernels  46.7 us (32%)
  starting transfers between devices  39.5 us (27%)
  local copies, waits for them, and re-layouts  5.27 us (4%)
    ppermute x22, waiting for transfers between devices, ring(): lax.ppermute(value, axis, [(i, (i + step) % SIDE) for i in range(SIDE)])  54.4 us
    ppermute x22, starting transfers between devices, ring(): lax.ppermute(value, axis, [(i, (i + step) % SIDE) for i in range(SIDE)])  32.9 us
    pallas_call x2, Pallas kernels, first_product(): pl.pallas_call(first_kernel, grid_spec=pltpu.PrefetchScalarGridSpec(num_s...  17.8 us
    pallas_call x6, Pallas kernels, last_product(): pl.pallas_call(kernel, grid_spec=pltpu.PrefetchScalarGridSpec(num_scalar_...  16.6 us
    pallas_call x1, Pallas kernels, pool(): pl.pallas_call(pool_kernel, grid=(columns // tile,), in_specs=[smem(), sm...  4.69 us
    ppermute x1, starting transfers between devices, per_device(): behind = lax.ppermute(teacher[:HALO], ('y', 'x'), down)  3.78 us
    pallas_call x2, Pallas kernels, final(): pl.pallas_call(final_kernel, grid_spec=pltpu.PrefetchScalarGridSpec(num_s...  3.66 us
    unnamed x14, local copies, waits for them, and re-layouts  3.44 us
  transfers between devices with their start and end apart: 30, of which 7 were waited for; matrix products, arithmetic and copies ran while one was open for 1% of the time, Pallas kernels for 30%

profile of v10, /device:TPU:0, one launch (start us, length us, event | category | flops | bytes accessed | tf_op | source)
XLA Modules:
  0.0 147.5 jit_solution(2736831078863029967)
XLA Ops:
  0.0 0.9 fusion
  0.9 1.6 %collective-permute-start = (bf16[16,1024]{1,0:T(8,128)(2,1)S(1)}, bf16[16,1024]{1,0:T(8,128)(2,1)S(1)}, u32[]{:S(2)}, u32[]{:S(2)}) collective-permute-start(bf16[16,1024]{1,0:T(8,128)(2,1)S(1)} %get-tuple-element.94), channel_id=1, source_target_pairs={{0,8},{8,16},{16,24},{24,32},{32,40},{40,48},{48,56},{56,64},{64,7... | collective-permute-start | bytes 98312 | tf_op jit(solution)/shard_map/ppermute | solution.py:544
  2.5 3.8 %collective-permute-start.1 = (bf16[16,1024]{1,0:T(8,128)(2,1)S(1)}, bf16[16,1024]{1,0:T(8,128)(2,1)S(1)}, u32[]{:S(2)}, u32[]{:S(2)}) collective-permute-start(bf16[16,1024]{1,0:T(8,128)(2,1)S(1)} %get-tuple-element.93), channel_id=1, source_target_pairs={{8,0},{16,8},{24,16},{32,24},{40,32},{48,40},{56,48},{64,56},{72,6... | collective-permute-start | bytes 98312 | tf_op jit(solution)/shard_map/ppermute | solution.py:545
  6.3 0.1 pad_add_fusion.place
  6.3 1.4 copy-done.3
  7.8 0.7 copy-done.5
  8.4 1.6 %shard_map.55 = (bf16[208,1024]{1,0:T(8,128)(2,1)S(1)}, bf16[208,1024]{1,0:T(8,128)(2,1)S(1)}, bf16[208,1024]{1,0:T(8,128)(2,1)S(1)}, bf16[208,1024]{1,0:T(8,128)(2,1)S(1)}) custom-call(s32[4]{0:T(128)S(1)} %pad_add_fusion.place, s32[1,4]{1,0:T(1,128)S(1)} %copy-done.5, bf16[192,4096]{1,0:T(8,128)(2,1)S(1)} %copy-done.3), custom_call_target="tpu_custom_call" | custom-call | flops 6291456 | bytes 3145728 | tf_op jit(solution)/shard_map/pallas_call | solution.py:81
  10.0 0.0 collective-permute-done.before
  10.1 0.1 collective-permute-start.2
  10.1 3.2 %collective-permute-start.3 = (bf16[208,1024]{1,0:T(8,128)(2,1)S(1)}, bf16[208,1024]{1,0:T(8,128)(2,1)S(1)}, u32[]{:S(2)}, u32[]{:S(2)}) collective-permute-start(bf16[208,1024]{1,0:T(8,128)(2,1)S(1)} %get-tuple-element.55), channel_id=1, source_target_pairs={{0,24},{8,0},{16,8},{24,16},{1,25},{9,1},{17,9},{25,17},{2,26},{10... | collective-permute-start | bytes 1277960 | tf_op jit(solution)/shard_map/ppermute | solution.py:21
  13.4 0.7 broadcast_in_dim.6.starts
  14.1 0.7 copy-done.4
  14.8 0.7 copy-done.6
  15.4 4.7 %shard_map.56.b0.refs_4_.refs_5_ = bf16[784,1024]{1,0:T(8,128)(2,1)S(1)} custom-call(s32[4]{0:T(128)S(1)} %pad_add_fusion.place, s32[1,4]{1,0:T(1,128)S(1)} %copy-done.6, bf16[16,1024]{1,0:T(8,128)(2,1)S(1)} %collective-permute-done.before, bf16[768,1024]{1,0:T(8,128)(2,1)S(1)} %copy-done.2, bf16[16,1024]{1,0:T(8,128)(2,1)S(1)} %collective-permute-done.1.behind, ...), custom_call_target="tpu_custom_call" | custom-call | flops 402653184 | bytes 4718592 | tf_op jit(solution)/shard_map/pallas_call | solution.py:303
  20.1 11.6 %collective-permute-done.2.p1 = bf16[208,1024]{1,0:T(8,128)(2,1)S(1)} collective-permute-done((bf16[208,1024]{1,0:T(8,128)(2,1)S(1)}, bf16[208,1024]{1,0:T(8,128)(2,1)S(1)}, u32[]{:S(2)}, u32[]{:S(2)}) %collective-permute-start.2) | collective-permute-done | bytes 426016 | tf_op jit(solution)/shard_map/ppermute | solution.py:21
  31.7 0.0 collective-permute-done.4.p3
  31.8 1.2 shard_map.57
  32.9 2.0 %collective-permute-start.7 = (bf16[1056,768]{1,0:T(8,128)(2,1)S(1)}, bf16[1056,768]{1,0:T(8,128)(2,1)S(1)}, u32[]{:S(2)}, u32[]{:S(2)}) collective-permute-start(bf16[1056,768]{1,0:T(8,128)(2,1)S(1)} %get-tuple-element.63.a0.refs_0_), channel_id=1, source_target_pairs={{0,2},{2,4},{4,6},{6,0},{1,3},{3,5},{5,7},{7,1},{8,10},{10,12},{12... | collective-permute-start | bytes 4866056 | tf_op jit(solution)/shard_map/ppermute | solution.py:21
  34.9 2.2 %collective-permute-start.8 = (bf16[1056,768]{1,0:T(8,128)(2,1)S(1)}, bf16[1056,768]{1,0:T(8,128)(2,1)S(1)}, u32[]{:S(2)}, u32[]{:S(2)}) collective-permute-start(bf16[1056,768]{1,0:T(8,128)(2,1)S(1)} %get-tuple-element.63.a0.refs_0_), channel_id=1, source_target_pairs={{0,6},{2,0},{4,2},{6,4},{1,7},{3,1},{5,3},{7,5},{8,14},{10,8},{12,... | collective-permute-start | bytes 4866056 | tf_op jit(solution)/shard_map/ppermute | solution.py:21
  37.1 0.9 collective-permute-start.5
  38.0 2.4 %collective-permute-start.6 = (bf16[784,1024]{1,0:T(8,128)(2,1)S(1)}, bf16[784,1024]{1,0:T(8,128)(2,1)S(1)}, u32[]{:S(2)}, u32[]{:S(2)}) collective-permute-start(bf16[784,1024]{1,0:T(8,128)(2,1)S(1)} %shard_map.56.b0.refs_4_.refs_5_), channel_id=1, source_target_pairs={{0,24},{8,0},{16,8},{24,16},{1,25},{9,1},{17,9},{25,17},{2,26},{10... | collective-permute-start | bytes 4816904 | tf_op jit(solution)/shard_map/ppermute | solution.py:21
  40.3 33.3 %collective-permute-done.5.b1.refs_5_.refs_6_ = bf16[784,1024]{1,0:T(8,128)(2,1)S(1)} collective-permute-done((bf16[784,1024]{1,0:T(8,128)(2,1)S(1)}, bf16[784,1024]{1,0:T(8,128)(2,1)S(1)}, u32[]{:S(2)}, u32[]{:S(2)}) %collective-permute-start.5) | collective-permute-done | bytes 1605664 | tf_op jit(solution)/shard_map/ppermute | solution.py:21
  73.6 0.0 collective-permute-done.6.b2.refs_6_.refs_7_
  73.6 0.1 collective-permute-start.14
  73.7 0.5 collective-permute-start.15
  74.2 0.1 slice.23
  74.3 1.7 %collective-permute-start.13 = (bf16[544,768]{1,0:T(8,128)(2,1)S(1)}, bf16[544,768]{1,0:T(8,128)(2,1)S(1)}, u32[]{:S(2)}, u32[]{:S(2)}) collective-permute-start(bf16[544,768]{1,0:T(8,128)(2,1)S(1)} %slice.23), channel_id=1, source_target_pairs={{0,6},{2,0},{4,2},{6,4},{1,7},{3,1},{5,3},{7,5},{8,14},{10,8},{12,... | collective-permute-start | bytes 2506760 | tf_op jit(solution)/shard_map/ppermute | solution.py:21
  76.0 0.1 slice.20
  76.1 0.1 slice.21
  76.2 0.1 collective-permute-start.10
  76.2 3.2 %collective-permute-start.11 = (bf16[784,512]{1,0:T(8,128)(2,1)S(1)}, bf16[784,512]{1,0:T(8,128)(2,1)S(1)}, u32[]{:S(2)}, u32[]{:S(2)}) collective-permute-start(bf16[784,512]{1,0:T(8,128)(2,1)S(1)} %slice.21), channel_id=1, source_target_pairs={{0,24},{8,0},{16,8},{24,16},{1,25},{9,1},{17,9},{25,17},{2,26},{10... | collective-permute-start | bytes 2408456 | tf_op jit(solution)/shard_map/ppermute | solution.py:21
  79.5 0.1 slice.22
  79.5 0.6 collective-permute-start.12
  80.1 8.9 %shard_map.58.refs_9_ = f32[1024,1024]{1,0:T(8,128)} custom-call(s32[4]{0:T(128)S(1)} %pad_add_fusion.place, bf16[1056,768]{1,0:T(8,128)(2,1)S(1)} %get-tuple-element.63.a0.refs_0_, bf16[1056,768]{1,0:T(8,128)(2,1)S(1)} %collective-permute-done.7.a1.refs_1_, bf16[1056,768]{1,0:T(8,128)(2,1)S(1)} %collective-permute-done.8.a2.refs_2_, ...), custom_call_target="tpu_custom_call" | custom-call | flops 4026531840 | bytes 13729792 | tf_op jit(solution)/shard_map/pallas_call | solution.py:359
  89.0 8.9 %shard_map.59.refs_14_ = f32[1024,1024]{1,0:T(8,128)} custom-call(s32[4]{0:T(128)S(1)} %pad_add_fusion.place, bf16[1056,768]{1,0:T(8,128)(2,1)S(1)} %get-tuple-element.63.a0.refs_0_, bf16[1056,768]{1,0:T(8,128)(2,1)S(1)} %collective-permute-done.7.a1.refs_1_, bf16[1056,768]{1,0:T(8,128)(2,1)S(1)} %collective-permute-done.8.a2.refs_2_, ...), custom_call_target="tpu_custom_call" | custom-call | flops 4026531840 | bytes 13729792 | tf_op jit(solution)/shard_map/pallas_call | solution.py:359
  97.9 1.8 %collective-permute-done.12.refs_3_ = bf16[512,768]{1,0:T(8,128)(2,1)S(1)} collective-permute-done((bf16[512,768]{1,0:T(8,128)(2,1)S(1)}, bf16[512,768]{1,0:T(8,128)(2,1)S(1)}, u32[]{:S(2)}, u32[]{:S(2)}) %collective-permute-start.12) | collective-permute-done | bytes 786464 | tf_op jit(solution)/shard_map/ppermute | solution.py:21
  99.8 0.1 collective-permute-start.25
  99.9 0.5 collective-permute-start.19
  100.4 0.9 shard_map.60.e0
  101.3 0.1 collective-permute-start.16
  101.4 3.2 %collective-permute-start.17 = (f32[24,1024]{1,0:T(8,128)S(1)}, f32[24,1024]{1,0:T(8,128)S(1)}, u32[]{:S(2)}, u32[]{:S(2)}) collective-permute-start(f32[24,1024]{1,0:T(8,128)S(1)} %shard_map.60.e0), channel_id=1, source_target_pairs={{0,96},{32,0},{64,32},{96,64},{1,97},{33,1},{65,33},{97,65},{2,98}... | collective-permute-start | bytes 294920 | tf_op jit(solution)/shard_map/ppermute | solution.py:21
  104.6 2.0 %shard_map.66 = (bf16[256,512]{1,0:T(8,128)(2,1)S(1)}, bf16[256,512]{1,0:T(8,128)(2,1)S(1)}) custom-call(s32[4]{0:T(128)S(1)} %pad_add_fusion.place, bf16[1056,768]{1,0:T(8,128)(2,1)S(1)} %get-tuple-element.63.a0.refs_0_, bf16[1056,768]{1,0:T(8,128)(2,1)S(1)} %collective-permute-done.7.a1.refs_1_, bf16[1056,768]{1,0:T(8,128)(2,1)S(1)} %collective-permute-done.8.a2.refs_2_, ...), custom_call_target="tpu_custom_call" | custom-call | flops 805306368 | bytes 3604480 | tf_op jit(solution)/shard_map/pallas_call | solution.py:475
  106.6 0.9 collective-permute-start.26
  107.5 2.4 %collective-permute-start.27 = (bf16[256,512]{1,0:T(8,128)(2,1)S(1)}, bf16[256,512]{1,0:T(8,128)(2,1)S(1)}, u32[]{:S(2)}, u32[]{:S(2)}) collective-permute-start(bf16[256,512]{1,0:T(8,128)(2,1)S(1)} %get-tuple-element.90), channel_id=1, source_target_pairs={{0,96},{32,0},{64,32},{96,64},{1,97},{33,1},{65,33},{97,65},{2,98}... | collective-permute-start | bytes 786440 | tf_op jit(solution)/shard_map/ppermute | solution.py:21
  109.9 1.2 collective-permute-done.18.e3
  111.1 2.0 %shard_map.63 = (bf16[256,512]{1,0:T(8,128)(2,1)S(1)}, bf16[256,512]{1,0:T(8,128)(2,1)S(1)}) custom-call(s32[4]{0:T(128)S(1)} %pad_add_fusion.place, bf16[1056,768]{1,0:T(8,128)(2,1)S(1)} %get-tuple-element.63.a0.refs_0_, bf16[1056,768]{1,0:T(8,128)(2,1)S(1)} %collective-permute-done.7.a1.refs_1_, bf16[1056,768]{1,0:T(8,128)(2,1)S(1)} %collective-permute-done.8.a2.refs_2_, ...), custom_call_target="tpu_custom_call" | custom-call | flops 805306368 | bytes 3604480 | tf_op jit(solution)/shard_map/pallas_call | solution.py:475
  113.2 0.1 collective-permute-start.21
  113.2 3.2 %collective-permute-start.22 = (bf16[256,512]{1,0:T(8,128)(2,1)S(1)}, bf16[256,512]{1,0:T(8,128)(2,1)S(1)}, u32[]{:S(2)}, u32[]{:S(2)}) collective-permute-start(bf16[256,512]{1,0:T(8,128)(2,1)S(1)} %get-tuple-element.86), channel_id=1, source_target_pairs={{0,96},{32,0},{64,32},{96,64},{1,97},{33,1},{65,33},{97,65},{2,98}... | collective-permute-start | bytes 786440 | tf_op jit(solution)/shard_map/ppermute | solution.py:21
  116.5 0.7 collective-permute-done.26.refs_15_
  117.1 0.0 collective-permute-done.27.refs_16_
  117.2 3.7 %shard_map.67 = (bf16[256,1024]{1,0:T(8,128)(2,1)S(1)}, bf16[256,1024]{1,0:T(8,128)(2,1)S(1)}) custom-call(s32[4]{0:T(128)S(1)} %pad_add_fusion.place, bf16[1056,768]{1,0:T(8,128)(2,1)S(1)} %get-tuple-element.63.a0.refs_0_, bf16[1056,768]{1,0:T(8,128)(2,1)S(1)} %collective-permute-done.7.a1.refs_1_, bf16[1056,768]{1,0:T(8,128)(2,1)S(1)} %collective-permute-done.8.a2.refs_2_, ...), custom_call_target="tpu_custom_call" | custom-call | flops 1610612736 | bytes 4194304 | tf_op jit(solution)/shard_map/pallas_call | solution.py:475
  120.8 1.7 %collective-permute-start.28 = (bf16[256,1024]{1,0:T(8,128)(2,1)S(1)}, bf16[256,1024]{1,0:T(8,128)(2,1)S(1)}, u32[]{:S(2)}, u32[]{:S(2)}) collective-permute-start(bf16[256,1024]{1,0:T(8,128)(2,1)S(1)} %get-tuple-element.91), channel_id=1, source_target_pairs={{0,32},{32,64},{64,96},{96,0},{1,33},{33,65},{65,97},{97,1},{2,34}... | collective-permute-start | bytes 1572872 | tf_op jit(solution)/shard_map/ppermute | solution.py:21
  122.5 1.7 %collective-permute-start.29 = (bf16[256,1024]{1,0:T(8,128)(2,1)S(1)}, bf16[256,1024]{1,0:T(8,128)(2,1)S(1)}, u32[]{:S(2)}, u32[]{:S(2)}) collective-permute-start(bf16[256,1024]{1,0:T(8,128)(2,1)S(1)} %get-tuple-element.92), channel_id=1, source_target_pairs={{0,96},{32,0},{64,32},{96,64},{1,97},{33,1},{65,33},{97,65},{2,98}... | collective-permute-start | bytes 1572872 | tf_op jit(solution)/shard_map/ppermute | solution.py:21
  124.1 3.7 %shard_map.64 = (bf16[256,1024]{1,0:T(8,128)(2,1)S(1)}, bf16[256,1024]{1,0:T(8,128)(2,1)S(1)}) custom-call(s32[4]{0:T(128)S(1)} %pad_add_fusion.place, bf16[1056,768]{1,0:T(8,128)(2,1)S(1)} %get-tuple-element.63.a0.refs_0_, bf16[1056,768]{1,0:T(8,128)(2,1)S(1)} %collective-permute-done.7.a1.refs_1_, bf16[1056,768]{1,0:T(8,128)(2,1)S(1)} %collective-permute-done.8.a2.refs_2_, ...), custom_call_target="tpu_custom_call" | custom-call | flops 1610612736 | bytes 4194304 | tf_op jit(solution)/shard_map/pallas_call | solution.py:475
  127.8 0.5 collective-permute-start.23
  128.3 2.9 %collective-permute-start.24 = (bf16[256,1024]{1,0:T(8,128)(2,1)S(1)}, bf16[256,1024]{1,0:T(8,128)(2,1)S(1)}, u32[]{:S(2)}, u32[]{:S(2)}) collective-permute-start(bf16[256,1024]{1,0:T(8,128)(2,1)S(1)} %get-tuple-element.88), channel_id=1, source_target_pairs={{0,96},{32,0},{64,32},{96,64},{1,97},{33,1},{65,33},{97,65},{2,98}... | collective-permute-start | bytes 1572872 | tf_op jit(solution)/shard_map/ppermute | solution.py:21
  131.1 0.2 shard_map.61
  131.3 0.1 collective-permute-start.20
  131.4 1.3 collective-permute-done.20.refs_17_.t_mate
  132.7 2.6 %shard_map.65.base = f32[256,1024]{1,0:T(8,128)S(1)} custom-call(s32[4]{0:T(128)S(1)} %pad_add_fusion.place, bf16[1056,768]{1,0:T(8,128)(2,1)S(1)} %get-tuple-element.63.a0.refs_0_, bf16[1056,768]{1,0:T(8,128)(2,1)S(1)} %collective-permute-done.7.a1.refs_1_, bf16[1056,768]{1,0:T(8,128)(2,1)S(1)} %collective-permute-done.8.a2.refs_2_, ...), custom_call_target="tpu_custom_call" | custom-call | flops 805306368 | bytes 3604480 | tf_op jit(solution)/shard_map/pallas_call | solution.py:475
  135.4 2.7 %shard_map.62.base = f32[256,1024]{1,0:T(8,128)S(1)} custom-call(s32[4]{0:T(128)S(1)} %pad_add_fusion.place, bf16[1056,768]{1,0:T(8,128)(2,1)S(1)} %get-tuple-element.63.a0.refs_0_, bf16[1056,768]{1,0:T(8,128)(2,1)S(1)} %collective-permute-done.7.a1.refs_1_, bf16[1056,768]{1,0:T(8,128)(2,1)S(1)} %collective-permute-done.8.a2.refs_2_, ...), custom_call_target="tpu_custom_call" | custom-call | flops 805306368 | bytes 3604480 | tf_op jit(solution)/shard_map/pallas_call | solution.py:475
  138.0 1.8 %shard_map.68.rest_0_ = f32[256,2048]{1,0:T(8,128)} custom-call(s32[4]{0:T(128)S(1)} %pad_add_fusion.place, f32[256,1024]{1,0:T(8,128)S(1)} %shard_map.65.base, bf16[256,1024]{1,0:T(8,128)(2,1)S(1)} %collective-permute-done.28.first, bf16[256,1024]{1,0:T(8,128)(2,1)S(1)} %collective-permute-done.29.second, f32[256,128]{1,0:T(8,128)S(1)} %get-tuple-element.83.refs_15_.s_left, ...), custom_call_target="tpu_custom_call" | custom-call | flops 1572864 | bytes 3145728 | tf_op jit(solution)/shard_map/pallas_call | solution.py:515
  139.9 5.8 %collective-permute-done.23.first = bf16[256,1024]{1,0:T(8,128)(2,1)S(1)} collective-permute-done((bf16[256,1024]{1,0:T(8,128)(2,1)S(1)}, bf16[256,1024]{1,0:T(8,128)(2,1)S(1)}, u32[]{:S(2)}, u32[]{:S(2)}) %collective-permute-start.23) | collective-permute-done | bytes 524320 | tf_op jit(solution)/shard_map/ppermute | solution.py:21
  145.6 1.8 %shard_map.69 = f32[256,2048]{1,0:T(8,128)} custom-call(s32[4]{0:T(128)S(1)} %pad_add_fusion.place, f32[256,1024]{1,0:T(8,128)S(1)} %shard_map.62.base, bf16[256,1024]{1,0:T(8,128)(2,1)S(1)} %collective-permute-done.23.first, bf16[256,1024]{1,0:T(8,128)(2,1)S(1)} %collective-permute-done.24.second, ...), custom_call_target="tpu_custom_call", output_to_operand_aliasing={{}: (7, {})} | custom-call | flops 1572864 | bytes 3145728 | tf_op jit(solution)/shard_map/pallas_call | solution.py:515
  (32 shorter events, 0.1 us)
Async XLA Ops:
  0.0 14.1 %copy-start.2 = (bf16[768,1024]{1,0:T(8,128)(2,1)S(1)}, bf16[768,1024]{1,0:T(8,128)(2,1)}, u32[]{:S(2)}) copy-start(bf16[768,1024]{1,0:T(8,128)(2,1)} %teacher.1) | copy-start | bytes 4718596
  0.9 9.1 %collective-permute-start = (bf16[16,1024]{1,0:T(8,128)(2,1)S(1)}, bf16[16,1024]{1,0:T(8,128)(2,1)S(1)}, u32[]{:S(2)}, u32[]{:S(2)}) collective-permute-start(bf16[16,1024]{1,0:T(8,128)(2,1)S(1)} %get-tuple-element.94), channel_id=1, source_target_pairs={{0,8},{8,16},{16,24},{24,32},{32,40},{40,48},{48,56},{56,64},{64,7... | collective-permute-start | bytes 98312 | tf_op jit(solution)/shard_map/ppermute | solution.py:544
  2.5 7.6 %collective-permute-start.1 = (bf16[16,1024]{1,0:T(8,128)(2,1)S(1)}, bf16[16,1024]{1,0:T(8,128)(2,1)S(1)}, u32[]{:S(2)}, u32[]{:S(2)}) collective-permute-start(bf16[16,1024]{1,0:T(8,128)(2,1)S(1)} %get-tuple-element.93), channel_id=1, source_target_pairs={{8,0},{16,8},{24,16},{32,24},{40,32},{48,40},{56,48},{64,56},{72,6... | collective-permute-start | bytes 98312 | tf_op jit(solution)/shard_map/ppermute | solution.py:545
  6.3 1.4 copy-start.3
  7.7 0.7 copy-start.5
  10.1 21.7 %collective-permute-start.2 = (bf16[208,1024]{1,0:T(8,128)(2,1)S(1)}, bf16[208,1024]{1,0:T(8,128)(2,1)S(1)}, u32[]{:S(2)}, u32[]{:S(2)}) collective-permute-start(bf16[208,1024]{1,0:T(8,128)(2,1)S(1)} %get-tuple-element.54), channel_id=1, source_target_pairs={{0,8},{8,16},{16,24},{24,0},{1,9},{9,17},{17,25},{25,1},{2,10},{10... | collective-permute-start | bytes 1277960 | tf_op jit(solution)/shard_map/ppermute | solution.py:21
  10.1 21.6 %collective-permute-start.3 = (bf16[208,1024]{1,0:T(8,128)(2,1)S(1)}, bf16[208,1024]{1,0:T(8,128)(2,1)S(1)}, u32[]{:S(2)}, u32[]{:S(2)}) collective-permute-start(bf16[208,1024]{1,0:T(8,128)(2,1)S(1)} %get-tuple-element.55), channel_id=1, source_target_pairs={{0,24},{8,0},{16,8},{24,16},{1,25},{9,1},{17,9},{25,17},{2,26},{10... | collective-permute-start | bytes 1277960 | tf_op jit(solution)/shard_map/ppermute | solution.py:21
  13.4 18.4 %collective-permute-start.4 = (bf16[208,1024]{1,0:T(8,128)(2,1)S(1)}, bf16[208,1024]{1,0:T(8,128)(2,1)S(1)}, u32[]{:S(2)}, u32[]{:S(2)}) collective-permute-start(bf16[208,1024]{1,0:T(8,128)(2,1)S(1)} %get-tuple-element.56), channel_id=1, source_target_pairs={{0,16},{8,24},{16,0},{24,8},{1,17},{9,25},{17,1},{25,9},{2,18},{10... | collective-permute-start | bytes 1277960 | tf_op jit(solution)/shard_map/ppermute | solution.py:21
  14.1 0.7 copy-start.4
  14.8 0.7 copy-start.6
  32.9 40.7 %collective-permute-start.7 = (bf16[1056,768]{1,0:T(8,128)(2,1)S(1)}, bf16[1056,768]{1,0:T(8,128)(2,1)S(1)}, u32[]{:S(2)}, u32[]{:S(2)}) collective-permute-start(bf16[1056,768]{1,0:T(8,128)(2,1)S(1)} %get-tuple-element.63.a0.refs_0_), channel_id=1, source_target_pairs={{0,2},{2,4},{4,6},{6,0},{1,3},{3,5},{5,7},{7,1},{8,10},{10,12},{12... | collective-permute-start | bytes 4866056 | tf_op jit(solution)/shard_map/ppermute | solution.py:21
  34.9 38.7 %collective-permute-start.8 = (bf16[1056,768]{1,0:T(8,128)(2,1)S(1)}, bf16[1056,768]{1,0:T(8,128)(2,1)S(1)}, u32[]{:S(2)}, u32[]{:S(2)}) collective-permute-start(bf16[1056,768]{1,0:T(8,128)(2,1)S(1)} %get-tuple-element.63.a0.refs_0_), channel_id=1, source_target_pairs={{0,6},{2,0},{4,2},{6,4},{1,7},{3,1},{5,3},{7,5},{8,14},{10,8},{12,... | collective-permute-start | bytes 4866056 | tf_op jit(solution)/shard_map/ppermute | solution.py:21
  37.1 36.5 %collective-permute-start.5 = (bf16[784,1024]{1,0:T(8,128)(2,1)S(1)}, bf16[784,1024]{1,0:T(8,128)(2,1)S(1)}, u32[]{:S(2)}, u32[]{:S(2)}) collective-permute-start(bf16[784,1024]{1,0:T(8,128)(2,1)S(1)} %shard_map.56.b0.refs_4_.refs_5_), channel_id=1, source_target_pairs={{0,8},{8,16},{16,24},{24,0},{1,9},{9,17},{17,25},{25,1},{2,10},{10... | collective-permute-start | bytes 4816904 | tf_op jit(solution)/shard_map/ppermute | solution.py:21
  38.0 35.6 %collective-permute-start.6 = (bf16[784,1024]{1,0:T(8,128)(2,1)S(1)}, bf16[784,1024]{1,0:T(8,128)(2,1)S(1)}, u32[]{:S(2)}, u32[]{:S(2)}) collective-permute-start(bf16[784,1024]{1,0:T(8,128)(2,1)S(1)} %shard_map.56.b0.refs_4_.refs_5_), channel_id=1, source_target_pairs={{0,24},{8,0},{16,8},{24,16},{1,25},{9,1},{17,9},{25,17},{2,26},{10... | collective-permute-start | bytes 4816904 | tf_op jit(solution)/shard_map/ppermute | solution.py:21
  40.3 33.3 %collective-permute-start.9 = (bf16[784,1024]{1,0:T(8,128)(2,1)S(1)}, bf16[784,1024]{1,0:T(8,128)(2,1)S(1)}, u32[]{:S(2)}, u32[]{:S(2)}) collective-permute-start(bf16[784,1024]{1,0:T(8,128)(2,1)S(1)} %shard_map.56.b0.refs_4_.refs_5_), channel_id=1, source_target_pairs={{0,1},{1,0},{2,3},{3,2},{4,5},{5,4},{6,7},{7,6},{8,9},{9,8},{10,11... | collective-permute-start | bytes 4816904 | tf_op jit(solution)/shard_map/ppermute | solution.py:29
  73.6 5.9 %collective-permute-start.14 = (bf16[784,1024]{1,0:T(8,128)(2,1)S(1)}, bf16[784,1024]{1,0:T(8,128)(2,1)S(1)}, u32[]{:S(2)}, u32[]{:S(2)}) collective-permute-start(bf16[784,1024]{1,0:T(8,128)(2,1)S(1)} %collective-permute-done.5.b1.refs_5_.refs_6_), channel_id=1, source_target_pairs={{0,1},{1,0},{2,3},{3,2},{4,5},{5,4},{6,7},{7,6},{8,9},{9,8},{10,11... | collective-permute-start | bytes 4816904 | tf_op jit(solution)/shard_map/ppermute | solution.py:29
  73.7 15.3 %collective-permute-start.15 = (bf16[784,1024]{1,0:T(8,128)(2,1)S(1)}, bf16[784,1024]{1,0:T(8,128)(2,1)S(1)}, u32[]{:S(2)}, u32[]{:S(2)}) collective-permute-start(bf16[784,1024]{1,0:T(8,128)(2,1)S(1)} %collective-permute-done.6.b2.refs_6_.refs_7_), channel_id=1, source_target_pairs={{0,1},{1,0},{2,3},{3,2},{4,5},{5,4},{6,7},{7,6},{8,9},{9,8},{10,11... | collective-permute-start | bytes 4816904 | tf_op jit(solution)/shard_map/ppermute | solution.py:29
  74.3 25.5 %collective-permute-start.13 = (bf16[544,768]{1,0:T(8,128)(2,1)S(1)}, bf16[544,768]{1,0:T(8,128)(2,1)S(1)}, u32[]{:S(2)}, u32[]{:S(2)}) collective-permute-start(bf16[544,768]{1,0:T(8,128)(2,1)S(1)} %slice.23), channel_id=1, source_target_pairs={{0,6},{2,0},{4,2},{6,4},{1,7},{3,1},{5,3},{7,5},{8,14},{10,8},{12,... | collective-permute-start | bytes 2506760 | tf_op jit(solution)/shard_map/ppermute | solution.py:21
  76.2 23.6 %collective-permute-start.10 = (bf16[784,512]{1,0:T(8,128)(2,1)S(1)}, bf16[784,512]{1,0:T(8,128)(2,1)S(1)}, u32[]{:S(2)}, u32[]{:S(2)}) collective-permute-start(bf16[784,512]{1,0:T(8,128)(2,1)S(1)} %slice.20), channel_id=1, source_target_pairs={{0,8},{8,16},{16,24},{24,0},{1,9},{9,17},{17,25},{25,1},{2,10},{10... | collective-permute-start | bytes 2408456 | tf_op jit(solution)/shard_map/ppermute | solution.py:21
  76.2 23.5 %collective-permute-start.11 = (bf16[784,512]{1,0:T(8,128)(2,1)S(1)}, bf16[784,512]{1,0:T(8,128)(2,1)S(1)}, u32[]{:S(2)}, u32[]{:S(2)}) collective-permute-start(bf16[784,512]{1,0:T(8,128)(2,1)S(1)} %slice.21), channel_id=1, source_target_pairs={{0,24},{8,0},{16,8},{24,16},{1,25},{9,1},{17,9},{25,17},{2,26},{10... | collective-permute-start | bytes 2408456 | tf_op jit(solution)/shard_map/ppermute | solution.py:21
  79.5 20.2 %collective-permute-start.12 = (bf16[512,768]{1,0:T(8,128)(2,1)S(1)}, bf16[512,768]{1,0:T(8,128)(2,1)S(1)}, u32[]{:S(2)}, u32[]{:S(2)}) collective-permute-start(bf16[512,768]{1,0:T(8,128)(2,1)S(1)} %slice.22), channel_id=1, source_target_pairs={{0,2},{2,4},{4,6},{6,0},{1,3},{3,5},{5,7},{7,1},{8,10},{10,12},{12... | collective-permute-start | bytes 2359304 | tf_op jit(solution)/shard_map/ppermute | solution.py:21
  99.8 4.8 %collective-permute-start.25 = (bf16[784,512]{1,0:T(8,128)(2,1)S(1)}, bf16[784,512]{1,0:T(8,128)(2,1)S(1)}, u32[]{:S(2)}, u32[]{:S(2)}) collective-permute-start(bf16[784,512]{1,0:T(8,128)(2,1)S(1)} %collective-permute-done.10.refs_7_.refs_8_), channel_id=1, source_target_pairs={{0,1},{1,0},{2,3},{3,2},{4,5},{5,4},{6,7},{7,6},{8,9},{9,8},{10,11... | collective-permute-start | bytes 2408456 | tf_op jit(solution)/shard_map/ppermute | solution.py:29
  99.9 11.3 %collective-permute-start.19 = (bf16[784,512]{1,0:T(8,128)(2,1)S(1)}, bf16[784,512]{1,0:T(8,128)(2,1)S(1)}, u32[]{:S(2)}, u32[]{:S(2)}) collective-permute-start(bf16[784,512]{1,0:T(8,128)(2,1)S(1)} %collective-permute-done.11.refs_8_), channel_id=1, source_target_pairs={{0,1},{1,0},{2,3},{3,2},{4,5},{5,4},{6,7},{7,6},{8,9},{9,8},{10,11... | collective-permute-start | bytes 2408456 | tf_op jit(solution)/shard_map/ppermute | solution.py:29
  100.4 4.2 %copy-start = (f32[1024,1024]{1,0:T(8,128)S(1)}, f32[1024,1024]{1,0:T(8,128)}, u32[]{:S(2)}) copy-start(f32[1024,1024]{1,0:T(8,128)} %shard_map.58.refs_9_) | copy-start | bytes 12582916
  100.4 4.2 %copy-start.1 = (f32[1024,1024]{1,0:T(8,128)S(1)}, f32[1024,1024]{1,0:T(8,128)}, u32[]{:S(2)}) copy-start(f32[1024,1024]{1,0:T(8,128)} %shard_map.59.refs_14_) | copy-start | bytes 12582916
  101.3 6.3 %collective-permute-start.16 = (f32[24,1024]{1,0:T(8,128)S(1)}, f32[24,1024]{1,0:T(8,128)S(1)}, u32[]{:S(2)}, u32[]{:S(2)}) collective-permute-start(f32[24,1024]{1,0:T(8,128)S(1)} %shard_map.60.e0), channel_id=1, source_target_pairs={{0,32},{32,64},{64,96},{96,0},{1,33},{33,65},{65,97},{97,1},{2,34}... | collective-permute-start | bytes 294920 | tf_op jit(solution)/shard_map/ppermute | solution.py:21
  101.4 8.6 %collective-permute-start.17 = (f32[24,1024]{1,0:T(8,128)S(1)}, f32[24,1024]{1,0:T(8,128)S(1)}, u32[]{:S(2)}, u32[]{:S(2)}) collective-permute-start(f32[24,1024]{1,0:T(8,128)S(1)} %shard_map.60.e0), channel_id=1, source_target_pairs={{0,96},{32,0},{64,32},{96,64},{1,97},{33,1},{65,33},{97,65},{2,98}... | collective-permute-start | bytes 294920 | tf_op jit(solution)/shard_map/ppermute | solution.py:21
  104.6 6.6 %collective-permute-start.18 = (f32[24,1024]{1,0:T(8,128)S(1)}, f32[24,1024]{1,0:T(8,128)S(1)}, u32[]{:S(2)}, u32[]{:S(2)}) collective-permute-start(f32[24,1024]{1,0:T(8,128)S(1)} %shard_map.60.e0), channel_id=1, source_target_pairs={{0,64},{32,96},{64,0},{96,32},{1,65},{33,97},{65,1},{97,33},{2,66}... | collective-permute-start | bytes 294920 | tf_op jit(solution)/shard_map/ppermute | solution.py:21
  106.6 10.5 %collective-permute-start.26 = (bf16[256,512]{1,0:T(8,128)(2,1)S(1)}, bf16[256,512]{1,0:T(8,128)(2,1)S(1)}, u32[]{:S(2)}, u32[]{:S(2)}) collective-permute-start(bf16[256,512]{1,0:T(8,128)(2,1)S(1)} %get-tuple-element.89), channel_id=1, source_target_pairs={{0,32},{32,64},{64,96},{96,0},{1,33},{33,65},{65,97},{97,1},{2,34}... | collective-permute-start | bytes 786440 | tf_op jit(solution)/shard_map/ppermute | solution.py:21
  107.5 9.6 %collective-permute-start.27 = (bf16[256,512]{1,0:T(8,128)(2,1)S(1)}, bf16[256,512]{1,0:T(8,128)(2,1)S(1)}, u32[]{:S(2)}, u32[]{:S(2)}) collective-permute-start(bf16[256,512]{1,0:T(8,128)(2,1)S(1)} %get-tuple-element.90), channel_id=1, source_target_pairs={{0,96},{32,0},{64,32},{96,64},{1,97},{33,1},{65,33},{97,65},{2,98}... | collective-permute-start | bytes 786440 | tf_op jit(solution)/shard_map/ppermute | solution.py:21
  113.2 11.0 %collective-permute-start.21 = (bf16[256,512]{1,0:T(8,128)(2,1)S(1)}, bf16[256,512]{1,0:T(8,128)(2,1)S(1)}, u32[]{:S(2)}, u32[]{:S(2)}) collective-permute-start(bf16[256,512]{1,0:T(8,128)(2,1)S(1)} %get-tuple-element.85), channel_id=1, source_target_pairs={{0,32},{32,64},{64,96},{96,0},{1,33},{33,65},{65,97},{97,1},{2,34}... | collective-permute-start | bytes 786440 | tf_op jit(solution)/shard_map/ppermute | solution.py:21
  113.2 10.9 %collective-permute-start.22 = (bf16[256,512]{1,0:T(8,128)(2,1)S(1)}, bf16[256,512]{1,0:T(8,128)(2,1)S(1)}, u32[]{:S(2)}, u32[]{:S(2)}) collective-permute-start(bf16[256,512]{1,0:T(8,128)(2,1)S(1)} %get-tuple-element.86), channel_id=1, source_target_pairs={{0,96},{32,0},{64,32},{96,64},{1,97},{33,1},{65,33},{97,65},{2,98}... | collective-permute-start | bytes 786440 | tf_op jit(solution)/shard_map/ppermute | solution.py:21
  120.8 17.2 %collective-permute-start.28 = (bf16[256,1024]{1,0:T(8,128)(2,1)S(1)}, bf16[256,1024]{1,0:T(8,128)(2,1)S(1)}, u32[]{:S(2)}, u32[]{:S(2)}) collective-permute-start(bf16[256,1024]{1,0:T(8,128)(2,1)S(1)} %get-tuple-element.91), channel_id=1, source_target_pairs={{0,32},{32,64},{64,96},{96,0},{1,33},{33,65},{65,97},{97,1},{2,34}... | collective-permute-start | bytes 1572872 | tf_op jit(solution)/shard_map/ppermute | solution.py:21
  122.5 15.5 %collective-permute-start.29 = (bf16[256,1024]{1,0:T(8,128)(2,1)S(1)}, bf16[256,1024]{1,0:T(8,128)(2,1)S(1)}, u32[]{:S(2)}, u32[]{:S(2)}) collective-permute-start(bf16[256,1024]{1,0:T(8,128)(2,1)S(1)} %get-tuple-element.92), channel_id=1, source_target_pairs={{0,96},{32,0},{64,32},{96,64},{1,97},{33,1},{65,33},{97,65},{2,98}... | collective-permute-start | bytes 1572872 | tf_op jit(solution)/shard_map/ppermute | solution.py:21
  127.8 17.8 %collective-permute-start.23 = (bf16[256,1024]{1,0:T(8,128)(2,1)S(1)}, bf16[256,1024]{1,0:T(8,128)(2,1)S(1)}, u32[]{:S(2)}, u32[]{:S(2)}) collective-permute-start(bf16[256,1024]{1,0:T(8,128)(2,1)S(1)} %get-tuple-element.87), channel_id=1, source_target_pairs={{0,32},{32,64},{64,96},{96,0},{1,33},{33,65},{65,97},{97,1},{2,34}... | collective-permute-start | bytes 1572872 | tf_op jit(solution)/shard_map/ppermute | solution.py:21
  128.3 17.4 %collective-permute-start.24 = (bf16[256,1024]{1,0:T(8,128)(2,1)S(1)}, bf16[256,1024]{1,0:T(8,128)(2,1)S(1)}, u32[]{:S(2)}, u32[]{:S(2)}) collective-permute-start(bf16[256,1024]{1,0:T(8,128)(2,1)S(1)} %get-tuple-element.88), channel_id=1, source_target_pairs={{0,96},{32,0},{64,32},{96,64},{1,97},{33,1},{65,33},{97,65},{2,98}... | collective-permute-start | bytes 1572872 | tf_op jit(solution)/shard_map/ppermute | solution.py:21
  131.3 1.4 collective-permute-start.20

commit v11 on v10

--- a/solution.py
+++ b/solution.py
@@ -494,19 +494,19 @@
     out = rest[-1]
     every = SIDE * SIDE
     last = slice(every, every + 1)
-    t = jnp.where(pl.program_id(0) == 0, t_own[last, :], t_mate[last, :])
+    t = jnp.where(pl.program_id(0) < 2, t_own[last, :], t_mate[last, :])
     inside = first[...].astype(f32) + second[...].astype(f32)
     out[...] = inside * s_left[:, last] * t + base[...]
 
 
 def final(place, k, kept, first, second, s_left, t_own, t_mate, whole=None):
     part, columns = kept.shape
-    half = columns // 2
-    block = pl.BlockSpec((part, half), lambda i, place: (0, i))
+    quarter = columns // 4
+    block = pl.BlockSpec((part, quarter), lambda i, place: (0, i))
     in_specs = (
         [block] * 3
         + [pl.BlockSpec(s_left.shape, lambda i, place: (0, 0))]
-        + [pl.BlockSpec((t_own.shape[0], half), lambda i, place: (0, k))] * 2
+        + [pl.BlockSpec((t_own.shape[0], quarter), lambda i, place: (0, 2 * k + lax.rem(i, 2)))] * 2
     )
     more, aliases = (), {}
     if whole is not None:
@@ -516,10 +516,10 @@
         final_kernel,
         grid_spec=pltpu.PrefetchScalarGridSpec(
             num_scalar_prefetch=1,
-            grid=(2,),
+            grid=(4,),
             in_specs=in_specs,
             out_specs=pl.BlockSpec(
-                (part, half), lambda i, place: (0, lax.rem(place[1] + i, 2) * 2 + k)
+                (part, quarter), lambda i, place: (0, (lax.rem(place[1] + i // 2, 2) * 2 + k) * 2 + lax.rem(i, 2))
             ),
         ),
         out_shape=jax.ShapeDtypeStruct((part, 2 * columns), f32),

time: 148 us -> 148 us (level)
  no operation moved by 1% of the time
where the time goes in v11:
time: 148 us
  waiting for transfers between devices  55 us (37%)
  Pallas kernels  48.1 us (32%)
  starting transfers between devices  39.5 us (27%)
  local copies, waits for them, and re-layouts  5.27 us (4%)
    ppermute x22, waiting for transfers between devices, ring(): lax.ppermute(value, axis, [(i, (i + step) % SIDE) for i in range(SIDE)])  53.7 us
    ppermute x22, starting transfers between devices, ring(): lax.ppermute(value, axis, [(i, (i + step) % SIDE) for i in range(SIDE)])  32.9 us
    pallas_call x2, Pallas kernels, first_product(): pl.pallas_call(first_kernel, grid_spec=pltpu.PrefetchScalarGridSpec(num_s...  17.8 us
    pallas_call x6, Pallas kernels, last_product(): pl.pallas_call(kernel, grid_spec=pltpu.PrefetchScalarGridSpec(num_scalar_...  16.6 us
    pallas_call x2, Pallas kernels, final(): pl.pallas_call(final_kernel, grid_spec=pltpu.PrefetchScalarGridSpec(num_s...  5.13 us
    pallas_call x1, Pallas kernels, pool(): pl.pallas_call(pool_kernel, grid=(columns // tile,), in_specs=[smem(), sm...  4.69 us
    ppermute x1, starting transfers between devices, per_device(): behind = lax.ppermute(teacher[:HALO], ('y', 'x'), down)  3.78 us
    unnamed x14, local copies, waits for them, and re-layouts  3.44 us
  transfers between devices with their start and end apart: 30, of which 7 were waited for; matrix products, arithmetic and copies ran while one was open for 1% of the time, Pallas kernels for 30%

profile of v11, /device:TPU:0, one launch (start us, length us, event | category | flops | bytes accessed | tf_op | source)
XLA Modules:
  0.0 148.2 jit_solution(3065623540818055509)
XLA Ops:
  0.0 0.9 fusion
  0.9 1.6 %collective-permute-start = (bf16[16,1024]{1,0:T(8,128)(2,1)S(1)}, bf16[16,1024]{1,0:T(8,128)(2,1)S(1)}, u32[]{:S(2)}, u32[]{:S(2)}) collective-permute-start(bf16[16,1024]{1,0:T(8,128)(2,1)S(1)} %get-tuple-element.94), channel_id=1, source_target_pairs={{0,8},{8,16},{16,24},{24,32},{32,40},{40,48},{48,56},{56,64},{64,7... | collective-permute-start | bytes 98312 | tf_op jit(solution)/shard_map/ppermute | solution.py:544
  2.5 3.8 %collective-permute-start.1 = (bf16[16,1024]{1,0:T(8,128)(2,1)S(1)}, bf16[16,1024]{1,0:T(8,128)(2,1)S(1)}, u32[]{:S(2)}, u32[]{:S(2)}) collective-permute-start(bf16[16,1024]{1,0:T(8,128)(2,1)S(1)} %get-tuple-element.93), channel_id=1, source_target_pairs={{8,0},{16,8},{24,16},{32,24},{40,32},{48,40},{56,48},{64,56},{72,6... | collective-permute-start | bytes 98312 | tf_op jit(solution)/shard_map/ppermute | solution.py:545
  6.3 0.1 pad_add_fusion.place
  6.3 1.4 copy-done.3
  7.8 0.7 copy-done.5
  8.4 1.6 %shard_map.55 = (bf16[208,1024]{1,0:T(8,128)(2,1)S(1)}, bf16[208,1024]{1,0:T(8,128)(2,1)S(1)}, bf16[208,1024]{1,0:T(8,128)(2,1)S(1)}, bf16[208,1024]{1,0:T(8,128)(2,1)S(1)}) custom-call(s32[4]{0:T(128)S(1)} %pad_add_fusion.place, s32[1,4]{1,0:T(1,128)S(1)} %copy-done.5, bf16[192,4096]{1,0:T(8,128)(2,1)S(1)} %copy-done.3), custom_call_target="tpu_custom_call" | custom-call | flops 6291456 | bytes 3145728 | tf_op jit(solution)/shard_map/pallas_call | solution.py:81
  10.0 0.0 collective-permute-done.before
  10.1 0.1 collective-permute-start.2
  10.1 3.2 %collective-permute-start.3 = (bf16[208,1024]{1,0:T(8,128)(2,1)S(1)}, bf16[208,1024]{1,0:T(8,128)(2,1)S(1)}, u32[]{:S(2)}, u32[]{:S(2)}) collective-permute-start(bf16[208,1024]{1,0:T(8,128)(2,1)S(1)} %get-tuple-element.55), channel_id=1, source_target_pairs={{0,24},{8,0},{16,8},{24,16},{1,25},{9,1},{17,9},{25,17},{2,26},{10... | collective-permute-start | bytes 1277960 | tf_op jit(solution)/shard_map/ppermute | solution.py:21
  13.4 0.7 broadcast_in_dim.6.starts
  14.1 0.7 copy-done.4
  14.8 0.7 copy-done.6
  15.4 4.7 %shard_map.56.b0.refs_4_.refs_5_ = bf16[784,1024]{1,0:T(8,128)(2,1)S(1)} custom-call(s32[4]{0:T(128)S(1)} %pad_add_fusion.place, s32[1,4]{1,0:T(1,128)S(1)} %copy-done.6, bf16[16,1024]{1,0:T(8,128)(2,1)S(1)} %collective-permute-done.before, bf16[768,1024]{1,0:T(8,128)(2,1)S(1)} %copy-done.2, bf16[16,1024]{1,0:T(8,128)(2,1)S(1)} %collective-permute-done.1.behind, ...), custom_call_target="tpu_custom_call" | custom-call | flops 402653184 | bytes 4718592 | tf_op jit(solution)/shard_map/pallas_call | solution.py:303
  20.1 11.6 %collective-permute-done.2.p1 = bf16[208,1024]{1,0:T(8,128)(2,1)S(1)} collective-permute-done((bf16[208,1024]{1,0:T(8,128)(2,1)S(1)}, bf16[208,1024]{1,0:T(8,128)(2,1)S(1)}, u32[]{:S(2)}, u32[]{:S(2)}) %collective-permute-start.2) | collective-permute-done | bytes 426016 | tf_op jit(solution)/shard_map/ppermute | solution.py:21
  31.7 0.0 collective-permute-done.4.p3
  31.8 1.2 shard_map.57
  32.9 2.0 %collective-permute-start.7 = (bf16[1056,768]{1,0:T(8,128)(2,1)S(1)}, bf16[1056,768]{1,0:T(8,128)(2,1)S(1)}, u32[]{:S(2)}, u32[]{:S(2)}) collective-permute-start(bf16[1056,768]{1,0:T(8,128)(2,1)S(1)} %get-tuple-element.63.a0.refs_0_), channel_id=1, source_target_pairs={{0,2},{2,4},{4,6},{6,0},{1,3},{3,5},{5,7},{7,1},{8,10},{10,12},{12... | collective-permute-start | bytes 4866056 | tf_op jit(solution)/shard_map/ppermute | solution.py:21
  34.9 2.2 %collective-permute-start.8 = (bf16[1056,768]{1,0:T(8,128)(2,1)S(1)}, bf16[1056,768]{1,0:T(8,128)(2,1)S(1)}, u32[]{:S(2)}, u32[]{:S(2)}) collective-permute-start(bf16[1056,768]{1,0:T(8,128)(2,1)S(1)} %get-tuple-element.63.a0.refs_0_), channel_id=1, source_target_pairs={{0,6},{2,0},{4,2},{6,4},{1,7},{3,1},{5,3},{7,5},{8,14},{10,8},{12,... | collective-permute-start | bytes 4866056 | tf_op jit(solution)/shard_map/ppermute | solution.py:21
  37.1 0.9 collective-permute-start.5
  38.0 2.4 %collective-permute-start.6 = (bf16[784,1024]{1,0:T(8,128)(2,1)S(1)}, bf16[784,1024]{1,0:T(8,128)(2,1)S(1)}, u32[]{:S(2)}, u32[]{:S(2)}) collective-permute-start(bf16[784,1024]{1,0:T(8,128)(2,1)S(1)} %shard_map.56.b0.refs_4_.refs_5_), channel_id=1, source_target_pairs={{0,24},{8,0},{16,8},{24,16},{1,25},{9,1},{17,9},{25,17},{2,26},{10... | collective-permute-start | bytes 4816904 | tf_op jit(solution)/shard_map/ppermute | solution.py:21
  40.3 33.3 %collective-permute-done.5.b1.refs_5_.refs_6_ = bf16[784,1024]{1,0:T(8,128)(2,1)S(1)} collective-permute-done((bf16[784,1024]{1,0:T(8,128)(2,1)S(1)}, bf16[784,1024]{1,0:T(8,128)(2,1)S(1)}, u32[]{:S(2)}, u32[]{:S(2)}) %collective-permute-start.5) | collective-permute-done | bytes 1605664 | tf_op jit(solution)/shard_map/ppermute | solution.py:21
  73.6 0.0 collective-permute-done.6.b2.refs_6_.refs_7_
  73.6 0.1 collective-permute-start.14
  73.7 0.5 collective-permute-start.15
  74.2 0.1 slice.23
  74.3 1.7 %collective-permute-start.13 = (bf16[544,768]{1,0:T(8,128)(2,1)S(1)}, bf16[544,768]{1,0:T(8,128)(2,1)S(1)}, u32[]{:S(2)}, u32[]{:S(2)}) collective-permute-start(bf16[544,768]{1,0:T(8,128)(2,1)S(1)} %slice.23), channel_id=1, source_target_pairs={{0,6},{2,0},{4,2},{6,4},{1,7},{3,1},{5,3},{7,5},{8,14},{10,8},{12,... | collective-permute-start | bytes 2506760 | tf_op jit(solution)/shard_map/ppermute | solution.py:21
  76.0 0.1 slice.20
  76.1 0.1 slice.21
  76.2 0.1 collective-permute-start.10
  76.2 3.2 %collective-permute-start.11 = (bf16[784,512]{1,0:T(8,128)(2,1)S(1)}, bf16[784,512]{1,0:T(8,128)(2,1)S(1)}, u32[]{:S(2)}, u32[]{:S(2)}) collective-permute-start(bf16[784,512]{1,0:T(8,128)(2,1)S(1)} %slice.21), channel_id=1, source_target_pairs={{0,24},{8,0},{16,8},{24,16},{1,25},{9,1},{17,9},{25,17},{2,26},{10... | collective-permute-start | bytes 2408456 | tf_op jit(solution)/shard_map/ppermute | solution.py:21
  79.5 0.1 slice.22
  79.5 0.6 collective-permute-start.12
  80.1 8.9 %shard_map.58.refs_9_ = f32[1024,1024]{1,0:T(8,128)} custom-call(s32[4]{0:T(128)S(1)} %pad_add_fusion.place, bf16[1056,768]{1,0:T(8,128)(2,1)S(1)} %get-tuple-element.63.a0.refs_0_, bf16[1056,768]{1,0:T(8,128)(2,1)S(1)} %collective-permute-done.7.a1.refs_1_, bf16[1056,768]{1,0:T(8,128)(2,1)S(1)} %collective-permute-done.8.a2.refs_2_, ...), custom_call_target="tpu_custom_call" | custom-call | flops 4026531840 | bytes 13729792 | tf_op jit(solution)/shard_map/pallas_call | solution.py:359
  89.0 8.9 %shard_map.59.refs_14_ = f32[1024,1024]{1,0:T(8,128)} custom-call(s32[4]{0:T(128)S(1)} %pad_add_fusion.place, bf16[1056,768]{1,0:T(8,128)(2,1)S(1)} %get-tuple-element.63.a0.refs_0_, bf16[1056,768]{1,0:T(8,128)(2,1)S(1)} %collective-permute-done.7.a1.refs_1_, bf16[1056,768]{1,0:T(8,128)(2,1)S(1)} %collective-permute-done.8.a2.refs_2_, ...), custom_call_target="tpu_custom_call" | custom-call | flops 4026531840 | bytes 13729792 | tf_op jit(solution)/shard_map/pallas_call | solution.py:359
  97.9 1.8 %collective-permute-done.12.refs_3_ = bf16[512,768]{1,0:T(8,128)(2,1)S(1)} collective-permute-done((bf16[512,768]{1,0:T(8,128)(2,1)S(1)}, bf16[512,768]{1,0:T(8,128)(2,1)S(1)}, u32[]{:S(2)}, u32[]{:S(2)}) %collective-permute-start.12) | collective-permute-done | bytes 786464 | tf_op jit(solution)/shard_map/ppermute | solution.py:21
  99.8 0.1 collective-permute-start.25
  99.9 0.5 collective-permute-start.19
  100.4 0.9 shard_map.60.e0
  101.3 0.1 collective-permute-start.16
  101.4 3.2 %collective-permute-start.17 = (f32[24,1024]{1,0:T(8,128)S(1)}, f32[24,1024]{1,0:T(8,128)S(1)}, u32[]{:S(2)}, u32[]{:S(2)}) collective-permute-start(f32[24,1024]{1,0:T(8,128)S(1)} %shard_map.60.e0), channel_id=1, source_target_pairs={{0,96},{32,0},{64,32},{96,64},{1,97},{33,1},{65,33},{97,65},{2,98}... | collective-permute-start | bytes 294920 | tf_op jit(solution)/shard_map/ppermute | solution.py:21
  104.6 2.0 %shard_map.66 = (bf16[256,512]{1,0:T(8,128)(2,1)S(1)}, bf16[256,512]{1,0:T(8,128)(2,1)S(1)}) custom-call(s32[4]{0:T(128)S(1)} %pad_add_fusion.place, bf16[1056,768]{1,0:T(8,128)(2,1)S(1)} %get-tuple-element.63.a0.refs_0_, bf16[1056,768]{1,0:T(8,128)(2,1)S(1)} %collective-permute-done.7.a1.refs_1_, bf16[1056,768]{1,0:T(8,128)(2,1)S(1)} %collective-permute-done.8.a2.refs_2_, ...), custom_call_target="tpu_custom_call" | custom-call | flops 805306368 | bytes 3604480 | tf_op jit(solution)/shard_map/pallas_call | solution.py:475
  106.6 0.9 collective-permute-start.26
  107.5 2.4 %collective-permute-start.27 = (bf16[256,512]{1,0:T(8,128)(2,1)S(1)}, bf16[256,512]{1,0:T(8,128)(2,1)S(1)}, u32[]{:S(2)}, u32[]{:S(2)}) collective-permute-start(bf16[256,512]{1,0:T(8,128)(2,1)S(1)} %get-tuple-element.90), channel_id=1, source_target_pairs={{0,96},{32,0},{64,32},{96,64},{1,97},{33,1},{65,33},{97,65},{2,98}... | collective-permute-start | bytes 786440 | tf_op jit(solution)/shard_map/ppermute | solution.py:21
  109.9 1.2 collective-permute-done.18.e3
  111.1 2.0 %shard_map.63 = (bf16[256,512]{1,0:T(8,128)(2,1)S(1)}, bf16[256,512]{1,0:T(8,128)(2,1)S(1)}) custom-call(s32[4]{0:T(128)S(1)} %pad_add_fusion.place, bf16[1056,768]{1,0:T(8,128)(2,1)S(1)} %get-tuple-element.63.a0.refs_0_, bf16[1056,768]{1,0:T(8,128)(2,1)S(1)} %collective-permute-done.7.a1.refs_1_, bf16[1056,768]{1,0:T(8,128)(2,1)S(1)} %collective-permute-done.8.a2.refs_2_, ...), custom_call_target="tpu_custom_call" | custom-call | flops 805306368 | bytes 3604480 | tf_op jit(solution)/shard_map/pallas_call | solution.py:475
  113.2 0.1 collective-permute-start.21
  113.2 3.2 %collective-permute-start.22 = (bf16[256,512]{1,0:T(8,128)(2,1)S(1)}, bf16[256,512]{1,0:T(8,128)(2,1)S(1)}, u32[]{:S(2)}, u32[]{:S(2)}) collective-permute-start(bf16[256,512]{1,0:T(8,128)(2,1)S(1)} %get-tuple-element.86), channel_id=1, source_target_pairs={{0,96},{32,0},{64,32},{96,64},{1,97},{33,1},{65,33},{97,65},{2,98}... | collective-permute-start | bytes 786440 | tf_op jit(solution)/shard_map/ppermute | solution.py:21
  116.5 0.7 collective-permute-done.26.refs_15_
  117.1 0.0 collective-permute-done.27.refs_16_
  117.2 3.7 %shard_map.67 = (bf16[256,1024]{1,0:T(8,128)(2,1)S(1)}, bf16[256,1024]{1,0:T(8,128)(2,1)S(1)}) custom-call(s32[4]{0:T(128)S(1)} %pad_add_fusion.place, bf16[1056,768]{1,0:T(8,128)(2,1)S(1)} %get-tuple-element.63.a0.refs_0_, bf16[1056,768]{1,0:T(8,128)(2,1)S(1)} %collective-permute-done.7.a1.refs_1_, bf16[1056,768]{1,0:T(8,128)(2,1)S(1)} %collective-permute-done.8.a2.refs_2_, ...), custom_call_target="tpu_custom_call" | custom-call | flops 1610612736 | bytes 4194304 | tf_op jit(solution)/shard_map/pallas_call | solution.py:475
  120.8 1.7 %collective-permute-start.28 = (bf16[256,1024]{1,0:T(8,128)(2,1)S(1)}, bf16[256,1024]{1,0:T(8,128)(2,1)S(1)}, u32[]{:S(2)}, u32[]{:S(2)}) collective-permute-start(bf16[256,1024]{1,0:T(8,128)(2,1)S(1)} %get-tuple-element.91), channel_id=1, source_target_pairs={{0,32},{32,64},{64,96},{96,0},{1,33},{33,65},{65,97},{97,1},{2,34}... | collective-permute-start | bytes 1572872 | tf_op jit(solution)/shard_map/ppermute | solution.py:21
  122.5 1.7 %collective-permute-start.29 = (bf16[256,1024]{1,0:T(8,128)(2,1)S(1)}, bf16[256,1024]{1,0:T(8,128)(2,1)S(1)}, u32[]{:S(2)}, u32[]{:S(2)}) collective-permute-start(bf16[256,1024]{1,0:T(8,128)(2,1)S(1)} %get-tuple-element.92), channel_id=1, source_target_pairs={{0,96},{32,0},{64,32},{96,64},{1,97},{33,1},{65,33},{97,65},{2,98}... | collective-permute-start | bytes 1572872 | tf_op jit(solution)/shard_map/ppermute | solution.py:21
  124.1 3.7 %shard_map.64 = (bf16[256,1024]{1,0:T(8,128)(2,1)S(1)}, bf16[256,1024]{1,0:T(8,128)(2,1)S(1)}) custom-call(s32[4]{0:T(128)S(1)} %pad_add_fusion.place, bf16[1056,768]{1,0:T(8,128)(2,1)S(1)} %get-tuple-element.63.a0.refs_0_, bf16[1056,768]{1,0:T(8,128)(2,1)S(1)} %collective-permute-done.7.a1.refs_1_, bf16[1056,768]{1,0:T(8,128)(2,1)S(1)} %collective-permute-done.8.a2.refs_2_, ...), custom_call_target="tpu_custom_call" | custom-call | flops 1610612736 | bytes 4194304 | tf_op jit(solution)/shard_map/pallas_call | solution.py:475
  127.8 0.5 collective-permute-start.23
  128.3 2.9 %collective-permute-start.24 = (bf16[256,1024]{1,0:T(8,128)(2,1)S(1)}, bf16[256,1024]{1,0:T(8,128)(2,1)S(1)}, u32[]{:S(2)}, u32[]{:S(2)}) collective-permute-start(bf16[256,1024]{1,0:T(8,128)(2,1)S(1)} %get-tuple-element.88), channel_id=1, source_target_pairs={{0,96},{32,0},{64,32},{96,64},{1,97},{33,1},{65,33},{97,65},{2,98}... | collective-permute-start | bytes 1572872 | tf_op jit(solution)/shard_map/ppermute | solution.py:21
  131.1 0.2 shard_map.61
  131.3 0.1 collective-permute-start.20
  131.4 1.3 collective-permute-done.20.refs_17_.t_mate
  132.7 2.6 %shard_map.65.base = f32[256,1024]{1,0:T(8,128)S(1)} custom-call(s32[4]{0:T(128)S(1)} %pad_add_fusion.place, bf16[1056,768]{1,0:T(8,128)(2,1)S(1)} %get-tuple-element.63.a0.refs_0_, bf16[1056,768]{1,0:T(8,128)(2,1)S(1)} %collective-permute-done.7.a1.refs_1_, bf16[1056,768]{1,0:T(8,128)(2,1)S(1)} %collective-permute-done.8.a2.refs_2_, ...), custom_call_target="tpu_custom_call" | custom-call | flops 805306368 | bytes 3604480 | tf_op jit(solution)/shard_map/pallas_call | solution.py:475
  135.4 2.7 %shard_map.62.base = f32[256,1024]{1,0:T(8,128)S(1)} custom-call(s32[4]{0:T(128)S(1)} %pad_add_fusion.place, bf16[1056,768]{1,0:T(8,128)(2,1)S(1)} %get-tuple-element.63.a0.refs_0_, bf16[1056,768]{1,0:T(8,128)(2,1)S(1)} %collective-permute-done.7.a1.refs_1_, bf16[1056,768]{1,0:T(8,128)(2,1)S(1)} %collective-permute-done.8.a2.refs_2_, ...), custom_call_target="tpu_custom_call" | custom-call | flops 805306368 | bytes 3604480 | tf_op jit(solution)/shard_map/pallas_call | solution.py:475
  138.0 2.6 %shard_map.68.rest_0_ = f32[256,2048]{1,0:T(8,128)} custom-call(s32[4]{0:T(128)S(1)} %pad_add_fusion.place, f32[256,1024]{1,0:T(8,128)S(1)} %shard_map.65.base, bf16[256,1024]{1,0:T(8,128)(2,1)S(1)} %collective-permute-done.28.first, bf16[256,1024]{1,0:T(8,128)(2,1)S(1)} %collective-permute-done.29.second, f32[256,128]{1,0:T(8,128)S(1)} %get-tuple-element.83.refs_15_.s_left, ...), custom_call_target="tpu_custom_call" | custom-call | flops 1572864 | bytes 3145728 | tf_op jit(solution)/shard_map/pallas_call | solution.py:515
  140.6 5.0 %collective-permute-done.23.first = bf16[256,1024]{1,0:T(8,128)(2,1)S(1)} collective-permute-done((bf16[256,1024]{1,0:T(8,128)(2,1)S(1)}, bf16[256,1024]{1,0:T(8,128)(2,1)S(1)}, u32[]{:S(2)}, u32[]{:S(2)}) %collective-permute-start.23) | collective-permute-done | bytes 524320 | tf_op jit(solution)/shard_map/ppermute | solution.py:21
  145.6 2.6 %shard_map.69 = f32[256,2048]{1,0:T(8,128)} custom-call(s32[4]{0:T(128)S(1)} %pad_add_fusion.place, f32[256,1024]{1,0:T(8,128)S(1)} %shard_map.62.base, bf16[256,1024]{1,0:T(8,128)(2,1)S(1)} %collective-permute-done.23.first, bf16[256,1024]{1,0:T(8,128)(2,1)S(1)} %collective-permute-done.24.second, ...), custom_call_target="tpu_custom_call", output_to_operand_aliasing={{}: (7, {})} | custom-call | flops 1572864 | bytes 3145728 | tf_op jit(solution)/shard_map/pallas_call | solution.py:515
  (32 shorter events, 0.1 us)
Async XLA Ops:
  0.0 14.1 %copy-start.2 = (bf16[768,1024]{1,0:T(8,128)(2,1)S(1)}, bf16[768,1024]{1,0:T(8,128)(2,1)}, u32[]{:S(2)}) copy-start(bf16[768,1024]{1,0:T(8,128)(2,1)} %teacher.1) | copy-start | bytes 4718596
  0.9 9.1 %collective-permute-start = (bf16[16,1024]{1,0:T(8,128)(2,1)S(1)}, bf16[16,1024]{1,0:T(8,128)(2,1)S(1)}, u32[]{:S(2)}, u32[]{:S(2)}) collective-permute-start(bf16[16,1024]{1,0:T(8,128)(2,1)S(1)} %get-tuple-element.94), channel_id=1, source_target_pairs={{0,8},{8,16},{16,24},{24,32},{32,40},{40,48},{48,56},{56,64},{64,7... | collective-permute-start | bytes 98312 | tf_op jit(solution)/shard_map/ppermute | solution.py:544
  2.5 7.6 %collective-permute-start.1 = (bf16[16,1024]{1,0:T(8,128)(2,1)S(1)}, bf16[16,1024]{1,0:T(8,128)(2,1)S(1)}, u32[]{:S(2)}, u32[]{:S(2)}) collective-permute-start(bf16[16,1024]{1,0:T(8,128)(2,1)S(1)} %get-tuple-element.93), channel_id=1, source_target_pairs={{8,0},{16,8},{24,16},{32,24},{40,32},{48,40},{56,48},{64,56},{72,6... | collective-permute-start | bytes 98312 | tf_op jit(solution)/shard_map/ppermute | solution.py:545
  6.3 1.4 copy-start.3
  7.7 0.7 copy-start.5
  10.1 21.7 %collective-permute-start.2 = (bf16[208,1024]{1,0:T(8,128)(2,1)S(1)}, bf16[208,1024]{1,0:T(8,128)(2,1)S(1)}, u32[]{:S(2)}, u32[]{:S(2)}) collective-permute-start(bf16[208,1024]{1,0:T(8,128)(2,1)S(1)} %get-tuple-element.54), channel_id=1, source_target_pairs={{0,8},{8,16},{16,24},{24,0},{1,9},{9,17},{17,25},{25,1},{2,10},{10... | collective-permute-start | bytes 1277960 | tf_op jit(solution)/shard_map/ppermute | solution.py:21
  10.1 21.6 %collective-permute-start.3 = (bf16[208,1024]{1,0:T(8,128)(2,1)S(1)}, bf16[208,1024]{1,0:T(8,128)(2,1)S(1)}, u32[]{:S(2)}, u32[]{:S(2)}) collective-permute-start(bf16[208,1024]{1,0:T(8,128)(2,1)S(1)} %get-tuple-element.55), channel_id=1, source_target_pairs={{0,24},{8,0},{16,8},{24,16},{1,25},{9,1},{17,9},{25,17},{2,26},{10... | collective-permute-start | bytes 1277960 | tf_op jit(solution)/shard_map/ppermute | solution.py:21
  13.4 18.4 %collective-permute-start.4 = (bf16[208,1024]{1,0:T(8,128)(2,1)S(1)}, bf16[208,1024]{1,0:T(8,128)(2,1)S(1)}, u32[]{:S(2)}, u32[]{:S(2)}) collective-permute-start(bf16[208,1024]{1,0:T(8,128)(2,1)S(1)} %get-tuple-element.56), channel_id=1, source_target_pairs={{0,16},{8,24},{16,0},{24,8},{1,17},{9,25},{17,1},{25,9},{2,18},{10... | collective-permute-start | bytes 1277960 | tf_op jit(solution)/shard_map/ppermute | solution.py:21
  14.1 0.7 copy-start.4
  14.8 0.7 copy-start.6
  32.9 40.7 %collective-permute-start.7 = (bf16[1056,768]{1,0:T(8,128)(2,1)S(1)}, bf16[1056,768]{1,0:T(8,128)(2,1)S(1)}, u32[]{:S(2)}, u32[]{:S(2)}) collective-permute-start(bf16[1056,768]{1,0:T(8,128)(2,1)S(1)} %get-tuple-element.63.a0.refs_0_), channel_id=1, source_target_pairs={{0,2},{2,4},{4,6},{6,0},{1,3},{3,5},{5,7},{7,1},{8,10},{10,12},{12... | collective-permute-start | bytes 4866056 | tf_op jit(solution)/shard_map/ppermute | solution.py:21
  34.9 38.7 %collective-permute-start.8 = (bf16[1056,768]{1,0:T(8,128)(2,1)S(1)}, bf16[1056,768]{1,0:T(8,128)(2,1)S(1)}, u32[]{:S(2)}, u32[]{:S(2)}) collective-permute-start(bf16[1056,768]{1,0:T(8,128)(2,1)S(1)} %get-tuple-element.63.a0.refs_0_), channel_id=1, source_target_pairs={{0,6},{2,0},{4,2},{6,4},{1,7},{3,1},{5,3},{7,5},{8,14},{10,8},{12,... | collective-permute-start | bytes 4866056 | tf_op jit(solution)/shard_map/ppermute | solution.py:21
  37.1 36.5 %collective-permute-start.5 = (bf16[784,1024]{1,0:T(8,128)(2,1)S(1)}, bf16[784,1024]{1,0:T(8,128)(2,1)S(1)}, u32[]{:S(2)}, u32[]{:S(2)}) collective-permute-start(bf16[784,1024]{1,0:T(8,128)(2,1)S(1)} %shard_map.56.b0.refs_4_.refs_5_), channel_id=1, source_target_pairs={{0,8},{8,16},{16,24},{24,0},{1,9},{9,17},{17,25},{25,1},{2,10},{10... | collective-permute-start | bytes 4816904 | tf_op jit(solution)/shard_map/ppermute | solution.py:21
  38.0 35.6 %collective-permute-start.6 = (bf16[784,1024]{1,0:T(8,128)(2,1)S(1)}, bf16[784,1024]{1,0:T(8,128)(2,1)S(1)}, u32[]{:S(2)}, u32[]{:S(2)}) collective-permute-start(bf16[784,1024]{1,0:T(8,128)(2,1)S(1)} %shard_map.56.b0.refs_4_.refs_5_), channel_id=1, source_target_pairs={{0,24},{8,0},{16,8},{24,16},{1,25},{9,1},{17,9},{25,17},{2,26},{10... | collective-permute-start | bytes 4816904 | tf_op jit(solution)/shard_map/ppermute | solution.py:21
  40.3 33.3 %collective-permute-start.9 = (bf16[784,1024]{1,0:T(8,128)(2,1)S(1)}, bf16[784,1024]{1,0:T(8,128)(2,1)S(1)}, u32[]{:S(2)}, u32[]{:S(2)}) collective-permute-start(bf16[784,1024]{1,0:T(8,128)(2,1)S(1)} %shard_map.56.b0.refs_4_.refs_5_), channel_id=1, source_target_pairs={{0,1},{1,0},{2,3},{3,2},{4,5},{5,4},{6,7},{7,6},{8,9},{9,8},{10,11... | collective-permute-start | bytes 4816904 | tf_op jit(solution)/shard_map/ppermute | solution.py:29
  73.6 5.9 %collective-permute-start.14 = (bf16[784,1024]{1,0:T(8,128)(2,1)S(1)}, bf16[784,1024]{1,0:T(8,128)(2,1)S(1)}, u32[]{:S(2)}, u32[]{:S(2)}) collective-permute-start(bf16[784,1024]{1,0:T(8,128)(2,1)S(1)} %collective-permute-done.5.b1.refs_5_.refs_6_), channel_id=1, source_target_pairs={{0,1},{1,0},{2,3},{3,2},{4,5},{5,4},{6,7},{7,6},{8,9},{9,8},{10,11... | collective-permute-start | bytes 4816904 | tf_op jit(solution)/shard_map/ppermute | solution.py:29
  73.7 15.3 %collective-permute-start.15 = (bf16[784,1024]{1,0:T(8,128)(2,1)S(1)}, bf16[784,1024]{1,0:T(8,128)(2,1)S(1)}, u32[]{:S(2)}, u32[]{:S(2)}) collective-permute-start(bf16[784,1024]{1,0:T(8,128)(2,1)S(1)} %collective-permute-done.6.b2.refs_6_.refs_7_), channel_id=1, source_target_pairs={{0,1},{1,0},{2,3},{3,2},{4,5},{5,4},{6,7},{7,6},{8,9},{9,8},{10,11... | collective-permute-start | bytes 4816904 | tf_op jit(solution)/shard_map/ppermute | solution.py:29
  74.3 25.5 %collective-permute-start.13 = (bf16[544,768]{1,0:T(8,128)(2,1)S(1)}, bf16[544,768]{1,0:T(8,128)(2,1)S(1)}, u32[]{:S(2)}, u32[]{:S(2)}) collective-permute-start(bf16[544,768]{1,0:T(8,128)(2,1)S(1)} %slice.23), channel_id=1, source_target_pairs={{0,6},{2,0},{4,2},{6,4},{1,7},{3,1},{5,3},{7,5},{8,14},{10,8},{12,... | collective-permute-start | bytes 2506760 | tf_op jit(solution)/shard_map/ppermute | solution.py:21
  76.2 23.6 %collective-permute-start.10 = (bf16[784,512]{1,0:T(8,128)(2,1)S(1)}, bf16[784,512]{1,0:T(8,128)(2,1)S(1)}, u32[]{:S(2)}, u32[]{:S(2)}) collective-permute-start(bf16[784,512]{1,0:T(8,128)(2,1)S(1)} %slice.20), channel_id=1, source_target_pairs={{0,8},{8,16},{16,24},{24,0},{1,9},{9,17},{17,25},{25,1},{2,10},{10... | collective-permute-start | bytes 2408456 | tf_op jit(solution)/shard_map/ppermute | solution.py:21
  76.2 23.5 %collective-permute-start.11 = (bf16[784,512]{1,0:T(8,128)(2,1)S(1)}, bf16[784,512]{1,0:T(8,128)(2,1)S(1)}, u32[]{:S(2)}, u32[]{:S(2)}) collective-permute-start(bf16[784,512]{1,0:T(8,128)(2,1)S(1)} %slice.21), channel_id=1, source_target_pairs={{0,24},{8,0},{16,8},{24,16},{1,25},{9,1},{17,9},{25,17},{2,26},{10... | collective-permute-start | bytes 2408456 | tf_op jit(solution)/shard_map/ppermute | solution.py:21
  79.5 20.2 %collective-permute-start.12 = (bf16[512,768]{1,0:T(8,128)(2,1)S(1)}, bf16[512,768]{1,0:T(8,128)(2,1)S(1)}, u32[]{:S(2)}, u32[]{:S(2)}) collective-permute-start(bf16[512,768]{1,0:T(8,128)(2,1)S(1)} %slice.22), channel_id=1, source_target_pairs={{0,2},{2,4},{4,6},{6,0},{1,3},{3,5},{5,7},{7,1},{8,10},{10,12},{12... | collective-permute-start | bytes 2359304 | tf_op jit(solution)/shard_map/ppermute | solution.py:21
  99.8 4.8 %collective-permute-start.25 = (bf16[784,512]{1,0:T(8,128)(2,1)S(1)}, bf16[784,512]{1,0:T(8,128)(2,1)S(1)}, u32[]{:S(2)}, u32[]{:S(2)}) collective-permute-start(bf16[784,512]{1,0:T(8,128)(2,1)S(1)} %collective-permute-done.10.refs_7_.refs_8_), channel_id=1, source_target_pairs={{0,1},{1,0},{2,3},{3,2},{4,5},{5,4},{6,7},{7,6},{8,9},{9,8},{10,11... | collective-permute-start | bytes 2408456 | tf_op jit(solution)/shard_map/ppermute | solution.py:29
  99.9 11.3 %collective-permute-start.19 = (bf16[784,512]{1,0:T(8,128)(2,1)S(1)}, bf16[784,512]{1,0:T(8,128)(2,1)S(1)}, u32[]{:S(2)}, u32[]{:S(2)}) collective-permute-start(bf16[784,512]{1,0:T(8,128)(2,1)S(1)} %collective-permute-done.11.refs_8_), channel_id=1, source_target_pairs={{0,1},{1,0},{2,3},{3,2},{4,5},{5,4},{6,7},{7,6},{8,9},{9,8},{10,11... | collective-permute-start | bytes 2408456 | tf_op jit(solution)/shard_map/ppermute | solution.py:29
  100.4 4.2 %copy-start = (f32[1024,1024]{1,0:T(8,128)S(1)}, f32[1024,1024]{1,0:T(8,128)}, u32[]{:S(2)}) copy-start(f32[1024,1024]{1,0:T(8,128)} %shard_map.58.refs_9_) | copy-start | bytes 12582916
  100.4 4.2 %copy-start.1 = (f32[1024,1024]{1,0:T(8,128)S(1)}, f32[1024,1024]{1,0:T(8,128)}, u32[]{:S(2)}) copy-start(f32[1024,1024]{1,0:T(8,128)} %shard_map.59.refs_14_) | copy-start | bytes 12582916
  101.3 6.3 %collective-permute-start.16 = (f32[24,1024]{1,0:T(8,128)S(1)}, f32[24,1024]{1,0:T(8,128)S(1)}, u32[]{:S(2)}, u32[]{:S(2)}) collective-permute-start(f32[24,1024]{1,0:T(8,128)S(1)} %shard_map.60.e0), channel_id=1, source_target_pairs={{0,32},{32,64},{64,96},{96,0},{1,33},{33,65},{65,97},{97,1},{2,34}... | collective-permute-start | bytes 294920 | tf_op jit(solution)/shard_map/ppermute | solution.py:21
  101.4 8.6 %collective-permute-start.17 = (f32[24,1024]{1,0:T(8,128)S(1)}, f32[24,1024]{1,0:T(8,128)S(1)}, u32[]{:S(2)}, u32[]{:S(2)}) collective-permute-start(f32[24,1024]{1,0:T(8,128)S(1)} %shard_map.60.e0), channel_id=1, source_target_pairs={{0,96},{32,0},{64,32},{96,64},{1,97},{33,1},{65,33},{97,65},{2,98}... | collective-permute-start | bytes 294920 | tf_op jit(solution)/shard_map/ppermute | solution.py:21
  104.6 6.6 %collective-permute-start.18 = (f32[24,1024]{1,0:T(8,128)S(1)}, f32[24,1024]{1,0:T(8,128)S(1)}, u32[]{:S(2)}, u32[]{:S(2)}) collective-permute-start(f32[24,1024]{1,0:T(8,128)S(1)} %shard_map.60.e0), channel_id=1, source_target_pairs={{0,64},{32,96},{64,0},{96,32},{1,65},{33,97},{65,1},{97,33},{2,66}... | collective-permute-start | bytes 294920 | tf_op jit(solution)/shard_map/ppermute | solution.py:21
  106.6 10.5 %collective-permute-start.26 = (bf16[256,512]{1,0:T(8,128)(2,1)S(1)}, bf16[256,512]{1,0:T(8,128)(2,1)S(1)}, u32[]{:S(2)}, u32[]{:S(2)}) collective-permute-start(bf16[256,512]{1,0:T(8,128)(2,1)S(1)} %get-tuple-element.89), channel_id=1, source_target_pairs={{0,32},{32,64},{64,96},{96,0},{1,33},{33,65},{65,97},{97,1},{2,34}... | collective-permute-start | bytes 786440 | tf_op jit(solution)/shard_map/ppermute | solution.py:21
  107.5 9.6 %collective-permute-start.27 = (bf16[256,512]{1,0:T(8,128)(2,1)S(1)}, bf16[256,512]{1,0:T(8,128)(2,1)S(1)}, u32[]{:S(2)}, u32[]{:S(2)}) collective-permute-start(bf16[256,512]{1,0:T(8,128)(2,1)S(1)} %get-tuple-element.90), channel_id=1, source_target_pairs={{0,96},{32,0},{64,32},{96,64},{1,97},{33,1},{65,33},{97,65},{2,98}... | collective-permute-start | bytes 786440 | tf_op jit(solution)/shard_map/ppermute | solution.py:21
  113.2 11.0 %collective-permute-start.21 = (bf16[256,512]{1,0:T(8,128)(2,1)S(1)}, bf16[256,512]{1,0:T(8,128)(2,1)S(1)}, u32[]{:S(2)}, u32[]{:S(2)}) collective-permute-start(bf16[256,512]{1,0:T(8,128)(2,1)S(1)} %get-tuple-element.85), channel_id=1, source_target_pairs={{0,32},{32,64},{64,96},{96,0},{1,33},{33,65},{65,97},{97,1},{2,34}... | collective-permute-start | bytes 786440 | tf_op jit(solution)/shard_map/ppermute | solution.py:21
  113.2 10.9 %collective-permute-start.22 = (bf16[256,512]{1,0:T(8,128)(2,1)S(1)}, bf16[256,512]{1,0:T(8,128)(2,1)S(1)}, u32[]{:S(2)}, u32[]{:S(2)}) collective-permute-start(bf16[256,512]{1,0:T(8,128)(2,1)S(1)} %get-tuple-element.86), channel_id=1, source_target_pairs={{0,96},{32,0},{64,32},{96,64},{1,97},{33,1},{65,33},{97,65},{2,98}... | collective-permute-start | bytes 786440 | tf_op jit(solution)/shard_map/ppermute | solution.py:21
  120.8 17.2 %collective-permute-start.28 = (bf16[256,1024]{1,0:T(8,128)(2,1)S(1)}, bf16[256,1024]{1,0:T(8,128)(2,1)S(1)}, u32[]{:S(2)}, u32[]{:S(2)}) collective-permute-start(bf16[256,1024]{1,0:T(8,128)(2,1)S(1)} %get-tuple-element.91), channel_id=1, source_target_pairs={{0,32},{32,64},{64,96},{96,0},{1,33},{33,65},{65,97},{97,1},{2,34}... | collective-permute-start | bytes 1572872 | tf_op jit(solution)/shard_map/ppermute | solution.py:21
  122.5 15.5 %collective-permute-start.29 = (bf16[256,1024]{1,0:T(8,128)(2,1)S(1)}, bf16[256,1024]{1,0:T(8,128)(2,1)S(1)}, u32[]{:S(2)}, u32[]{:S(2)}) collective-permute-start(bf16[256,1024]{1,0:T(8,128)(2,1)S(1)} %get-tuple-element.92), channel_id=1, source_target_pairs={{0,96},{32,0},{64,32},{96,64},{1,97},{33,1},{65,33},{97,65},{2,98}... | collective-permute-start | bytes 1572872 | tf_op jit(solution)/shard_map/ppermute | solution.py:21
  127.8 17.8 %collective-permute-start.23 = (bf16[256,1024]{1,0:T(8,128)(2,1)S(1)}, bf16[256,1024]{1,0:T(8,128)(2,1)S(1)}, u32[]{:S(2)}, u32[]{:S(2)}) collective-permute-start(bf16[256,1024]{1,0:T(8,128)(2,1)S(1)} %get-tuple-element.87), channel_id=1, source_target_pairs={{0,32},{32,64},{64,96},{96,0},{1,33},{33,65},{65,97},{97,1},{2,34}... | collective-permute-start | bytes 1572872 | tf_op jit(solution)/shard_map/ppermute | solution.py:21
  128.3 17.4 %collective-permute-start.24 = (bf16[256,1024]{1,0:T(8,128)(2,1)S(1)}, bf16[256,1024]{1,0:T(8,128)(2,1)S(1)}, u32[]{:S(2)}, u32[]{:S(2)}) collective-permute-start(bf16[256,1024]{1,0:T(8,128)(2,1)S(1)} %get-tuple-element.88), channel_id=1, source_target_pairs={{0,96},{32,0},{64,32},{96,64},{1,97},{33,1},{65,33},{97,65},{2,98}... | collective-permute-start | bytes 1572872 | tf_op jit(solution)/shard_map/ppermute | solution.py:21
  131.3 1.4 collective-permute-start.20
